TPU v7x, 32 devices: a whole 2x2x4 slice. The times are simulated.
32 devices in a mesh: groups: 2 (over x), expert: 16 (over z, y, core).
Axes of the slice: x: 2, y: 2, z: 4, core: 2. Of those that a mesh axis runs over, the one named last changes fastest.
Arguments:
- hidden_states: bfloat16 [2, 512, 4096], P(None, ('groups', 'expert')), parts along dimension 1, may hold values from -6 to 6
- expert_ids: int32 [2, 512, 8], P(None, ('groups', 'expert')), parts along dimension 1, may hold values from 0 to 15, all different within a row; in each aligned block of 16 rows (0 to 15, 16 to 31, ..., all dimensions but the last counted through in order) at most 16 rows name the same one
- router_probs: float32 [2, 512, 8], P(None, ('groups', 'expert')), parts along dimension 1, may hold values from 0.05 to 1
- swap_flags: int32 [16], replicated, may hold values from 0 to 1, as said below
- w_gate: bfloat16 [16, 4096, 768], P('expert'), may hold values from -0.09375 to 0.09375
- w_up: bfloat16 [16, 4096, 768], P('expert'), may hold values from -0.09375 to 0.09375
- w_down: bfloat16 [16, 768, 4096], P('expert'), may hold values from -0.21875 to 0.21875
Outputs:
- mixed: bfloat16 [2, 512, 4096], P(None, ('groups', 'expert')), parts along dimension 1
There are 2 independent parts, one for each index of `groups`. A program takes and returns all parts, laid end to end along the dimension named above; an argument that names none is the same for every part. Nothing has to cross between parts.
Inputs may be any that keep to these rules, and one draw needn't show every extreme that they name: `expert_ids`: within one step, the 16 rows of one device (aligned blocks of 16 rows) name any one slot at most 16 times, a bound that some block reaches; the 8 ids of a row differ. swap_flags[e] equals swap_flags[e XOR 1] for every slot e.
All inputs are finite; a program needn't handle non-finite values.
Results may differ from a plain program's by a relative error of at most 0.0058.
Values may be sent and summed in bfloat16 or wider, within the bound.
No kernel may reach another device: no remote copies, remote signals or barrier semaphores. Data moves between devices by JAX's collectives and lax.ppermute only.
A program may use at most 128 MiB of HBM per device.

v0:
```python
import jax
import jax.numpy as jnp
from jax import lax
from jax.sharding import PartitionSpec as P


def expert_mlp(rows, gate_matrix, up_matrix, down_matrix):
    gate = jnp.dot(rows, gate_matrix, preferred_element_type=jnp.float32)
    up_part = jnp.dot(rows, up_matrix, preferred_element_type=jnp.float32)
    hidden = (jax.nn.silu(gate) * up_part).astype(jnp.bfloat16)
    return jnp.dot(hidden, down_matrix, preferred_element_type=jnp.float32).astype(jnp.bfloat16)


def send_back(results):
    return lax.all_to_all(results, "expert", split_axis=0, concat_axis=0, tiled=True)


def on_device(hidden_states, expert_ids, router_probs, swap_flags, w_gate, w_up, w_down):
    devices = lax.axis_size("expert")
    owner = lax.axis_index("expert")
    step_count = hidden_states.shape[0]
    tokens_here = hidden_states.shape[1]
    model_width = hidden_states.shape[2]
    top_count = expert_ids.shape[2]
    capacity = 2 * tokens_here * top_count // devices
    experts_iota = jnp.arange(devices, dtype=jnp.int32)
    own_gate = w_gate[0]
    own_up = w_up[0]
    own_down = w_down[0]
    later_gate, later_up, later_down = (own_gate, own_up, own_down)
    outputs = []
    for step_index in range(step_count):
        states = hidden_states[step_index]
        routed = expert_ids[step_index]
        weights_raw = router_probs[step_index]
        if step_index == 0:
            gate_matrix, up_matrix, down_matrix = (own_gate, own_up, own_down)
        else:
            gate_matrix, up_matrix, down_matrix = (later_gate, later_up, later_down)
            matches = (routed[:, :, None] == experts_iota[None, None, :]).astype(jnp.int32)
            flag_of = jnp.sum(matches * swap_flags[None, None, :], axis=2)
            routed = jnp.where(flag_of == 1, jnp.bitwise_xor(routed, 1), routed)
        flat_routes = routed.reshape(-1)
        onehot = (flat_routes[:, None] == experts_iota[None, :]).astype(jnp.int32)
        before = (jnp.cumsum(onehot, axis=0) - onehot) * onehot
        slot_rank = jnp.sum(before, axis=1)
        position = flat_routes * capacity + slot_rank
        everyone, all_routes = (
            lax.all_gather(states, "expert", axis=0, tiled=True),
            lax.all_gather(routed, "expert", axis=0, tiled=True),
        )
        blocks = all_routes.reshape(devices, tokens_here * top_count)
        is_mine = (blocks == owner).astype(jnp.int32)
        rank_mine = jnp.cumsum(is_mine, axis=1) - is_mine
        source = jnp.arange(devices, dtype=jnp.int32)[:, None]
        target = jnp.where(is_mine > 0, source * capacity + rank_mine, devices * capacity).reshape(
            -1
        )
        token_row = (
            source * tokens_here
            + jnp.arange(tokens_here * top_count, dtype=jnp.int32)[None, :] // top_count
        ).reshape(-1)
        row_table = (
            jnp.full((devices * capacity,), devices * tokens_here, jnp.int32)
            .at[target]
            .set(token_row, mode="drop")
        )
        padded = jnp.concatenate([everyone, jnp.zeros((1, model_width), jnp.bfloat16)], axis=0)
        results = expert_mlp(padded[row_table], gate_matrix, up_matrix, down_matrix)
        returned = send_back(results.reshape(devices, capacity, model_width))
        picked = (
            returned.reshape(-1, model_width)[position]
            .reshape(tokens_here, top_count, model_width)
            .astype(jnp.float32)
        )
        shares = weights_raw / jnp.sum(weights_raw, axis=-1, keepdims=True)
        outputs.append(jnp.sum(shares[:, :, None] * picked, axis=1).astype(jnp.bfloat16))
    return jnp.stack(outputs)


def solution(mesh):
    return jax.shard_map(
        on_device,
        mesh=mesh,
        in_specs=(
            P(None, ("groups", "expert"), None),
            P(None, ("groups", "expert"), None),
            P(None, ("groups", "expert"), None),
            P(),
            P("expert", None, None),
            P("expert", None, None),
            P("expert", None, None),
        ),
        out_specs=P(None, ("groups", "expert"), None),
        check_vma=False,
    )
```

profile of v0, /device:TPU:13, one launch (start us, length us, event | category | flops | bytes accessed | tf_op | source)
XLA Modules:
  0.0 199.0 jit_solution(17438425062962475423)
XLA Ops:
  6.5 0.0 all-gather.9.cloned.1.call-start
  6.5 1.7 fusion.51
  8.2 0.0 all-gather.9.cloned.1.call-update
  8.2 0.0 all-gather.7.cloned.1.call-start
  8.3 0.7 all-gather.7.cloned.1.call-update
  9.0 0.7 slice_bitcast_fusion.1
  9.7 0.1 copy.45
  9.8 1.1 select_reduce_fusion.1
  10.9 0.1 copy.48
  10.9 15.8 %all-gather.3 = s32[16,16,8]{1,2,0:T(8,128)S(1)} all-gather(s32[1,16,8]{1,2,0:T(8,128)S(1)} %bitcast.96), channel_id=1, replica_groups=mesh['groups'=2,'expert'=16] {'expert'}, dimensions={0}, use_global_device_ids=true | all-gather | bytes 8704 | tf_op jit(solution)/shard_map/all_gather | solution.py:50
  26.7 0.1 copy.49
  26.8 0.1 copy.50
  26.9 0.1 reshape.344
  27.1 0.1 copy.54
  27.2 22.0 %all-gather.1 = s32[1,256,8]{2,0,1:T(1,128)S(1)} all-gather(s32[1,16,8]{2,0,1:T(1,128)S(1)} %copy.54), channel_id=3, replica_groups=mesh['groups'=2,'expert'=16] {'expert'}, dimensions={1}, use_global_device_ids=true | all-gather | bytes 8704 | tf_op jit(solution)/shard_map/all_gather | solution.py:50
  49.2 0.3 reduce_window_sum.41
  49.5 0.5 broadcast.342
  50.0 1.0 fusion.50
  51.0 0.1 reshape.342
  51.1 0.3 reduce_window_sum.38
  51.4 0.1 reshape.341
  51.5 0.1 add_bitcast_fusion
  51.6 0.1 add.151
  51.7 8.0 %scatter_custom_fusion.1 = s32[256]{0:T(256)S(1)} fusion(s32[2048]{0:T(1024)S(1)} %bitcast.98, s32[2048]{0:T(1024)S(1)} %add_bitcast_fusion, s32[]{:T(128)} %constant.49.clone.1), kind=kCustom, calls=%fused_computation.75 | custom fusion | bytes 1028 | tf_op jit(solution)/shard_map/scatter | solution.py:66
  59.8 0.0 all-gather.9.cloned.1.call-done
  59.8 1.8 concatenate.7
  61.6 3.1 %gather_fusion.2 = bf16[256,4096]{1,0:T(8,128)(2,1)} fusion(bf16[257,4096]{1,0:T(8,128)(2,1)S(1)} %concatenate.7, s32[1024]{0:T(1024)S(1)} %pad_clamp_fusion.1), kind=kCustom, calls=%fused_computation.2 | custom fusion | bytes 4195328 | tf_op jit(solution)/shard_map/gather | solution.py:69
  64.8 0.0 copy-start
  64.8 5.4 %fusion.8 = f32[256,768]{1,0:T(8,128)S(1)} fusion(bf16[256,4096]{1,0:T(8,128)(2,1)} %gather_fusion.2, bf16[1,4096,768]{2,1,0:T(8,128)(2,1)} %param.11), kind=kOutput, calls=%fused_computation.14 | convolution fusion | flops 1610612736 | bytes 9175040 | tf_op jit(solution)/shard_map/dot_general | solution.py:8
  70.2 0.0 copy-done
  70.2 10.5 %fusion.15 = bf16[256,4096]{1,0:T(8,128)(2,1)} fusion(bf16[1,768,4096]{2,1,0:T(8,128)(2,1)} %param.13, bf16[256,4096]{1,0:T(8,128)(2,1)S(1)} %copy-done, bf16[1,4096,768]{2,1,0:T(8,128)(2,1)} %param.12, f32[256,768]{1,0:T(8,128)S(1)} %fusion.8), kind=kOutput, calls=%fused_computation.19 | convolution fusion | flops 3223453696 | bytes 17563648 | tf_op jit(solution)/shard_map/dot_general | solution.py:11
  80.7 6.9 %all-to-all-start.1 = ((bf16[16,16,4096]{2,1,0:T(8,128)(2,1)}), bf16[16,16,4096]{2,1,0:T(8,128)(2,1)}, u32[]{:S(2)}, u32[]{:S(2)}) async-start(bf16[16,16,4096]{2,1,0:T(8,128)(2,1)} %bitcast.88), calls=%async_computation.1 | async-start | bytes 4194304 | tf_op jit(solution)/shard_map/all_to_all | solution.py:15
  87.5 8.2 %scatter_custom_fusion = s32[256]{0:T(256)S(1)} fusion(s32[2048]{0:T(1024)S(1)} %bitcast.97, s32[2048]{0:T(1024)S(1)} %add_bitcast_fusion, s32[]{:T(128)} %constant.49.clone.1), kind=kCustom, calls=%fused_computation.77 | custom fusion | bytes 1028 | tf_op jit(solution)/shard_map/scatter | solution.py:66
  95.8 0.0 all-gather.7.cloned.1.call-done
  95.8 1.8 concatenate.6
  97.6 3.2 %gather_fusion = bf16[256,4096]{1,0:T(8,128)(2,1)} fusion(bf16[257,4096]{1,0:T(8,128)(2,1)S(1)} %concatenate.6, s32[1024]{0:T(1024)S(1)} %pad_clamp_fusion.3), kind=kCustom, calls=%fused_computation | custom fusion | bytes 4195328 | tf_op jit(solution)/shard_map/gather | solution.py:69
  100.8 5.3 %fusion.10 = f32[256,768]{1,0:T(8,128)S(1)} fusion(bf16[256,4096]{1,0:T(8,128)(2,1)} %gather_fusion, bf16[1,4096,768]{2,1,0:T(8,128)(2,1)} %param.11), kind=kOutput, calls=%fused_computation.16 | convolution fusion | flops 1610612736 | bytes 9175040 | tf_op jit(solution)/shard_map/dot_general | solution.py:8
  106.2 0.0 copy-done.1
  106.2 10.5 %fusion.12 = bf16[256,4096]{1,0:T(8,128)(2,1)} fusion(bf16[1,768,4096]{2,1,0:T(8,128)(2,1)} %param.13, bf16[256,4096]{1,0:T(8,128)(2,1)S(1)} %copy-done.1, bf16[1,4096,768]{2,1,0:T(8,128)(2,1)} %param.12, f32[256,768]{1,0:T(8,128)S(1)} %fusion.10), kind=kOutput, calls=%fused_computation.18 | convolution fusion | flops 3223453696 | bytes 17563648 | tf_op jit(solution)/shard_map/dot_general | solution.py:11
  116.7 20.4 %all-to-all-done.1 = bf16[16,16,4096]{2,1,0:T(8,128)(2,1)} async-done(((bf16[16,16,4096]{2,1,0:T(8,128)(2,1)}), bf16[16,16,4096]{2,1,0:T(8,128)(2,1)}, u32[]{:S(2)}, u32[]{:S(2)}) %all-to-all-start.1) | async-done | bytes 2097184 | tf_op jit(solution)/shard_map/all_to_all | solution.py:15
  137.1 5.0 %all-to-all-start = ((bf16[16,16,4096]{2,1,0:T(8,128)(2,1)}), bf16[16,16,4096]{2,1,0:T(8,128)(2,1)S(1)}, u32[]{:S(2)}, u32[]{:S(2)}) async-start(bf16[16,16,4096]{2,1,0:T(8,128)(2,1)} %bitcast.87), calls=%async_computation | async-start | bytes 4194304 | tf_op jit(solution)/shard_map/all_to_all | solution.py:15
  142.0 0.1 eq.106
  142.1 0.1 eq.105
  142.2 0.1 copy.52
  142.3 0.1 squeeze.38
  142.4 0.1 squeeze.37
  142.5 0.1 fusion.38
  142.6 0.2 reduce_window_sum.43
  142.7 0.0 copy-done.2
  142.8 0.1 copy.44
  142.9 0.1 copy.55
  142.9 0.1 eq.95
  143.0 0.1 fusion.39
  143.1 0.2 reduce_window_sum.40
  143.3 0.1 mul.88
  143.4 0.1 copy.42
  143.5 0.2 select_reduce_fusion
  143.7 0.2 select_reduce_fusion.2
  143.9 4.1 %gather_fusion.3 = bf16[128,4096]{1,0:T(8,128)(2,1)S(1)} fusion(bf16[256,4096]{1,0:T(8,128)(2,1)} %bitcast.23, s32[1024]{0:T(1024)S(1)} %pad_clamp_fusion), kind=kCustom, calls=%fused_computation.3 | custom fusion | bytes 2097664 | tf_op jit(solution)/shard_map/gather | solution.py:72
  148.0 0.8 fusion.18
  148.8 40.7 %all-to-all-done = bf16[16,16,4096]{2,1,0:T(8,128)(2,1)S(1)} async-done(((bf16[16,16,4096]{2,1,0:T(8,128)(2,1)}), bf16[16,16,4096]{2,1,0:T(8,128)(2,1)S(1)}, u32[]{:S(2)}, u32[]{:S(2)}) %all-to-all-start) | async-done | bytes 2097184 | tf_op jit(solution)/shard_map/all_to_all | solution.py:15
  189.4 1.2 gather_fusion.1
  190.6 0.8 fusion.19
  191.4 0.7 pad_maximum_fusion
  (20 shorter events, 0.2 us)
Async XLA Ops:
  6.5 53.3 %all-gather.9.cloned.1.call-start = ((), (), s32[]{:S(2)}) async-start(), calls=%async_computation.3 | async-start | bytes 2228224 | tf_op jit(solution)/shard_map/all_gather | solution.py:49
  8.2 87.6 %all-gather.7.cloned.1.call-start = ((), (), s32[]{:S(2)}) async-start(), calls=%async_computation.2 | async-start | bytes 2228224 | tf_op jit(solution)/shard_map/all_gather | solution.py:49
  64.8 5.4 %copy-start = (bf16[256,4096]{1,0:T(8,128)(2,1)S(1)}, bf16[256,4096]{1,0:T(8,128)(2,1)}, u32[]{:S(2)}) copy-start(bf16[256,4096]{1,0:T(8,128)(2,1)} %gather_fusion.2) | copy-start | bytes 6291460
  80.7 56.4 %all-to-all-start.1 = ((bf16[16,16,4096]{2,1,0:T(8,128)(2,1)}), bf16[16,16,4096]{2,1,0:T(8,128)(2,1)}, u32[]{:S(2)}, u32[]{:S(2)}) async-start(bf16[16,16,4096]{2,1,0:T(8,128)(2,1)} %bitcast.88), calls=%async_computation.1 | async-start | bytes 4194304 | tf_op jit(solution)/shard_map/all_to_all | solution.py:15
  100.8 5.4 %copy-start.1 = (bf16[256,4096]{1,0:T(8,128)(2,1)S(1)}, bf16[256,4096]{1,0:T(8,128)(2,1)}, u32[]{:S(2)}) copy-start(bf16[256,4096]{1,0:T(8,128)(2,1)} %gather_fusion) | copy-start | bytes 6291460
  137.1 5.7 %copy-start.2 = (f32[2,16,8]{1,2,0:T(8,128)S(1)}, f32[2,16,8]{1,2,0:T(8,128)}, u32[]{:S(2)}) copy-start(f32[2,16,8]{1,2,0:T(8,128)} %param.9) | copy-start | bytes 3076
  137.1 52.4 %all-to-all-start = ((bf16[16,16,4096]{2,1,0:T(8,128)(2,1)}), bf16[16,16,4096]{2,1,0:T(8,128)(2,1)S(1)}, u32[]{:S(2)}, u32[]{:S(2)}) async-start(bf16[16,16,4096]{2,1,0:T(8,128)(2,1)} %bitcast.87), calls=%async_computation | async-start | bytes 4194304 | tf_op jit(solution)/shard_map/all_to_all | solution.py:15
Sparse Core Ops, SparseCore 0:
  9.5 41.9 all-gather.8
  53.6 40.9 all-gather.6
where the time goes:
time: 199 us
  waiting for transfers between devices  61.8 us (31%)
  blocking collectives  37.8 us (19%)
  local copies, waits for them, and re-layouts  36.1 us (18%)
  matrix products  31.7 us (16%)
  between operations  13.7 us (7%)
  starting transfers between devices  11.9 us (6%)
  other arithmetic  6.04 us (3%)
    all_to_all x2, waiting for transfers between devices, send_back(): lax.all_to_all(results, 'expert', split_axis=0, concat_axis=0, tiled=True)  61.1 us
    all_gather x2, blocking collectives, on_device(): lax.all_gather(routed, 'expert', axis=0, tiled=True)  37.8 us
    dot_general x2, matrix products, expert_mlp(): jnp.dot(hidden, down_matrix, preferred_element_type=jnp.float32)  21 us
    scatter x2, local copies, waits for them, and re-layouts, on_device(): row_table = jnp.full((devices * capacity,), devices * tokens_here, jnp.in...  16.2 us
    all_to_all x2, starting transfers between devices, send_back(): lax.all_to_all(results, 'expert', split_axis=0, concat_axis=0, tiled=True)  11.8 us
    dot_general x2, matrix products, expert_mlp(): gate = jnp.dot(rows, gate_matrix, preferred_element_type=jnp.float32)  10.7 us
    gather x2, local copies, waits for them, and re-layouts, on_device(): results = expert_mlp(padded[row_table], gate_matrix, up_matrix, down_matrix)  6.35 us
    gather x2, local copies, waits for them, and re-layouts, on_device(): returned.reshape(-1, model_width)[position]  5.25 us
  transfers between devices with their start and end apart: 4, of which 2 were waited for; matrix products, arithmetic and copies ran while one was open for 35% of the time, Pallas kernels for 0%

commit v1 on v0

v1 whole, which is shorter than its diff:
```python
import functools

import jax
import jax.numpy as jnp
from jax import lax
from jax.experimental import pallas as pl
from jax.experimental.pallas import tpu as pltpu
from jax.sharding import PartitionSpec as P

LANES = 128
MIB = 1 << 20


def in_vmem():
    return pl.BlockSpec(memory_space=pltpu.VMEM)


def message_kernel(states_ref, ids_ref, probs_ref, *message_refs):
    width = states_ref.shape[2]
    tail = message_refs[0].shape[1] - width
    half = tail // 2
    for step, message_ref in enumerate(message_refs):
        probs = probs_ref[step]
        share = probs / jnp.sum(probs, axis=1, keepdims=True)
        ids = ids_ref[step]
        lane = lax.broadcasted_iota(jnp.int32, (ids.shape[0], tail), 1)
        slot = lane % half
        dense = jnp.zeros((ids.shape[0], tail), jnp.float32)
        for k in range(ids.shape[1]):
            dense += jnp.where(ids[:, k : k + 1] == slot, share[:, k : k + 1], 0.0)
        high = dense.astype(jnp.bfloat16).astype(jnp.float32)
        message_ref[:, :width] = states_ref[step]
        message_ref[:, width:] = jnp.where(lane < half, high, dense - high).astype(jnp.bfloat16)


def make_messages(states, ids, probs, tail):
    steps, tokens, width = states.shape
    return pl.pallas_call(
        message_kernel,
        out_shape=[jax.ShapeDtypeStruct((tokens, width + tail), jnp.bfloat16)] * steps,
        in_specs=[in_vmem()] * 3,
        out_specs=[in_vmem()] * steps,
        name="messages",
    )(states, ids, probs)


def expert_kernel(
    slot_ref, first, second, third, fourth, gate_ref, up_ref, down_ref, own_ref, other_ref, rows, hidden
):
    width, units = gate_ref.shape
    tail = first.shape[1] - width
    count = first.shape[0]
    slot = slot_ref[0]
    for part, source in enumerate((first, second, third, fourth)):
        rows[part * count : (part + 1) * count] = source[...]
    total = rows.shape[0]
    lane = lax.broadcasted_iota(jnp.int32, (total, tail), 1)
    terms = rows[:, width:].astype(jnp.float32)
    weight = jnp.sum(jnp.where(lane % (tail // 2) == slot, terms, 0.0), axis=1, keepdims=True)
    step = 256
    for at in range(0, units, step):
        gate = jnp.dot(rows[:, :width], gate_ref[:, at : at + step], preferred_element_type=jnp.float32)
        up = jnp.dot(rows[:, :width], up_ref[:, at : at + step], preferred_element_type=jnp.float32)
        value = gate / (1.0 + jnp.exp(-gate)) * up
        hidden[:, at : at + step] = (value * weight).astype(jnp.bfloat16)

    def columns(index, _):
        at = pl.ds(pl.multiple_of(index * 512, 512), 512)
        out = jnp.dot(hidden[...], down_ref[:, at], preferred_element_type=jnp.float32)
        out = out.astype(jnp.bfloat16)
        own_ref[:, at] = out[: total // 2]
        other_ref[:, at] = out[total // 2 :]
        return 0

    lax.fori_loop(0, width // 512, columns, 0)


def run_expert(slot, parts, gate, up, down):
    count = parts[0].shape[0]
    width, units = gate.shape
    gate, up, down = (pltpu.with_memory_space_constraint(w, pltpu.VMEM) for w in (gate, up, down))
    return pl.pallas_call(
        expert_kernel,
        out_shape=[jax.ShapeDtypeStruct((2 * count, width), jnp.bfloat16)] * 2,
        in_specs=[pl.BlockSpec(memory_space=pltpu.SMEM)] + [in_vmem()] * 7,
        out_specs=[in_vmem()] * 2,
        scratch_shapes=[
            pltpu.VMEM((4 * count, parts[0].shape[1]), jnp.bfloat16),
            pltpu.VMEM((4 * count, units), jnp.bfloat16),
        ],
        compiler_params=pltpu.CompilerParams(vmem_limit_bytes=28 * MIB),
        cost_estimate=pl.CostEstimate(
            flops=4 * count * width * units * 6, bytes_accessed=16 * count * width, transcendentals=0
        ),
        name="expert",
    )(slot, *parts, gate, up, down)


def on_device(states, ids, probs, flags, w_gate, w_up, w_down):
    devices = lax.axis_size("expert")
    owner = lax.axis_index("expert")
    lines = devices // 4
    steps, tokens, width = states.shape

    def index(far, near, core):
        return far * 4 + near * 2 + core

    every = [(z, y, c) for z in range(lines) for y in range(2) for c in range(2)]

    def swap_core(x):
        return lax.ppermute(x, "expert", [(index(z, y, c), index(z, y, 1 - c)) for z, y, c in every])

    def swap_near(x):
        return lax.ppermute(x, "expert", [(index(z, y, c), index(z, 1 - y, c)) for z, y, c in every])

    def shift_far(x, by):
        return lax.ppermute(x, "expert", [(index(z, y, c), index((z + by) % lines, y, c)) for z, y, c in every])

    tail = 2 * devices
    tail = -(-tail // LANES) * LANES
    messages = list(make_messages(states, ids, probs, tail))
    gate, up, down = w_gate[0], w_up[0], w_down[0]
    flag = lax.dynamic_index_in_dim(flags, owner, keepdims=True)
    outputs = []
    gathered = []
    for step in range(steps):
        message = messages[step]
        if step:
            message, _ = lax.optimization_barrier((message, gathered[step - 1][0]))
        line = jnp.concatenate([message] + [shift_far(message, by) for by in range(1, lines)], axis=0)
        near = swap_near(line)
        gathered.append((line, near, swap_core(line), swap_core(near)))
    for step in range(steps):
        slot = jnp.bitwise_xor(owner, flag) if step else jnp.full((1,), 0, jnp.int32) + owner
        own, other = run_expert(slot.astype(jnp.int32), gathered[step], gate, up, down)
        other = swap_core(other)
        half = own.shape[0] // 2
        both = own.astype(jnp.float32) + other.astype(jnp.float32)
        near = swap_near(both[half:].astype(jnp.bfloat16))
        line = both[:half] + near.astype(jnp.float32)
        line = line.reshape(lines, tokens, width)
        mixed = line[0]
        for by in range(1, lines):
            mixed += shift_far(line[by].astype(jnp.bfloat16), lines - by).astype(jnp.float32)
        outputs.append(mixed.astype(jnp.bfloat16))
    return jnp.stack(outputs)


def solution(mesh):
    rows = P(None, ("groups", "expert"), None)
    weights = P("expert", None, None)
    return jax.shard_map(
        on_device,
        mesh=mesh,
        in_specs=(rows, rows, rows, P(), weights, weights, weights),
        out_specs=rows,
        check_vma=False,
    )
```

time: 199 us -> 120 us (0.60)
  the two profiles are of different devices: /device:TPU:13 before, /device:TPU:0 now
where the time goes in v1:
time: 120 us
  waiting for transfers between devices  48.4 us (40%)
  starting transfers between devices  26.9 us (22%)
  local copies, waits for them, and re-layouts  24.1 us (20%)
  Pallas kernels  16.9 us (14%)
  other arithmetic  2.86 us (2%)
    ppermute x4, waiting for transfers between devices, swap_near(): lax.ppermute(x, 'expert', [(index(z, y, c), index(z, 1 - y, c)) for z, y,...  25.6 us
    unnamed x26, local copies, waits for them, and re-layouts  23.3 us
    ppermute x12, waiting for transfers between devices, shift_far(): lax.ppermute(x, 'expert', [(index(z, y, c), index((z + by) % lines, y, c)...  20.6 us
    ppermute x12, starting transfers between devices, shift_far(): lax.ppermute(x, 'expert', [(index(z, y, c), index((z + by) % lines, y, c)...  20.5 us
    pallas_call x2, Pallas kernels, run_expert(): pl.pallas_call(expert_kernel, out_shape=[jax.ShapeDtypeStruct((2 * count,...  15 us
    ppermute x4, starting transfers between devices, swap_near(): lax.ppermute(x, 'expert', [(index(z, y, c), index(z, 1 - y, c)) for z, y,...  5.26 us
  transfers between devices with their start and end apart: 22, of which 10 were waited for; matrix products, arithmetic and copies ran while one was open for 4% of the time, Pallas kernels for 12%

profile of v1, /device:TPU:0, one launch (start us, length us, event | category | flops | bytes accessed | tf_op | source)
XLA Modules:
  0.0 119.9 jit_solution(13329403917527401794)
XLA Ops:
  0.0 1.4 %copy.8.ids_ref = s32[2,16,8]{2,1,0:T(8,128)} copy(s32[2,16,8]{1,2,0:T(8,128)} %param.8) | data formatting | bytes 2048 | tf_op args[1]
  1.4 1.4 %copy.9.probs_ref = f32[2,16,8]{2,1,0:T(8,128)} copy(f32[2,16,8]{1,2,0:T(8,128)} %param.9) | data formatting | bytes 2048 | tf_op args[2]
  2.7 1.9 %messages.1 = (bf16[16,4224]{1,0:T(8,128)(2,1)}, bf16[16,4224]{1,0:T(8,128)(2,1)}) custom-call(bf16[2,16,4096]{2,1,0:T(8,128)(2,1)} %states_ref.1, s32[2,16,8]{2,1,0:T(8,128)} %copy.8.ids_ref, f32[2,16,8]{2,1,0:T(8,128)} %copy.9.probs_ref), custom_call_target="tpu_custom_call" | custom-call | tf_op jit(solution)/shard_map/messages/pallas_call | solution.py:38
  4.6 3.0 %collective-permute-start = (bf16[16,4224]{1,0:T(8,128)(2,1)}, bf16[16,4224]{1,0:T(8,128)(2,1)S(1)}, u32[]{:S(2)}, u32[]{:S(2)}) collective-permute-start(bf16[16,4224]{1,0:T(8,128)(2,1)} %get-tuple-element.12), channel_id=1, source_target_pairs={{0,4},{1,5},{2,6},{3,7},{4,8},{5,9},{6,10},{7,11},{8,12},{9,13},{1... | collective-permute-start | bytes 405512 | tf_op jit(solution)/shard_map/ppermute | solution.py:117
  7.7 2.6 %collective-permute-start.1 = (bf16[16,4224]{1,0:T(8,128)(2,1)}, bf16[16,4224]{1,0:T(8,128)(2,1)S(1)}, u32[]{:S(2)}, u32[]{:S(2)}) collective-permute-start(bf16[16,4224]{1,0:T(8,128)(2,1)} %get-tuple-element.12), channel_id=1, source_target_pairs={{0,8},{1,9},{2,10},{3,11},{4,12},{5,13},{6,14},{7,15},{8,0},{9,1},... | collective-permute-start | bytes 405512 | tf_op jit(solution)/shard_map/ppermute | solution.py:117
  10.2 1.3 %collective-permute-start.2 = (bf16[16,4224]{1,0:T(8,128)(2,1)}, bf16[16,4224]{1,0:T(8,128)(2,1)S(1)}, u32[]{:S(2)}, u32[]{:S(2)}) collective-permute-start(bf16[16,4224]{1,0:T(8,128)(2,1)} %get-tuple-element.12), channel_id=1, source_target_pairs={{0,12},{1,13},{2,14},{3,15},{4,0},{5,1},{6,2},{7,3},{8,4},{9,5},{1... | collective-permute-start | bytes 405512 | tf_op jit(solution)/shard_map/ppermute | solution.py:117
  11.6 0.9 constant_dynamic-update-slice_fusion.3
  12.5 1.9 %collective-permute-done = bf16[16,4224]{1,0:T(8,128)(2,1)S(1)} collective-permute-done((bf16[16,4224]{1,0:T(8,128)(2,1)}, bf16[16,4224]{1,0:T(8,128)(2,1)S(1)}, u32[]{:S(2)}, u32[]{:S(2)}) %collective-permute-start) | collective-permute-done | bytes 135200 | tf_op jit(solution)/shard_map/ppermute | solution.py:117
  14.4 4.9 %collective-permute-done.1 = bf16[16,4224]{1,0:T(8,128)(2,1)S(1)} collective-permute-done((bf16[16,4224]{1,0:T(8,128)(2,1)}, bf16[16,4224]{1,0:T(8,128)(2,1)S(1)}, u32[]{:S(2)}, u32[]{:S(2)}) %collective-permute-start.1) | collective-permute-done | bytes 135200 | tf_op jit(solution)/shard_map/ppermute | solution.py:117
  19.4 0.0 collective-permute-done.2
  19.4 3.4 %collective-permute-start.11 = (bf16[16,4224]{1,0:T(8,128)(2,1)}, bf16[16,4224]{1,0:T(8,128)(2,1)S(1)}, u32[]{:S(2)}, u32[]{:S(2)}) collective-permute-start(bf16[16,4224]{1,0:T(8,128)(2,1)} %get-tuple-element.16), channel_id=1, source_target_pairs={{0,4},{1,5},{2,6},{3,7},{4,8},{5,9},{6,10},{7,11},{8,12},{9,13},{1... | collective-permute-start | bytes 405512 | tf_op jit(solution)/shard_map/ppermute | solution.py:117
  22.8 0.9 constant_dynamic-update-slice_fusion.7
  23.7 1.7 %collective-permute-start.12 = (bf16[16,4224]{1,0:T(8,128)(2,1)}, bf16[16,4224]{1,0:T(8,128)(2,1)S(1)}, u32[]{:S(2)}, u32[]{:S(2)}) collective-permute-start(bf16[16,4224]{1,0:T(8,128)(2,1)} %get-tuple-element.16), channel_id=1, source_target_pairs={{0,8},{1,9},{2,10},{3,11},{4,12},{5,13},{6,14},{7,15},{8,0},{9,1},... | collective-permute-start | bytes 405512 | tf_op jit(solution)/shard_map/ppermute | solution.py:117
  25.5 0.7 collective-permute-start.13
  26.2 1.5 %collective-permute-start.3 = (bf16[64,4224]{1,0:T(8,128)(2,1)S(1)}, bf16[64,4224]{1,0:T(8,128)(2,1)S(1)}, u32[]{:S(2)}, u32[]{:S(2)}) collective-permute-start(bf16[64,4224]{1,0:T(8,128)(2,1)S(1)} %constant_dynamic-update-slice_fusion.first), channel_id=1, source_target_pairs={{0,2},{1,3},{2,0},{3,1},{4,6},{5,7},{6,4},{7,5},{8,10},{9,11},{10,... | collective-permute-start | bytes 1622024 | tf_op jit(solution)/shard_map/ppermute | solution.py:114
  27.7 0.0 collective-permute-start.4
  27.7 0.0 collective-permute-done.11
  27.7 5.3 %collective-permute-done.12 = bf16[16,4224]{1,0:T(8,128)(2,1)S(1)} collective-permute-done((bf16[16,4224]{1,0:T(8,128)(2,1)}, bf16[16,4224]{1,0:T(8,128)(2,1)S(1)}, u32[]{:S(2)}, u32[]{:S(2)}) %collective-permute-start.12) | collective-permute-done | bytes 135200 | tf_op jit(solution)/shard_map/ppermute | solution.py:117
  33.0 6.8 %collective-permute-done.3.second = bf16[64,4224]{1,0:T(8,128)(2,1)S(1)} collective-permute-done((bf16[64,4224]{1,0:T(8,128)(2,1)S(1)}, bf16[64,4224]{1,0:T(8,128)(2,1)S(1)}, u32[]{:S(2)}, u32[]{:S(2)}) %collective-permute-start.3) | collective-permute-done | bytes 540704 | tf_op jit(solution)/shard_map/ppermute | solution.py:114
  39.8 0.0 collective-permute-start.5
  39.8 0.0 collective-permute-done.13
  39.8 1.6 %collective-permute-start.14 = (bf16[64,4224]{1,0:T(8,128)(2,1)S(1)}, bf16[64,4224]{1,0:T(8,128)(2,1)S(1)}, u32[]{:S(2)}, u32[]{:S(2)}) collective-permute-start(bf16[64,4224]{1,0:T(8,128)(2,1)S(1)} %constant_dynamic-update-slice_fusion.4.first), channel_id=1, source_target_pairs={{0,2},{1,3},{2,0},{3,1},{4,6},{5,7},{6,4},{7,5},{8,10},{9,11},{10,... | collective-permute-start | bytes 1622024 | tf_op jit(solution)/shard_map/ppermute | solution.py:114
  41.4 0.8 copy-done.6
  42.2 0.0 collective-permute-done.5.fourth
  42.2 2.8 %copy-done = bf16[1,4096,768]{2,1,0:T(8,128)(2,1)S(1)} copy-done((bf16[1,4096,768]{2,1,0:T(8,128)(2,1)S(1)}, bf16[1,4096,768]{2,1,0:T(8,128)(2,1)}, u32[]{:S(2)}) %copy-start) | copy-done | bytes 6291480
  45.0 2.8 %copy-done.2 = bf16[1,4096,768]{2,1,0:T(8,128)(2,1)S(1)} copy-done((bf16[1,4096,768]{2,1,0:T(8,128)(2,1)S(1)}, bf16[1,4096,768]{2,1,0:T(8,128)(2,1)}, u32[]{:S(2)}) %copy-start.2) | copy-done | bytes 6291480
  47.8 2.8 %copy-done.4 = bf16[1,768,4096]{2,1,0:T(8,128)(2,1)S(1)} copy-done((bf16[1,768,4096]{2,1,0:T(8,128)(2,1)S(1)}, bf16[1,768,4096]{2,1,0:T(8,128)(2,1)}, u32[]{:S(2)}) %copy-start.4) | copy-done | bytes 6291480
  50.6 1.0 copy-done.7
  51.6 8.5 %expert.2 = (bf16[128,4096]{1,0:T(8,128)(2,1)S(1)}, bf16[128,4096]{1,0:T(8,128)(2,1)}) custom-call(s32[1]{0:T(128)} %bitcast.slot_ref, bf16[64,4224]{1,0:T(8,128)(2,1)S(1)} %constant_dynamic-update-slice_fusion.first, bf16[64,4224]{1,0:T(8,128)(2,1)S(1)} %collective-permute-done.3.second, bf16[64,4224]{1,0:T(8,128)(2,1)S(1)} %copy-done.7, ...), custom_call_target="tpu_custom_call" | custom-call | flops 4831838208 | bytes 4194304 | tf_op jit(solution)/shard_map/expert/pallas_call | solution.py:82
  60.1 0.3 collective-permute-start.6
  60.4 0.3 collective-permute-start.15
  60.6 0.3 collective-permute-start.16
  60.9 0.6 dynamic_slice.4
  62.2 1.4 %collective-permute-done.15.third = bf16[64,4224]{1,0:T(8,128)(2,1)S(1)} collective-permute-done((bf16[64,4224]{1,0:T(8,128)(2,1)S(1)}, bf16[64,4224]{1,0:T(8,128)(2,1)S(1)}, u32[]{:S(2)}, u32[]{:S(2)}) %collective-permute-start.15) | collective-permute-done | bytes 540704 | tf_op jit(solution)/shard_map/ppermute | solution.py:111
  63.6 0.8 collective-permute-done.16.fourth
  64.3 2.8 %copy-done.1 = bf16[1,4096,768]{2,1,0:T(8,128)(2,1)S(1)} copy-done((bf16[1,4096,768]{2,1,0:T(8,128)(2,1)S(1)}, bf16[1,4096,768]{2,1,0:T(8,128)(2,1)}, u32[]{:S(2)}) %copy-start.1) | copy-done | bytes 6291480
  67.1 2.8 %copy-done.3 = bf16[1,4096,768]{2,1,0:T(8,128)(2,1)S(1)} copy-done((bf16[1,4096,768]{2,1,0:T(8,128)(2,1)S(1)}, bf16[1,4096,768]{2,1,0:T(8,128)(2,1)}, u32[]{:S(2)}) %copy-start.3) | copy-done | bytes 6291480
  69.9 2.8 %copy-done.5 = bf16[1,768,4096]{2,1,0:T(8,128)(2,1)S(1)} copy-done((bf16[1,768,4096]{2,1,0:T(8,128)(2,1)S(1)}, bf16[1,768,4096]{2,1,0:T(8,128)(2,1)}, u32[]{:S(2)}) %copy-start.5) | copy-done | bytes 6291480
  72.7 6.5 %expert.3 = (bf16[128,4096]{1,0:T(8,128)(2,1)S(1)}, bf16[128,4096]{1,0:T(8,128)(2,1)S(1)}) custom-call(s32[1]{0:T(128)S(6)} %xor.4.slot_ref, bf16[64,4224]{1,0:T(8,128)(2,1)S(1)} %constant_dynamic-update-slice_fusion.4.first, bf16[64,4224]{1,0:T(8,128)(2,1)S(1)} %collective-permute-done.14.second, bf16[64,4224]{1,0:T(8,128)(2,1)S(1)} %collective-permute-done.15.third, ...), custom_call_target="tpu_custom_call" | custom-call | flops 4831838208 | bytes 4194304 | tf_op jit(solution)/shard_map/expert/pallas_call | solution.py:82
  79.2 0.3 collective-permute-start.17
  79.5 1.5 %convert_add_fusion.1 = f32[128,4096]{1,0:T(8,128)S(1)} fusion(bf16[128,4096]{1,0:T(8,128)(2,1)} %collective-permute-done.6, bf16[128,4096]{1,0:T(8,128)(2,1)S(1)} %get-tuple-element.13), kind=kLoop, calls=%fused_computation.1 | loop fusion | flops 1572864 | bytes 4194304 | tf_op jit(solution)/shard_map/add | solution.py:138
  81.0 0.1 slice.99
  81.0 1.2 collective-permute-start.7
  82.2 0.2 convert_add_fusion
  82.5 0.1 slice.98
  82.5 1.0 collective-permute-start.18
  83.5 12.3 %collective-permute-done.7 = bf16[64,4096]{1,0:T(8,128)(2,1)S(1)} collective-permute-done((bf16[64,4096]{1,0:T(8,128)(2,1)S(1)}, bf16[64,4096]{1,0:T(8,128)(2,1)S(1)}, u32[]{:S(2)}, u32[]{:S(2)}) %collective-permute-start.7) | collective-permute-done | bytes 524320 | tf_op jit(solution)/shard_map/ppermute | solution.py:114
  95.8 0.1 fusion.8
  96.0 0.1 collective-permute-start.10
  96.1 2.3 %collective-permute-start.9 = (bf16[16,4096]{1,0:T(8,128)(2,1)S(1)}, bf16[16,4096]{1,0:T(8,128)(2,1)S(1)}, u32[]{:S(2)}, u32[]{:S(2)}) collective-permute-start(bf16[16,4096]{1,0:T(8,128)(2,1)S(1)} %get-tuple-element.25), channel_id=1, source_target_pairs={{0,8},{1,9},{2,10},{3,11},{4,12},{5,13},{6,14},{7,15},{8,0},{9,1},... | collective-permute-start | bytes 393224 | tf_op jit(solution)/shard_map/ppermute | solution.py:117
  98.4 1.5 %collective-permute-start.8 = (bf16[16,4096]{1,0:T(8,128)(2,1)S(1)}, bf16[16,4096]{1,0:T(8,128)(2,1)S(1)}, u32[]{:S(2)}, u32[]{:S(2)}) collective-permute-start(bf16[16,4096]{1,0:T(8,128)(2,1)S(1)} %get-tuple-element.23), channel_id=1, source_target_pairs={{0,12},{1,13},{2,14},{3,15},{4,0},{5,1},{6,2},{7,3},{8,4},{9,5},{1... | collective-permute-start | bytes 393224 | tf_op jit(solution)/shard_map/ppermute | solution.py:117
  99.9 6.5 %collective-permute-done.18 = bf16[64,4096]{1,0:T(8,128)(2,1)S(1)} collective-permute-done((bf16[64,4096]{1,0:T(8,128)(2,1)S(1)}, bf16[64,4096]{1,0:T(8,128)(2,1)S(1)}, u32[]{:S(2)}, u32[]{:S(2)}) %collective-permute-start.18) | collective-permute-done | bytes 524320 | tf_op jit(solution)/shard_map/ppermute | solution.py:114
  106.4 0.1 fusion.9
  106.6 0.1 collective-permute-start.21
  106.7 2.3 %collective-permute-start.20 = (bf16[16,4096]{1,0:T(8,128)(2,1)S(1)}, bf16[16,4096]{1,0:T(8,128)(2,1)S(1)}, u32[]{:S(2)}, u32[]{:S(2)}) collective-permute-start(bf16[16,4096]{1,0:T(8,128)(2,1)S(1)} %get-tuple-element.28), channel_id=1, source_target_pairs={{0,8},{1,9},{2,10},{3,11},{4,12},{5,13},{6,14},{7,15},{8,0},{9,1},... | collective-permute-start | bytes 393224 | tf_op jit(solution)/shard_map/ppermute | solution.py:117
  109.0 0.0 collective-permute-done.10
  109.0 1.5 %collective-permute-start.19 = (bf16[16,4096]{1,0:T(8,128)(2,1)S(1)}, bf16[16,4096]{1,0:T(8,128)(2,1)S(1)}, u32[]{:S(2)}, u32[]{:S(2)}) collective-permute-start(bf16[16,4096]{1,0:T(8,128)(2,1)S(1)} %get-tuple-element.26), channel_id=1, source_target_pairs={{0,12},{1,13},{2,14},{3,15},{4,0},{5,1},{6,2},{7,3},{8,4},{9,5},{1... | collective-permute-start | bytes 393224 | tf_op jit(solution)/shard_map/ppermute | solution.py:117
  110.5 0.0 collective-permute-done.9
  110.5 0.0 collective-permute-done.8
  110.5 0.1 fusion.6
  110.6 4.3 %collective-permute-done.21 = bf16[16,4096]{1,0:T(8,128)(2,1)S(1)} collective-permute-done((bf16[16,4096]{1,0:T(8,128)(2,1)S(1)}, bf16[16,4096]{1,0:T(8,128)(2,1)S(1)}, u32[]{:S(2)}, u32[]{:S(2)}) %collective-permute-start.21) | collective-permute-done | bytes 131104 | tf_op jit(solution)/shard_map/ppermute | solution.py:117
  114.9 4.2 %collective-permute-done.20 = bf16[16,4096]{1,0:T(8,128)(2,1)S(1)} collective-permute-done((bf16[16,4096]{1,0:T(8,128)(2,1)S(1)}, bf16[16,4096]{1,0:T(8,128)(2,1)S(1)}, u32[]{:S(2)}, u32[]{:S(2)}) %collective-permute-start.20) | collective-permute-done | bytes 131104 | tf_op jit(solution)/shard_map/ppermute | solution.py:117
  119.1 0.1 fusion.7
  119.2 0.7 pad_maximum_fusion
  (23 shorter events, 0.2 us)
Async XLA Ops:
  4.6 9.8 %collective-permute-start = (bf16[16,4224]{1,0:T(8,128)(2,1)}, bf16[16,4224]{1,0:T(8,128)(2,1)S(1)}, u32[]{:S(2)}, u32[]{:S(2)}) collective-permute-start(bf16[16,4224]{1,0:T(8,128)(2,1)} %get-tuple-element.12), channel_id=1, source_target_pairs={{0,4},{1,5},{2,6},{3,7},{4,8},{5,9},{6,10},{7,11},{8,12},{9,13},{1... | collective-permute-start | bytes 405512 | tf_op jit(solution)/shard_map/ppermute | solution.py:117
  7.7 11.7 %collective-permute-start.1 = (bf16[16,4224]{1,0:T(8,128)(2,1)}, bf16[16,4224]{1,0:T(8,128)(2,1)S(1)}, u32[]{:S(2)}, u32[]{:S(2)}) collective-permute-start(bf16[16,4224]{1,0:T(8,128)(2,1)} %get-tuple-element.12), channel_id=1, source_target_pairs={{0,8},{1,9},{2,10},{3,11},{4,12},{5,13},{6,14},{7,15},{8,0},{9,1},... | collective-permute-start | bytes 405512 | tf_op jit(solution)/shard_map/ppermute | solution.py:117
  10.2 9.1 %collective-permute-start.2 = (bf16[16,4224]{1,0:T(8,128)(2,1)}, bf16[16,4224]{1,0:T(8,128)(2,1)S(1)}, u32[]{:S(2)}, u32[]{:S(2)}) collective-permute-start(bf16[16,4224]{1,0:T(8,128)(2,1)} %get-tuple-element.12), channel_id=1, source_target_pairs={{0,12},{1,13},{2,14},{3,15},{4,0},{5,1},{6,2},{7,3},{8,4},{9,5},{1... | collective-permute-start | bytes 405512 | tf_op jit(solution)/shard_map/ppermute | solution.py:117
  19.4 8.3 %collective-permute-start.11 = (bf16[16,4224]{1,0:T(8,128)(2,1)}, bf16[16,4224]{1,0:T(8,128)(2,1)S(1)}, u32[]{:S(2)}, u32[]{:S(2)}) collective-permute-start(bf16[16,4224]{1,0:T(8,128)(2,1)} %get-tuple-element.16), channel_id=1, source_target_pairs={{0,4},{1,5},{2,6},{3,7},{4,8},{5,9},{6,10},{7,11},{8,12},{9,13},{1... | collective-permute-start | bytes 405512 | tf_op jit(solution)/shard_map/ppermute | solution.py:117
  23.7 9.3 %collective-permute-start.12 = (bf16[16,4224]{1,0:T(8,128)(2,1)}, bf16[16,4224]{1,0:T(8,128)(2,1)S(1)}, u32[]{:S(2)}, u32[]{:S(2)}) collective-permute-start(bf16[16,4224]{1,0:T(8,128)(2,1)} %get-tuple-element.16), channel_id=1, source_target_pairs={{0,8},{1,9},{2,10},{3,11},{4,12},{5,13},{6,14},{7,15},{8,0},{9,1},... | collective-permute-start | bytes 405512 | tf_op jit(solution)/shard_map/ppermute | solution.py:117
  25.5 14.3 %collective-permute-start.13 = (bf16[16,4224]{1,0:T(8,128)(2,1)}, bf16[16,4224]{1,0:T(8,128)(2,1)S(1)}, u32[]{:S(2)}, u32[]{:S(2)}) collective-permute-start(bf16[16,4224]{1,0:T(8,128)(2,1)} %get-tuple-element.16), channel_id=1, source_target_pairs={{0,12},{1,13},{2,14},{3,15},{4,0},{5,1},{6,2},{7,3},{8,4},{9,5},{1... | collective-permute-start | bytes 405512 | tf_op jit(solution)/shard_map/ppermute | solution.py:117
  26.2 13.6 %collective-permute-start.3 = (bf16[64,4224]{1,0:T(8,128)(2,1)S(1)}, bf16[64,4224]{1,0:T(8,128)(2,1)S(1)}, u32[]{:S(2)}, u32[]{:S(2)}) collective-permute-start(bf16[64,4224]{1,0:T(8,128)(2,1)S(1)} %constant_dynamic-update-slice_fusion.first), channel_id=1, source_target_pairs={{0,2},{1,3},{2,0},{3,1},{4,6},{5,7},{6,4},{7,5},{8,10},{9,11},{10,... | collective-permute-start | bytes 1622024 | tf_op jit(solution)/shard_map/ppermute | solution.py:114
  27.7 13.7 %collective-permute-start.4 = (bf16[64,4224]{1,0:T(8,128)(2,1)S(1)}, bf16[64,4224]{1,0:T(8,128)(2,1)S(1)}, u32[]{:S(2)}, u32[]{:S(2)}) collective-permute-start(bf16[64,4224]{1,0:T(8,128)(2,1)S(1)} %constant_dynamic-update-slice_fusion.first), channel_id=1, source_target_pairs={{0,1},{1,0},{2,3},{3,2},{4,5},{5,4},{6,7},{7,6},{8,9},{9,8},{10,11... | collective-permute-start | bytes 1622024 | tf_op jit(solution)/shard_map/ppermute | solution.py:111
  39.8 2.4 %collective-permute-start.5 = (bf16[64,4224]{1,0:T(8,128)(2,1)S(1)}, bf16[64,4224]{1,0:T(8,128)(2,1)}, u32[]{:S(2)}, u32[]{:S(2)}) collective-permute-start(bf16[64,4224]{1,0:T(8,128)(2,1)S(1)} %collective-permute-done.3.second), channel_id=1, source_target_pairs={{0,1},{1,0},{2,3},{3,2},{4,5},{5,4},{6,7},{7,6},{8,9},{9,8},{10,11... | collective-permute-start | bytes 1622024 | tf_op jit(solution)/shard_map/ppermute | solution.py:111
  39.8 20.8 %collective-permute-start.14 = (bf16[64,4224]{1,0:T(8,128)(2,1)S(1)}, bf16[64,4224]{1,0:T(8,128)(2,1)S(1)}, u32[]{:S(2)}, u32[]{:S(2)}) collective-permute-start(bf16[64,4224]{1,0:T(8,128)(2,1)S(1)} %constant_dynamic-update-slice_fusion.4.first), channel_id=1, source_target_pairs={{0,2},{1,3},{2,0},{3,1},{4,6},{5,7},{6,4},{7,5},{8,10},{9,11},{10,... | collective-permute-start | bytes 1622024 | tf_op jit(solution)/shard_map/ppermute | solution.py:114
  41.4 0.8 copy-start.6
  42.2 2.8 %copy-start = (bf16[1,4096,768]{2,1,0:T(8,128)(2,1)S(1)}, bf16[1,4096,768]{2,1,0:T(8,128)(2,1)}, u32[]{:S(2)}) copy-start(bf16[1,4096,768]{2,1,0:T(8,128)(2,1)} %param.11) | copy-start | bytes 18874372
  45.0 2.8 %copy-start.2 = (bf16[1,4096,768]{2,1,0:T(8,128)(2,1)S(1)}, bf16[1,4096,768]{2,1,0:T(8,128)(2,1)}, u32[]{:S(2)}) copy-start(bf16[1,4096,768]{2,1,0:T(8,128)(2,1)} %param.12) | copy-start | bytes 18874372
  47.8 2.8 %copy-start.4 = (bf16[1,768,4096]{2,1,0:T(8,128)(2,1)S(1)}, bf16[1,768,4096]{2,1,0:T(8,128)(2,1)}, u32[]{:S(2)}) copy-start(bf16[1,768,4096]{2,1,0:T(8,128)(2,1)} %param.13) | copy-start | bytes 18874372
  50.6 1.0 copy-start.7
  51.6 9.3 %copy-start.8 = (s32[16]{0:T(128)S(1)}, s32[16]{0:T(128)}, u32[]{:S(2)}) copy-start(s32[16]{0:T(128)} %param.10) | copy-start | bytes 196
  60.1 19.4 %collective-permute-start.6 = (bf16[128,4096]{1,0:T(8,128)(2,1)}, bf16[128,4096]{1,0:T(8,128)(2,1)}, u32[]{:S(2)}, u32[]{:S(2)}) collective-permute-start(bf16[128,4096]{1,0:T(8,128)(2,1)} %get-tuple-element.14), channel_id=1, source_target_pairs={{0,1},{1,0},{2,3},{3,2},{4,5},{5,4},{6,7},{7,6},{8,9},{9,8},{10,11... | collective-permute-start | bytes 3145736 | tf_op jit(solution)/shard_map/ppermute | solution.py:111
  60.4 3.2 %collective-permute-start.15 = (bf16[64,4224]{1,0:T(8,128)(2,1)S(1)}, bf16[64,4224]{1,0:T(8,128)(2,1)S(1)}, u32[]{:S(2)}, u32[]{:S(2)}) collective-permute-start(bf16[64,4224]{1,0:T(8,128)(2,1)S(1)} %constant_dynamic-update-slice_fusion.4.first), channel_id=1, source_target_pairs={{0,1},{1,0},{2,3},{3,2},{4,5},{5,4},{6,7},{7,6},{8,9},{9,8},{10,11... | collective-permute-start | bytes 1622024 | tf_op jit(solution)/shard_map/ppermute | solution.py:111
  60.6 3.7 %collective-permute-start.16 = (bf16[64,4224]{1,0:T(8,128)(2,1)S(1)}, bf16[64,4224]{1,0:T(8,128)(2,1)S(1)}, u32[]{:S(2)}, u32[]{:S(2)}) collective-permute-start(bf16[64,4224]{1,0:T(8,128)(2,1)S(1)} %collective-permute-done.14.second), channel_id=1, source_target_pairs={{0,1},{1,0},{2,3},{3,2},{4,5},{5,4},{6,7},{7,6},{8,9},{9,8},{10,11... | collective-permute-start | bytes 1622024 | tf_op jit(solution)/shard_map/ppermute | solution.py:111
  64.3 2.8 %copy-start.1 = (bf16[1,4096,768]{2,1,0:T(8,128)(2,1)S(1)}, bf16[1,4096,768]{2,1,0:T(8,128)(2,1)}, u32[]{:S(2)}) copy-start(bf16[1,4096,768]{2,1,0:T(8,128)(2,1)} %param.11) | copy-start | bytes 18874372
  67.1 2.8 %copy-start.3 = (bf16[1,4096,768]{2,1,0:T(8,128)(2,1)S(1)}, bf16[1,4096,768]{2,1,0:T(8,128)(2,1)}, u32[]{:S(2)}) copy-start(bf16[1,4096,768]{2,1,0:T(8,128)(2,1)} %param.12) | copy-start | bytes 18874372
  69.9 2.8 %copy-start.5 = (bf16[1,768,4096]{2,1,0:T(8,128)(2,1)S(1)}, bf16[1,768,4096]{2,1,0:T(8,128)(2,1)}, u32[]{:S(2)}) copy-start(bf16[1,768,4096]{2,1,0:T(8,128)(2,1)} %param.13) | copy-start | bytes 18874372
  79.2 3.0 %collective-permute-start.17 = (bf16[128,4096]{1,0:T(8,128)(2,1)S(1)}, bf16[128,4096]{1,0:T(8,128)(2,1)S(1)}, u32[]{:S(2)}, u32[]{:S(2)}) collective-permute-start(bf16[128,4096]{1,0:T(8,128)(2,1)S(1)} %get-tuple-element.18), channel_id=1, source_target_pairs={{0,1},{1,0},{2,3},{3,2},{4,5},{5,4},{6,7},{7,6},{8,9},{9,8},{10,11... | collective-permute-start | bytes 3145736 | tf_op jit(solution)/shard_map/ppermute | solution.py:111
  81.0 14.8 %collective-permute-start.7 = (bf16[64,4096]{1,0:T(8,128)(2,1)S(1)}, bf16[64,4096]{1,0:T(8,128)(2,1)S(1)}, u32[]{:S(2)}, u32[]{:S(2)}) collective-permute-start(bf16[64,4096]{1,0:T(8,128)(2,1)S(1)} %slice.99), channel_id=1, source_target_pairs={{0,2},{1,3},{2,0},{3,1},{4,6},{5,7},{6,4},{7,5},{8,10},{9,11},{10,... | collective-permute-start | bytes 1572872 | tf_op jit(solution)/shard_map/ppermute | solution.py:114
  82.5 23.9 %collective-permute-start.18 = (bf16[64,4096]{1,0:T(8,128)(2,1)S(1)}, bf16[64,4096]{1,0:T(8,128)(2,1)S(1)}, u32[]{:S(2)}, u32[]{:S(2)}) collective-permute-start(bf16[64,4096]{1,0:T(8,128)(2,1)S(1)} %slice.98), channel_id=1, source_target_pairs={{0,2},{1,3},{2,0},{3,1},{4,6},{5,7},{6,4},{7,5},{8,10},{9,11},{10,... | collective-permute-start | bytes 1572872 | tf_op jit(solution)/shard_map/ppermute | solution.py:114
  96.0 13.0 %collective-permute-start.10 = (bf16[16,4096]{1,0:T(8,128)(2,1)S(1)}, bf16[16,4096]{1,0:T(8,128)(2,1)S(1)}, u32[]{:S(2)}, u32[]{:S(2)}) collective-permute-start(bf16[16,4096]{1,0:T(8,128)(2,1)S(1)} %get-tuple-element.24), channel_id=1, source_target_pairs={{0,4},{1,5},{2,6},{3,7},{4,8},{5,9},{6,10},{7,11},{8,12},{9,13},{1... | collective-permute-start | bytes 393224 | tf_op jit(solution)/shard_map/ppermute | solution.py:117
  96.1 14.4 %collective-permute-start.9 = (bf16[16,4096]{1,0:T(8,128)(2,1)S(1)}, bf16[16,4096]{1,0:T(8,128)(2,1)S(1)}, u32[]{:S(2)}, u32[]{:S(2)}) collective-permute-start(bf16[16,4096]{1,0:T(8,128)(2,1)S(1)} %get-tuple-element.25), channel_id=1, source_target_pairs={{0,8},{1,9},{2,10},{3,11},{4,12},{5,13},{6,14},{7,15},{8,0},{9,1},... | collective-permute-start | bytes 393224 | tf_op jit(solution)/shard_map/ppermute | solution.py:117
  98.4 12.1 %collective-permute-start.8 = (bf16[16,4096]{1,0:T(8,128)(2,1)S(1)}, bf16[16,4096]{1,0:T(8,128)(2,1)S(1)}, u32[]{:S(2)}, u32[]{:S(2)}) collective-permute-start(bf16[16,4096]{1,0:T(8,128)(2,1)S(1)} %get-tuple-element.23), channel_id=1, source_target_pairs={{0,12},{1,13},{2,14},{3,15},{4,0},{5,1},{6,2},{7,3},{8,4},{9,5},{1... | collective-permute-start | bytes 393224 | tf_op jit(solution)/shard_map/ppermute | solution.py:117
  106.6 8.3 %collective-permute-start.21 = (bf16[16,4096]{1,0:T(8,128)(2,1)S(1)}, bf16[16,4096]{1,0:T(8,128)(2,1)S(1)}, u32[]{:S(2)}, u32[]{:S(2)}) collective-permute-start(bf16[16,4096]{1,0:T(8,128)(2,1)S(1)} %get-tuple-element.27), channel_id=1, source_target_pairs={{0,4},{1,5},{2,6},{3,7},{4,8},{5,9},{6,10},{7,11},{8,12},{9,13},{1... | collective-permute-start | bytes 393224 | tf_op jit(solution)/shard_map/ppermute | solution.py:117
  106.7 12.4 %collective-permute-start.20 = (bf16[16,4096]{1,0:T(8,128)(2,1)S(1)}, bf16[16,4096]{1,0:T(8,128)(2,1)S(1)}, u32[]{:S(2)}, u32[]{:S(2)}) collective-permute-start(bf16[16,4096]{1,0:T(8,128)(2,1)S(1)} %get-tuple-element.28), channel_id=1, source_target_pairs={{0,8},{1,9},{2,10},{3,11},{4,12},{5,13},{6,14},{7,15},{8,0},{9,1},... | collective-permute-start | bytes 393224 | tf_op jit(solution)/shard_map/ppermute | solution.py:117
  109.0 10.1 %collective-permute-start.19 = (bf16[16,4096]{1,0:T(8,128)(2,1)S(1)}, bf16[16,4096]{1,0:T(8,128)(2,1)S(1)}, u32[]{:S(2)}, u32[]{:S(2)}) collective-permute-start(bf16[16,4096]{1,0:T(8,128)(2,1)S(1)} %get-tuple-element.26), channel_id=1, source_target_pairs={{0,12},{1,13},{2,14},{3,15},{4,0},{5,1},{6,2},{7,3},{8,4},{9,5},{1... | collective-permute-start | bytes 393224 | tf_op jit(solution)/shard_map/ppermute | solution.py:117

commit v2 on v1

v2 whole, which is shorter than its diff:
```python
import functools

import jax
import jax.numpy as jnp
from jax import lax
from jax.experimental import pallas as pl
from jax.experimental.pallas import tpu as pltpu
from jax.sharding import PartitionSpec as P

LANES = 128
MIB = 1 << 20


def in_vmem():
    return pl.BlockSpec(memory_space=pltpu.VMEM)


def message_kernel(states_ref, ids_ref, probs_ref, message_ref):
    tokens, width = states_ref.shape
    tail = message_ref.shape[1] - width
    half = tail // 2
    probs = probs_ref[...]
    share = probs / jnp.sum(probs, axis=0, keepdims=True)
    ids = ids_ref[...]
    place = lax.broadcasted_iota(jnp.int32, (tail, tokens), 0)
    dense = jnp.zeros((tail, tokens), jnp.float32)
    for k in range(ids.shape[0]):
        dense += jnp.where(ids[k : k + 1] == place % half, share[k : k + 1], 0.0)
    high = dense.astype(jnp.bfloat16).astype(jnp.float32)
    terms = jnp.where(place < half, high, dense - high).astype(jnp.bfloat16)
    row = lax.broadcasted_iota(jnp.int32, (tokens, tokens), 0)
    column = lax.broadcasted_iota(jnp.int32, (tokens, tokens), 1)
    one = jnp.where(row == column, 1.0, 0.0).astype(jnp.bfloat16)
    upright = lax.dot_general(one, terms, (((1,), (1,)), ((), ())), preferred_element_type=jnp.float32)
    message_ref[:, :width] = states_ref[...]
    message_ref[:, width:] = upright.astype(jnp.bfloat16)


def make_message(states, ids, probs, step, tail):
    _, tokens, width = states.shape

    def of_step(x):
        return pl.BlockSpec((None,) + x.shape[1:], lambda i: (step, 0, 0))

    return pl.pallas_call(
        message_kernel,
        grid=(1,),
        out_shape=jax.ShapeDtypeStruct((tokens, width + tail), jnp.bfloat16),
        in_specs=[of_step(states), of_step(ids), of_step(probs)],
        out_specs=pl.BlockSpec((tokens, width + tail), lambda i: (0, 0)),
        compiler_params=pltpu.CompilerParams(vmem_limit_bytes=4 * MIB),
        name="message",
    )(states, ids, probs)


def load_kernel(*refs):
    count = len(refs) // 3
    copies = [
        pltpu.make_async_copy(refs[i], refs[count + i], refs[2 * count + i]) for i in range(count)
    ]
    for copy in copies:
        copy.start()
    for copy in copies:
        copy.wait()


def load_weights(*arrays):
    arrays = [pltpu.with_memory_space_constraint(x, pltpu.HBM) for x in arrays]
    return pl.pallas_call(
        load_kernel,
        out_shape=[pltpu.VMEM(x.shape, x.dtype) for x in arrays],
        in_specs=[pl.BlockSpec(memory_space=pltpu.HBM)] * len(arrays),
        out_specs=[in_vmem()] * len(arrays),
        scratch_shapes=[pltpu.SemaphoreType.DMA(())] * len(arrays),
        cost_estimate=pl.CostEstimate(
            flops=0, bytes_accessed=sum(2 * x.size for x in arrays), transcendentals=0
        ),
        compiler_params=pltpu.CompilerParams(vmem_limit_bytes=4 * MIB),
        name="load_weights",
    )(*arrays)


def expert_kernel(
    swapped, flags_ref, first, second, third, fourth, gate_ref, up_ref, down_ref, own_ref, near_ref, other_ref, rows, hidden
):
    width, units = gate_ref.shape
    tail = first.shape[1] - width
    count = first.shape[0]
    owner = lax.axis_index("expert")
    slot = jnp.bitwise_xor(owner, flags_ref[owner]) if swapped else owner
    for part, source in enumerate((first, second, third, fourth)):
        rows[part * count : (part + 1) * count] = source[...]
    total = rows.shape[0]
    lane = lax.broadcasted_iota(jnp.int32, (total, tail), 1)
    terms = rows[:, width:].astype(jnp.float32)
    weight = jnp.sum(jnp.where(lane % (tail // 2) == slot, terms, 0.0), axis=1, keepdims=True)
    step = 256
    for at in range(0, units, step):
        gate = jnp.dot(rows[:, :width], gate_ref[:, at : at + step], preferred_element_type=jnp.float32)
        up = jnp.dot(rows[:, :width], up_ref[:, at : at + step], preferred_element_type=jnp.float32)
        value = gate / (1.0 + jnp.exp(-gate)) * up
        hidden[:, at : at + step] = (value * weight).astype(jnp.bfloat16)

    def columns(index, _):
        at = pl.ds(pl.multiple_of(index * 512, 512), 512)
        out = jnp.dot(hidden[...], down_ref[:, at], preferred_element_type=jnp.float32)
        out = out.astype(jnp.bfloat16)
        own_ref[:, at] = out[:count]
        near_ref[:, at] = out[count : 2 * count]
        other_ref[:, at] = out[2 * count :]
        return 0

    lax.fori_loop(0, width // 512, columns, 0)


def run_expert(swapped, flags, parts, gate, up, down):
    count = parts[0].shape[0]
    width, units = gate.shape
    gate, up, down = (pltpu.with_memory_space_constraint(w, pltpu.VMEM) for w in (gate, up, down))
    return pl.pallas_call(
        functools.partial(expert_kernel, swapped),
        out_shape=[jax.ShapeDtypeStruct((k * count, width), jnp.bfloat16) for k in (1, 1, 2)],
        in_specs=[pl.BlockSpec(memory_space=pltpu.SMEM)] + [in_vmem()] * 7,
        out_specs=[in_vmem()] * 3,
        scratch_shapes=[
            pltpu.VMEM((4 * count, parts[0].shape[1]), jnp.bfloat16),
            pltpu.VMEM((4 * count, units), jnp.bfloat16),
        ],
        compiler_params=pltpu.CompilerParams(vmem_limit_bytes=16 * MIB),
        cost_estimate=pl.CostEstimate(
            flops=4 * count * width * units * 6, bytes_accessed=16 * count * width, transcendentals=0
        ),
        name="expert",
    )(flags, *parts, gate, up, down)


def on_device(states, ids, probs, flags, w_gate, w_up, w_down):
    devices = lax.axis_size("expert")
    lines = devices // 4
    steps, tokens, width = states.shape

    def index(far, near, core):
        return far * 4 + near * 2 + core

    every = [(z, y, c) for z in range(lines) for y in range(2) for c in range(2)]

    def swap_core(x):
        return lax.ppermute(x, "expert", [(index(z, y, c), index(z, y, 1 - c)) for z, y, c in every])

    def swap_near(x):
        return lax.ppermute(x, "expert", [(index(z, y, c), index(z, 1 - y, c)) for z, y, c in every])

    def shift_far(x, by):
        return lax.ppermute(x, "expert", [(index(z, y, c), index((z + by) % lines, y, c)) for z, y, c in every])

    tail = 2 * devices
    tail = -(-tail // LANES) * LANES
    ids, probs = jnp.swapaxes(ids, 1, 2), jnp.swapaxes(probs, 1, 2)
    weights = load_weights(w_gate[0], w_up[0], w_down[0])
    messages = [make_message(states, ids, probs, step, tail) for step in range(steps)]
    gathered = []
    for step in range(steps):
        message = messages[step]
        if step:
            message, _ = lax.optimization_barrier((message, gathered[step - 1][2]))
        blocks = [message] + [shift_far(message, by) for by in range(1, lines)]
        if not step:
            blocks, weights, messages[1:] = lax.optimization_barrier((blocks, weights, messages[1:]))
        line = jnp.concatenate(blocks, axis=0)
        near = swap_near(line)
        gathered.append((line, near, swap_core(line), swap_core(near)))
    outputs = []
    other = None
    for step in range(steps):
        parts = gathered[step]
        if step:
            parts, _ = lax.optimization_barrier((parts, other))
        own, peer, other = run_expert(step > 0, flags, parts, *weights)
        other = swap_core(other)
        half = own.shape[0]
        peer = peer.astype(jnp.float32) + other[half:].astype(jnp.float32)
        near = swap_near(peer.astype(jnp.bfloat16))
        line = own.astype(jnp.float32) + other[:half].astype(jnp.float32) + near.astype(jnp.float32)
        line = line.reshape(lines, tokens, width)
        mixed = line[0]
        for by in range(1, lines):
            mixed += shift_far(line[by].astype(jnp.bfloat16), lines - by).astype(jnp.float32)
        outputs.append(mixed.astype(jnp.bfloat16))
    return jnp.stack(outputs)


def solution(mesh):
    rows = P(None, ("groups", "expert"), None)
    weights = P("expert", None, None)
    return jax.shard_map(
        on_device,
        mesh=mesh,
        in_specs=(rows, rows, rows, P(), weights, weights, weights),
        out_specs=rows,
        check_vma=False,
    )
```

time: 120 us -> 101 us (0.84)
  local copies, waits for them, and re-layouts: 24.1 us -> 2.52 us
  Pallas kernels: 16.9 us -> 20.8 us
  starting transfers between devices: 26.9 us -> 29.9 us
  waiting for transfers between devices: 48.4 us -> 46 us
  other arithmetic: 2.86 us -> 1.49 us
    unnamed x26 -> x14, local copies, waits for them, and re-layouts: 23.3 us -> 2.43 us
    ppermute x12, waiting for transfers between devices: 20.6 us -> 12.7 us  [shift_far(): lax.ppermute(x, 'expert', [(index(z, y, c), index((z + by) % lines, y, c)...]
    ppermute x4, waiting for transfers between devices: 25.6 us -> 32.2 us  [swap_near(): lax.ppermute(x, 'expert', [(index(z, y, c), index(z, 1 - y, c)) for z, y,...]
    pallas_call x3 -> x5, Pallas kernels: 16.9 us -> 20.8 us  [the longest x2 14 us: run_expert(): pl.pallas_call(functools.partial(expert_kernel, swapped), out_shape=[jax....]
    ppermute x12, starting transfers between devices: 20.5 us -> 22.9 us  [shift_far(): lax.ppermute(x, 'expert', [(index(z, y, c), index((z + by) % lines, y, c)...]
    add x2 -> x0, other arithmetic: 1.71 us -> none  [on_device(): both = own.astype(jnp.float32) + other.astype(jnp.float32)]
  transfers between devices with their start and end apart: 22 -> 22, of which waited for: 10 -> 11; matrix products, arithmetic and copies ran while one was open for 4% -> 1% of each run, Pallas kernels for 12% -> 20%
where the time goes in v2:
time: 101 us
  waiting for transfers between devices  46 us (46%)
  starting transfers between devices  29.9 us (30%)
  Pallas kernels  20.8 us (21%)
  local copies, waits for them, and re-layouts  2.52 us (2%)
  other arithmetic  1.49 us (1%)
    ppermute x4, waiting for transfers between devices, swap_near(): lax.ppermute(x, 'expert', [(index(z, y, c), index(z, 1 - y, c)) for z, y,...  32.2 us
    ppermute x12, starting transfers between devices, shift_far(): lax.ppermute(x, 'expert', [(index(z, y, c), index((z + by) % lines, y, c)...  22.9 us
    pallas_call x2, Pallas kernels, run_expert(): pl.pallas_call(functools.partial(expert_kernel, swapped), out_shape=[jax....  14 us
    ppermute x12, waiting for transfers between devices, shift_far(): lax.ppermute(x, 'expert', [(index(z, y, c), index((z + by) % lines, y, c)...  12.7 us
    pallas_call x1, Pallas kernels, load_weights(): pl.pallas_call(load_kernel, out_shape=[pltpu.VMEM(x.shape, x.dtype) for x...  6.44 us
    ppermute x4, starting transfers between devices, swap_near(): lax.ppermute(x, 'expert', [(index(z, y, c), index(z, 1 - y, c)) for z, y,...  6.42 us
    unnamed x14, local copies, waits for them, and re-layouts  2.43 us
  transfers between devices with their start and end apart: 22, of which 11 were waited for; matrix products, arithmetic and copies ran while one was open for 1% of the time, Pallas kernels for 20%

profile of v2, /device:TPU:0, one launch (start us, length us, event | category | flops | bytes accessed | tf_op | source)
XLA Modules:
  0.0 100.8 jit_solution(9422589125500227637)
XLA Ops:
  0.0 0.0 copy-start
  0.0 0.9 copy-done
  1.0 0.0 copy-start.1
  1.0 0.7 copy-done.1
  1.6 0.0 copy-start.2
  1.7 0.7 copy-done.2
  2.3 0.2 message.2
  2.5 3.0 %collective-permute-start = (bf16[16,4224]{1,0:T(8,128)(2,1)S(1)}, bf16[16,4224]{1,0:T(8,128)(2,1)S(1)}, u32[]{:S(2)}, u32[]{:S(2)}) collective-permute-start(bf16[16,4224]{1,0:T(8,128)(2,1)S(1)} %message.2), channel_id=1, source_target_pairs={{0,4},{1,5},{2,6},{3,7},{4,8},{5,9},{6,10},{7,11},{8,12},{9,13},{1... | collective-permute-start | bytes 405512 | tf_op jit(solution)/shard_map/ppermute | solution.py:154
  5.6 2.6 %collective-permute-start.1 = (bf16[16,4224]{1,0:T(8,128)(2,1)S(1)}, bf16[16,4224]{1,0:T(8,128)(2,1)S(1)}, u32[]{:S(2)}, u32[]{:S(2)}) collective-permute-start(bf16[16,4224]{1,0:T(8,128)(2,1)S(1)} %message.2), channel_id=1, source_target_pairs={{0,8},{1,9},{2,10},{3,11},{4,12},{5,13},{6,14},{7,15},{8,0},{9,1},... | collective-permute-start | bytes 405512 | tf_op jit(solution)/shard_map/ppermute | solution.py:154
  8.2 1.3 %collective-permute-start.2 = (bf16[16,4224]{1,0:T(8,128)(2,1)S(1)}, bf16[16,4224]{1,0:T(8,128)(2,1)S(1)}, u32[]{:S(2)}, u32[]{:S(2)}) collective-permute-start(bf16[16,4224]{1,0:T(8,128)(2,1)S(1)} %message.2), channel_id=1, source_target_pairs={{0,12},{1,13},{2,14},{3,15},{4,0},{5,1},{6,2},{7,3},{8,4},{9,5},{1... | collective-permute-start | bytes 405512 | tf_op jit(solution)/shard_map/ppermute | solution.py:154
  9.5 0.2 message.3
  9.7 0.0 copy-start.3
  9.7 6.4 %load_weights.1 = (bf16[4096,768]{1,0:T(8,128)(2,1)S(1)}, bf16[4096,768]{1,0:T(8,128)(2,1)S(1)}, bf16[768,4096]{1,0:T(8,128)(2,1)S(1)}) custom-call(bf16[4096,768]{1,0:T(8,128)(2,1)} %bitcast.13, bf16[4096,768]{1,0:T(8,128)(2,1)} %bitcast.14, bf16[768,4096]{1,0:T(8,128)(2,1)} %bitcast.15), custom_call_target="tpu_custom_call" | custom-call | bytes 18874368 | tf_op jit(solution)/shard_map/load_weights/pallas_call | solution.py:69
  16.1 0.0 collective-permute-done
  16.1 0.9 collective-permute-done.1
  17.1 0.0 collective-permute-done.2
  17.1 0.1 collective-permute-start.4
  17.2 1.6 %collective-permute-start.3 = (bf16[64,4224]{1,0:T(8,128)(2,1)S(1)}, bf16[64,4224]{1,0:T(8,128)(2,1)S(1)}, u32[]{:S(2)}, u32[]{:S(2)}) collective-permute-start(bf16[64,4224]{1,0:T(8,128)(2,1)S(1)} %constant_dynamic-update-slice_fusion.first), channel_id=1, source_target_pairs={{0,2},{1,3},{2,0},{3,1},{4,6},{5,7},{6,4},{7,5},{8,10},{9,11},{10,... | collective-permute-start | bytes 1622024 | tf_op jit(solution)/shard_map/ppermute | solution.py:151
  18.8 0.3 collective-permute-done.4.third
  19.1 3.4 %collective-permute-start.11 = (bf16[16,4224]{1,0:T(8,128)(2,1)S(1)}, bf16[16,4224]{1,0:T(8,128)(2,1)S(1)}, u32[]{:S(2)}, u32[]{:S(2)}) collective-permute-start(bf16[16,4224]{1,0:T(8,128)(2,1)S(1)} %message.3), channel_id=1, source_target_pairs={{0,4},{1,5},{2,6},{3,7},{4,8},{5,9},{6,10},{7,11},{8,12},{9,13},{1... | collective-permute-start | bytes 405512 | tf_op jit(solution)/shard_map/ppermute | solution.py:154
  22.5 1.7 %collective-permute-start.12 = (bf16[16,4224]{1,0:T(8,128)(2,1)S(1)}, bf16[16,4224]{1,0:T(8,128)(2,1)S(1)}, u32[]{:S(2)}, u32[]{:S(2)}) collective-permute-start(bf16[16,4224]{1,0:T(8,128)(2,1)S(1)} %message.3), channel_id=1, source_target_pairs={{0,8},{1,9},{2,10},{3,11},{4,12},{5,13},{6,14},{7,15},{8,0},{9,1},... | collective-permute-start | bytes 405512 | tf_op jit(solution)/shard_map/ppermute | solution.py:154
  24.2 0.7 collective-permute-start.13
  24.9 7.0 %collective-permute-done.3.second = bf16[64,4224]{1,0:T(8,128)(2,1)S(1)} collective-permute-done((bf16[64,4224]{1,0:T(8,128)(2,1)S(1)}, bf16[64,4224]{1,0:T(8,128)(2,1)S(1)}, u32[]{:S(2)}, u32[]{:S(2)}) %collective-permute-start.3) | collective-permute-done | bytes 540704 | tf_op jit(solution)/shard_map/ppermute | solution.py:151
  31.9 0.0 collective-permute-start.5
  31.9 0.0 collective-permute-done.11
  31.9 1.4 %collective-permute-done.12 = bf16[16,4224]{1,0:T(8,128)(2,1)S(1)} collective-permute-done((bf16[16,4224]{1,0:T(8,128)(2,1)S(1)}, bf16[16,4224]{1,0:T(8,128)(2,1)S(1)}, u32[]{:S(2)}, u32[]{:S(2)}) %collective-permute-start.12) | collective-permute-done | bytes 135200 | tf_op jit(solution)/shard_map/ppermute | solution.py:154
  33.4 0.5 collective-permute-done.5.fourth
  33.8 0.0 copy-done.3
  33.8 7.0 %expert.2 = (bf16[64,4096]{1,0:T(8,128)(2,1)S(1)}, bf16[64,4096]{1,0:T(8,128)(2,1)S(1)}, bf16[128,4096]{1,0:T(8,128)(2,1)S(1)}) custom-call(s32[16]{0:T(128)S(1)} %copy-done.3, bf16[64,4224]{1,0:T(8,128)(2,1)S(1)} %constant_dynamic-update-slice_fusion.first, bf16[64,4224]{1,0:T(8,128)(2,1)S(1)} %collective-permute-done.3.second, ...), custom_call_target="tpu_custom_call" | custom-call | flops 4831838208 | bytes 4194304 | tf_op jit(solution)/shard_map/expert/pallas_call | solution.py:120
  40.9 0.2 collective-permute-start.6
  41.1 0.0 collective-permute-done.13
  41.1 1.6 %collective-permute-start.14 = (bf16[64,4224]{1,0:T(8,128)(2,1)S(1)}, bf16[64,4224]{1,0:T(8,128)(2,1)S(1)}, u32[]{:S(2)}, u32[]{:S(2)}) collective-permute-start(bf16[64,4224]{1,0:T(8,128)(2,1)S(1)} %constant_dynamic-update-slice_fusion.4.first), channel_id=1, source_target_pairs={{0,2},{1,3},{2,0},{3,1},{4,6},{5,7},{6,4},{7,5},{8,10},{9,11},{10,... | collective-permute-start | bytes 1622024 | tf_op jit(solution)/shard_map/ppermute | solution.py:151
  42.7 0.1 collective-permute-start.15
  42.8 12.9 %collective-permute-done.14.second = bf16[64,4224]{1,0:T(8,128)(2,1)S(1)} collective-permute-done((bf16[64,4224]{1,0:T(8,128)(2,1)S(1)}, bf16[64,4224]{1,0:T(8,128)(2,1)S(1)}, u32[]{:S(2)}, u32[]{:S(2)}) %collective-permute-start.14) | collective-permute-done | bytes 540704 | tf_op jit(solution)/shard_map/ppermute | solution.py:151
  55.7 0.0 collective-permute-start.16
  55.7 0.0 collective-permute-done.6
  55.7 0.1 add_convert_fusion.1
  55.8 1.6 %collective-permute-start.7 = (bf16[64,4096]{1,0:T(8,128)(2,1)S(1)}, bf16[64,4096]{1,0:T(8,128)(2,1)S(1)}, u32[]{:S(2)}, u32[]{:S(2)}) collective-permute-start(bf16[64,4096]{1,0:T(8,128)(2,1)S(1)} %add_convert_fusion.1), channel_id=1, source_target_pairs={{0,2},{1,3},{2,0},{3,1},{4,6},{5,7},{6,4},{7,5},{8,10},{9,11},{10,... | collective-permute-start | bytes 1572872 | tf_op jit(solution)/shard_map/ppermute | solution.py:151
  57.5 0.0 collective-permute-done.15.third
  57.5 0.2 collective-permute-done.16.fourth
  57.6 7.0 %expert.3 = (bf16[64,4096]{1,0:T(8,128)(2,1)S(1)}, bf16[64,4096]{1,0:T(8,128)(2,1)S(1)}, bf16[128,4096]{1,0:T(8,128)(2,1)S(1)}) custom-call(s32[16]{0:T(128)S(1)} %copy-done.3, bf16[64,4224]{1,0:T(8,128)(2,1)S(1)} %constant_dynamic-update-slice_fusion.4.first, bf16[64,4224]{1,0:T(8,128)(2,1)S(1)} %collective-permute-done.14.second, ...), custom_call_target="tpu_custom_call" | custom-call | flops 4831838208 | bytes 4194304 | tf_op jit(solution)/shard_map/expert/pallas_call | solution.py:120
  64.6 0.2 collective-permute-start.17
  64.8 5.4 %collective-permute-done.7 = bf16[64,4096]{1,0:T(8,128)(2,1)S(1)} collective-permute-done((bf16[64,4096]{1,0:T(8,128)(2,1)S(1)}, bf16[64,4096]{1,0:T(8,128)(2,1)S(1)}, u32[]{:S(2)}, u32[]{:S(2)}) %collective-permute-start.7) | collective-permute-done | bytes 524320 | tf_op jit(solution)/shard_map/ppermute | solution.py:151
  70.2 0.2 fusion.8
  70.4 0.0 collective-permute-done.17
  70.5 0.1 add_convert_fusion
  70.6 1.6 %collective-permute-start.18 = (bf16[64,4096]{1,0:T(8,128)(2,1)S(1)}, bf16[64,4096]{1,0:T(8,128)(2,1)S(1)}, u32[]{:S(2)}, u32[]{:S(2)}) collective-permute-start(bf16[64,4096]{1,0:T(8,128)(2,1)S(1)} %add_convert_fusion), channel_id=1, source_target_pairs={{0,2},{1,3},{2,0},{3,1},{4,6},{5,7},{6,4},{7,5},{8,10},{9,11},{10,... | collective-permute-start | bytes 1572872 | tf_op jit(solution)/shard_map/ppermute | solution.py:151
  72.2 3.4 %collective-permute-start.10 = (bf16[16,4096]{1,0:T(8,128)(2,1)S(1)}, bf16[16,4096]{1,0:T(8,128)(2,1)S(1)}, u32[]{:S(2)}, u32[]{:S(2)}) collective-permute-start(bf16[16,4096]{1,0:T(8,128)(2,1)S(1)} %get-tuple-element.54), channel_id=1, source_target_pairs={{0,4},{1,5},{2,6},{3,7},{4,8},{5,9},{6,10},{7,11},{8,12},{9,13},{1... | collective-permute-start | bytes 393224 | tf_op jit(solution)/shard_map/ppermute | solution.py:154
  75.7 1.1 %collective-permute-start.8 = (bf16[16,4096]{1,0:T(8,128)(2,1)S(1)}, bf16[16,4096]{1,0:T(8,128)(2,1)S(1)}, u32[]{:S(2)}, u32[]{:S(2)}) collective-permute-start(bf16[16,4096]{1,0:T(8,128)(2,1)S(1)} %get-tuple-element.53), channel_id=1, source_target_pairs={{0,12},{1,13},{2,14},{3,15},{4,0},{5,1},{6,2},{7,3},{8,4},{9,5},{1... | collective-permute-start | bytes 393224 | tf_op jit(solution)/shard_map/ppermute | solution.py:154
  76.7 0.5 collective-permute-start.9
  77.2 7.0 %collective-permute-done.18 = bf16[64,4096]{1,0:T(8,128)(2,1)S(1)} collective-permute-done((bf16[64,4096]{1,0:T(8,128)(2,1)S(1)}, bf16[64,4096]{1,0:T(8,128)(2,1)S(1)}, u32[]{:S(2)}, u32[]{:S(2)}) %collective-permute-start.18) | collective-permute-done | bytes 524320 | tf_op jit(solution)/shard_map/ppermute | solution.py:151
  84.2 0.2 fusion.9
  84.4 4.5 %collective-permute-start.19 = (bf16[16,4096]{1,0:T(8,128)(2,1)S(1)}, bf16[16,4096]{1,0:T(8,128)(2,1)S(1)}, u32[]{:S(2)}, u32[]{:S(2)}) collective-permute-start(bf16[16,4096]{1,0:T(8,128)(2,1)S(1)} %get-tuple-element.56), channel_id=1, source_target_pairs={{0,12},{1,13},{2,14},{3,15},{4,0},{5,1},{6,2},{7,3},{8,4},{9,5},{1... | collective-permute-start | bytes 393224 | tf_op jit(solution)/shard_map/ppermute | solution.py:154
  88.9 0.4 collective-permute-start.20
  89.4 0.0 collective-permute-done.10
  89.4 0.2 collective-permute-start.21
  89.6 0.0 collective-permute-done.8
  89.6 0.0 collective-permute-done.9
  89.6 0.1 fusion.6
  89.6 3.2 %collective-permute-done.19 = bf16[16,4096]{1,0:T(8,128)(2,1)S(1)} collective-permute-done((bf16[16,4096]{1,0:T(8,128)(2,1)S(1)}, bf16[16,4096]{1,0:T(8,128)(2,1)S(1)}, u32[]{:S(2)}, u32[]{:S(2)}) %collective-permute-start.19) | collective-permute-done | bytes 131104 | tf_op jit(solution)/shard_map/ppermute | solution.py:154
  92.9 7.2 %collective-permute-done.20 = bf16[16,4096]{1,0:T(8,128)(2,1)S(1)} collective-permute-done((bf16[16,4096]{1,0:T(8,128)(2,1)S(1)}, bf16[16,4096]{1,0:T(8,128)(2,1)S(1)}, u32[]{:S(2)}, u32[]{:S(2)}) %collective-permute-start.20) | collective-permute-done | bytes 131104 | tf_op jit(solution)/shard_map/ppermute | solution.py:154
  100.0 0.0 collective-permute-done.21
  100.0 0.1 fusion.7
  100.1 0.7 pad_maximum_fusion
  (10 shorter events, 0.2 us)
Async XLA Ops:
  0.0 0.9 copy-start
  1.0 0.7 copy-start.1
  1.6 0.7 copy-start.2
  2.5 13.6 %collective-permute-start = (bf16[16,4224]{1,0:T(8,128)(2,1)S(1)}, bf16[16,4224]{1,0:T(8,128)(2,1)S(1)}, u32[]{:S(2)}, u32[]{:S(2)}) collective-permute-start(bf16[16,4224]{1,0:T(8,128)(2,1)S(1)} %message.2), channel_id=1, source_target_pairs={{0,4},{1,5},{2,6},{3,7},{4,8},{5,9},{6,10},{7,11},{8,12},{9,13},{1... | collective-permute-start | bytes 405512 | tf_op jit(solution)/shard_map/ppermute | solution.py:154
  5.6 11.5 %collective-permute-start.1 = (bf16[16,4224]{1,0:T(8,128)(2,1)S(1)}, bf16[16,4224]{1,0:T(8,128)(2,1)S(1)}, u32[]{:S(2)}, u32[]{:S(2)}) collective-permute-start(bf16[16,4224]{1,0:T(8,128)(2,1)S(1)} %message.2), channel_id=1, source_target_pairs={{0,8},{1,9},{2,10},{3,11},{4,12},{5,13},{6,14},{7,15},{8,0},{9,1},... | collective-permute-start | bytes 405512 | tf_op jit(solution)/shard_map/ppermute | solution.py:154
  8.2 8.9 %collective-permute-start.2 = (bf16[16,4224]{1,0:T(8,128)(2,1)S(1)}, bf16[16,4224]{1,0:T(8,128)(2,1)S(1)}, u32[]{:S(2)}, u32[]{:S(2)}) collective-permute-start(bf16[16,4224]{1,0:T(8,128)(2,1)S(1)} %message.2), channel_id=1, source_target_pairs={{0,12},{1,13},{2,14},{3,15},{4,0},{5,1},{6,2},{7,3},{8,4},{9,5},{1... | collective-permute-start | bytes 405512 | tf_op jit(solution)/shard_map/ppermute | solution.py:154
  9.7 24.2 %copy-start.3 = (s32[16]{0:T(128)S(1)}, s32[16]{0:T(128)}, u32[]{:S(2)}) copy-start(s32[16]{0:T(128)} %flags_ref.3) | copy-start | bytes 196
  17.1 2.0 %collective-permute-start.4 = (bf16[64,4224]{1,0:T(8,128)(2,1)S(1)}, bf16[64,4224]{1,0:T(8,128)(2,1)S(1)}, u32[]{:S(2)}, u32[]{:S(2)}) collective-permute-start(bf16[64,4224]{1,0:T(8,128)(2,1)S(1)} %constant_dynamic-update-slice_fusion.first), channel_id=1, source_target_pairs={{0,1},{1,0},{2,3},{3,2},{4,5},{5,4},{6,7},{7,6},{8,9},{9,8},{10,11... | collective-permute-start | bytes 1622024 | tf_op jit(solution)/shard_map/ppermute | solution.py:148
  17.2 14.7 %collective-permute-start.3 = (bf16[64,4224]{1,0:T(8,128)(2,1)S(1)}, bf16[64,4224]{1,0:T(8,128)(2,1)S(1)}, u32[]{:S(2)}, u32[]{:S(2)}) collective-permute-start(bf16[64,4224]{1,0:T(8,128)(2,1)S(1)} %constant_dynamic-update-slice_fusion.first), channel_id=1, source_target_pairs={{0,2},{1,3},{2,0},{3,1},{4,6},{5,7},{6,4},{7,5},{8,10},{9,11},{10,... | collective-permute-start | bytes 1622024 | tf_op jit(solution)/shard_map/ppermute | solution.py:151
  19.1 12.8 %collective-permute-start.11 = (bf16[16,4224]{1,0:T(8,128)(2,1)S(1)}, bf16[16,4224]{1,0:T(8,128)(2,1)S(1)}, u32[]{:S(2)}, u32[]{:S(2)}) collective-permute-start(bf16[16,4224]{1,0:T(8,128)(2,1)S(1)} %message.3), channel_id=1, source_target_pairs={{0,4},{1,5},{2,6},{3,7},{4,8},{5,9},{6,10},{7,11},{8,12},{9,13},{1... | collective-permute-start | bytes 405512 | tf_op jit(solution)/shard_map/ppermute | solution.py:154
  22.5 10.8 %collective-permute-start.12 = (bf16[16,4224]{1,0:T(8,128)(2,1)S(1)}, bf16[16,4224]{1,0:T(8,128)(2,1)S(1)}, u32[]{:S(2)}, u32[]{:S(2)}) collective-permute-start(bf16[16,4224]{1,0:T(8,128)(2,1)S(1)} %message.3), channel_id=1, source_target_pairs={{0,8},{1,9},{2,10},{3,11},{4,12},{5,13},{6,14},{7,15},{8,0},{9,1},... | collective-permute-start | bytes 405512 | tf_op jit(solution)/shard_map/ppermute | solution.py:154
  24.2 16.8 %collective-permute-start.13 = (bf16[16,4224]{1,0:T(8,128)(2,1)S(1)}, bf16[16,4224]{1,0:T(8,128)(2,1)S(1)}, u32[]{:S(2)}, u32[]{:S(2)}) collective-permute-start(bf16[16,4224]{1,0:T(8,128)(2,1)S(1)} %message.3), channel_id=1, source_target_pairs={{0,12},{1,13},{2,14},{3,15},{4,0},{5,1},{6,2},{7,3},{8,4},{9,5},{1... | collective-permute-start | bytes 405512 | tf_op jit(solution)/shard_map/ppermute | solution.py:154
  31.9 1.9 %collective-permute-start.5 = (bf16[64,4224]{1,0:T(8,128)(2,1)S(1)}, bf16[64,4224]{1,0:T(8,128)(2,1)S(1)}, u32[]{:S(2)}, u32[]{:S(2)}) collective-permute-start(bf16[64,4224]{1,0:T(8,128)(2,1)S(1)} %collective-permute-done.3.second), channel_id=1, source_target_pairs={{0,1},{1,0},{2,3},{3,2},{4,5},{5,4},{6,7},{7,6},{8,9},{9,8},{10,11... | collective-permute-start | bytes 1622024 | tf_op jit(solution)/shard_map/ppermute | solution.py:148
  40.9 14.8 %collective-permute-start.6 = (bf16[128,4096]{1,0:T(8,128)(2,1)S(1)}, bf16[128,4096]{1,0:T(8,128)(2,1)S(1)}, u32[]{:S(2)}, u32[]{:S(2)}) collective-permute-start(bf16[128,4096]{1,0:T(8,128)(2,1)S(1)} %get-tuple-element.38), channel_id=1, source_target_pairs={{0,1},{1,0},{2,3},{3,2},{4,5},{5,4},{6,7},{7,6},{8,9},{9,8},{10,11... | collective-permute-start | bytes 3145736 | tf_op jit(solution)/shard_map/ppermute | solution.py:148
  41.1 14.6 %collective-permute-start.14 = (bf16[64,4224]{1,0:T(8,128)(2,1)S(1)}, bf16[64,4224]{1,0:T(8,128)(2,1)S(1)}, u32[]{:S(2)}, u32[]{:S(2)}) collective-permute-start(bf16[64,4224]{1,0:T(8,128)(2,1)S(1)} %constant_dynamic-update-slice_fusion.4.first), channel_id=1, source_target_pairs={{0,2},{1,3},{2,0},{3,1},{4,6},{5,7},{6,4},{7,5},{8,10},{9,11},{10,... | collective-permute-start | bytes 1622024 | tf_op jit(solution)/shard_map/ppermute | solution.py:151
  42.7 14.8 %collective-permute-start.15 = (bf16[64,4224]{1,0:T(8,128)(2,1)S(1)}, bf16[64,4224]{1,0:T(8,128)(2,1)S(1)}, u32[]{:S(2)}, u32[]{:S(2)}) collective-permute-start(bf16[64,4224]{1,0:T(8,128)(2,1)S(1)} %constant_dynamic-update-slice_fusion.4.first), channel_id=1, source_target_pairs={{0,1},{1,0},{2,3},{3,2},{4,5},{5,4},{6,7},{7,6},{8,9},{9,8},{10,11... | collective-permute-start | bytes 1622024 | tf_op jit(solution)/shard_map/ppermute | solution.py:148
  55.7 1.9 %collective-permute-start.16 = (bf16[64,4224]{1,0:T(8,128)(2,1)S(1)}, bf16[64,4224]{1,0:T(8,128)(2,1)S(1)}, u32[]{:S(2)}, u32[]{:S(2)}) collective-permute-start(bf16[64,4224]{1,0:T(8,128)(2,1)S(1)} %collective-permute-done.14.second), channel_id=1, source_target_pairs={{0,1},{1,0},{2,3},{3,2},{4,5},{5,4},{6,7},{7,6},{8,9},{9,8},{10,11... | collective-permute-start | bytes 1622024 | tf_op jit(solution)/shard_map/ppermute | solution.py:148
  55.8 14.4 %collective-permute-start.7 = (bf16[64,4096]{1,0:T(8,128)(2,1)S(1)}, bf16[64,4096]{1,0:T(8,128)(2,1)S(1)}, u32[]{:S(2)}, u32[]{:S(2)}) collective-permute-start(bf16[64,4096]{1,0:T(8,128)(2,1)S(1)} %add_convert_fusion.1), channel_id=1, source_target_pairs={{0,2},{1,3},{2,0},{3,1},{4,6},{5,7},{6,4},{7,5},{8,10},{9,11},{10,... | collective-permute-start | bytes 1572872 | tf_op jit(solution)/shard_map/ppermute | solution.py:151
  64.6 5.8 %collective-permute-start.17 = (bf16[128,4096]{1,0:T(8,128)(2,1)S(1)}, bf16[128,4096]{1,0:T(8,128)(2,1)S(1)}, u32[]{:S(2)}, u32[]{:S(2)}) collective-permute-start(bf16[128,4096]{1,0:T(8,128)(2,1)S(1)} %get-tuple-element.47), channel_id=1, source_target_pairs={{0,1},{1,0},{2,3},{3,2},{4,5},{5,4},{6,7},{7,6},{8,9},{9,8},{10,11... | collective-permute-start | bytes 3145736 | tf_op jit(solution)/shard_map/ppermute | solution.py:148
  70.6 13.6 %collective-permute-start.18 = (bf16[64,4096]{1,0:T(8,128)(2,1)S(1)}, bf16[64,4096]{1,0:T(8,128)(2,1)S(1)}, u32[]{:S(2)}, u32[]{:S(2)}) collective-permute-start(bf16[64,4096]{1,0:T(8,128)(2,1)S(1)} %add_convert_fusion), channel_id=1, source_target_pairs={{0,2},{1,3},{2,0},{3,1},{4,6},{5,7},{6,4},{7,5},{8,10},{9,11},{10,... | collective-permute-start | bytes 1572872 | tf_op jit(solution)/shard_map/ppermute | solution.py:151
  72.2 17.1 %collective-permute-start.10 = (bf16[16,4096]{1,0:T(8,128)(2,1)S(1)}, bf16[16,4096]{1,0:T(8,128)(2,1)S(1)}, u32[]{:S(2)}, u32[]{:S(2)}) collective-permute-start(bf16[16,4096]{1,0:T(8,128)(2,1)S(1)} %get-tuple-element.54), channel_id=1, source_target_pairs={{0,4},{1,5},{2,6},{3,7},{4,8},{5,9},{6,10},{7,11},{8,12},{9,13},{1... | collective-permute-start | bytes 393224 | tf_op jit(solution)/shard_map/ppermute | solution.py:154
  75.7 13.9 %collective-permute-start.8 = (bf16[16,4096]{1,0:T(8,128)(2,1)S(1)}, bf16[16,4096]{1,0:T(8,128)(2,1)S(1)}, u32[]{:S(2)}, u32[]{:S(2)}) collective-permute-start(bf16[16,4096]{1,0:T(8,128)(2,1)S(1)} %get-tuple-element.53), channel_id=1, source_target_pairs={{0,12},{1,13},{2,14},{3,15},{4,0},{5,1},{6,2},{7,3},{8,4},{9,5},{1... | collective-permute-start | bytes 393224 | tf_op jit(solution)/shard_map/ppermute | solution.py:154
  76.7 12.8 %collective-permute-start.9 = (bf16[16,4096]{1,0:T(8,128)(2,1)S(1)}, bf16[16,4096]{1,0:T(8,128)(2,1)S(1)}, u32[]{:S(2)}, u32[]{:S(2)}) collective-permute-start(bf16[16,4096]{1,0:T(8,128)(2,1)S(1)} %get-tuple-element.55), channel_id=1, source_target_pairs={{0,8},{1,9},{2,10},{3,11},{4,12},{5,13},{6,14},{7,15},{8,0},{9,1},... | collective-permute-start | bytes 393224 | tf_op jit(solution)/shard_map/ppermute | solution.py:154
  84.4 8.4 %collective-permute-start.19 = (bf16[16,4096]{1,0:T(8,128)(2,1)S(1)}, bf16[16,4096]{1,0:T(8,128)(2,1)S(1)}, u32[]{:S(2)}, u32[]{:S(2)}) collective-permute-start(bf16[16,4096]{1,0:T(8,128)(2,1)S(1)} %get-tuple-element.56), channel_id=1, source_target_pairs={{0,12},{1,13},{2,14},{3,15},{4,0},{5,1},{6,2},{7,3},{8,4},{9,5},{1... | collective-permute-start | bytes 393224 | tf_op jit(solution)/shard_map/ppermute | solution.py:154
  88.9 11.1 %collective-permute-start.20 = (bf16[16,4096]{1,0:T(8,128)(2,1)S(1)}, bf16[16,4096]{1,0:T(8,128)(2,1)S(1)}, u32[]{:S(2)}, u32[]{:S(2)}) collective-permute-start(bf16[16,4096]{1,0:T(8,128)(2,1)S(1)} %get-tuple-element.58), channel_id=1, source_target_pairs={{0,8},{1,9},{2,10},{3,11},{4,12},{5,13},{6,14},{7,15},{8,0},{9,1},... | collective-permute-start | bytes 393224 | tf_op jit(solution)/shard_map/ppermute | solution.py:154
  89.4 10.7 %collective-permute-start.21 = (bf16[16,4096]{1,0:T(8,128)(2,1)S(1)}, bf16[16,4096]{1,0:T(8,128)(2,1)S(1)}, u32[]{:S(2)}, u32[]{:S(2)}) collective-permute-start(bf16[16,4096]{1,0:T(8,128)(2,1)S(1)} %get-tuple-element.57), channel_id=1, source_target_pairs={{0,4},{1,5},{2,6},{3,7},{4,8},{5,9},{6,10},{7,11},{8,12},{9,13},{1... | collective-permute-start | bytes 393224 | tf_op jit(solution)/shard_map/ppermute | solution.py:154

commit v3 on v2

--- a/solution.py
+++ b/solution.py
@@ -38,6 +38,7 @@
 
 def make_message(states, ids, probs, step, tail):
     _, tokens, width = states.shape
+    states, ids, probs = (pltpu.with_memory_space_constraint(x, pltpu.HBM) for x in (states, ids, probs))
 
     def of_step(x):
         return pl.BlockSpec((None,) + x.shape[1:], lambda i: (step, 0, 0))
@@ -80,16 +81,16 @@
     )(*arrays)
 
 
-def expert_kernel(
-    swapped, flags_ref, first, second, third, fourth, gate_ref, up_ref, down_ref, own_ref, near_ref, other_ref, rows, hidden
-):
+def expert_kernel(swapped, count, flags_ref, gate_ref, up_ref, down_ref, *refs):
+    *sources, own_ref, near_ref, other_ref, rows, hidden = refs
     width, units = gate_ref.shape
-    tail = first.shape[1] - width
-    count = first.shape[0]
+    tail = rows.shape[1] - width
     owner = lax.axis_index("expert")
     slot = jnp.bitwise_xor(owner, flags_ref[owner]) if swapped else owner
-    for part, source in enumerate((first, second, third, fourth)):
-        rows[part * count : (part + 1) * count] = source[...]
+    at = 0
+    for source in sources:
+        rows[at : at + source.shape[0]] = source[...]
+        at += source.shape[0]
     total = rows.shape[0]
     lane = lax.broadcasted_iota(jnp.int32, (total, tail), 1)
     terms = rows[:, width:].astype(jnp.float32)
@@ -113,25 +114,26 @@
     lax.fori_loop(0, width // 512, columns, 0)
 
 
-def run_expert(swapped, flags, parts, gate, up, down):
-    count = parts[0].shape[0]
-    width, units = gate.shape
-    gate, up, down = (pltpu.with_memory_space_constraint(w, pltpu.VMEM) for w in (gate, up, down))
+def run_expert(swapped, flags, weights, parts):
+    total = sum(part.shape[0] for part in parts)
+    count = total // 4
+    width, units = weights[0].shape
+    weights = [pltpu.with_memory_space_constraint(w, pltpu.VMEM) for w in weights]
     return pl.pallas_call(
-        functools.partial(expert_kernel, swapped),
+        functools.partial(expert_kernel, swapped, count),
         out_shape=[jax.ShapeDtypeStruct((k * count, width), jnp.bfloat16) for k in (1, 1, 2)],
-        in_specs=[pl.BlockSpec(memory_space=pltpu.SMEM)] + [in_vmem()] * 7,
+        in_specs=[pl.BlockSpec(memory_space=pltpu.SMEM)] + [in_vmem()] * (3 + len(parts)),
         out_specs=[in_vmem()] * 3,
         scratch_shapes=[
-            pltpu.VMEM((4 * count, parts[0].shape[1]), jnp.bfloat16),
-            pltpu.VMEM((4 * count, units), jnp.bfloat16),
+            pltpu.VMEM((total, parts[0].shape[1]), jnp.bfloat16),
+            pltpu.VMEM((total, units), jnp.bfloat16),
         ],
         compiler_params=pltpu.CompilerParams(vmem_limit_bytes=16 * MIB),
         cost_estimate=pl.CostEstimate(
-            flops=4 * count * width * units * 6, bytes_accessed=16 * count * width, transcendentals=0
+            flops=total * width * units * 6, bytes_accessed=4 * total * width, transcendentals=0
         ),
         name="expert",
-    )(flags, *parts, gate, up, down)
+    )(flags, *weights, *parts)
 
 
 def on_device(states, ids, probs, flags, w_gate, w_up, w_down):
@@ -156,35 +158,49 @@
     tail = 2 * devices
     tail = -(-tail // LANES) * LANES
     ids, probs = jnp.swapaxes(ids, 1, 2), jnp.swapaxes(probs, 1, 2)
+    order = sorted(range(lines), key=lambda by: min(by, lines - by))
+    close, far = order[1 : 1 + lines // 2], order[1 + lines // 2 :]
     weights = load_weights(w_gate[0], w_up[0], w_down[0])
     messages = [make_message(states, ids, probs, step, tail) for step in range(steps)]
     gathered = []
+    blocks = None
     for step in range(steps):
         message = messages[step]
+        near_own = swap_near(message)
         if step:
-            message, _ = lax.optimization_barrier((message, gathered[step - 1][2]))
-        blocks = [message] + [shift_far(message, by) for by in range(1, lines)]
+            message, _ = lax.optimization_barrier((message, blocks))
+        blocks = [shift_far(message, by) for by in order[1:]]
         if not step:
             blocks, weights, messages[1:] = lax.optimization_barrier((blocks, weights, messages[1:]))
-        line = jnp.concatenate(blocks, axis=0)
-        near = swap_near(line)
-        gathered.append((line, near, swap_core(line), swap_core(near)))
+            split = len(close)
+            near = [near_own, swap_near(jnp.concatenate(blocks[:split])), swap_near(jnp.concatenate(blocks[split:]))]
+            core = [swap_core(jnp.concatenate(near[:2])), swap_core(near[2])]
+        else:
+            near = [near_own, swap_near(jnp.concatenate(blocks))]
+            core = [swap_core(jnp.concatenate(near))]
+        line = [message, *blocks]
+        gathered.append((*line, *near, swap_core(jnp.concatenate(line)), *core))
     outputs = []
     other = None
     for step in range(steps):
         parts = gathered[step]
         if step:
             parts, _ = lax.optimization_barrier((parts, other))
-        own, peer, other = run_expert(step > 0, flags, parts, *weights)
+        own, peer, other = run_expert(step > 0, flags, weights, parts)
         other = swap_core(other)
         half = own.shape[0]
-        peer = peer.astype(jnp.float32) + other[half:].astype(jnp.float32)
-        near = swap_near(peer.astype(jnp.bfloat16))
-        line = own.astype(jnp.float32) + other[:half].astype(jnp.float32) + near.astype(jnp.float32)
-        line = line.reshape(lines, tokens, width)
-        mixed = line[0]
-        for by in range(1, lines):
-            mixed += shift_far(line[by].astype(jnp.bfloat16), lines - by).astype(jnp.float32)
+        own = own.astype(jnp.float32) + other[:half].astype(jnp.float32)
+        peer = (peer.astype(jnp.float32) + other[half:].astype(jnp.float32)).astype(jnp.bfloat16)
+        cuts = [0, half] if step + 1 < steps else [0, tokens, (1 + len(close)) * tokens, half]
+        places = list(zip(cuts[:-1], cuts[1:]))
+        blocks = []
+        for low, high in places[::-1]:
+            near = swap_near(peer[low:high])
+            both = own[low:high] + near.astype(jnp.float32)
+            blocks = [both[at : at + tokens] for at in range(0, high - low, tokens)] + blocks
+        mixed = blocks[0]
+        for by, block in zip(order[1:], blocks[1:]):
+            mixed += shift_far(block.astype(jnp.bfloat16), lines - by).astype(jnp.float32)
         outputs.append(mixed.astype(jnp.bfloat16))
     return jnp.stack(outputs)
 

time: 101 us -> 86.2 us (0.85)
  waiting for transfers between devices: 46 us -> 29.8 us
  local copies, waits for them, and re-layouts: 2.52 us -> 0.09 us
  Pallas kernels: 20.8 us -> 22.8 us
  starting transfers between devices: 29.9 us -> 31.5 us
    ppermute x4 -> x9, waiting for transfers between devices: 32.2 us -> 16.7 us  [swap_near(): lax.ppermute(x, 'expert', [(index(z, y, c), index(z, 1 - y, c)) for z, y,...]
    ppermute x4 -> x9, starting transfers between devices: 6.42 us -> 12.5 us  [swap_near(): lax.ppermute(x, 'expert', [(index(z, y, c), index(z, 1 - y, c)) for z, y,...]
    ppermute x12, starting transfers between devices: 22.9 us -> 17.5 us  [shift_far(): lax.ppermute(x, 'expert', [(index(z, y, c), index((z + by) % lines, y, c)...]
    unnamed x14 -> x2, local copies, waits for them, and re-layouts: 2.43 us -> 0.01 us
    pallas_call x2, Pallas kernels: 0.37 us -> 2.23 us  [make_message(): pl.pallas_call(message_kernel, grid=(1,), out_shape=jax.ShapeDtypeStruct(...]
  transfers between devices with their start and end apart: 22 -> 28, of which waited for: 11 -> 12; matrix products, arithmetic and copies ran while one was open for 1% -> 1% of each run, Pallas kernels for 20% -> 25%
where the time goes in v3:
time: 86.2 us; the launch traced here: 86.1 us
  starting transfers between devices  31.5 us (37%)
  waiting for transfers between devices  29.8 us (35%)
  Pallas kernels  22.8 us (26%)
  other arithmetic  1.76 us (2%)
    ppermute x12, starting transfers between devices, shift_far(): lax.ppermute(x, 'expert', [(index(z, y, c), index((z + by) % lines, y, c)...  17.5 us
    ppermute x9, waiting for transfers between devices, swap_near(): lax.ppermute(x, 'expert', [(index(z, y, c), index(z, 1 - y, c)) for z, y,...  16.7 us
    pallas_call x2, Pallas kernels, run_expert(): pl.pallas_call(functools.partial(expert_kernel, swapped, count), out_shap...  14.1 us
    ppermute x9, starting transfers between devices, swap_near(): lax.ppermute(x, 'expert', [(index(z, y, c), index(z, 1 - y, c)) for z, y,...  12.5 us
    ppermute x12, waiting for transfers between devices, shift_far(): lax.ppermute(x, 'expert', [(index(z, y, c), index((z + by) % lines, y, c)...  12.2 us
    pallas_call x1, Pallas kernels, load_weights(): pl.pallas_call(load_kernel, out_shape=[pltpu.VMEM(x.shape, x.dtype) for x...  6.43 us
    pallas_call x2, Pallas kernels, make_message(): pl.pallas_call(message_kernel, grid=(1,), out_shape=jax.ShapeDtypeStruct(...  2.23 us
  transfers between devices with their start and end apart: 28, of which 12 were waited for; matrix products, arithmetic and copies ran while one was open for 1% of the time, Pallas kernels for 25%

profile of v3, /device:TPU:0, one launch (start us, length us, event | category | flops | bytes accessed | tf_op | source)
XLA Modules:
  0.0 86.1 jit_solution(13258135619375749928)
XLA Ops:
  0.0 1.1 %message.2.refs_0_ = bf16[16,4224]{1,0:T(8,128)(2,1)S(1)} custom-call(bf16[2,16,4096]{2,1,0:T(8,128)(2,1)} %states_ref.3, s32[2,8,16]{2,1,0:T(8,128)} %bitcast.12, f32[2,8,16]{2,1,0:T(8,128)} %bitcast.14), custom_call_target="tpu_custom_call" | custom-call | tf_op jit(solution)/shard_map/message/pallas_call | solution.py:46
  1.1 3.0 %collective-permute-start = (bf16[16,4224]{1,0:T(8,128)(2,1)S(1)}, bf16[16,4224]{1,0:T(8,128)(2,1)S(1)}, u32[]{:S(2)}, u32[]{:S(2)}) collective-permute-start(bf16[16,4224]{1,0:T(8,128)(2,1)S(1)} %message.2.refs_0_), channel_id=1, source_target_pairs={{0,4},{1,5},{2,6},{3,7},{4,8},{5,9},{6,10},{7,11},{8,12},{9,13},{1... | collective-permute-start | bytes 405512 | tf_op jit(solution)/shard_map/ppermute | solution.py:156
  4.1 2.0 %collective-permute-start.1 = (bf16[16,4224]{1,0:T(8,128)(2,1)S(1)}, bf16[16,4224]{1,0:T(8,128)(2,1)S(1)}, u32[]{:S(2)}, u32[]{:S(2)}) collective-permute-start(bf16[16,4224]{1,0:T(8,128)(2,1)S(1)} %message.2.refs_0_), channel_id=1, source_target_pairs={{0,12},{1,13},{2,14},{3,15},{4,0},{5,1},{6,2},{7,3},{8,4},{9,5},{1... | collective-permute-start | bytes 405512 | tf_op jit(solution)/shard_map/ppermute | solution.py:156
  6.2 1.0 %collective-permute-start.2 = (bf16[16,4224]{1,0:T(8,128)(2,1)S(1)}, bf16[16,4224]{1,0:T(8,128)(2,1)S(1)}, u32[]{:S(2)}, u32[]{:S(2)}) collective-permute-start(bf16[16,4224]{1,0:T(8,128)(2,1)S(1)} %message.2.refs_0_), channel_id=1, source_target_pairs={{0,8},{1,9},{2,10},{3,11},{4,12},{5,13},{6,14},{7,15},{8,0},{9,1},... | collective-permute-start | bytes 405512 | tf_op jit(solution)/shard_map/ppermute | solution.py:156
  7.2 1.5 %collective-permute-start.3 = (bf16[16,4224]{1,0:T(8,128)(2,1)S(1)}, bf16[16,4224]{1,0:T(8,128)(2,1)S(1)}, u32[]{:S(2)}, u32[]{:S(2)}) collective-permute-start(bf16[16,4224]{1,0:T(8,128)(2,1)S(1)} %message.2.refs_0_), channel_id=1, source_target_pairs={{0,2},{1,3},{2,0},{3,1},{4,6},{5,7},{6,4},{7,5},{8,10},{9,11},{10,... | collective-permute-start | bytes 405512 | tf_op jit(solution)/shard_map/ppermute | solution.py:153
  8.7 1.1 %message.3.refs_0_ = bf16[16,4224]{1,0:T(8,128)(2,1)S(1)} custom-call(bf16[2,16,4096]{2,1,0:T(8,128)(2,1)} %states_ref.3, s32[2,8,16]{2,1,0:T(8,128)} %bitcast.13, f32[2,8,16]{2,1,0:T(8,128)} %bitcast.15), custom_call_target="tpu_custom_call" | custom-call | tf_op jit(solution)/shard_map/message/pallas_call | solution.py:46
  9.8 6.4 %load_weights.1 = (bf16[4096,768]{1,0:T(8,128)(2,1)S(1)}, bf16[4096,768]{1,0:T(8,128)(2,1)S(1)}, bf16[768,4096]{1,0:T(8,128)(2,1)S(1)}) custom-call(bf16[4096,768]{1,0:T(8,128)(2,1)} %bitcast.9, bf16[4096,768]{1,0:T(8,128)(2,1)} %bitcast.10, bf16[768,4096]{1,0:T(8,128)(2,1)} %bitcast.11), custom_call_target="tpu_custom_call" | custom-call | bytes 18874368 | tf_op jit(solution)/shard_map/load_weights/pallas_call | solution.py:70
  16.3 0.0 collective-permute-done.refs_1_
  16.3 0.0 collective-permute-done.1.refs_2_
  16.3 2.2 %collective-permute-done.2.refs_3_ = bf16[16,4224]{1,0:T(8,128)(2,1)S(1)} collective-permute-done((bf16[16,4224]{1,0:T(8,128)(2,1)S(1)}, bf16[16,4224]{1,0:T(8,128)(2,1)S(1)}, u32[]{:S(2)}, u32[]{:S(2)}) %collective-permute-start.2) | collective-permute-done | bytes 135200 | tf_op jit(solution)/shard_map/ppermute | solution.py:156
  18.5 1.6 %collective-permute-start.4 = (bf16[32,4224]{1,0:T(8,128)(2,1)S(1)}, bf16[32,4224]{1,0:T(8,128)(2,1)S(1)}, u32[]{:S(2)}, u32[]{:S(2)}) collective-permute-start(bf16[32,4224]{1,0:T(8,128)(2,1)S(1)} %pad_maximum_fusion.5), channel_id=1, source_target_pairs={{0,2},{1,3},{2,0},{3,1},{4,6},{5,7},{6,4},{7,5},{8,10},{9,11},{10,... | collective-permute-start | bytes 811016 | tf_op jit(solution)/shard_map/ppermute | solution.py:153
  20.1 0.0 copy-start
  20.1 0.6 collective-permute-start.5
  20.7 0.0 collective-permute-start.14
  20.7 3.8 %collective-permute-start.15 = (bf16[16,4224]{1,0:T(8,128)(2,1)S(1)}, bf16[16,4224]{1,0:T(8,128)(2,1)S(1)}, u32[]{:S(2)}, u32[]{:S(2)}) collective-permute-start(bf16[16,4224]{1,0:T(8,128)(2,1)S(1)} %message.3.refs_0_), channel_id=1, source_target_pairs={{0,12},{1,13},{2,14},{3,15},{4,0},{5,1},{6,2},{7,3},{8,4},{9,5},{1... | collective-permute-start | bytes 405512 | tf_op jit(solution)/shard_map/ppermute | solution.py:156
  24.5 0.0 collective-permute-done.3.refs_4_
  24.5 0.0 collective-permute-start.16
  24.5 3.4 %collective-permute-done.4.refs_5_ = bf16[32,4224]{1,0:T(8,128)(2,1)S(1)} collective-permute-done((bf16[32,4224]{1,0:T(8,128)(2,1)S(1)}, bf16[32,4224]{1,0:T(8,128)(2,1)S(1)}, u32[]{:S(2)}, u32[]{:S(2)}) %collective-permute-start.4) | collective-permute-done | bytes 270368 | tf_op jit(solution)/shard_map/ppermute | solution.py:153
  27.9 1.5 %collective-permute-start.17 = (bf16[16,4224]{1,0:T(8,128)(2,1)S(1)}, bf16[16,4224]{1,0:T(8,128)(2,1)S(1)}, u32[]{:S(2)}, u32[]{:S(2)}) collective-permute-start(bf16[16,4224]{1,0:T(8,128)(2,1)S(1)} %message.3.refs_0_), channel_id=1, source_target_pairs={{0,2},{1,3},{2,0},{3,1},{4,6},{5,7},{6,4},{7,5},{8,10},{9,11},{10,... | collective-permute-start | bytes 405512 | tf_op jit(solution)/shard_map/ppermute | solution.py:153
  29.5 1.3 %collective-permute-done.5.refs_6_ = bf16[16,4224]{1,0:T(8,128)(2,1)S(1)} collective-permute-done((bf16[16,4224]{1,0:T(8,128)(2,1)S(1)}, bf16[16,4224]{1,0:T(8,128)(2,1)S(1)}, u32[]{:S(2)}, u32[]{:S(2)}) %collective-permute-start.5) | collective-permute-done | bytes 135200 | tf_op jit(solution)/shard_map/ppermute | solution.py:153
  30.8 0.0 collective-permute-start.6
  30.8 0.0 collective-permute-done.14.refs_1_
  30.8 0.5 collective-permute-start.8
  31.3 0.0 collective-permute-done.15.refs_2_
  31.3 0.1 collective-permute-start.7
  31.4 3.2 %collective-permute-done.16.refs_3_ = bf16[16,4224]{1,0:T(8,128)(2,1)S(1)} collective-permute-done((bf16[16,4224]{1,0:T(8,128)(2,1)S(1)}, bf16[16,4224]{1,0:T(8,128)(2,1)S(1)}, u32[]{:S(2)}, u32[]{:S(2)}) %collective-permute-start.16) | collective-permute-done | bytes 135200 | tf_op jit(solution)/shard_map/ppermute | solution.py:156
  34.6 1.6 %collective-permute-start.18 = (bf16[48,4224]{1,0:T(8,128)(2,1)S(1)}, bf16[48,4224]{1,0:T(8,128)(2,1)S(1)}, u32[]{:S(2)}, u32[]{:S(2)}) collective-permute-start(bf16[48,4224]{1,0:T(8,128)(2,1)S(1)} %pad_maximum_fusion.4), channel_id=1, source_target_pairs={{0,2},{1,3},{2,0},{3,1},{4,6},{5,7},{6,4},{7,5},{8,10},{9,11},{10,... | collective-permute-start | bytes 1216520 | tf_op jit(solution)/shard_map/ppermute | solution.py:153
  36.2 0.0 collective-permute-done.8.refs_9_
  36.2 0.0 collective-permute-done.7.refs_8_
  36.2 7.1 %expert.2 = (bf16[64,4096]{1,0:T(8,128)(2,1)S(1)}, bf16[64,4096]{1,0:T(8,128)(2,1)S(1)}, bf16[128,4096]{1,0:T(8,128)(2,1)S(1)}) custom-call(s32[16]{0:T(128)S(1)} %copy-done, bf16[4096,768]{1,0:T(8,128)(2,1)S(1)} %get-tuple-element.33.gate_ref, bf16[4096,768]{1,0:T(8,128)(2,1)S(1)} %get-tuple-element.34.up_ref, ...), custom_call_target="tpu_custom_call" | custom-call | flops 4831838208 | bytes 4194304 | tf_op jit(solution)/shard_map/expert/pallas_call | solution.py:122
  43.3 0.1 collective-permute-start.9
  43.3 0.1 pad_maximum_fusion.1
  43.4 0.6 collective-permute-start.19
  44.0 0.0 collective-permute-done.17.refs_4_
  44.0 1.4 %collective-permute-done.18.refs_5_ = bf16[48,4224]{1,0:T(8,128)(2,1)S(1)} collective-permute-done((bf16[48,4224]{1,0:T(8,128)(2,1)S(1)}, bf16[48,4224]{1,0:T(8,128)(2,1)S(1)}, u32[]{:S(2)}, u32[]{:S(2)}) %collective-permute-start.18) | collective-permute-done | bytes 405536 | tf_op jit(solution)/shard_map/ppermute | solution.py:153
  45.4 0.1 collective-permute-start.20
  45.4 0.6 collective-permute-done.9
  46.0 0.1 add_convert_fusion.1
  46.1 1.0 %collective-permute-start.10 = (bf16[64,4096]{1,0:T(8,128)(2,1)S(1)}, bf16[64,4096]{1,0:T(8,128)(2,1)S(1)}, u32[]{:S(2)}, u32[]{:S(2)}) collective-permute-start(bf16[64,4096]{1,0:T(8,128)(2,1)S(1)} %add_convert_fusion.1), channel_id=1, source_target_pairs={{0,2},{1,3},{2,0},{3,1},{4,6},{5,7},{6,4},{7,5},{8,10},{9,11},{10,... | collective-permute-start | bytes 1572872 | tf_op jit(solution)/shard_map/ppermute | solution.py:153
  47.2 0.0 collective-permute-done.19.refs_6_
  47.2 0.4 collective-permute-done.20.refs_7_
  47.5 7.1 %expert.3 = (bf16[64,4096]{1,0:T(8,128)(2,1)S(1)}, bf16[64,4096]{1,0:T(8,128)(2,1)S(1)}, bf16[128,4096]{1,0:T(8,128)(2,1)S(1)}) custom-call(s32[16]{0:T(128)S(1)} %copy-done, bf16[4096,768]{1,0:T(8,128)(2,1)S(1)} %get-tuple-element.33.gate_ref, bf16[4096,768]{1,0:T(8,128)(2,1)S(1)} %get-tuple-element.34.up_ref, ...), custom_call_target="tpu_custom_call" | custom-call | flops 4831838208 | bytes 4194304 | tf_op jit(solution)/shard_map/expert/pallas_call | solution.py:122
  54.6 0.2 collective-permute-start.21
  54.8 5.4 %collective-permute-done.10 = bf16[64,4096]{1,0:T(8,128)(2,1)S(1)} collective-permute-done((bf16[64,4096]{1,0:T(8,128)(2,1)S(1)}, bf16[64,4096]{1,0:T(8,128)(2,1)S(1)}, u32[]{:S(2)}, u32[]{:S(2)}) %collective-permute-start.10) | collective-permute-done | bytes 524320 | tf_op jit(solution)/shard_map/ppermute | solution.py:153
  60.2 0.2 fusion.11
  60.4 0.2 add_convert_fusion
  60.7 1.4 %collective-permute-start.26 = (bf16[16,4096]{1,0:T(8,128)(2,1)S(1)}, bf16[16,4096]{1,0:T(8,128)(2,1)S(1)}, u32[]{:S(2)}, u32[]{:S(2)}) collective-permute-start(bf16[16,4096]{1,0:T(8,128)(2,1)S(1)} %get-tuple-element.63), channel_id=1, source_target_pairs={{0,2},{1,3},{2,0},{3,1},{4,6},{5,7},{6,4},{7,5},{8,10},{9,11},{10,... | collective-permute-start | bytes 393224 | tf_op jit(solution)/shard_map/ppermute | solution.py:153
  62.1 1.1 %collective-permute-start.11 = (bf16[16,4096]{1,0:T(8,128)(2,1)S(1)}, bf16[16,4096]{1,0:T(8,128)(2,1)S(1)}, u32[]{:S(2)}, u32[]{:S(2)}) collective-permute-start(bf16[16,4096]{1,0:T(8,128)(2,1)S(1)} %get-tuple-element.59), channel_id=1, source_target_pairs={{0,12},{1,13},{2,14},{3,15},{4,0},{5,1},{6,2},{7,3},{8,4},{9,5},{1... | collective-permute-start | bytes 393224 | tf_op jit(solution)/shard_map/ppermute | solution.py:156
  63.2 1.0 %collective-permute-start.12 = (bf16[16,4096]{1,0:T(8,128)(2,1)S(1)}, bf16[16,4096]{1,0:T(8,128)(2,1)S(1)}, u32[]{:S(2)}, u32[]{:S(2)}) collective-permute-start(bf16[16,4096]{1,0:T(8,128)(2,1)S(1)} %get-tuple-element.61), channel_id=1, source_target_pairs={{0,4},{1,5},{2,6},{3,7},{4,8},{5,9},{6,10},{7,11},{8,12},{9,13},{1... | collective-permute-start | bytes 393224 | tf_op jit(solution)/shard_map/ppermute | solution.py:156
  64.2 0.8 collective-permute-start.23
  64.9 0.9 %collective-permute-done.26 = bf16[16,4096]{1,0:T(8,128)(2,1)S(1)} collective-permute-done((bf16[16,4096]{1,0:T(8,128)(2,1)S(1)}, bf16[16,4096]{1,0:T(8,128)(2,1)S(1)}, u32[]{:S(2)}, u32[]{:S(2)}) %collective-permute-start.26) | collective-permute-done | bytes 131104 | tf_op jit(solution)/shard_map/ppermute | solution.py:153
  65.8 2.5 %collective-permute-start.22 = (bf16[16,4096]{1,0:T(8,128)(2,1)S(1)}, bf16[16,4096]{1,0:T(8,128)(2,1)S(1)}, u32[]{:S(2)}, u32[]{:S(2)}) collective-permute-start(bf16[16,4096]{1,0:T(8,128)(2,1)S(1)} %get-tuple-element.62), channel_id=1, source_target_pairs={{0,2},{1,3},{2,0},{3,1},{4,6},{5,7},{6,4},{7,5},{8,10},{9,11},{10,... | collective-permute-start | bytes 393224 | tf_op jit(solution)/shard_map/ppermute | solution.py:153
  68.3 4.4 %collective-permute-done.23 = bf16[32,4096]{1,0:T(8,128)(2,1)S(1)} collective-permute-done((bf16[32,4096]{1,0:T(8,128)(2,1)S(1)}, bf16[32,4096]{1,0:T(8,128)(2,1)S(1)}, u32[]{:S(2)}, u32[]{:S(2)}) %collective-permute-start.23) | collective-permute-done | bytes 262176 | tf_op jit(solution)/shard_map/ppermute | solution.py:153
  72.7 2.6 %collective-permute-start.27 = (bf16[16,4096]{1,0:T(8,128)(2,1)S(1)}, bf16[16,4096]{1,0:T(8,128)(2,1)S(1)}, u32[]{:S(2)}, u32[]{:S(2)}) collective-permute-start(bf16[16,4096]{1,0:T(8,128)(2,1)S(1)} %fusion.1), channel_id=1, source_target_pairs={{0,8},{1,9},{2,10},{3,11},{4,12},{5,13},{6,14},{7,15},{8,0},{9,1},... | collective-permute-start | bytes 393224 | tf_op jit(solution)/shard_map/ppermute | solution.py:156
  75.5 0.0 collective-permute-done.11
  75.5 2.9 %collective-permute-start.24 = (bf16[16,4096]{1,0:T(8,128)(2,1)S(1)}, bf16[16,4096]{1,0:T(8,128)(2,1)S(1)}, u32[]{:S(2)}, u32[]{:S(2)}) collective-permute-start(bf16[16,4096]{1,0:T(8,128)(2,1)S(1)} %get-tuple-element.64), channel_id=1, source_target_pairs={{0,12},{1,13},{2,14},{3,15},{4,0},{5,1},{6,2},{7,3},{8,4},{9,5},{1... | collective-permute-start | bytes 393224 | tf_op jit(solution)/shard_map/ppermute | solution.py:156
  78.4 0.0 collective-permute-done.12
  78.4 0.0 collective-permute-start.25
  78.4 0.0 collective-permute-done.13
  78.4 0.1 fusion.9
  78.5 4.4 %collective-permute-done.27 = bf16[16,4096]{1,0:T(8,128)(2,1)S(1)} collective-permute-done((bf16[16,4096]{1,0:T(8,128)(2,1)S(1)}, bf16[16,4096]{1,0:T(8,128)(2,1)S(1)}, u32[]{:S(2)}, u32[]{:S(2)}) %collective-permute-start.27) | collective-permute-done | bytes 131104 | tf_op jit(solution)/shard_map/ppermute | solution.py:156
  82.9 2.4 %collective-permute-done.25 = bf16[16,4096]{1,0:T(8,128)(2,1)S(1)} collective-permute-done((bf16[16,4096]{1,0:T(8,128)(2,1)S(1)}, bf16[16,4096]{1,0:T(8,128)(2,1)S(1)}, u32[]{:S(2)}, u32[]{:S(2)}) %collective-permute-start.25) | collective-permute-done | bytes 131104 | tf_op jit(solution)/shard_map/ppermute | solution.py:156
  85.2 0.1 fusion.10
  85.3 0.7 pad_maximum_fusion.6
  (17 shorter events, 0.3 us)
Async XLA Ops:
  1.1 15.1 %collective-permute-start = (bf16[16,4224]{1,0:T(8,128)(2,1)S(1)}, bf16[16,4224]{1,0:T(8,128)(2,1)S(1)}, u32[]{:S(2)}, u32[]{:S(2)}) collective-permute-start(bf16[16,4224]{1,0:T(8,128)(2,1)S(1)} %message.2.refs_0_), channel_id=1, source_target_pairs={{0,4},{1,5},{2,6},{3,7},{4,8},{5,9},{6,10},{7,11},{8,12},{9,13},{1... | collective-permute-start | bytes 405512 | tf_op jit(solution)/shard_map/ppermute | solution.py:156
  4.1 12.1 %collective-permute-start.1 = (bf16[16,4224]{1,0:T(8,128)(2,1)S(1)}, bf16[16,4224]{1,0:T(8,128)(2,1)S(1)}, u32[]{:S(2)}, u32[]{:S(2)}) collective-permute-start(bf16[16,4224]{1,0:T(8,128)(2,1)S(1)} %message.2.refs_0_), channel_id=1, source_target_pairs={{0,12},{1,13},{2,14},{3,15},{4,0},{5,1},{6,2},{7,3},{8,4},{9,5},{1... | collective-permute-start | bytes 405512 | tf_op jit(solution)/shard_map/ppermute | solution.py:156
  6.2 12.3 %collective-permute-start.2 = (bf16[16,4224]{1,0:T(8,128)(2,1)S(1)}, bf16[16,4224]{1,0:T(8,128)(2,1)S(1)}, u32[]{:S(2)}, u32[]{:S(2)}) collective-permute-start(bf16[16,4224]{1,0:T(8,128)(2,1)S(1)} %message.2.refs_0_), channel_id=1, source_target_pairs={{0,8},{1,9},{2,10},{3,11},{4,12},{5,13},{6,14},{7,15},{8,0},{9,1},... | collective-permute-start | bytes 405512 | tf_op jit(solution)/shard_map/ppermute | solution.py:156
  7.2 17.3 %collective-permute-start.3 = (bf16[16,4224]{1,0:T(8,128)(2,1)S(1)}, bf16[16,4224]{1,0:T(8,128)(2,1)S(1)}, u32[]{:S(2)}, u32[]{:S(2)}) collective-permute-start(bf16[16,4224]{1,0:T(8,128)(2,1)S(1)} %message.2.refs_0_), channel_id=1, source_target_pairs={{0,2},{1,3},{2,0},{3,1},{4,6},{5,7},{6,4},{7,5},{8,10},{9,11},{10,... | collective-permute-start | bytes 405512 | tf_op jit(solution)/shard_map/ppermute | solution.py:153
  18.5 9.4 %collective-permute-start.4 = (bf16[32,4224]{1,0:T(8,128)(2,1)S(1)}, bf16[32,4224]{1,0:T(8,128)(2,1)S(1)}, u32[]{:S(2)}, u32[]{:S(2)}) collective-permute-start(bf16[32,4224]{1,0:T(8,128)(2,1)S(1)} %pad_maximum_fusion.5), channel_id=1, source_target_pairs={{0,2},{1,3},{2,0},{3,1},{4,6},{5,7},{6,4},{7,5},{8,10},{9,11},{10,... | collective-permute-start | bytes 811016 | tf_op jit(solution)/shard_map/ppermute | solution.py:153
  20.1 16.1 %copy-start = (s32[16]{0:T(128)S(1)}, s32[16]{0:T(128)}, u32[]{:S(2)}) copy-start(s32[16]{0:T(128)} %flags_ref.3) | copy-start | bytes 196
  20.1 10.6 %collective-permute-start.5 = (bf16[16,4224]{1,0:T(8,128)(2,1)S(1)}, bf16[16,4224]{1,0:T(8,128)(2,1)S(1)}, u32[]{:S(2)}, u32[]{:S(2)}) collective-permute-start(bf16[16,4224]{1,0:T(8,128)(2,1)S(1)} %collective-permute-done.2.refs_3_), channel_id=1, source_target_pairs={{0,2},{1,3},{2,0},{3,1},{4,6},{5,7},{6,4},{7,5},{8,10},{9,11},{10,... | collective-permute-start | bytes 405512 | tf_op jit(solution)/shard_map/ppermute | solution.py:153
  20.7 10.1 %collective-permute-start.14 = (bf16[16,4224]{1,0:T(8,128)(2,1)S(1)}, bf16[16,4224]{1,0:T(8,128)(2,1)S(1)}, u32[]{:S(2)}, u32[]{:S(2)}) collective-permute-start(bf16[16,4224]{1,0:T(8,128)(2,1)S(1)} %message.3.refs_0_), channel_id=1, source_target_pairs={{0,4},{1,5},{2,6},{3,7},{4,8},{5,9},{6,10},{7,11},{8,12},{9,13},{1... | collective-permute-start | bytes 405512 | tf_op jit(solution)/shard_map/ppermute | solution.py:156
  20.7 10.6 %collective-permute-start.15 = (bf16[16,4224]{1,0:T(8,128)(2,1)S(1)}, bf16[16,4224]{1,0:T(8,128)(2,1)S(1)}, u32[]{:S(2)}, u32[]{:S(2)}) collective-permute-start(bf16[16,4224]{1,0:T(8,128)(2,1)S(1)} %message.3.refs_0_), channel_id=1, source_target_pairs={{0,12},{1,13},{2,14},{3,15},{4,0},{5,1},{6,2},{7,3},{8,4},{9,5},{1... | collective-permute-start | bytes 405512 | tf_op jit(solution)/shard_map/ppermute | solution.py:156
  24.5 10.0 %collective-permute-start.16 = (bf16[16,4224]{1,0:T(8,128)(2,1)S(1)}, bf16[16,4224]{1,0:T(8,128)(2,1)S(1)}, u32[]{:S(2)}, u32[]{:S(2)}) collective-permute-start(bf16[16,4224]{1,0:T(8,128)(2,1)S(1)} %message.3.refs_0_), channel_id=1, source_target_pairs={{0,8},{1,9},{2,10},{3,11},{4,12},{5,13},{6,14},{7,15},{8,0},{9,1},... | collective-permute-start | bytes 405512 | tf_op jit(solution)/shard_map/ppermute | solution.py:156
  27.9 16.1 %collective-permute-start.17 = (bf16[16,4224]{1,0:T(8,128)(2,1)S(1)}, bf16[16,4224]{1,0:T(8,128)(2,1)S(1)}, u32[]{:S(2)}, u32[]{:S(2)}) collective-permute-start(bf16[16,4224]{1,0:T(8,128)(2,1)S(1)} %message.3.refs_0_), channel_id=1, source_target_pairs={{0,2},{1,3},{2,0},{3,1},{4,6},{5,7},{6,4},{7,5},{8,10},{9,11},{10,... | collective-permute-start | bytes 405512 | tf_op jit(solution)/shard_map/ppermute | solution.py:153
  30.8 5.4 %collective-permute-start.6 = (bf16[64,4224]{1,0:T(8,128)(2,1)S(1)}, bf16[64,4224]{1,0:T(8,128)(2,1)S(1)}, u32[]{:S(2)}, u32[]{:S(2)}) collective-permute-start(bf16[64,4224]{1,0:T(8,128)(2,1)S(1)} %pad_maximum_fusion), channel_id=1, source_target_pairs={{0,1},{1,0},{2,3},{3,2},{4,5},{5,4},{6,7},{7,6},{8,9},{9,8},{10,11... | collective-permute-start | bytes 1622024 | tf_op jit(solution)/shard_map/ppermute | solution.py:150
  30.8 5.4 %collective-permute-start.8 = (bf16[16,4224]{1,0:T(8,128)(2,1)S(1)}, bf16[16,4224]{1,0:T(8,128)(2,1)S(1)}, u32[]{:S(2)}, u32[]{:S(2)}) collective-permute-start(bf16[16,4224]{1,0:T(8,128)(2,1)S(1)} %collective-permute-done.5.refs_6_), channel_id=1, source_target_pairs={{0,1},{1,0},{2,3},{3,2},{4,5},{5,4},{6,7},{7,6},{8,9},{9,8},{10,11... | collective-permute-start | bytes 405512 | tf_op jit(solution)/shard_map/ppermute | solution.py:150
  31.3 4.9 %collective-permute-start.7 = (bf16[48,4224]{1,0:T(8,128)(2,1)S(1)}, bf16[48,4224]{1,0:T(8,128)(2,1)S(1)}, u32[]{:S(2)}, u32[]{:S(2)}) collective-permute-start(bf16[48,4224]{1,0:T(8,128)(2,1)S(1)} %pad_maximum_fusion.3), channel_id=1, source_target_pairs={{0,1},{1,0},{2,3},{3,2},{4,5},{5,4},{6,7},{7,6},{8,9},{9,8},{10,11... | collective-permute-start | bytes 1216520 | tf_op jit(solution)/shard_map/ppermute | solution.py:150
  34.6 10.7 %collective-permute-start.18 = (bf16[48,4224]{1,0:T(8,128)(2,1)S(1)}, bf16[48,4224]{1,0:T(8,128)(2,1)S(1)}, u32[]{:S(2)}, u32[]{:S(2)}) collective-permute-start(bf16[48,4224]{1,0:T(8,128)(2,1)S(1)} %pad_maximum_fusion.4), channel_id=1, source_target_pairs={{0,2},{1,3},{2,0},{3,1},{4,6},{5,7},{6,4},{7,5},{8,10},{9,11},{10,... | collective-permute-start | bytes 1216520 | tf_op jit(solution)/shard_map/ppermute | solution.py:153
  43.3 2.7 %collective-permute-start.9 = (bf16[128,4096]{1,0:T(8,128)(2,1)S(1)}, bf16[128,4096]{1,0:T(8,128)(2,1)S(1)}, u32[]{:S(2)}, u32[]{:S(2)}) collective-permute-start(bf16[128,4096]{1,0:T(8,128)(2,1)S(1)} %get-tuple-element.40), channel_id=1, source_target_pairs={{0,1},{1,0},{2,3},{3,2},{4,5},{5,4},{6,7},{7,6},{8,9},{9,8},{10,11... | collective-permute-start | bytes 3145736 | tf_op jit(solution)/shard_map/ppermute | solution.py:150
  43.4 3.8 %collective-permute-start.19 = (bf16[64,4224]{1,0:T(8,128)(2,1)S(1)}, bf16[64,4224]{1,0:T(8,128)(2,1)S(1)}, u32[]{:S(2)}, u32[]{:S(2)}) collective-permute-start(bf16[64,4224]{1,0:T(8,128)(2,1)S(1)} %pad_maximum_fusion.1), channel_id=1, source_target_pairs={{0,1},{1,0},{2,3},{3,2},{4,5},{5,4},{6,7},{7,6},{8,9},{9,8},{10,11... | collective-permute-start | bytes 1622024 | tf_op jit(solution)/shard_map/ppermute | solution.py:150
  45.4 2.2 %collective-permute-start.20 = (bf16[64,4224]{1,0:T(8,128)(2,1)S(1)}, bf16[64,4224]{1,0:T(8,128)(2,1)S(1)}, u32[]{:S(2)}, u32[]{:S(2)}) collective-permute-start(bf16[64,4224]{1,0:T(8,128)(2,1)S(1)} %pad_maximum_fusion.2), channel_id=1, source_target_pairs={{0,1},{1,0},{2,3},{3,2},{4,5},{5,4},{6,7},{7,6},{8,9},{9,8},{10,11... | collective-permute-start | bytes 1622024 | tf_op jit(solution)/shard_map/ppermute | solution.py:150
  46.1 14.0 %collective-permute-start.10 = (bf16[64,4096]{1,0:T(8,128)(2,1)S(1)}, bf16[64,4096]{1,0:T(8,128)(2,1)S(1)}, u32[]{:S(2)}, u32[]{:S(2)}) collective-permute-start(bf16[64,4096]{1,0:T(8,128)(2,1)S(1)} %add_convert_fusion.1), channel_id=1, source_target_pairs={{0,2},{1,3},{2,0},{3,1},{4,6},{5,7},{6,4},{7,5},{8,10},{9,11},{10,... | collective-permute-start | bytes 1572872 | tf_op jit(solution)/shard_map/ppermute | solution.py:153
  54.6 5.8 %collective-permute-start.21 = (bf16[128,4096]{1,0:T(8,128)(2,1)S(1)}, bf16[128,4096]{1,0:T(8,128)(2,1)S(1)}, u32[]{:S(2)}, u32[]{:S(2)}) collective-permute-start(bf16[128,4096]{1,0:T(8,128)(2,1)S(1)} %get-tuple-element.53), channel_id=1, source_target_pairs={{0,1},{1,0},{2,3},{3,2},{4,5},{5,4},{6,7},{7,6},{8,9},{9,8},{10,11... | collective-permute-start | bytes 3145736 | tf_op jit(solution)/shard_map/ppermute | solution.py:150
  60.7 5.2 %collective-permute-start.26 = (bf16[16,4096]{1,0:T(8,128)(2,1)S(1)}, bf16[16,4096]{1,0:T(8,128)(2,1)S(1)}, u32[]{:S(2)}, u32[]{:S(2)}) collective-permute-start(bf16[16,4096]{1,0:T(8,128)(2,1)S(1)} %get-tuple-element.63), channel_id=1, source_target_pairs={{0,2},{1,3},{2,0},{3,1},{4,6},{5,7},{6,4},{7,5},{8,10},{9,11},{10,... | collective-permute-start | bytes 393224 | tf_op jit(solution)/shard_map/ppermute | solution.py:153
  62.1 13.4 %collective-permute-start.11 = (bf16[16,4096]{1,0:T(8,128)(2,1)S(1)}, bf16[16,4096]{1,0:T(8,128)(2,1)S(1)}, u32[]{:S(2)}, u32[]{:S(2)}) collective-permute-start(bf16[16,4096]{1,0:T(8,128)(2,1)S(1)} %get-tuple-element.59), channel_id=1, source_target_pairs={{0,12},{1,13},{2,14},{3,15},{4,0},{5,1},{6,2},{7,3},{8,4},{9,5},{1... | collective-permute-start | bytes 393224 | tf_op jit(solution)/shard_map/ppermute | solution.py:156
  63.2 15.2 %collective-permute-start.12 = (bf16[16,4096]{1,0:T(8,128)(2,1)S(1)}, bf16[16,4096]{1,0:T(8,128)(2,1)S(1)}, u32[]{:S(2)}, u32[]{:S(2)}) collective-permute-start(bf16[16,4096]{1,0:T(8,128)(2,1)S(1)} %get-tuple-element.61), channel_id=1, source_target_pairs={{0,4},{1,5},{2,6},{3,7},{4,8},{5,9},{6,10},{7,11},{8,12},{9,13},{1... | collective-permute-start | bytes 393224 | tf_op jit(solution)/shard_map/ppermute | solution.py:156
  64.2 14.2 %collective-permute-start.13 = (bf16[16,4096]{1,0:T(8,128)(2,1)S(1)}, bf16[16,4096]{1,0:T(8,128)(2,1)S(1)}, u32[]{:S(2)}, u32[]{:S(2)}) collective-permute-start(bf16[16,4096]{1,0:T(8,128)(2,1)S(1)} %get-tuple-element.60), channel_id=1, source_target_pairs={{0,8},{1,9},{2,10},{3,11},{4,12},{5,13},{6,14},{7,15},{8,0},{9,1},... | collective-permute-start | bytes 393224 | tf_op jit(solution)/shard_map/ppermute | solution.py:156
  64.2 8.6 %collective-permute-start.23 = (bf16[32,4096]{1,0:T(8,128)(2,1)S(1)}, bf16[32,4096]{1,0:T(8,128)(2,1)S(1)}, u32[]{:S(2)}, u32[]{:S(2)}) collective-permute-start(bf16[32,4096]{1,0:T(8,128)(2,1)S(1)} %slice.80), channel_id=1, source_target_pairs={{0,2},{1,3},{2,0},{3,1},{4,6},{5,7},{6,4},{7,5},{8,10},{9,11},{10,... | collective-permute-start | bytes 786440 | tf_op jit(solution)/shard_map/ppermute | solution.py:153
  65.8 12.6 %collective-permute-start.22 = (bf16[16,4096]{1,0:T(8,128)(2,1)S(1)}, bf16[16,4096]{1,0:T(8,128)(2,1)S(1)}, u32[]{:S(2)}, u32[]{:S(2)}) collective-permute-start(bf16[16,4096]{1,0:T(8,128)(2,1)S(1)} %get-tuple-element.62), channel_id=1, source_target_pairs={{0,2},{1,3},{2,0},{3,1},{4,6},{5,7},{6,4},{7,5},{8,10},{9,11},{10,... | collective-permute-start | bytes 393224 | tf_op jit(solution)/shard_map/ppermute | solution.py:153
  72.7 10.1 %collective-permute-start.27 = (bf16[16,4096]{1,0:T(8,128)(2,1)S(1)}, bf16[16,4096]{1,0:T(8,128)(2,1)S(1)}, u32[]{:S(2)}, u32[]{:S(2)}) collective-permute-start(bf16[16,4096]{1,0:T(8,128)(2,1)S(1)} %fusion.1), channel_id=1, source_target_pairs={{0,8},{1,9},{2,10},{3,11},{4,12},{5,13},{6,14},{7,15},{8,0},{9,1},... | collective-permute-start | bytes 393224 | tf_op jit(solution)/shard_map/ppermute | solution.py:156
  75.5 7.4 %collective-permute-start.24 = (bf16[16,4096]{1,0:T(8,128)(2,1)S(1)}, bf16[16,4096]{1,0:T(8,128)(2,1)S(1)}, u32[]{:S(2)}, u32[]{:S(2)}) collective-permute-start(bf16[16,4096]{1,0:T(8,128)(2,1)S(1)} %get-tuple-element.64), channel_id=1, source_target_pairs={{0,12},{1,13},{2,14},{3,15},{4,0},{5,1},{6,2},{7,3},{8,4},{9,5},{1... | collective-permute-start | bytes 393224 | tf_op jit(solution)/shard_map/ppermute | solution.py:156
  78.4 6.9 %collective-permute-start.25 = (bf16[16,4096]{1,0:T(8,128)(2,1)S(1)}, bf16[16,4096]{1,0:T(8,128)(2,1)S(1)}, u32[]{:S(2)}, u32[]{:S(2)}) collective-permute-start(bf16[16,4096]{1,0:T(8,128)(2,1)S(1)} %get-tuple-element.65), channel_id=1, source_target_pairs={{0,4},{1,5},{2,6},{3,7},{4,8},{5,9},{6,10},{7,11},{8,12},{9,13},{1... | collective-permute-start | bytes 393224 | tf_op jit(solution)/shard_map/ppermute | solution.py:156

commit v4 on v3

--- a/solution.py
+++ b/solution.py
@@ -81,16 +81,16 @@
     )(*arrays)
 
 
-def expert_kernel(swapped, count, flags_ref, gate_ref, up_ref, down_ref, *refs):
+def expert_kernel(swapped, count, plan, flags_ref, gate_ref, up_ref, down_ref, *refs):
     *sources, own_ref, near_ref, other_ref, rows, hidden = refs
     width, units = gate_ref.shape
     tail = rows.shape[1] - width
     owner = lax.axis_index("expert")
     slot = jnp.bitwise_xor(owner, flags_ref[owner]) if swapped else owner
     at = 0
-    for source in sources:
-        rows[at : at + source.shape[0]] = source[...]
-        at += source.shape[0]
+    for source, low, high in plan:
+        rows[at : at + high - low] = sources[source][low:high]
+        at += high - low
     total = rows.shape[0]
     lane = lax.broadcasted_iota(jnp.int32, (total, tail), 1)
     terms = rows[:, width:].astype(jnp.float32)
@@ -114,13 +114,13 @@
     lax.fori_loop(0, width // 512, columns, 0)
 
 
-def run_expert(swapped, flags, weights, parts):
-    total = sum(part.shape[0] for part in parts)
+def run_expert(swapped, flags, weights, parts, plan):
+    total = sum(high - low for _, low, high in plan)
     count = total // 4
     width, units = weights[0].shape
     weights = [pltpu.with_memory_space_constraint(w, pltpu.VMEM) for w in weights]
     return pl.pallas_call(
-        functools.partial(expert_kernel, swapped, count),
+        functools.partial(expert_kernel, swapped, count, plan),
         out_shape=[jax.ShapeDtypeStruct((k * count, width), jnp.bfloat16) for k in (1, 1, 2)],
         in_specs=[pl.BlockSpec(memory_space=pltpu.SMEM)] + [in_vmem()] * (3 + len(parts)),
         out_specs=[in_vmem()] * 3,
@@ -152,55 +152,61 @@
     def swap_near(x):
         return lax.ppermute(x, "expert", [(index(z, y, c), index(z, 1 - y, c)) for z, y, c in every])
 
-    def shift_far(x, by):
-        return lax.ppermute(x, "expert", [(index(z, y, c), index((z + by) % lines, y, c)) for z, y, c in every])
+    def swap_far(x, by):
+        return lax.ppermute(x, "expert", [(index(z, y, c), index(z ^ by, y, c)) for z, y, c in every])
+
+    def stack(blocks):
+        return jnp.concatenate(blocks) if len(blocks) > 1 else blocks[0]
 
     tail = 2 * devices
     tail = -(-tail // LANES) * LANES
     ids, probs = jnp.swapaxes(ids, 1, 2), jnp.swapaxes(probs, 1, 2)
-    order = sorted(range(lines), key=lambda by: min(by, lines - by))
-    close, far = order[1 : 1 + lines // 2], order[1 + lines // 2 :]
-    weights = load_weights(w_gate[0], w_up[0], w_down[0])
+    middle = lines // 2
+    head, half = middle * tokens, lines * tokens
+    plan = (
+        *((0, 0, head), (1, 0, head), (0, head, half), (2, 0, head)),
+        *((3, 0, head), (4, 0, head), (3, head, half), (5, 0, head)),
+    )
     messages = [make_message(states, ids, probs, step, tail) for step in range(steps)]
-    gathered = []
-    blocks = None
+    weights = [w_gate[0], w_up[0], w_down[0]]
+    near_owns = [swap_near(message) for message in messages]
+    gathered, far = [], None
     for step in range(steps):
-        message = messages[step]
-        near_own = swap_near(message)
+        message, near_own = messages[step], near_owns[step]
         if step:
-            message, _ = lax.optimization_barrier((message, blocks))
-        blocks = [shift_far(message, by) for by in order[1:]]
+            message, _ = lax.optimization_barrier((message, far))
+        close = stack([swap_far(message, by) for by in range(1, middle)])
+        far = [swap_far(message, by) for by in range(middle, lines)]
+        near_close = swap_near(close)
         if not step:
-            blocks, weights, messages[1:] = lax.optimization_barrier((blocks, weights, messages[1:]))
-            split = len(close)
-            near = [near_own, swap_near(jnp.concatenate(blocks[:split])), swap_near(jnp.concatenate(blocks[split:]))]
-            core = [swap_core(jnp.concatenate(near[:2])), swap_core(near[2])]
-        else:
-            near = [near_own, swap_near(jnp.concatenate(blocks))]
-            core = [swap_core(jnp.concatenate(near))]
-        line = [message, *blocks]
-        gathered.append((*line, *near, swap_core(jnp.concatenate(line)), *core))
+            weights, close = lax.optimization_barrier((weights, close))
+            weights = load_weights(*weights)
+            far, weights, near_close, near_owns = lax.optimization_barrier((far, weights, near_close, near_owns))
+        far = stack(far)
+        near_far = swap_near(far)
+        line = jnp.concatenate([message, close, near_own, near_close])
+        gathered.append((line, far, near_far, swap_core(line), swap_core(far), swap_core(near_far)))
     outputs = []
-    other = None
     for step in range(steps):
         parts = gathered[step]
         if step:
-            parts, _ = lax.optimization_barrier((parts, other))
-        own, peer, other = run_expert(step > 0, flags, weights, parts)
+            parts, _ = lax.optimization_barrier((parts, ready))
+        own, peer, other = run_expert(step > 0, flags, weights, parts, plan)
         other = swap_core(other)
-        half = own.shape[0]
         own = own.astype(jnp.float32) + other[:half].astype(jnp.float32)
         peer = (peer.astype(jnp.float32) + other[half:].astype(jnp.float32)).astype(jnp.bfloat16)
-        cuts = [0, half] if step + 1 < steps else [0, tokens, (1 + len(close)) * tokens, half]
-        places = list(zip(cuts[:-1], cuts[1:]))
-        blocks = []
-        for low, high in places[::-1]:
-            near = swap_near(peer[low:high])
-            both = own[low:high] + near.astype(jnp.float32)
-            blocks = [both[at : at + tokens] for at in range(0, high - low, tokens)] + blocks
-        mixed = blocks[0]
-        for by, block in zip(order[1:], blocks[1:]):
-            mixed += shift_far(block.astype(jnp.bfloat16), lines - by).astype(jnp.float32)
+        ready = peer
+        near_far = swap_near(peer[head:])
+        near_close = peer[:head]
+        if step + 1 == steps:
+            near_close, _ = lax.optimization_barrier((near_close, near_far))
+        far = own[head:] + near_far.astype(jnp.float32)
+        _, close = lax.optimization_barrier((far, swap_near(near_close)))
+        close = own[:head] + close.astype(jnp.float32)
+        mixed = close[:tokens]
+        for by in range(lines - 1, 0, -1):
+            block = far[by * tokens - head :][:tokens] if by >= middle else close[by * tokens :][:tokens]
+            mixed += swap_far(block.astype(jnp.bfloat16), by).astype(jnp.float32)
         outputs.append(mixed.astype(jnp.bfloat16))
     return jnp.stack(outputs)
 

time: 86.2 us -> 89.8 us (1.042)
  starting transfers between devices: 31.5 us -> 35.8 us
    ppermute x9 -> x10, waiting for transfers between devices: 16.7 us -> 9.67 us  [swap_near(): lax.ppermute(x, 'expert', [(index(z, y, c), index(z, 1 - y, c)) for z, y,...]
    ppermute x12, waiting for transfers between devices: 12.2 us -> 18.3 us  [swap_far(): lax.ppermute(x, 'expert', [(index(z, y, c), index(z ^ by, y, c)) for z, y...]
    ppermute x12, starting transfers between devices: 17.5 us -> 23 us  [swap_far(): lax.ppermute(x, 'expert', [(index(z, y, c), index(z ^ by, y, c)) for z, y...]
    ppermute x9 -> x10, starting transfers between devices: 12.5 us -> 11.4 us  [swap_near(): lax.ppermute(x, 'expert', [(index(z, y, c), index(z, 1 - y, c)) for z, y,...]
  transfers between devices with their start and end apart: 28 -> 30, of which waited for: 12 -> 10; matrix products, arithmetic and copies ran while one was open for 1% -> 1% of each run, Pallas kernels for 25% -> 24%
where the time goes in v4:
time: 89.8 us; the launch traced here: 89.6 us
  starting transfers between devices  35.8 us (40%)
  waiting for transfers between devices  29 us (32%)
  Pallas kernels  22.7 us (25%)
  other arithmetic  1.59 us (2%)
    ppermute x12, starting transfers between devices, swap_far(): lax.ppermute(x, 'expert', [(index(z, y, c), index(z ^ by, y, c)) for z, y...  23 us
    ppermute x12, waiting for transfers between devices, swap_far(): lax.ppermute(x, 'expert', [(index(z, y, c), index(z ^ by, y, c)) for z, y...  18.3 us
    pallas_call x2, Pallas kernels, run_expert(): pl.pallas_call(functools.partial(expert_kernel, swapped, count, plan), ou...  14 us
    ppermute x10, starting transfers between devices, swap_near(): lax.ppermute(x, 'expert', [(index(z, y, c), index(z, 1 - y, c)) for z, y,...  11.4 us
    ppermute x10, waiting for transfers between devices, swap_near(): lax.ppermute(x, 'expert', [(index(z, y, c), index(z, 1 - y, c)) for z, y,...  9.67 us
    pallas_call x1, Pallas kernels, load_weights(): pl.pallas_call(load_kernel, out_shape=[pltpu.VMEM(x.shape, x.dtype) for x...  6.42 us
    pallas_call x2, Pallas kernels, make_message(): pl.pallas_call(message_kernel, grid=(1,), out_shape=jax.ShapeDtypeStruct(...  2.23 us
  transfers between devices with their start and end apart: 30, of which 10 were waited for; matrix products, arithmetic and copies ran while one was open for 1% of the time, Pallas kernels for 24%

profile of v4, /device:TPU:0, one launch (start us, length us, event | category | flops | bytes accessed | tf_op | source)
XLA Modules:
  0.0 89.6 jit_solution(7507048721308142413)
XLA Ops:
  0.0 1.1 %message.2 = bf16[16,4224]{1,0:T(8,128)(2,1)S(1)} custom-call(bf16[2,16,4096]{2,1,0:T(8,128)(2,1)} %states_ref.3, s32[2,8,16]{2,1,0:T(8,128)} %bitcast.12, f32[2,8,16]{2,1,0:T(8,128)} %bitcast.14), custom_call_target="tpu_custom_call" | custom-call | tf_op jit(solution)/shard_map/message/pallas_call | solution.py:46
  1.1 3.0 %collective-permute-start.2 = (bf16[16,4224]{1,0:T(8,128)(2,1)S(1)}, bf16[16,4224]{1,0:T(8,128)(2,1)S(1)}, u32[]{:S(2)}, u32[]{:S(2)}) collective-permute-start(bf16[16,4224]{1,0:T(8,128)(2,1)S(1)} %message.2), channel_id=1, source_target_pairs={{0,4},{1,5},{2,6},{3,7},{4,0},{5,1},{6,2},{7,3},{8,12},{9,13},{10,... | collective-permute-start | bytes 405512 | tf_op jit(solution)/shard_map/ppermute | solution.py:156
  4.1 1.5 %collective-permute-start.4 = (bf16[16,4224]{1,0:T(8,128)(2,1)S(1)}, bf16[16,4224]{1,0:T(8,128)(2,1)S(1)}, u32[]{:S(2)}, u32[]{:S(2)}) collective-permute-start(bf16[16,4224]{1,0:T(8,128)(2,1)S(1)} %message.2), channel_id=1, source_target_pairs={{0,2},{1,3},{2,0},{3,1},{4,6},{5,7},{6,4},{7,5},{8,10},{9,11},{10,... | collective-permute-start | bytes 405512 | tf_op jit(solution)/shard_map/ppermute | solution.py:153
  5.7 2.6 %collective-permute-start = (bf16[16,4224]{1,0:T(8,128)(2,1)S(1)}, bf16[16,4224]{1,0:T(8,128)(2,1)S(1)}, u32[]{:S(2)}, u32[]{:S(2)}) collective-permute-start(bf16[16,4224]{1,0:T(8,128)(2,1)S(1)} %message.2), channel_id=1, source_target_pairs={{0,8},{1,9},{2,10},{3,11},{4,12},{5,13},{6,14},{7,15},{8,0},{9,1},... | collective-permute-start | bytes 405512 | tf_op jit(solution)/shard_map/ppermute | solution.py:156
  8.3 0.2 collective-permute-start.1
  8.5 1.1 %message.3 = bf16[16,4224]{1,0:T(8,128)(2,1)S(1)} custom-call(bf16[2,16,4096]{2,1,0:T(8,128)(2,1)} %states_ref.3, s32[2,8,16]{2,1,0:T(8,128)} %bitcast.13, f32[2,8,16]{2,1,0:T(8,128)} %bitcast.15), custom_call_target="tpu_custom_call" | custom-call | tf_op jit(solution)/shard_map/message/pallas_call | solution.py:46
  9.6 0.3 collective-permute-start.5
  9.9 0.0 collective-permute-done.2
  9.9 1.7 %collective-permute-start.3 = (bf16[16,4224]{1,0:T(8,128)(2,1)S(1)}, bf16[16,4224]{1,0:T(8,128)(2,1)S(1)}, u32[]{:S(2)}, u32[]{:S(2)}) collective-permute-start(bf16[16,4224]{1,0:T(8,128)(2,1)S(1)} %collective-permute-done.2), channel_id=1, source_target_pairs={{0,2},{1,3},{2,0},{3,1},{4,6},{5,7},{6,4},{7,5},{8,10},{9,11},{10,... | collective-permute-start | bytes 405512 | tf_op jit(solution)/shard_map/ppermute | solution.py:153
  11.6 6.4 %load_weights.1 = (bf16[4096,768]{1,0:T(8,128)(2,1)S(1)}, bf16[4096,768]{1,0:T(8,128)(2,1)S(1)}, bf16[768,4096]{1,0:T(8,128)(2,1)S(1)}) custom-call(bf16[4096,768]{1,0:T(8,128)(2,1)} %bitcast.9, bf16[4096,768]{1,0:T(8,128)(2,1)} %bitcast.10, bf16[768,4096]{1,0:T(8,128)(2,1)} %bitcast.11), custom_call_target="tpu_custom_call" | custom-call | bytes 18874368 | tf_op jit(solution)/shard_map/load_weights/pallas_call | solution.py:70
  18.1 0.0 collective-permute-done.4
  18.1 0.1 collective-permute-done
  18.2 0.0 collective-permute-done.3
  18.3 0.0 copy-start
  18.3 1.0 %collective-permute-start.6 = (bf16[32,4224]{1,0:T(8,128)(2,1)S(1)}, bf16[32,4224]{1,0:T(8,128)(2,1)S(1)}, u32[]{:S(2)}, u32[]{:S(2)}) collective-permute-start(bf16[32,4224]{1,0:T(8,128)(2,1)S(1)} %constant_dynamic-update-slice_fusion.refs_1_), channel_id=1, source_target_pairs={{0,2},{1,3},{2,0},{3,1},{4,6},{5,7},{6,4},{7,5},{8,10},{9,11},{10,... | collective-permute-start | bytes 811016 | tf_op jit(solution)/shard_map/ppermute | solution.py:153
  19.3 0.0 collective-permute-start.8
  19.3 3.0 %collective-permute-start.18 = (bf16[16,4224]{1,0:T(8,128)(2,1)S(1)}, bf16[16,4224]{1,0:T(8,128)(2,1)S(1)}, u32[]{:S(2)}, u32[]{:S(2)}) collective-permute-start(bf16[16,4224]{1,0:T(8,128)(2,1)S(1)} %message.3), channel_id=1, source_target_pairs={{0,8},{1,9},{2,10},{3,11},{4,12},{5,13},{6,14},{7,15},{8,0},{9,1},... | collective-permute-start | bytes 405512 | tf_op jit(solution)/shard_map/ppermute | solution.py:156
  22.3 1.3 %collective-permute-start.19 = (bf16[16,4224]{1,0:T(8,128)(2,1)S(1)}, bf16[16,4224]{1,0:T(8,128)(2,1)S(1)}, u32[]{:S(2)}, u32[]{:S(2)}) collective-permute-start(bf16[16,4224]{1,0:T(8,128)(2,1)S(1)} %message.3), channel_id=1, source_target_pairs={{0,12},{1,13},{2,14},{3,15},{4,8},{5,9},{6,10},{7,11},{8,4},{9,5},... | collective-permute-start | bytes 405512 | tf_op jit(solution)/shard_map/ppermute | solution.py:156
  23.6 0.1 collective-permute-start.16
  23.7 0.1 pad_maximum_fusion.refs_0_
  23.8 8.8 %collective-permute-done.18 = bf16[16,4224]{1,0:T(8,128)(2,1)S(1)} collective-permute-done((bf16[16,4224]{1,0:T(8,128)(2,1)S(1)}, bf16[16,4224]{1,0:T(8,128)(2,1)S(1)}, u32[]{:S(2)}, u32[]{:S(2)}) %collective-permute-start.18) | collective-permute-done | bytes 135200 | tf_op jit(solution)/shard_map/ppermute | solution.py:156
  32.6 0.0 collective-permute-done.19
  32.6 1.6 %collective-permute-start.20 = (bf16[32,4224]{1,0:T(8,128)(2,1)S(1)}, bf16[32,4224]{1,0:T(8,128)(2,1)S(1)}, u32[]{:S(2)}, u32[]{:S(2)}) collective-permute-start(bf16[32,4224]{1,0:T(8,128)(2,1)S(1)} %constant_dynamic-update-slice_fusion.6.refs_1_), channel_id=1, source_target_pairs={{0,2},{1,3},{2,0},{3,1},{4,6},{5,7},{6,4},{7,5},{8,10},{9,11},{10,... | collective-permute-start | bytes 811016 | tf_op jit(solution)/shard_map/ppermute | solution.py:153
  34.2 0.0 collective-permute-done.16
  34.2 0.2 collective-permute-start.22
  34.4 0.0 collective-permute-done.6.refs_2_
  34.4 0.3 collective-permute-start.9
  34.7 1.2 %collective-permute-start.17 = (bf16[16,4224]{1,0:T(8,128)(2,1)S(1)}, bf16[16,4224]{1,0:T(8,128)(2,1)S(1)}, u32[]{:S(2)}, u32[]{:S(2)}) collective-permute-start(bf16[16,4224]{1,0:T(8,128)(2,1)S(1)} %collective-permute-done.16), channel_id=1, source_target_pairs={{0,2},{1,3},{2,0},{3,1},{4,6},{5,7},{6,4},{7,5},{8,10},{9,11},{10,... | collective-permute-start | bytes 405512 | tf_op jit(solution)/shard_map/ppermute | solution.py:153
  35.9 0.2 collective-permute-done.9.refs_5_
  36.1 0.0 collective-permute-done.7.refs_3_
  36.1 7.0 %expert.2 = (bf16[64,4096]{1,0:T(8,128)(2,1)S(1)}, bf16[64,4096]{1,0:T(8,128)(2,1)S(1)}, bf16[128,4096]{1,0:T(8,128)(2,1)S(1)}) custom-call(s32[16]{0:T(128)S(1)} %copy-done, bf16[4096,768]{1,0:T(8,128)(2,1)S(1)} %get-tuple-element.41.gate_ref, bf16[4096,768]{1,0:T(8,128)(2,1)S(1)} %get-tuple-element.42.up_ref, ...), custom_call_target="tpu_custom_call" | custom-call | flops 4831838208 | bytes 4194304 | tf_op jit(solution)/shard_map/expert/pallas_call | solution.py:122
  43.1 0.3 collective-permute-start.10
  43.5 1.0 %collective-permute-done.17 = bf16[16,4224]{1,0:T(8,128)(2,1)S(1)} collective-permute-done((bf16[16,4224]{1,0:T(8,128)(2,1)S(1)}, bf16[16,4224]{1,0:T(8,128)(2,1)S(1)}, u32[]{:S(2)}, u32[]{:S(2)}) %collective-permute-start.17) | collective-permute-done | bytes 135200 | tf_op jit(solution)/shard_map/ppermute | solution.py:153
  44.5 0.1 collective-permute-start.21
  44.5 0.0 collective-permute-done.20.refs_2_
  44.6 0.5 collective-permute-start.23
  45.0 0.8 collective-permute-done.10
  45.9 0.2 convert_add_fusion.1
  46.2 1.2 %collective-permute-start.11 = (bf16[32,4096]{1,0:T(8,128)(2,1)S(1)}, bf16[32,4096]{1,0:T(8,128)(2,1)S(1)}, u32[]{:S(2)}, u32[]{:S(2)}) collective-permute-start(bf16[32,4096]{1,0:T(8,128)(2,1)S(1)} %get-tuple-element.70), channel_id=1, source_target_pairs={{0,2},{1,3},{2,0},{3,1},{4,6},{5,7},{6,4},{7,5},{8,10},{9,11},{10,... | collective-permute-start | bytes 786440 | tf_op jit(solution)/shard_map/ppermute | solution.py:153
  47.3 0.9 %collective-permute-start.12 = (bf16[32,4096]{1,0:T(8,128)(2,1)S(1)}, bf16[32,4096]{1,0:T(8,128)(2,1)S(1)}, u32[]{:S(2)}, u32[]{:S(2)}) collective-permute-start(bf16[32,4096]{1,0:T(8,128)(2,1)S(1)} %get-tuple-element.69), channel_id=1, source_target_pairs={{0,2},{1,3},{2,0},{3,1},{4,6},{5,7},{6,4},{7,5},{8,10},{9,11},{10,... | collective-permute-start | bytes 786440 | tf_op jit(solution)/shard_map/ppermute | solution.py:153
  48.2 0.0 collective-permute-done.22.refs_4_
  48.2 0.0 collective-permute-done.23.refs_5_
  48.2 0.0 collective-permute-done.21.refs_3_
  48.3 7.0 %expert.3 = (bf16[64,4096]{1,0:T(8,128)(2,1)S(1)}, bf16[64,4096]{1,0:T(8,128)(2,1)S(1)}, bf16[128,4096]{1,0:T(8,128)(2,1)S(1)}) custom-call(s32[16]{0:T(128)S(1)} %copy-done, bf16[4096,768]{1,0:T(8,128)(2,1)S(1)} %get-tuple-element.41.gate_ref, bf16[4096,768]{1,0:T(8,128)(2,1)S(1)} %get-tuple-element.42.up_ref, ...), custom_call_target="tpu_custom_call" | custom-call | flops 4831838208 | bytes 4194304 | tf_op jit(solution)/shard_map/expert/pallas_call | solution.py:122
  55.3 0.1 collective-permute-start.24
  55.4 0.1 slice_add_fusion.2
  55.4 4.8 %collective-permute-done.12 = bf16[32,4096]{1,0:T(8,128)(2,1)S(1)} collective-permute-done((bf16[32,4096]{1,0:T(8,128)(2,1)S(1)}, bf16[32,4096]{1,0:T(8,128)(2,1)S(1)}, u32[]{:S(2)}, u32[]{:S(2)}) %collective-permute-start.12) | collective-permute-done | bytes 262176 | tf_op jit(solution)/shard_map/ppermute | solution.py:153
  60.3 0.1 slice_add_fusion.3
  60.3 0.2 add_convert_fusion
  60.6 1.1 %collective-permute-start.25 = (bf16[32,4096]{1,0:T(8,128)(2,1)S(1)}, bf16[32,4096]{1,0:T(8,128)(2,1)S(1)}, u32[]{:S(2)}, u32[]{:S(2)}) collective-permute-start(bf16[32,4096]{1,0:T(8,128)(2,1)S(1)} %get-tuple-element.72), channel_id=1, source_target_pairs={{0,2},{1,3},{2,0},{3,1},{4,6},{5,7},{6,4},{7,5},{8,10},{9,11},{10,... | collective-permute-start | bytes 786440 | tf_op jit(solution)/shard_map/ppermute | solution.py:153
  61.7 2.9 %collective-permute-start.15 = (bf16[16,4096]{1,0:T(8,128)(2,1)S(1)}, bf16[16,4096]{1,0:T(8,128)(2,1)S(1)}, u32[]{:S(2)}, u32[]{:S(2)}) collective-permute-start(bf16[16,4096]{1,0:T(8,128)(2,1)S(1)} %slice.135), channel_id=1, source_target_pairs={{0,4},{1,5},{2,6},{3,7},{4,0},{5,1},{6,2},{7,3},{8,12},{9,13},{10,... | collective-permute-start | bytes 393224 | tf_op jit(solution)/shard_map/ppermute | solution.py:156
  64.7 2.7 %collective-permute-start.13 = (bf16[16,4096]{1,0:T(8,128)(2,1)S(1)}, bf16[16,4096]{1,0:T(8,128)(2,1)S(1)}, u32[]{:S(2)}, u32[]{:S(2)}) collective-permute-start(bf16[16,4096]{1,0:T(8,128)(2,1)S(1)} %get-tuple-element.73), channel_id=1, source_target_pairs={{0,12},{1,13},{2,14},{3,15},{4,8},{5,9},{6,10},{7,11},{8,4},{9,5},... | collective-permute-start | bytes 393224 | tf_op jit(solution)/shard_map/ppermute | solution.py:156
  67.4 0.9 %collective-permute-done.25 = bf16[32,4096]{1,0:T(8,128)(2,1)S(1)} collective-permute-done((bf16[32,4096]{1,0:T(8,128)(2,1)S(1)}, bf16[32,4096]{1,0:T(8,128)(2,1)S(1)}, u32[]{:S(2)}, u32[]{:S(2)}) %collective-permute-start.25) | collective-permute-done | bytes 262176 | tf_op jit(solution)/shard_map/ppermute | solution.py:153
  68.3 0.9 %collective-permute-start.26 = (bf16[32,4096]{1,0:T(8,128)(2,1)S(1)}, bf16[32,4096]{1,0:T(8,128)(2,1)S(1)}, u32[]{:S(2)}, u32[]{:S(2)}) collective-permute-start(bf16[32,4096]{1,0:T(8,128)(2,1)S(1)} %get-tuple-element.63), channel_id=1, source_target_pairs={{0,2},{1,3},{2,0},{3,1},{4,6},{5,7},{6,4},{7,5},{8,10},{9,11},{10,... | collective-permute-start | bytes 786440 | tf_op jit(solution)/shard_map/ppermute | solution.py:153
  69.3 2.8 %collective-permute-start.27 = (bf16[16,4096]{1,0:T(8,128)(2,1)S(1)}, bf16[16,4096]{1,0:T(8,128)(2,1)S(1)}, u32[]{:S(2)}, u32[]{:S(2)}) collective-permute-start(bf16[16,4096]{1,0:T(8,128)(2,1)S(1)} %get-tuple-element.75), channel_id=1, source_target_pairs={{0,12},{1,13},{2,14},{3,15},{4,8},{5,9},{6,10},{7,11},{8,4},{9,5},... | collective-permute-start | bytes 393224 | tf_op jit(solution)/shard_map/ppermute | solution.py:156
  72.1 2.9 %collective-permute-done.26 = bf16[32,4096]{1,0:T(8,128)(2,1)S(1)} collective-permute-done((bf16[32,4096]{1,0:T(8,128)(2,1)S(1)}, bf16[32,4096]{1,0:T(8,128)(2,1)S(1)}, u32[]{:S(2)}, u32[]{:S(2)}) %collective-permute-start.26) | collective-permute-done | bytes 262176 | tf_op jit(solution)/shard_map/ppermute | solution.py:153
  75.0 4.2 %collective-permute-start.28 = (bf16[16,4096]{1,0:T(8,128)(2,1)S(1)}, bf16[16,4096]{1,0:T(8,128)(2,1)S(1)}, u32[]{:S(2)}, u32[]{:S(2)}) collective-permute-start(bf16[16,4096]{1,0:T(8,128)(2,1)S(1)} %get-tuple-element.76), channel_id=1, source_target_pairs={{0,8},{1,9},{2,10},{3,11},{4,12},{5,13},{6,14},{7,15},{8,0},{9,1},... | collective-permute-start | bytes 393224 | tf_op jit(solution)/shard_map/ppermute | solution.py:156
  79.2 0.1 slice_add_fusion.1
  79.3 0.1 collective-permute-start.29
  79.4 4.5 %collective-permute-done.14 = bf16[16,4096]{1,0:T(8,128)(2,1)S(1)} collective-permute-done((bf16[16,4096]{1,0:T(8,128)(2,1)S(1)}, bf16[16,4096]{1,0:T(8,128)(2,1)S(1)}, u32[]{:S(2)}, u32[]{:S(2)}) %collective-permute-start.14) | collective-permute-done | bytes 131104 | tf_op jit(solution)/shard_map/ppermute | solution.py:156
  83.9 0.1 fusion.6
  84.0 4.8 %collective-permute-done.28 = bf16[16,4096]{1,0:T(8,128)(2,1)S(1)} collective-permute-done((bf16[16,4096]{1,0:T(8,128)(2,1)S(1)}, bf16[16,4096]{1,0:T(8,128)(2,1)S(1)}, u32[]{:S(2)}, u32[]{:S(2)}) %collective-permute-start.28) | collective-permute-done | bytes 131104 | tf_op jit(solution)/shard_map/ppermute | solution.py:156
  88.8 0.1 fusion.7
  88.9 0.7 pad_maximum_fusion.1
  (27 shorter events, 0.3 us)
Async XLA Ops:
  1.1 8.8 %collective-permute-start.2 = (bf16[16,4224]{1,0:T(8,128)(2,1)S(1)}, bf16[16,4224]{1,0:T(8,128)(2,1)S(1)}, u32[]{:S(2)}, u32[]{:S(2)}) collective-permute-start(bf16[16,4224]{1,0:T(8,128)(2,1)S(1)} %message.2), channel_id=1, source_target_pairs={{0,4},{1,5},{2,6},{3,7},{4,0},{5,1},{6,2},{7,3},{8,12},{9,13},{10,... | collective-permute-start | bytes 405512 | tf_op jit(solution)/shard_map/ppermute | solution.py:156
  4.1 13.9 %collective-permute-start.4 = (bf16[16,4224]{1,0:T(8,128)(2,1)S(1)}, bf16[16,4224]{1,0:T(8,128)(2,1)S(1)}, u32[]{:S(2)}, u32[]{:S(2)}) collective-permute-start(bf16[16,4224]{1,0:T(8,128)(2,1)S(1)} %message.2), channel_id=1, source_target_pairs={{0,2},{1,3},{2,0},{3,1},{4,6},{5,7},{6,4},{7,5},{8,10},{9,11},{10,... | collective-permute-start | bytes 405512 | tf_op jit(solution)/shard_map/ppermute | solution.py:153
  5.7 12.5 %collective-permute-start = (bf16[16,4224]{1,0:T(8,128)(2,1)S(1)}, bf16[16,4224]{1,0:T(8,128)(2,1)S(1)}, u32[]{:S(2)}, u32[]{:S(2)}) collective-permute-start(bf16[16,4224]{1,0:T(8,128)(2,1)S(1)} %message.2), channel_id=1, source_target_pairs={{0,8},{1,9},{2,10},{3,11},{4,12},{5,13},{6,14},{7,15},{8,0},{9,1},... | collective-permute-start | bytes 405512 | tf_op jit(solution)/shard_map/ppermute | solution.py:156
  8.3 10.0 %collective-permute-start.1 = (bf16[16,4224]{1,0:T(8,128)(2,1)S(1)}, bf16[16,4224]{1,0:T(8,128)(2,1)S(1)}, u32[]{:S(2)}, u32[]{:S(2)}) collective-permute-start(bf16[16,4224]{1,0:T(8,128)(2,1)S(1)} %message.2), channel_id=1, source_target_pairs={{0,12},{1,13},{2,14},{3,15},{4,8},{5,9},{6,10},{7,11},{8,4},{9,5},... | collective-permute-start | bytes 405512 | tf_op jit(solution)/shard_map/ppermute | solution.py:156
  9.6 8.6 %collective-permute-start.5 = (bf16[16,4224]{1,0:T(8,128)(2,1)S(1)}, bf16[16,4224]{1,0:T(8,128)(2,1)S(1)}, u32[]{:S(2)}, u32[]{:S(2)}) collective-permute-start(bf16[16,4224]{1,0:T(8,128)(2,1)S(1)} %message.3), channel_id=1, source_target_pairs={{0,2},{1,3},{2,0},{3,1},{4,6},{5,7},{6,4},{7,5},{8,10},{9,11},{10,... | collective-permute-start | bytes 405512 | tf_op jit(solution)/shard_map/ppermute | solution.py:153
  9.9 8.3 %collective-permute-start.3 = (bf16[16,4224]{1,0:T(8,128)(2,1)S(1)}, bf16[16,4224]{1,0:T(8,128)(2,1)S(1)}, u32[]{:S(2)}, u32[]{:S(2)}) collective-permute-start(bf16[16,4224]{1,0:T(8,128)(2,1)S(1)} %collective-permute-done.2), channel_id=1, source_target_pairs={{0,2},{1,3},{2,0},{3,1},{4,6},{5,7},{6,4},{7,5},{8,10},{9,11},{10,... | collective-permute-start | bytes 405512 | tf_op jit(solution)/shard_map/ppermute | solution.py:153
  18.3 17.9 %copy-start = (s32[16]{0:T(128)S(1)}, s32[16]{0:T(128)}, u32[]{:S(2)}) copy-start(s32[16]{0:T(128)} %flags_ref.3) | copy-start | bytes 196
  18.3 16.1 %collective-permute-start.6 = (bf16[32,4224]{1,0:T(8,128)(2,1)S(1)}, bf16[32,4224]{1,0:T(8,128)(2,1)S(1)}, u32[]{:S(2)}, u32[]{:S(2)}) collective-permute-start(bf16[32,4224]{1,0:T(8,128)(2,1)S(1)} %constant_dynamic-update-slice_fusion.refs_1_), channel_id=1, source_target_pairs={{0,2},{1,3},{2,0},{3,1},{4,6},{5,7},{6,4},{7,5},{8,10},{9,11},{10,... | collective-permute-start | bytes 811016 | tf_op jit(solution)/shard_map/ppermute | solution.py:153
  19.3 15.5 %collective-permute-start.8 = (bf16[32,4224]{1,0:T(8,128)(2,1)S(1)}, bf16[32,4224]{1,0:T(8,128)(2,1)S(1)}, u32[]{:S(2)}, u32[]{:S(2)}) collective-permute-start(bf16[32,4224]{1,0:T(8,128)(2,1)S(1)} %constant_dynamic-update-slice_fusion.refs_1_), channel_id=1, source_target_pairs={{0,1},{1,0},{2,3},{3,2},{4,5},{5,4},{6,7},{7,6},{8,9},{9,8},{10,11... | collective-permute-start | bytes 811016 | tf_op jit(solution)/shard_map/ppermute | solution.py:150
  19.3 13.3 %collective-permute-start.18 = (bf16[16,4224]{1,0:T(8,128)(2,1)S(1)}, bf16[16,4224]{1,0:T(8,128)(2,1)S(1)}, u32[]{:S(2)}, u32[]{:S(2)}) collective-permute-start(bf16[16,4224]{1,0:T(8,128)(2,1)S(1)} %message.3), channel_id=1, source_target_pairs={{0,8},{1,9},{2,10},{3,11},{4,12},{5,13},{6,14},{7,15},{8,0},{9,1},... | collective-permute-start | bytes 405512 | tf_op jit(solution)/shard_map/ppermute | solution.py:156
  22.3 10.3 %collective-permute-start.19 = (bf16[16,4224]{1,0:T(8,128)(2,1)S(1)}, bf16[16,4224]{1,0:T(8,128)(2,1)S(1)}, u32[]{:S(2)}, u32[]{:S(2)}) collective-permute-start(bf16[16,4224]{1,0:T(8,128)(2,1)S(1)} %message.3), channel_id=1, source_target_pairs={{0,12},{1,13},{2,14},{3,15},{4,8},{5,9},{6,10},{7,11},{8,4},{9,5},... | collective-permute-start | bytes 405512 | tf_op jit(solution)/shard_map/ppermute | solution.py:156
  23.6 10.5 %collective-permute-start.16 = (bf16[16,4224]{1,0:T(8,128)(2,1)S(1)}, bf16[16,4224]{1,0:T(8,128)(2,1)S(1)}, u32[]{:S(2)}, u32[]{:S(2)}) collective-permute-start(bf16[16,4224]{1,0:T(8,128)(2,1)S(1)} %message.3), channel_id=1, source_target_pairs={{0,4},{1,5},{2,6},{3,7},{4,0},{5,1},{6,2},{7,3},{8,12},{9,13},{10,... | collective-permute-start | bytes 405512 | tf_op jit(solution)/shard_map/ppermute | solution.py:156
  32.6 3.6 %collective-permute-start.7 = (bf16[64,4224]{1,0:T(8,128)(2,1)S(1)}, bf16[64,4224]{1,0:T(8,128)(2,1)S(1)}, u32[]{:S(2)}, u32[]{:S(2)}) collective-permute-start(bf16[64,4224]{1,0:T(8,128)(2,1)S(1)} %pad_maximum_fusion.refs_0_), channel_id=1, source_target_pairs={{0,1},{1,0},{2,3},{3,2},{4,5},{5,4},{6,7},{7,6},{8,9},{9,8},{10,11... | collective-permute-start | bytes 1622024 | tf_op jit(solution)/shard_map/ppermute | solution.py:150
  32.6 12.0 %collective-permute-start.20 = (bf16[32,4224]{1,0:T(8,128)(2,1)S(1)}, bf16[32,4224]{1,0:T(8,128)(2,1)S(1)}, u32[]{:S(2)}, u32[]{:S(2)}) collective-permute-start(bf16[32,4224]{1,0:T(8,128)(2,1)S(1)} %constant_dynamic-update-slice_fusion.6.refs_1_), channel_id=1, source_target_pairs={{0,2},{1,3},{2,0},{3,1},{4,6},{5,7},{6,4},{7,5},{8,10},{9,11},{10,... | collective-permute-start | bytes 811016 | tf_op jit(solution)/shard_map/ppermute | solution.py:153
  34.2 14.1 %collective-permute-start.22 = (bf16[32,4224]{1,0:T(8,128)(2,1)S(1)}, bf16[32,4224]{1,0:T(8,128)(2,1)S(1)}, u32[]{:S(2)}, u32[]{:S(2)}) collective-permute-start(bf16[32,4224]{1,0:T(8,128)(2,1)S(1)} %constant_dynamic-update-slice_fusion.6.refs_1_), channel_id=1, source_target_pairs={{0,1},{1,0},{2,3},{3,2},{4,5},{5,4},{6,7},{7,6},{8,9},{9,8},{10,11... | collective-permute-start | bytes 811016 | tf_op jit(solution)/shard_map/ppermute | solution.py:150
  34.4 1.7 %collective-permute-start.9 = (bf16[32,4224]{1,0:T(8,128)(2,1)S(1)}, bf16[32,4224]{1,0:T(8,128)(2,1)S(1)}, u32[]{:S(2)}, u32[]{:S(2)}) collective-permute-start(bf16[32,4224]{1,0:T(8,128)(2,1)S(1)} %collective-permute-done.6.refs_2_), channel_id=1, source_target_pairs={{0,1},{1,0},{2,3},{3,2},{4,5},{5,4},{6,7},{7,6},{8,9},{9,8},{10,11... | collective-permute-start | bytes 811016 | tf_op jit(solution)/shard_map/ppermute | solution.py:150
  34.7 9.7 %collective-permute-start.17 = (bf16[16,4224]{1,0:T(8,128)(2,1)S(1)}, bf16[16,4224]{1,0:T(8,128)(2,1)S(1)}, u32[]{:S(2)}, u32[]{:S(2)}) collective-permute-start(bf16[16,4224]{1,0:T(8,128)(2,1)S(1)} %collective-permute-done.16), channel_id=1, source_target_pairs={{0,2},{1,3},{2,0},{3,1},{4,6},{5,7},{6,4},{7,5},{8,10},{9,11},{10,... | collective-permute-start | bytes 405512 | tf_op jit(solution)/shard_map/ppermute | solution.py:153
  43.1 2.7 %collective-permute-start.10 = (bf16[128,4096]{1,0:T(8,128)(2,1)S(1)}, bf16[128,4096]{1,0:T(8,128)(2,1)S(1)}, u32[]{:S(2)}, u32[]{:S(2)}) collective-permute-start(bf16[128,4096]{1,0:T(8,128)(2,1)S(1)} %get-tuple-element.49), channel_id=1, source_target_pairs={{0,1},{1,0},{2,3},{3,2},{4,5},{5,4},{6,7},{7,6},{8,9},{9,8},{10,11... | collective-permute-start | bytes 3145736 | tf_op jit(solution)/shard_map/ppermute | solution.py:150
  44.5 3.8 %collective-permute-start.21 = (bf16[64,4224]{1,0:T(8,128)(2,1)S(1)}, bf16[64,4224]{1,0:T(8,128)(2,1)S(1)}, u32[]{:S(2)}, u32[]{:S(2)}) collective-permute-start(bf16[64,4224]{1,0:T(8,128)(2,1)S(1)} %constant_dynamic-update-slice_fusion.2.refs_0_), channel_id=1, source_target_pairs={{0,1},{1,0},{2,3},{3,2},{4,5},{5,4},{6,7},{7,6},{8,9},{9,8},{10,11... | collective-permute-start | bytes 1622024 | tf_op jit(solution)/shard_map/ppermute | solution.py:150
  44.6 3.7 %collective-permute-start.23 = (bf16[32,4224]{1,0:T(8,128)(2,1)S(1)}, bf16[32,4224]{1,0:T(8,128)(2,1)S(1)}, u32[]{:S(2)}, u32[]{:S(2)}) collective-permute-start(bf16[32,4224]{1,0:T(8,128)(2,1)S(1)} %collective-permute-done.20.refs_2_), channel_id=1, source_target_pairs={{0,1},{1,0},{2,3},{3,2},{4,5},{5,4},{6,7},{7,6},{8,9},{9,8},{10,11... | collective-permute-start | bytes 811016 | tf_op jit(solution)/shard_map/ppermute | solution.py:150
  46.2 9.2 %collective-permute-start.11 = (bf16[32,4096]{1,0:T(8,128)(2,1)S(1)}, bf16[32,4096]{1,0:T(8,128)(2,1)S(1)}, u32[]{:S(2)}, u32[]{:S(2)}) collective-permute-start(bf16[32,4096]{1,0:T(8,128)(2,1)S(1)} %get-tuple-element.70), channel_id=1, source_target_pairs={{0,2},{1,3},{2,0},{3,1},{4,6},{5,7},{6,4},{7,5},{8,10},{9,11},{10,... | collective-permute-start | bytes 786440 | tf_op jit(solution)/shard_map/ppermute | solution.py:153
  47.3 13.0 %collective-permute-start.12 = (bf16[32,4096]{1,0:T(8,128)(2,1)S(1)}, bf16[32,4096]{1,0:T(8,128)(2,1)S(1)}, u32[]{:S(2)}, u32[]{:S(2)}) collective-permute-start(bf16[32,4096]{1,0:T(8,128)(2,1)S(1)} %get-tuple-element.69), channel_id=1, source_target_pairs={{0,2},{1,3},{2,0},{3,1},{4,6},{5,7},{6,4},{7,5},{8,10},{9,11},{10,... | collective-permute-start | bytes 786440 | tf_op jit(solution)/shard_map/ppermute | solution.py:153
  55.3 5.0 %collective-permute-start.24 = (bf16[128,4096]{1,0:T(8,128)(2,1)S(1)}, bf16[128,4096]{1,0:T(8,128)(2,1)S(1)}, u32[]{:S(2)}, u32[]{:S(2)}) collective-permute-start(bf16[128,4096]{1,0:T(8,128)(2,1)S(1)} %get-tuple-element.61), channel_id=1, source_target_pairs={{0,1},{1,0},{2,3},{3,2},{4,5},{5,4},{6,7},{7,6},{8,9},{9,8},{10,11... | collective-permute-start | bytes 3145736 | tf_op jit(solution)/shard_map/ppermute | solution.py:150
  60.6 7.7 %collective-permute-start.25 = (bf16[32,4096]{1,0:T(8,128)(2,1)S(1)}, bf16[32,4096]{1,0:T(8,128)(2,1)S(1)}, u32[]{:S(2)}, u32[]{:S(2)}) collective-permute-start(bf16[32,4096]{1,0:T(8,128)(2,1)S(1)} %get-tuple-element.72), channel_id=1, source_target_pairs={{0,2},{1,3},{2,0},{3,1},{4,6},{5,7},{6,4},{7,5},{8,10},{9,11},{10,... | collective-permute-start | bytes 786440 | tf_op jit(solution)/shard_map/ppermute | solution.py:153
  61.7 17.6 %collective-permute-start.15 = (bf16[16,4096]{1,0:T(8,128)(2,1)S(1)}, bf16[16,4096]{1,0:T(8,128)(2,1)S(1)}, u32[]{:S(2)}, u32[]{:S(2)}) collective-permute-start(bf16[16,4096]{1,0:T(8,128)(2,1)S(1)} %slice.135), channel_id=1, source_target_pairs={{0,4},{1,5},{2,6},{3,7},{4,0},{5,1},{6,2},{7,3},{8,12},{9,13},{10,... | collective-permute-start | bytes 393224 | tf_op jit(solution)/shard_map/ppermute | solution.py:156
  64.7 14.7 %collective-permute-start.13 = (bf16[16,4096]{1,0:T(8,128)(2,1)S(1)}, bf16[16,4096]{1,0:T(8,128)(2,1)S(1)}, u32[]{:S(2)}, u32[]{:S(2)}) collective-permute-start(bf16[16,4096]{1,0:T(8,128)(2,1)S(1)} %get-tuple-element.73), channel_id=1, source_target_pairs={{0,12},{1,13},{2,14},{3,15},{4,8},{5,9},{6,10},{7,11},{8,4},{9,5},... | collective-permute-start | bytes 393224 | tf_op jit(solution)/shard_map/ppermute | solution.py:156
  67.4 16.6 %collective-permute-start.14 = (bf16[16,4096]{1,0:T(8,128)(2,1)S(1)}, bf16[16,4096]{1,0:T(8,128)(2,1)S(1)}, u32[]{:S(2)}, u32[]{:S(2)}) collective-permute-start(bf16[16,4096]{1,0:T(8,128)(2,1)S(1)} %get-tuple-element.74), channel_id=1, source_target_pairs={{0,8},{1,9},{2,10},{3,11},{4,12},{5,13},{6,14},{7,15},{8,0},{9,1},... | collective-permute-start | bytes 393224 | tf_op jit(solution)/shard_map/ppermute | solution.py:156
  68.3 6.7 %collective-permute-start.26 = (bf16[32,4096]{1,0:T(8,128)(2,1)S(1)}, bf16[32,4096]{1,0:T(8,128)(2,1)S(1)}, u32[]{:S(2)}, u32[]{:S(2)}) collective-permute-start(bf16[32,4096]{1,0:T(8,128)(2,1)S(1)} %get-tuple-element.63), channel_id=1, source_target_pairs={{0,2},{1,3},{2,0},{3,1},{4,6},{5,7},{6,4},{7,5},{8,10},{9,11},{10,... | collective-permute-start | bytes 786440 | tf_op jit(solution)/shard_map/ppermute | solution.py:153
  69.3 14.7 %collective-permute-start.27 = (bf16[16,4096]{1,0:T(8,128)(2,1)S(1)}, bf16[16,4096]{1,0:T(8,128)(2,1)S(1)}, u32[]{:S(2)}, u32[]{:S(2)}) collective-permute-start(bf16[16,4096]{1,0:T(8,128)(2,1)S(1)} %get-tuple-element.75), channel_id=1, source_target_pairs={{0,12},{1,13},{2,14},{3,15},{4,8},{5,9},{6,10},{7,11},{8,4},{9,5},... | collective-permute-start | bytes 393224 | tf_op jit(solution)/shard_map/ppermute | solution.py:156
  75.0 13.9 %collective-permute-start.28 = (bf16[16,4096]{1,0:T(8,128)(2,1)S(1)}, bf16[16,4096]{1,0:T(8,128)(2,1)S(1)}, u32[]{:S(2)}, u32[]{:S(2)}) collective-permute-start(bf16[16,4096]{1,0:T(8,128)(2,1)S(1)} %get-tuple-element.76), channel_id=1, source_target_pairs={{0,8},{1,9},{2,10},{3,11},{4,12},{5,13},{6,14},{7,15},{8,0},{9,1},... | collective-permute-start | bytes 393224 | tf_op jit(solution)/shard_map/ppermute | solution.py:156
  79.3 9.5 %collective-permute-start.29 = (bf16[16,4096]{1,0:T(8,128)(2,1)S(1)}, bf16[16,4096]{1,0:T(8,128)(2,1)S(1)}, u32[]{:S(2)}, u32[]{:S(2)}) collective-permute-start(bf16[16,4096]{1,0:T(8,128)(2,1)S(1)} %slice.134), channel_id=1, source_target_pairs={{0,4},{1,5},{2,6},{3,7},{4,0},{5,1},{6,2},{7,3},{8,12},{9,13},{10,... | collective-permute-start | bytes 393224 | tf_op jit(solution)/shard_map/ppermute | solution.py:156

commit v5 on v4

v5 whole, which is shorter than its diff:
```python
import functools

import jax
import jax.numpy as jnp
from jax import lax
from jax.experimental import pallas as pl
from jax.experimental.pallas import tpu as pltpu
from jax.sharding import PartitionSpec as P

LANES = 128
MIB = 1 << 20


def in_vmem():
    return pl.BlockSpec(memory_space=pltpu.VMEM)


def message_kernel(states_ref, ids_ref, probs_ref, *message_refs):
    steps, tokens, width = states_ref.shape
    tail = message_refs[0].shape[1] - width
    half = tail // 2
    place = lax.broadcasted_iota(jnp.int32, (tail, tokens), 0)
    row = lax.broadcasted_iota(jnp.int32, (tokens, tokens), 0)
    column = lax.broadcasted_iota(jnp.int32, (tokens, tokens), 1)
    one = jnp.where(row == column, 1.0, 0.0).astype(jnp.bfloat16)
    for step in range(steps):
        probs = probs_ref[step]
        share = probs / jnp.sum(probs, axis=0, keepdims=True)
        ids = ids_ref[step]
        dense = jnp.zeros((tail, tokens), jnp.float32)
        for k in range(ids.shape[0]):
            dense += jnp.where(ids[k : k + 1] == place % half, share[k : k + 1], 0.0)
        high = dense.astype(jnp.bfloat16).astype(jnp.float32)
        terms = jnp.where(place < half, high, dense - high).astype(jnp.bfloat16)
        upright = lax.dot_general(one, terms, (((1,), (1,)), ((), ())), preferred_element_type=jnp.float32)
        upright = upright.astype(jnp.bfloat16)
        for message_ref, at in ((message_refs[0], step * tokens), (message_refs[step + 1], 0)):
            message_ref[at : at + tokens, :width] = states_ref[step]
            message_ref[at : at + tokens, width:] = upright


def make_messages(states, ids, probs, tail):
    steps, tokens, width = states.shape
    states, ids, probs = (pltpu.with_memory_space_constraint(x, pltpu.HBM) for x in (states, ids, probs))

    def whole(shape):
        return pl.BlockSpec(shape, lambda i: (0,) * len(shape))

    shapes = [(steps * tokens, width + tail)] + [(tokens, width + tail)] * steps
    return pl.pallas_call(
        message_kernel,
        grid=(1,),
        out_shape=[jax.ShapeDtypeStruct(shape, jnp.bfloat16) for shape in shapes],
        in_specs=[whole(x.shape) for x in (states, ids, probs)],
        out_specs=[whole(shape) for shape in shapes],
        compiler_params=pltpu.CompilerParams(vmem_limit_bytes=4 * MIB),
        name="messages",
    )(states, ids, probs)


def load_kernel(*refs):
    count = len(refs) // 3
    copies = [
        pltpu.make_async_copy(refs[i], refs[count + i], refs[2 * count + i]) for i in range(count)
    ]
    for copy in copies:
        copy.start()
    for copy in copies:
        copy.wait()


def load_weights(*arrays):
    arrays = [pltpu.with_memory_space_constraint(x, pltpu.HBM) for x in arrays]
    return pl.pallas_call(
        load_kernel,
        out_shape=[pltpu.VMEM(x.shape, x.dtype) for x in arrays],
        in_specs=[pl.BlockSpec(memory_space=pltpu.HBM)] * len(arrays),
        out_specs=[in_vmem()] * len(arrays),
        scratch_shapes=[pltpu.SemaphoreType.DMA(())] * len(arrays),
        cost_estimate=pl.CostEstimate(flops=0, bytes_accessed=0, transcendentals=0),
        compiler_params=pltpu.CompilerParams(vmem_limit_bytes=4 * MIB),
        name="load_weights",
    )(*arrays)


def expert_kernel(swapped, count, plan, flags_ref, gate_ref, up_ref, down_ref, *refs):
    *sources, own_ref, near_ref, other_ref, rows, hidden = refs
    width, units = gate_ref.shape
    tail = rows.shape[1] - width
    owner = lax.axis_index("expert")
    slot = jnp.bitwise_xor(owner, flags_ref[owner]) if swapped else owner
    at = 0
    for source, low, high in plan:
        rows[at : at + high - low] = sources[source][low:high]
        at += high - low
    total = rows.shape[0]
    lane = lax.broadcasted_iota(jnp.int32, (total, tail), 1)
    terms = rows[:, width:].astype(jnp.float32)
    weight = jnp.sum(jnp.where(lane % (tail // 2) == slot, terms, 0.0), axis=1, keepdims=True)
    step = 256
    for at in range(0, units, step):
        gate = jnp.dot(rows[:, :width], gate_ref[:, at : at + step], preferred_element_type=jnp.float32)
        up = jnp.dot(rows[:, :width], up_ref[:, at : at + step], preferred_element_type=jnp.float32)
        value = gate / (1.0 + jnp.exp(-gate)) * up
        hidden[:, at : at + step] = (value * weight).astype(jnp.bfloat16)

    def columns(index, _):
        at = pl.ds(pl.multiple_of(index * 512, 512), 512)
        out = jnp.dot(hidden[...], down_ref[:, at], preferred_element_type=jnp.float32)
        out = out.astype(jnp.bfloat16)
        own_ref[:, at] = out[:count]
        near_ref[:, at] = out[count : 2 * count]
        other_ref[:, at] = out[2 * count :]
        return 0

    lax.fori_loop(0, width // 512, columns, 0)


def run_expert(swapped, flags, weights, parts, plan):
    total = sum(high - low for _, low, high in plan)
    count = total // 4
    width, units = weights[0].shape
    weights = [pltpu.with_memory_space_constraint(w, pltpu.VMEM) for w in weights]
    return pl.pallas_call(
        functools.partial(expert_kernel, swapped, count, plan),
        out_shape=[jax.ShapeDtypeStruct((k * count, width), jnp.bfloat16) for k in (1, 1, 2)],
        in_specs=[pl.BlockSpec(memory_space=pltpu.SMEM)] + [in_vmem()] * (3 + len(parts)),
        out_specs=[in_vmem()] * 3,
        scratch_shapes=[
            pltpu.VMEM((total, parts[0].shape[1]), jnp.bfloat16),
            pltpu.VMEM((total, units), jnp.bfloat16),
        ],
        compiler_params=pltpu.CompilerParams(vmem_limit_bytes=16 * MIB),
        cost_estimate=pl.CostEstimate(flops=0, bytes_accessed=0, transcendentals=0),
        name="expert",
    )(flags, *weights, *parts)


def on_device(states, ids, probs, flags, w_gate, w_up, w_down):
    devices = lax.axis_size("expert")
    lines = devices // 4
    steps, tokens, width = states.shape

    def index(far, near, core):
        return far * 4 + near * 2 + core

    every = [(z, y, c) for z in range(lines) for y in range(2) for c in range(2)]

    def swap_core(x):
        return lax.ppermute(x, "expert", [(index(z, y, c), index(z, y, 1 - c)) for z, y, c in every])

    def swap_near(x):
        return lax.ppermute(x, "expert", [(index(z, y, c), index(z, 1 - y, c)) for z, y, c in every])

    def swap_far(x, by):
        return lax.ppermute(x, "expert", [(index(z, y, c), index(z ^ by, y, c)) for z, y, c in every])

    tail = 2 * devices
    tail = -(-tail // LANES) * LANES
    ids, probs = jnp.swapaxes(ids, 1, 2), jnp.swapaxes(probs, 1, 2)
    strides = [lines >> shift for shift in range(1, lines.bit_length())]
    half = lines * tokens
    message, *own_messages = make_messages(states, ids, probs, tail)
    near_message = swap_near(message)
    w_gate, w_up, w_down = w_gate[0], w_up[0], w_down[0]
    pieces, nears, held = [[] for _ in range(steps)], [[] for _ in range(steps)], own_messages
    for place, by in enumerate(strides):
        for step in range(steps):
            mine = held[step]
            if step:
                mine, _ = lax.optimization_barrier((mine, pieces[step - 1][place]))
            piece = swap_far(mine, by)
            if not step and not place:
                loaded = load_weights(w_gate, w_up)
                piece, loaded, near_message = lax.optimization_barrier((piece, loaded, near_message))
            if step == 1 and not place:
                w_down, _ = lax.optimization_barrier((w_down, pieces[0][0]))
                loaded += load_weights(w_down)
                piece, loaded = lax.optimization_barrier((piece, loaded))
            pieces[step].append(piece)
            nears[step].append(swap_near(piece))
            if place + 1 < len(strides):
                held[step] = jnp.concatenate([held[step], piece])
    weights = loaded
    shared = jnp.concatenate([message, near_message, *pieces[0][:-1], *nears[0][:-1]])
    shared = [shared, swap_core(shared)]
    outputs, ready = [], None
    for step in range(steps):
        blocks, near = pieces[step][-1], nears[step][-1]
        parts = [*shared, blocks, near, swap_core(blocks), swap_core(near)]
        if step:
            own = jnp.concatenate([*pieces[step][:-1], *nears[step][:-1]])
            parts += [own, swap_core(own)]
        plan = []
        some = half // 2 - tokens
        for core in range(2):
            for side in range(2):
                at = (side * steps + step) * tokens
                plan.append((core, at, at + tokens))
                at = side * some + (0 if step else 2 * steps * tokens)
                plan.append((core + 6 if step else core, at, at + some))
                plan.append((2 + 2 * core + side, 0, half // 2))
        parts, _ = lax.optimization_barrier((parts, ready if step else pieces))
        own, peer, other = run_expert(step > 0, flags, weights, parts, tuple(plan))
        other, _ = lax.optimization_barrier((other, near_high if step else nears[1][-1]))
        other = swap_core(other)
        own = own.astype(jnp.float32) + other[:half].astype(jnp.float32)
        peer = (peer.astype(jnp.float32) + other[half:].astype(jnp.float32)).astype(jnp.bfloat16)
        ready = peer
        size = half // 2
        near_high, near_low = swap_near(peer[size:]), peer[:size]
        if step + 1 == steps:
            near_low, _ = lax.optimization_barrier((near_low, near_high))
        high = own[size:] + near_high.astype(jnp.float32)
        _, near_low = lax.optimization_barrier((high, swap_near(near_low)))
        line = own[:size] + near_low.astype(jnp.float32)
        for by in strides[::-1]:
            line += swap_far(high.astype(jnp.bfloat16), by).astype(jnp.float32)
            size //= 2
            line, high = line[:size], line[size:]
        outputs.append(jnp.concatenate([line, high]).astype(jnp.bfloat16))
    return jnp.stack(outputs)


def solution(mesh):
    rows = P(None, ("groups", "expert"), None)
    weights = P("expert", None, None)
    return jax.shard_map(
        on_device,
        mesh=mesh,
        in_specs=(rows, rows, rows, P(), weights, weights, weights),
        out_specs=rows,
        check_vma=False,
    )
```

time: 89.8 us -> 92.6 us (1.031)
  waiting for transfers between devices: 29 us -> 45.1 us
  starting transfers between devices: 35.8 us -> 22.5 us
    ppermute x12 -> x8, starting transfers between devices: 23 us -> 10.6 us  [swap_far(): lax.ppermute(x, 'expert', [(index(z, y, c), index(z ^ by, y, c)) for z, y...]
    ppermute x10 -> x9, waiting for transfers between devices: 9.67 us -> 21.8 us  [swap_near(): lax.ppermute(x, 'expert', [(index(z, y, c), index(z, 1 - y, c)) for z, y,...]
    ppermute x12 -> x8, waiting for transfers between devices: 18.3 us -> 21 us  [swap_far(): lax.ppermute(x, 'expert', [(index(z, y, c), index(z ^ by, y, c)) for z, y...]
    ppermute x8, waiting for transfers between devices: 1.07 us -> 2.36 us  [swap_core(): lax.ppermute(x, 'expert', [(index(z, y, c), index(z, y, 1 - c)) for z, y,...]
    pallas_call x1 -> x2, Pallas kernels: 6.42 us -> 7.43 us  [load_weights(): pl.pallas_call(load_kernel, out_shape=[pltpu.VMEM(x.shape, x.dtype) for x...]
    pallas_call x2 -> x1, Pallas kernels: 2.23 us -> 1.23 us  [make_messages(): pl.pallas_call(message_kernel, grid=(1,), out_shape=[jax.ShapeDtypeStruct...]
    ppermute x10 -> x9, starting transfers between devices: 11.4 us -> 11.2 us  [swap_near(): lax.ppermute(x, 'expert', [(index(z, y, c), index(z, 1 - y, c)) for z, y,...]
  transfers between devices with their start and end apart: 30 -> 25, of which waited for: 10 -> 14; matrix products, arithmetic and copies ran while one was open for 1% -> 1% of each run, Pallas kernels for 24% -> 23%
where the time goes in v5:
time: 92.6 us; the launch traced here: 92.5 us
  waiting for transfers between devices  45.1 us (49%)
  Pallas kernels  22.9 us (25%)
  starting transfers between devices  22.5 us (24%)
  other arithmetic  1.56 us (2%)
    ppermute x9, waiting for transfers between devices, swap_near(): lax.ppermute(x, 'expert', [(index(z, y, c), index(z, 1 - y, c)) for z, y,...  21.8 us
    ppermute x8, waiting for transfers between devices, swap_far(): lax.ppermute(x, 'expert', [(index(z, y, c), index(z ^ by, y, c)) for z, y...  21 us
    pallas_call x2, Pallas kernels, run_expert(): pl.pallas_call(functools.partial(expert_kernel, swapped, count, plan), ou...  14.2 us
    ppermute x9, starting transfers between devices, swap_near(): lax.ppermute(x, 'expert', [(index(z, y, c), index(z, 1 - y, c)) for z, y,...  11.2 us
    ppermute x8, starting transfers between devices, swap_far(): lax.ppermute(x, 'expert', [(index(z, y, c), index(z ^ by, y, c)) for z, y...  10.6 us
    pallas_call x2, Pallas kernels, load_weights(): pl.pallas_call(load_kernel, out_shape=[pltpu.VMEM(x.shape, x.dtype) for x...  7.43 us
    ppermute x8, waiting for transfers between devices, swap_core(): lax.ppermute(x, 'expert', [(index(z, y, c), index(z, y, 1 - c)) for z, y,...  2.36 us
  transfers between devices with their start and end apart: 25, of which 14 were waited for; matrix products, arithmetic and copies ran while one was open for 1% of the time, Pallas kernels for 23%

profile of v5, /device:TPU:0, one launch (start us, length us, event | category | flops | bytes accessed | tf_op | source)
XLA Modules:
  0.0 92.5 jit_solution(971490719528414215)
XLA Ops:
  0.0 1.2 %messages.1 = (bf16[32,4224]{1,0:T(8,128)(2,1)S(1)}, bf16[16,4224]{1,0:T(8,128)(2,1)S(1)}, bf16[16,4224]{1,0:T(8,128)(2,1)S(1)}) custom-call(bf16[2,16,4096]{2,1,0:T(8,128)(2,1)} %states_ref.1, s32[2,8,16]{2,1,0:T(8,128)} %bitcast.12, f32[2,8,16]{2,1,0:T(8,128)} %bitcast.13), custom_call_target="tpu_custom_call" | custom-call | tf_op jit(solution)/shard_map/messages/pallas_call | solution.py:50
  1.2 3.0 %collective-permute-start.1 = (bf16[32,4224]{1,0:T(8,128)(2,1)S(1)}, bf16[32,4224]{1,0:T(8,128)(2,1)S(1)}, u32[]{:S(2)}, u32[]{:S(2)}) collective-permute-start(bf16[32,4224]{1,0:T(8,128)(2,1)S(1)} %get-tuple-element.50), channel_id=1, source_target_pairs={{0,2},{1,3},{2,0},{3,1},{4,6},{5,7},{6,4},{7,5},{8,10},{9,11},{10,... | collective-permute-start | bytes 811016 | tf_op jit(solution)/shard_map/ppermute | solution.py:153
  4.2 2.6 %collective-permute-start = (bf16[16,4224]{1,0:T(8,128)(2,1)S(1)}, bf16[16,4224]{1,0:T(8,128)(2,1)S(1)}, u32[]{:S(2)}, u32[]{:S(2)}) collective-permute-start(bf16[16,4224]{1,0:T(8,128)(2,1)S(1)} %get-tuple-element.47), channel_id=1, source_target_pairs={{0,8},{1,9},{2,10},{3,11},{4,12},{5,13},{6,14},{7,15},{8,0},{9,1},... | collective-permute-start | bytes 405512 | tf_op jit(solution)/shard_map/ppermute | solution.py:156
  6.8 4.6 %load_weights.2 = (bf16[4096,768]{1,0:T(8,128)(2,1)S(1)}, bf16[4096,768]{1,0:T(8,128)(2,1)S(1)}) custom-call(bf16[4096,768]{1,0:T(8,128)(2,1)} %bitcast.9, bf16[4096,768]{1,0:T(8,128)(2,1)} %bitcast.10), custom_call_target="tpu_custom_call" | custom-call | tf_op jit(solution)/shard_map/load_weights/pallas_call | solution.py:74
  11.4 1.6 %collective-permute-done = bf16[16,4224]{1,0:T(8,128)(2,1)S(1)} collective-permute-done((bf16[16,4224]{1,0:T(8,128)(2,1)S(1)}, bf16[16,4224]{1,0:T(8,128)(2,1)S(1)}, u32[]{:S(2)}, u32[]{:S(2)}) %collective-permute-start) | collective-permute-done | bytes 135200 | tf_op jit(solution)/shard_map/ppermute | solution.py:156
  13.0 0.0 collective-permute-done.1
  13.1 0.5 collective-permute-start.3
  13.6 1.5 %collective-permute-start.2 = (bf16[16,4224]{1,0:T(8,128)(2,1)S(1)}, bf16[16,4224]{1,0:T(8,128)(2,1)S(1)}, u32[]{:S(2)}, u32[]{:S(2)}) collective-permute-start(bf16[16,4224]{1,0:T(8,128)(2,1)S(1)} %get-tuple-element.52), channel_id=1, source_target_pairs={{0,8},{1,9},{2,10},{3,11},{4,12},{5,13},{6,14},{7,15},{8,0},{9,1},... | collective-permute-start | bytes 405512 | tf_op jit(solution)/shard_map/ppermute | solution.py:156
  15.1 0.0 copy-start
  15.1 2.8 %load_weights.3.down_ref = bf16[768,4096]{1,0:T(8,128)(2,1)S(1)} custom-call(bf16[768,4096]{1,0:T(8,128)(2,1)} %bitcast.11), custom_call_target="tpu_custom_call" | custom-call | tf_op jit(solution)/shard_map/load_weights/pallas_call | solution.py:74
  17.9 2.7 %collective-permute-start.5 = (bf16[32,4224]{1,0:T(8,128)(2,1)S(1)}, bf16[32,4224]{1,0:T(8,128)(2,1)S(1)}, u32[]{:S(2)}, u32[]{:S(2)}) collective-permute-start(bf16[32,4224]{1,0:T(8,128)(2,1)S(1)} %pad_maximum_fusion), channel_id=1, source_target_pairs={{0,4},{1,5},{2,6},{3,7},{4,0},{5,1},{6,2},{7,3},{8,12},{9,13},{10,... | collective-permute-start | bytes 811016 | tf_op jit(solution)/shard_map/ppermute | solution.py:156
  20.6 0.0 collective-permute-done.3
  20.7 1.5 %collective-permute-done.2 = bf16[16,4224]{1,0:T(8,128)(2,1)S(1)} collective-permute-done((bf16[16,4224]{1,0:T(8,128)(2,1)S(1)}, bf16[16,4224]{1,0:T(8,128)(2,1)S(1)}, u32[]{:S(2)}, u32[]{:S(2)}) %collective-permute-start.2) | collective-permute-done | bytes 135200 | tf_op jit(solution)/shard_map/ppermute | solution.py:156
  22.2 0.0 collective-permute-start.4
  22.2 5.7 %collective-permute-done.5.refs_2_ = bf16[32,4224]{1,0:T(8,128)(2,1)S(1)} collective-permute-done((bf16[32,4224]{1,0:T(8,128)(2,1)S(1)}, bf16[32,4224]{1,0:T(8,128)(2,1)S(1)}, u32[]{:S(2)}, u32[]{:S(2)}) %collective-permute-start.5) | collective-permute-done | bytes 270368 | tf_op jit(solution)/shard_map/ppermute | solution.py:156
  27.9 1.5 %collective-permute-start.6 = (bf16[32,4224]{1,0:T(8,128)(2,1)S(1)}, bf16[32,4224]{1,0:T(8,128)(2,1)S(1)}, u32[]{:S(2)}, u32[]{:S(2)}) collective-permute-start(bf16[32,4224]{1,0:T(8,128)(2,1)S(1)} %collective-permute-done.5.refs_2_), channel_id=1, source_target_pairs={{0,2},{1,3},{2,0},{3,1},{4,6},{5,7},{6,4},{7,5},{8,10},{9,11},{10,... | collective-permute-start | bytes 811016 | tf_op jit(solution)/shard_map/ppermute | solution.py:153
  29.4 0.6 collective-permute-start.9
  30.0 0.0 collective-permute-start.7
  30.0 6.2 %collective-permute-done.6.refs_3_ = bf16[32,4224]{1,0:T(8,128)(2,1)S(1)} collective-permute-done((bf16[32,4224]{1,0:T(8,128)(2,1)S(1)}, bf16[32,4224]{1,0:T(8,128)(2,1)S(1)}, u32[]{:S(2)}, u32[]{:S(2)}) %collective-permute-start.6) | collective-permute-done | bytes 270368 | tf_op jit(solution)/shard_map/ppermute | solution.py:153
  36.3 0.0 collective-permute-start.8
  36.3 1.3 %collective-permute-done.9.refs_2_ = bf16[32,4224]{1,0:T(8,128)(2,1)S(1)} collective-permute-done((bf16[32,4224]{1,0:T(8,128)(2,1)S(1)}, bf16[32,4224]{1,0:T(8,128)(2,1)S(1)}, u32[]{:S(2)}, u32[]{:S(2)}) %collective-permute-start.9) | collective-permute-done | bytes 270368 | tf_op jit(solution)/shard_map/ppermute | solution.py:156
  37.6 0.5 collective-permute-start.10
  38.1 1.5 %collective-permute-start.18 = (bf16[16,4224]{1,0:T(8,128)(2,1)S(1)}, bf16[16,4224]{1,0:T(8,128)(2,1)S(1)}, u32[]{:S(2)}, u32[]{:S(2)}) collective-permute-start(bf16[16,4224]{1,0:T(8,128)(2,1)S(1)} %collective-permute-done.2), channel_id=1, source_target_pairs={{0,2},{1,3},{2,0},{3,1},{4,6},{5,7},{6,4},{7,5},{8,10},{9,11},{10,... | collective-permute-start | bytes 405512 | tf_op jit(solution)/shard_map/ppermute | solution.py:153
  39.6 0.0 collective-permute-done.7.refs_4_
  39.6 0.0 collective-permute-done.8.refs_5_
  39.6 0.0 collective-permute-done.4.refs_1_
  39.6 0.0 copy-done
  39.6 7.1 %expert.2 = (bf16[64,4096]{1,0:T(8,128)(2,1)S(1)}, bf16[64,4096]{1,0:T(8,128)(2,1)S(1)}, bf16[128,4096]{1,0:T(8,128)(2,1)S(1)}) custom-call(s32[16]{0:T(128)S(1)} %copy-done, bf16[4096,768]{1,0:T(8,128)(2,1)S(1)} %get-tuple-element.56.gate_ref, bf16[4096,768]{1,0:T(8,128)(2,1)S(1)} %get-tuple-element.57.up_ref, bf16[768,4096]{1,0:T(8,128)(2,1)S(1)} %load_weights.3.down_ref, ...), custom_call_target="tpu_custom_call" | custom-call | tf_op jit(solution)/shard_map/expert/pallas_call | solution.py:124
  46.8 0.0 collective-permute-done.10.refs_3_
  46.8 0.1 collective-permute-start.11
  46.9 1.2 %collective-permute-done.18 = bf16[16,4224]{1,0:T(8,128)(2,1)S(1)} collective-permute-done((bf16[16,4224]{1,0:T(8,128)(2,1)S(1)}, bf16[16,4224]{1,0:T(8,128)(2,1)S(1)}, u32[]{:S(2)}, u32[]{:S(2)}) %collective-permute-start.18) | collective-permute-done | bytes 135200 | tf_op jit(solution)/shard_map/ppermute | solution.py:153
  48.1 0.1 collective-permute-start.19
  48.2 0.5 collective-permute-start.16
  48.7 0.1 collective-permute-start.17
  48.7 0.8 collective-permute-done.11
  49.5 0.2 convert_add_fusion.1
  49.8 0.8 collective-permute-start.12
  50.6 0.0 collective-permute-done.19.refs_7_
  50.6 0.0 collective-permute-done.16.refs_4_
  50.6 0.0 collective-permute-done.17.refs_5_
  50.7 7.1 %expert.3 = (bf16[64,4096]{1,0:T(8,128)(2,1)S(1)}, bf16[64,4096]{1,0:T(8,128)(2,1)S(1)}, bf16[128,4096]{1,0:T(8,128)(2,1)S(1)}) custom-call(s32[16]{0:T(128)S(1)} %copy-done, bf16[4096,768]{1,0:T(8,128)(2,1)S(1)} %get-tuple-element.56.gate_ref, bf16[4096,768]{1,0:T(8,128)(2,1)S(1)} %get-tuple-element.57.up_ref, bf16[768,4096]{1,0:T(8,128)(2,1)S(1)} %load_weights.3.down_ref, ...), custom_call_target="tpu_custom_call" | custom-call | tf_op jit(solution)/shard_map/expert/pallas_call | solution.py:124
  57.8 0.4 collective-permute-done.12
  58.2 0.0 collective-permute-start.20
  58.2 1.1 %collective-permute-start.13 = (bf16[32,4096]{1,0:T(8,128)(2,1)S(1)}, bf16[32,4096]{1,0:T(8,128)(2,1)S(1)}, u32[]{:S(2)}, u32[]{:S(2)}) collective-permute-start(bf16[32,4096]{1,0:T(8,128)(2,1)S(1)} %get-tuple-element.91), channel_id=1, source_target_pairs={{0,2},{1,3},{2,0},{3,1},{4,6},{5,7},{6,4},{7,5},{8,10},{9,11},{10,... | collective-permute-start | bytes 786440 | tf_op jit(solution)/shard_map/ppermute | solution.py:153
  59.3 1.5 %collective-permute-done.20 = bf16[128,4096]{1,0:T(8,128)(2,1)S(1)} collective-permute-done((bf16[128,4096]{1,0:T(8,128)(2,1)S(1)}, bf16[128,4096]{1,0:T(8,128)(2,1)S(1)}, u32[]{:S(2)}, u32[]{:S(2)}) %collective-permute-start.20) | collective-permute-done | bytes 1048608 | tf_op jit(solution)/shard_map/ppermute | solution.py:150
  60.8 0.2 add_convert_fusion
  61.1 1.1 %collective-permute-start.21 = (bf16[32,4096]{1,0:T(8,128)(2,1)S(1)}, bf16[32,4096]{1,0:T(8,128)(2,1)S(1)}, u32[]{:S(2)}, u32[]{:S(2)}) collective-permute-start(bf16[32,4096]{1,0:T(8,128)(2,1)S(1)} %get-tuple-element.94), channel_id=1, source_target_pairs={{0,2},{1,3},{2,0},{3,1},{4,6},{5,7},{6,4},{7,5},{8,10},{9,11},{10,... | collective-permute-start | bytes 786440 | tf_op jit(solution)/shard_map/ppermute | solution.py:153
  62.3 0.1 slice_add_fusion.2
  62.3 0.2 collective-permute-start.14
  62.5 4.8 %collective-permute-done.13 = bf16[32,4096]{1,0:T(8,128)(2,1)S(1)} collective-permute-done((bf16[32,4096]{1,0:T(8,128)(2,1)S(1)}, bf16[32,4096]{1,0:T(8,128)(2,1)S(1)}, u32[]{:S(2)}, u32[]{:S(2)}) %collective-permute-start.13) | collective-permute-done | bytes 262176 | tf_op jit(solution)/shard_map/ppermute | solution.py:153
  67.3 5.2 %collective-permute-done.21 = bf16[32,4096]{1,0:T(8,128)(2,1)S(1)} collective-permute-done((bf16[32,4096]{1,0:T(8,128)(2,1)S(1)}, bf16[32,4096]{1,0:T(8,128)(2,1)S(1)}, u32[]{:S(2)}, u32[]{:S(2)}) %collective-permute-start.21) | collective-permute-done | bytes 262176 | tf_op jit(solution)/shard_map/ppermute | solution.py:153
  72.5 1.1 %collective-permute-start.22 = (bf16[32,4096]{1,0:T(8,128)(2,1)S(1)}, bf16[32,4096]{1,0:T(8,128)(2,1)S(1)}, u32[]{:S(2)}, u32[]{:S(2)}) collective-permute-start(bf16[32,4096]{1,0:T(8,128)(2,1)S(1)} %get-tuple-element.85), channel_id=1, source_target_pairs={{0,2},{1,3},{2,0},{3,1},{4,6},{5,7},{6,4},{7,5},{8,10},{9,11},{10,... | collective-permute-start | bytes 786440 | tf_op jit(solution)/shard_map/ppermute | solution.py:153
  73.6 0.2 collective-permute-start.23
  73.8 0.0 collective-permute-done.14
  73.8 0.1 fusion.1
  73.9 2.6 %collective-permute-start.15 = (bf16[16,4096]{1,0:T(8,128)(2,1)S(1)}, bf16[16,4096]{1,0:T(8,128)(2,1)S(1)}, u32[]{:S(2)}, u32[]{:S(2)}) collective-permute-start(bf16[16,4096]{1,0:T(8,128)(2,1)S(1)} %slice.113), channel_id=1, source_target_pairs={{0,8},{1,9},{2,10},{3,11},{4,12},{5,13},{6,14},{7,15},{8,0},{9,1},... | collective-permute-start | bytes 393224 | tf_op jit(solution)/shard_map/ppermute | solution.py:156
  76.5 3.9 %collective-permute-done.22 = bf16[32,4096]{1,0:T(8,128)(2,1)S(1)} collective-permute-done((bf16[32,4096]{1,0:T(8,128)(2,1)S(1)}, bf16[32,4096]{1,0:T(8,128)(2,1)S(1)}, u32[]{:S(2)}, u32[]{:S(2)}) %collective-permute-start.22) | collective-permute-done | bytes 262176 | tf_op jit(solution)/shard_map/ppermute | solution.py:153
  80.5 3.7 %collective-permute-done.23 = bf16[32,4096]{1,0:T(8,128)(2,1)S(1)} collective-permute-done((bf16[32,4096]{1,0:T(8,128)(2,1)S(1)}, bf16[32,4096]{1,0:T(8,128)(2,1)S(1)}, u32[]{:S(2)}, u32[]{:S(2)}) %collective-permute-start.23) | collective-permute-done | bytes 262176 | tf_op jit(solution)/shard_map/ppermute | solution.py:156
  84.1 0.1 fusion
  84.2 0.3 collective-permute-start.24
  84.5 0.0 collective-permute-done.15
  84.5 7.2 %collective-permute-done.24 = bf16[16,4096]{1,0:T(8,128)(2,1)S(1)} collective-permute-done((bf16[16,4096]{1,0:T(8,128)(2,1)S(1)}, bf16[16,4096]{1,0:T(8,128)(2,1)S(1)}, u32[]{:S(2)}, u32[]{:S(2)}) %collective-permute-start.24) | collective-permute-done | bytes 131104 | tf_op jit(solution)/shard_map/ppermute | solution.py:156
  91.8 0.7 pad_maximum_fusion.2
  (15 shorter events, 0.4 us)
Async XLA Ops:
  1.2 11.8 %collective-permute-start.1 = (bf16[32,4224]{1,0:T(8,128)(2,1)S(1)}, bf16[32,4224]{1,0:T(8,128)(2,1)S(1)}, u32[]{:S(2)}, u32[]{:S(2)}) collective-permute-start(bf16[32,4224]{1,0:T(8,128)(2,1)S(1)} %get-tuple-element.50), channel_id=1, source_target_pairs={{0,2},{1,3},{2,0},{3,1},{4,6},{5,7},{6,4},{7,5},{8,10},{9,11},{10,... | collective-permute-start | bytes 811016 | tf_op jit(solution)/shard_map/ppermute | solution.py:153
  4.2 8.8 %collective-permute-start = (bf16[16,4224]{1,0:T(8,128)(2,1)S(1)}, bf16[16,4224]{1,0:T(8,128)(2,1)S(1)}, u32[]{:S(2)}, u32[]{:S(2)}) collective-permute-start(bf16[16,4224]{1,0:T(8,128)(2,1)S(1)} %get-tuple-element.47), channel_id=1, source_target_pairs={{0,8},{1,9},{2,10},{3,11},{4,12},{5,13},{6,14},{7,15},{8,0},{9,1},... | collective-permute-start | bytes 405512 | tf_op jit(solution)/shard_map/ppermute | solution.py:156
  13.1 7.6 %collective-permute-start.3 = (bf16[16,4224]{1,0:T(8,128)(2,1)S(1)}, bf16[16,4224]{1,0:T(8,128)(2,1)S(1)}, u32[]{:S(2)}, u32[]{:S(2)}) collective-permute-start(bf16[16,4224]{1,0:T(8,128)(2,1)S(1)} %collective-permute-done), channel_id=1, source_target_pairs={{0,2},{1,3},{2,0},{3,1},{4,6},{5,7},{6,4},{7,5},{8,10},{9,11},{10,... | collective-permute-start | bytes 405512 | tf_op jit(solution)/shard_map/ppermute | solution.py:153
  13.6 8.6 %collective-permute-start.2 = (bf16[16,4224]{1,0:T(8,128)(2,1)S(1)}, bf16[16,4224]{1,0:T(8,128)(2,1)S(1)}, u32[]{:S(2)}, u32[]{:S(2)}) collective-permute-start(bf16[16,4224]{1,0:T(8,128)(2,1)S(1)} %get-tuple-element.52), channel_id=1, source_target_pairs={{0,8},{1,9},{2,10},{3,11},{4,12},{5,13},{6,14},{7,15},{8,0},{9,1},... | collective-permute-start | bytes 405512 | tf_op jit(solution)/shard_map/ppermute | solution.py:156
  15.1 24.5 %copy-start = (s32[16]{0:T(128)S(1)}, s32[16]{0:T(128)}, u32[]{:S(2)}) copy-start(s32[16]{0:T(128)} %flags_ref.3) | copy-start | bytes 196
  17.9 9.9 %collective-permute-start.5 = (bf16[32,4224]{1,0:T(8,128)(2,1)S(1)}, bf16[32,4224]{1,0:T(8,128)(2,1)S(1)}, u32[]{:S(2)}, u32[]{:S(2)}) collective-permute-start(bf16[32,4224]{1,0:T(8,128)(2,1)S(1)} %pad_maximum_fusion), channel_id=1, source_target_pairs={{0,4},{1,5},{2,6},{3,7},{4,0},{5,1},{6,2},{7,3},{8,12},{9,13},{10,... | collective-permute-start | bytes 811016 | tf_op jit(solution)/shard_map/ppermute | solution.py:156
  22.2 17.5 %collective-permute-start.4 = (bf16[96,4224]{1,0:T(8,128)(2,1)S(1)}, bf16[96,4224]{1,0:T(8,128)(2,1)S(1)}, u32[]{:S(2)}, u32[]{:S(2)}) collective-permute-start(bf16[96,4224]{1,0:T(8,128)(2,1)S(1)} %constant_dynamic-update-slice_fusion.refs_0_), channel_id=1, source_target_pairs={{0,1},{1,0},{2,3},{3,2},{4,5},{5,4},{6,7},{7,6},{8,9},{9,8},{10,11... | collective-permute-start | bytes 2433032 | tf_op jit(solution)/shard_map/ppermute | solution.py:150
  27.9 8.4 %collective-permute-start.6 = (bf16[32,4224]{1,0:T(8,128)(2,1)S(1)}, bf16[32,4224]{1,0:T(8,128)(2,1)S(1)}, u32[]{:S(2)}, u32[]{:S(2)}) collective-permute-start(bf16[32,4224]{1,0:T(8,128)(2,1)S(1)} %collective-permute-done.5.refs_2_), channel_id=1, source_target_pairs={{0,2},{1,3},{2,0},{3,1},{4,6},{5,7},{6,4},{7,5},{8,10},{9,11},{10,... | collective-permute-start | bytes 811016 | tf_op jit(solution)/shard_map/ppermute | solution.py:153
  29.4 8.2 %collective-permute-start.9 = (bf16[32,4224]{1,0:T(8,128)(2,1)S(1)}, bf16[32,4224]{1,0:T(8,128)(2,1)S(1)}, u32[]{:S(2)}, u32[]{:S(2)}) collective-permute-start(bf16[32,4224]{1,0:T(8,128)(2,1)S(1)} %pad_maximum_fusion.1), channel_id=1, source_target_pairs={{0,4},{1,5},{2,6},{3,7},{4,0},{5,1},{6,2},{7,3},{8,12},{9,13},{10,... | collective-permute-start | bytes 811016 | tf_op jit(solution)/shard_map/ppermute | solution.py:156
  30.0 9.6 %collective-permute-start.7 = (bf16[32,4224]{1,0:T(8,128)(2,1)S(1)}, bf16[32,4224]{1,0:T(8,128)(2,1)S(1)}, u32[]{:S(2)}, u32[]{:S(2)}) collective-permute-start(bf16[32,4224]{1,0:T(8,128)(2,1)S(1)} %collective-permute-done.5.refs_2_), channel_id=1, source_target_pairs={{0,1},{1,0},{2,3},{3,2},{4,5},{5,4},{6,7},{7,6},{8,9},{9,8},{10,11... | collective-permute-start | bytes 811016 | tf_op jit(solution)/shard_map/ppermute | solution.py:150
  36.3 3.4 %collective-permute-start.8 = (bf16[32,4224]{1,0:T(8,128)(2,1)S(1)}, bf16[32,4224]{1,0:T(8,128)(2,1)S(1)}, u32[]{:S(2)}, u32[]{:S(2)}) collective-permute-start(bf16[32,4224]{1,0:T(8,128)(2,1)S(1)} %collective-permute-done.6.refs_3_), channel_id=1, source_target_pairs={{0,1},{1,0},{2,3},{3,2},{4,5},{5,4},{6,7},{7,6},{8,9},{9,8},{10,11... | collective-permute-start | bytes 811016 | tf_op jit(solution)/shard_map/ppermute | solution.py:150
  37.6 9.2 %collective-permute-start.10 = (bf16[32,4224]{1,0:T(8,128)(2,1)S(1)}, bf16[32,4224]{1,0:T(8,128)(2,1)S(1)}, u32[]{:S(2)}, u32[]{:S(2)}) collective-permute-start(bf16[32,4224]{1,0:T(8,128)(2,1)S(1)} %collective-permute-done.9.refs_2_), channel_id=1, source_target_pairs={{0,2},{1,3},{2,0},{3,1},{4,6},{5,7},{6,4},{7,5},{8,10},{9,11},{10,... | collective-permute-start | bytes 811016 | tf_op jit(solution)/shard_map/ppermute | solution.py:153
  38.1 10.0 %collective-permute-start.18 = (bf16[16,4224]{1,0:T(8,128)(2,1)S(1)}, bf16[16,4224]{1,0:T(8,128)(2,1)S(1)}, u32[]{:S(2)}, u32[]{:S(2)}) collective-permute-start(bf16[16,4224]{1,0:T(8,128)(2,1)S(1)} %collective-permute-done.2), channel_id=1, source_target_pairs={{0,2},{1,3},{2,0},{3,1},{4,6},{5,7},{6,4},{7,5},{8,10},{9,11},{10,... | collective-permute-start | bytes 405512 | tf_op jit(solution)/shard_map/ppermute | solution.py:153
  46.8 2.7 %collective-permute-start.11 = (bf16[128,4096]{1,0:T(8,128)(2,1)S(1)}, bf16[128,4096]{1,0:T(8,128)(2,1)S(1)}, u32[]{:S(2)}, u32[]{:S(2)}) collective-permute-start(bf16[128,4096]{1,0:T(8,128)(2,1)S(1)} %get-tuple-element.70), channel_id=1, source_target_pairs={{0,1},{1,0},{2,3},{3,2},{4,5},{5,4},{6,7},{7,6},{8,9},{9,8},{10,11... | collective-permute-start | bytes 3145736 | tf_op jit(solution)/shard_map/ppermute | solution.py:150
  48.1 2.5 %collective-permute-start.19 = (bf16[32,4224]{1,0:T(8,128)(2,1)S(1)}, bf16[32,4224]{1,0:T(8,128)(2,1)S(1)}, u32[]{:S(2)}, u32[]{:S(2)}) collective-permute-start(bf16[32,4224]{1,0:T(8,128)(2,1)S(1)} %constant_dynamic-update-slice_fusion.4.refs_6_), channel_id=1, source_target_pairs={{0,1},{1,0},{2,3},{3,2},{4,5},{5,4},{6,7},{7,6},{8,9},{9,8},{10,11... | collective-permute-start | bytes 811016 | tf_op jit(solution)/shard_map/ppermute | solution.py:150
  48.2 2.4 %collective-permute-start.16 = (bf16[32,4224]{1,0:T(8,128)(2,1)S(1)}, bf16[32,4224]{1,0:T(8,128)(2,1)S(1)}, u32[]{:S(2)}, u32[]{:S(2)}) collective-permute-start(bf16[32,4224]{1,0:T(8,128)(2,1)S(1)} %collective-permute-done.9.refs_2_), channel_id=1, source_target_pairs={{0,1},{1,0},{2,3},{3,2},{4,5},{5,4},{6,7},{7,6},{8,9},{9,8},{10,11... | collective-permute-start | bytes 811016 | tf_op jit(solution)/shard_map/ppermute | solution.py:150
  48.7 2.0 %collective-permute-start.17 = (bf16[32,4224]{1,0:T(8,128)(2,1)S(1)}, bf16[32,4224]{1,0:T(8,128)(2,1)S(1)}, u32[]{:S(2)}, u32[]{:S(2)}) collective-permute-start(bf16[32,4224]{1,0:T(8,128)(2,1)S(1)} %collective-permute-done.10.refs_3_), channel_id=1, source_target_pairs={{0,1},{1,0},{2,3},{3,2},{4,5},{5,4},{6,7},{7,6},{8,9},{9,8},{10,11... | collective-permute-start | bytes 811016 | tf_op jit(solution)/shard_map/ppermute | solution.py:150
  49.8 8.4 %collective-permute-start.12 = (bf16[32,4096]{1,0:T(8,128)(2,1)S(1)}, bf16[32,4096]{1,0:T(8,128)(2,1)S(1)}, u32[]{:S(2)}, u32[]{:S(2)}) collective-permute-start(bf16[32,4096]{1,0:T(8,128)(2,1)S(1)} %get-tuple-element.92), channel_id=1, source_target_pairs={{0,2},{1,3},{2,0},{3,1},{4,6},{5,7},{6,4},{7,5},{8,10},{9,11},{10,... | collective-permute-start | bytes 786440 | tf_op jit(solution)/shard_map/ppermute | solution.py:153
  58.2 2.7 %collective-permute-start.20 = (bf16[128,4096]{1,0:T(8,128)(2,1)S(1)}, bf16[128,4096]{1,0:T(8,128)(2,1)S(1)}, u32[]{:S(2)}, u32[]{:S(2)}) collective-permute-start(bf16[128,4096]{1,0:T(8,128)(2,1)S(1)} %get-tuple-element.83), channel_id=1, source_target_pairs={{0,1},{1,0},{2,3},{3,2},{4,5},{5,4},{6,7},{7,6},{8,9},{9,8},{10,11... | collective-permute-start | bytes 3145736 | tf_op jit(solution)/shard_map/ppermute | solution.py:150
  58.2 9.1 %collective-permute-start.13 = (bf16[32,4096]{1,0:T(8,128)(2,1)S(1)}, bf16[32,4096]{1,0:T(8,128)(2,1)S(1)}, u32[]{:S(2)}, u32[]{:S(2)}) collective-permute-start(bf16[32,4096]{1,0:T(8,128)(2,1)S(1)} %get-tuple-element.91), channel_id=1, source_target_pairs={{0,2},{1,3},{2,0},{3,1},{4,6},{5,7},{6,4},{7,5},{8,10},{9,11},{10,... | collective-permute-start | bytes 786440 | tf_op jit(solution)/shard_map/ppermute | solution.py:153
  61.1 11.4 %collective-permute-start.21 = (bf16[32,4096]{1,0:T(8,128)(2,1)S(1)}, bf16[32,4096]{1,0:T(8,128)(2,1)S(1)}, u32[]{:S(2)}, u32[]{:S(2)}) collective-permute-start(bf16[32,4096]{1,0:T(8,128)(2,1)S(1)} %get-tuple-element.94), channel_id=1, source_target_pairs={{0,2},{1,3},{2,0},{3,1},{4,6},{5,7},{6,4},{7,5},{8,10},{9,11},{10,... | collective-permute-start | bytes 786440 | tf_op jit(solution)/shard_map/ppermute | solution.py:153
  62.3 11.5 %collective-permute-start.14 = (bf16[32,4096]{1,0:T(8,128)(2,1)S(1)}, bf16[32,4096]{1,0:T(8,128)(2,1)S(1)}, u32[]{:S(2)}, u32[]{:S(2)}) collective-permute-start(bf16[32,4096]{1,0:T(8,128)(2,1)S(1)} %slice_add_fusion.2), channel_id=1, source_target_pairs={{0,4},{1,5},{2,6},{3,7},{4,0},{5,1},{6,2},{7,3},{8,12},{9,13},{10,... | collective-permute-start | bytes 786440 | tf_op jit(solution)/shard_map/ppermute | solution.py:156
  72.5 7.9 %collective-permute-start.22 = (bf16[32,4096]{1,0:T(8,128)(2,1)S(1)}, bf16[32,4096]{1,0:T(8,128)(2,1)S(1)}, u32[]{:S(2)}, u32[]{:S(2)}) collective-permute-start(bf16[32,4096]{1,0:T(8,128)(2,1)S(1)} %get-tuple-element.85), channel_id=1, source_target_pairs={{0,2},{1,3},{2,0},{3,1},{4,6},{5,7},{6,4},{7,5},{8,10},{9,11},{10,... | collective-permute-start | bytes 786440 | tf_op jit(solution)/shard_map/ppermute | solution.py:153
  73.6 10.5 %collective-permute-start.23 = (bf16[32,4096]{1,0:T(8,128)(2,1)S(1)}, bf16[32,4096]{1,0:T(8,128)(2,1)S(1)}, u32[]{:S(2)}, u32[]{:S(2)}) collective-permute-start(bf16[32,4096]{1,0:T(8,128)(2,1)S(1)} %slice_add_fusion), channel_id=1, source_target_pairs={{0,4},{1,5},{2,6},{3,7},{4,0},{5,1},{6,2},{7,3},{8,12},{9,13},{10,... | collective-permute-start | bytes 786440 | tf_op jit(solution)/shard_map/ppermute | solution.py:156
  73.9 10.6 %collective-permute-start.15 = (bf16[16,4096]{1,0:T(8,128)(2,1)S(1)}, bf16[16,4096]{1,0:T(8,128)(2,1)S(1)}, u32[]{:S(2)}, u32[]{:S(2)}) collective-permute-start(bf16[16,4096]{1,0:T(8,128)(2,1)S(1)} %slice.113), channel_id=1, source_target_pairs={{0,8},{1,9},{2,10},{3,11},{4,12},{5,13},{6,14},{7,15},{8,0},{9,1},... | collective-permute-start | bytes 393224 | tf_op jit(solution)/shard_map/ppermute | solution.py:156
  84.2 7.5 %collective-permute-start.24 = (bf16[16,4096]{1,0:T(8,128)(2,1)S(1)}, bf16[16,4096]{1,0:T(8,128)(2,1)S(1)}, u32[]{:S(2)}, u32[]{:S(2)}) collective-permute-start(bf16[16,4096]{1,0:T(8,128)(2,1)S(1)} %slice.112), channel_id=1, source_target_pairs={{0,8},{1,9},{2,10},{3,11},{4,12},{5,13},{6,14},{7,15},{8,0},{9,1},... | collective-permute-start | bytes 393224 | tf_op jit(solution)/shard_map/ppermute | solution.py:156

commit v6 on v5

--- a/solution.py
+++ b/solution.py
@@ -158,67 +158,90 @@
     tail = 2 * devices
     tail = -(-tail // LANES) * LANES
     ids, probs = jnp.swapaxes(ids, 1, 2), jnp.swapaxes(probs, 1, 2)
-    strides = [lines >> shift for shift in range(1, lines.bit_length())]
-    half = lines * tokens
+    middle = lines // 2
+    strides = [middle >> shift for shift in range(1, middle.bit_length())]
+    head, half = middle * tokens, lines * tokens
+
+    def grow(block):
+        for by in strides:
+            block = jnp.concatenate([block, swap_far(block, by)])
+        return block
+
+    def collapse(block):
+        for by in strides[::-1]:
+            keep = block.shape[0] // 2
+            block = block[:keep] + swap_far(block[keep:].astype(jnp.bfloat16), by).astype(jnp.float32)
+        return block
+
+    def after(x, *events):
+        return lax.optimization_barrier((x, events))[0]
+
+    def of_step(x, step):
+        return jnp.concatenate([x[at : at + tokens] for at in range(step * tokens, x.shape[0], steps * tokens)])
+
+    w_gate, w_up, w_down = w_gate[0], w_up[0], w_down[0]
     message, *own_messages = make_messages(states, ids, probs, tail)
     near_message = swap_near(message)
-    w_gate, w_up, w_down = w_gate[0], w_up[0], w_down[0]
-    pieces, nears, held = [[] for _ in range(steps)], [[] for _ in range(steps)], own_messages
-    for place, by in enumerate(strides):
-        for step in range(steps):
-            mine = held[step]
-            if step:
-                mine, _ = lax.optimization_barrier((mine, pieces[step - 1][place]))
-            piece = swap_far(mine, by)
-            if not step and not place:
-                loaded = load_weights(w_gate, w_up)
-                piece, loaded, near_message = lax.optimization_barrier((piece, loaded, near_message))
-            if step == 1 and not place:
-                w_down, _ = lax.optimization_barrier((w_down, pieces[0][0]))
-                loaded += load_weights(w_down)
-                piece, loaded = lax.optimization_barrier((piece, loaded))
-            pieces[step].append(piece)
-            nears[step].append(swap_near(piece))
-            if place + 1 < len(strides):
-                held[step] = jnp.concatenate([held[step], piece])
-    weights = loaded
-    shared = jnp.concatenate([message, near_message, *pieces[0][:-1], *nears[0][:-1]])
+    close = message
+    received = []
+    for by in strides:
+        received.append(swap_far(close, by))
+        close = jnp.concatenate([close, received[-1]])
+    cross = swap_far(own_messages[0], middle)
+    loaded = load_weights(w_gate, w_up)
+    received, cross, near_message, loaded = lax.optimization_barrier((received, cross, near_message, loaded))
+    close = jnp.concatenate([message, *received])
+    far, near_far = [], []
+    for step in range(steps):
+        if step:
+            far.append(grow(crossed))
+            near_far.append(swap_near(jnp.concatenate([far[step], of_step(close, step)[tokens:]])))
+            if step + 1 < steps:
+                crossed = swap_far(after(own_messages[step + 1], crossed), middle)
+        else:
+            near = swap_near(of_step(close, step)[tokens:])
+            if steps > 1:
+                crossed = swap_far(after(own_messages[1], cross), middle)
+            far.append(grow(cross))
+            w_down = after(w_down, cross)
+            last = load_weights(w_down)
+            far[0], near, last = lax.optimization_barrier((far[0], near, last))
+            loaded += last
+            near_close = near
+            near_far.append(swap_near(far[0]))
+    shared = jnp.concatenate([close, near_message, near_close])
     shared = [shared, swap_core(shared)]
-    outputs, ready = [], None
+    outputs, ready = [], far
     for step in range(steps):
-        blocks, near = pieces[step][-1], nears[step][-1]
-        parts = [*shared, blocks, near, swap_core(blocks), swap_core(near)]
         if step:
-            own = jnp.concatenate([*pieces[step][:-1], *nears[step][:-1]])
-            parts += [own, swap_core(own)]
+            rest = jnp.concatenate([far[step], near_far[step]])
+            parts = [*shared, rest, swap_core(rest)]
+        else:
+            parts = [*shared, far[0], swap_core(after(far[0], crossed)), near_far[0], swap_core(near_far[0])]
         plan = []
-        some = half // 2 - tokens
         for core in range(2):
-            for side in range(2):
-                at = (side * steps + step) * tokens
+            for by in range(middle):
+                at = (by * steps + step) * tokens
                 plan.append((core, at, at + tokens))
-                at = side * some + (0 if step else 2 * steps * tokens)
-                plan.append((core + 6 if step else core, at, at + some))
-                plan.append((2 + 2 * core + side, 0, half // 2))
-        parts, _ = lax.optimization_barrier((parts, ready if step else pieces))
-        own, peer, other = run_expert(step > 0, flags, weights, parts, tuple(plan))
-        other, _ = lax.optimization_barrier((other, near_high if step else nears[1][-1]))
-        other = swap_core(other)
+            plan.append((2 + core, 0, head))
+            at = (middle * steps + step) * tokens
+            plan.append((core, at, at + tokens))
+            at = 2 * head if step else (middle + 1) * steps * tokens
+            plan.append((2 * (step > 0) + core, at, at + head - tokens))
+            at = head if step else 0
+            plan.append(((2 if step else 4) + core, at, at + head))
+        own, peer, other = run_expert(step > 0, flags, loaded, after(parts, ready), tuple(plan))
+        other = swap_core(after(other, near_high if step else near_far[1]))
         own = own.astype(jnp.float32) + other[:half].astype(jnp.float32)
         peer = (peer.astype(jnp.float32) + other[half:].astype(jnp.float32)).astype(jnp.bfloat16)
         ready = peer
-        size = half // 2
-        near_high, near_low = swap_near(peer[size:]), peer[:size]
+        near_high, near_low = swap_near(peer[head:]), peer[:head]
         if step + 1 == steps:
-            near_low, _ = lax.optimization_barrier((near_low, near_high))
-        high = own[size:] + near_high.astype(jnp.float32)
-        _, near_low = lax.optimization_barrier((high, swap_near(near_low)))
-        line = own[:size] + near_low.astype(jnp.float32)
-        for by in strides[::-1]:
-            line += swap_far(high.astype(jnp.bfloat16), by).astype(jnp.float32)
-            size //= 2
-            line, high = line[:size], line[size:]
-        outputs.append(jnp.concatenate([line, high]).astype(jnp.bfloat16))
+            near_low = after(near_low, near_high)
+        high = own[head:] + near_high.astype(jnp.float32)
+        low = own[:head] + after(swap_near(near_low), high).astype(jnp.float32)
+        high = swap_far(collapse(high).astype(jnp.bfloat16), middle)
+        outputs.append((collapse(low) + high.astype(jnp.float32)).astype(jnp.bfloat16))
     return jnp.stack(outputs)
 
 

time: 92.6 us -> 89.5 us (0.967)
  waiting for transfers between devices: 45.1 us -> 36.2 us
  starting transfers between devices: 22.5 us -> 28.2 us
    ppermute x8 -> x11, starting transfers between devices: 10.6 us -> 19.6 us  [swap_far(): lax.ppermute(x, 'expert', [(index(z, y, c), index(z ^ by, y, c)) for z, y...]
    ppermute x8 -> x11, waiting for transfers between devices: 21 us -> 14.1 us  [swap_far(): lax.ppermute(x, 'expert', [(index(z, y, c), index(z ^ by, y, c)) for z, y...]
    ppermute x9 -> x8, waiting for transfers between devices: 21.8 us -> 18.3 us  [swap_near(): lax.ppermute(x, 'expert', [(index(z, y, c), index(z, 1 - y, c)) for z, y,...]
    ppermute x9 -> x8, starting transfers between devices: 11.2 us -> 7.73 us  [swap_near(): lax.ppermute(x, 'expert', [(index(z, y, c), index(z, 1 - y, c)) for z, y,...]
    ppermute x8 -> x6, waiting for transfers between devices: 2.36 us -> 3.74 us  [swap_core(): lax.ppermute(x, 'expert', [(index(z, y, c), index(z, y, 1 - c)) for z, y,...]
  transfers between devices with their start and end apart: 25 -> 25, of which waited for: 14 -> 15; matrix products, arithmetic and copies ran while one was open for 1% -> 1% of each run, Pallas kernels for 23% -> 24%
where the time goes in v6:
time: 89.5 us; the launch traced here: 89.4 us
  waiting for transfers between devices  36.2 us (40%)
  starting transfers between devices  28.2 us (32%)
  Pallas kernels  22.9 us (26%)
  other arithmetic  1.59 us (2%)
    ppermute x11, starting transfers between devices, swap_far(): lax.ppermute(x, 'expert', [(index(z, y, c), index(z ^ by, y, c)) for z, y...  19.6 us
    ppermute x8, waiting for transfers between devices, swap_near(): lax.ppermute(x, 'expert', [(index(z, y, c), index(z, 1 - y, c)) for z, y,...  18.3 us
    pallas_call x2, Pallas kernels, run_expert(): pl.pallas_call(functools.partial(expert_kernel, swapped, count, plan), ou...  14.2 us
    ppermute x11, waiting for transfers between devices, swap_far(): lax.ppermute(x, 'expert', [(index(z, y, c), index(z ^ by, y, c)) for z, y...  14.1 us
    ppermute x8, starting transfers between devices, swap_near(): lax.ppermute(x, 'expert', [(index(z, y, c), index(z, 1 - y, c)) for z, y,...  7.73 us
    pallas_call x2, Pallas kernels, load_weights(): pl.pallas_call(load_kernel, out_shape=[pltpu.VMEM(x.shape, x.dtype) for x...  7.43 us
    ppermute x6, waiting for transfers between devices, swap_core(): lax.ppermute(x, 'expert', [(index(z, y, c), index(z, y, 1 - c)) for z, y,...  3.74 us
  transfers between devices with their start and end apart: 25, of which 15 were waited for; matrix products, arithmetic and copies ran while one was open for 1% of the time, Pallas kernels for 24%

profile of v6, /device:TPU:0, one launch (start us, length us, event | category | flops | bytes accessed | tf_op | source)
XLA Modules:
  0.0 89.4 jit_solution(17020978830906877819)
XLA Ops:
  0.0 1.2 %messages.1 = (bf16[32,4224]{1,0:T(8,128)(2,1)S(1)}, bf16[16,4224]{1,0:T(8,128)(2,1)S(1)}, bf16[16,4224]{1,0:T(8,128)(2,1)S(1)}) custom-call(bf16[2,16,4096]{2,1,0:T(8,128)(2,1)} %states_ref.1, s32[2,8,16]{2,1,0:T(8,128)} %bitcast.12, f32[2,8,16]{2,1,0:T(8,128)} %bitcast.13), custom_call_target="tpu_custom_call" | custom-call | tf_op jit(solution)/shard_map/messages/pallas_call | solution.py:50
  1.2 3.0 %collective-permute-start = (bf16[32,4224]{1,0:T(8,128)(2,1)S(1)}, bf16[32,4224]{1,0:T(8,128)(2,1)S(1)}, u32[]{:S(2)}, u32[]{:S(2)}) collective-permute-start(bf16[32,4224]{1,0:T(8,128)(2,1)S(1)} %get-tuple-element.42), channel_id=1, source_target_pairs={{0,4},{1,5},{2,6},{3,7},{4,0},{5,1},{6,2},{7,3},{8,12},{9,13},{10,... | collective-permute-start | bytes 811016 | tf_op jit(solution)/shard_map/ppermute | solution.py:156
  4.3 1.5 %collective-permute-start.2 = (bf16[32,4224]{1,0:T(8,128)(2,1)S(1)}, bf16[32,4224]{1,0:T(8,128)(2,1)S(1)}, u32[]{:S(2)}, u32[]{:S(2)}) collective-permute-start(bf16[32,4224]{1,0:T(8,128)(2,1)S(1)} %get-tuple-element.42), channel_id=1, source_target_pairs={{0,2},{1,3},{2,0},{3,1},{4,6},{5,7},{6,4},{7,5},{8,10},{9,11},{10,... | collective-permute-start | bytes 811016 | tf_op jit(solution)/shard_map/ppermute | solution.py:153
  5.8 2.6 %collective-permute-start.1 = (bf16[16,4224]{1,0:T(8,128)(2,1)S(1)}, bf16[16,4224]{1,0:T(8,128)(2,1)S(1)}, u32[]{:S(2)}, u32[]{:S(2)}) collective-permute-start(bf16[16,4224]{1,0:T(8,128)(2,1)S(1)} %get-tuple-element.43), channel_id=1, source_target_pairs={{0,8},{1,9},{2,10},{3,11},{4,12},{5,13},{6,14},{7,15},{8,0},{9,1},... | collective-permute-start | bytes 405512 | tf_op jit(solution)/shard_map/ppermute | solution.py:156
  8.4 4.6 %load_weights.2 = (bf16[4096,768]{1,0:T(8,128)(2,1)S(1)}, bf16[4096,768]{1,0:T(8,128)(2,1)S(1)}) custom-call(bf16[4096,768]{1,0:T(8,128)(2,1)} %bitcast.9, bf16[4096,768]{1,0:T(8,128)(2,1)} %bitcast.10), custom_call_target="tpu_custom_call" | custom-call | tf_op jit(solution)/shard_map/load_weights/pallas_call | solution.py:74
  13.0 0.0 collective-permute-done.1
  13.0 0.6 collective-permute-done
  13.6 0.0 collective-permute-done.2
  13.6 2.8 %collective-permute-start.3 = (bf16[16,4224]{1,0:T(8,128)(2,1)S(1)}, bf16[16,4224]{1,0:T(8,128)(2,1)S(1)}, u32[]{:S(2)}, u32[]{:S(2)}) collective-permute-start(bf16[16,4224]{1,0:T(8,128)(2,1)S(1)} %collective-permute-done.1), channel_id=1, source_target_pairs={{0,4},{1,5},{2,6},{3,7},{4,0},{5,1},{6,2},{7,3},{8,12},{9,13},{10,... | collective-permute-start | bytes 405512 | tf_op jit(solution)/shard_map/ppermute | solution.py:156
  16.4 1.6 %collective-permute-start.4 = (bf16[16,4224]{1,0:T(8,128)(2,1)S(1)}, bf16[16,4224]{1,0:T(8,128)(2,1)S(1)}, u32[]{:S(2)}, u32[]{:S(2)}) collective-permute-start(bf16[16,4224]{1,0:T(8,128)(2,1)S(1)} %get-tuple-element.88), channel_id=1, source_target_pairs={{0,2},{1,3},{2,0},{3,1},{4,6},{5,7},{6,4},{7,5},{8,10},{9,11},{10,... | collective-permute-start | bytes 405512 | tf_op jit(solution)/shard_map/ppermute | solution.py:153
  18.0 1.6 %collective-permute-start.6 = (bf16[16,4224]{1,0:T(8,128)(2,1)S(1)}, bf16[16,4224]{1,0:T(8,128)(2,1)S(1)}, u32[]{:S(2)}, u32[]{:S(2)}) collective-permute-start(bf16[16,4224]{1,0:T(8,128)(2,1)S(1)} %get-tuple-element.56), channel_id=1, source_target_pairs={{0,8},{1,9},{2,10},{3,11},{4,12},{5,13},{6,14},{7,15},{8,0},{9,1},... | collective-permute-start | bytes 405512 | tf_op jit(solution)/shard_map/ppermute | solution.py:156
  19.7 0.0 copy-start
  19.7 2.8 %load_weights.3.down_ref = bf16[768,4096]{1,0:T(8,128)(2,1)S(1)} custom-call(bf16[768,4096]{1,0:T(8,128)(2,1)} %bitcast.11), custom_call_target="tpu_custom_call" | custom-call | tf_op jit(solution)/shard_map/load_weights/pallas_call | solution.py:74
  22.5 0.0 collective-permute-done.3
  22.6 0.0 collective-permute-done.4
  22.6 3.0 %collective-permute-done.6 = bf16[16,4224]{1,0:T(8,128)(2,1)S(1)} collective-permute-done((bf16[16,4224]{1,0:T(8,128)(2,1)S(1)}, bf16[16,4224]{1,0:T(8,128)(2,1)S(1)}, u32[]{:S(2)}, u32[]{:S(2)}) %collective-permute-start.6) | collective-permute-done | bytes 135200 | tf_op jit(solution)/shard_map/ppermute | solution.py:156
  25.6 0.0 collective-permute-start.10
  25.6 0.1 collective-permute-start.5
  25.7 0.5 collective-permute-start.8
  26.2 0.2 collective-permute-start.7
  26.4 4.2 %collective-permute-done.10 = bf16[16,4224]{1,0:T(8,128)(2,1)S(1)} collective-permute-done((bf16[16,4224]{1,0:T(8,128)(2,1)S(1)}, bf16[16,4224]{1,0:T(8,128)(2,1)S(1)}, u32[]{:S(2)}, u32[]{:S(2)}) %collective-permute-start.10) | collective-permute-done | bytes 135200 | tf_op jit(solution)/shard_map/ppermute | solution.py:156
  30.7 0.5 collective-permute-start.11
  31.2 3.9 %collective-permute-done.8.refs_4_ = bf16[32,4224]{1,0:T(8,128)(2,1)S(1)} collective-permute-done((bf16[32,4224]{1,0:T(8,128)(2,1)S(1)}, bf16[32,4224]{1,0:T(8,128)(2,1)S(1)}, u32[]{:S(2)}, u32[]{:S(2)}) %collective-permute-start.8) | collective-permute-done | bytes 270368 | tf_op jit(solution)/shard_map/ppermute | solution.py:153
  35.1 0.0 collective-permute-start.9
  35.1 0.0 collective-permute-done.7.refs_3_
  35.1 1.5 %collective-permute-done.9.refs_5_ = bf16[32,4224]{1,0:T(8,128)(2,1)S(1)} collective-permute-done((bf16[32,4224]{1,0:T(8,128)(2,1)S(1)}, bf16[32,4224]{1,0:T(8,128)(2,1)S(1)}, u32[]{:S(2)}, u32[]{:S(2)}) %collective-permute-start.9) | collective-permute-done | bytes 270368 | tf_op jit(solution)/shard_map/ppermute | solution.py:150
  36.6 0.0 collective-permute-done.5.refs_1_
  36.6 0.0 copy-done
  36.6 7.1 %expert.2 = (bf16[64,4096]{1,0:T(8,128)(2,1)S(1)}, bf16[64,4096]{1,0:T(8,128)(2,1)S(1)}, bf16[128,4096]{1,0:T(8,128)(2,1)S(1)}) custom-call(s32[16]{0:T(128)S(1)} %copy-done, bf16[4096,768]{1,0:T(8,128)(2,1)S(1)} %get-tuple-element.46.gate_ref, bf16[4096,768]{1,0:T(8,128)(2,1)S(1)} %get-tuple-element.47.up_ref, bf16[768,4096]{1,0:T(8,128)(2,1)S(1)} %load_weights.3.down_ref, ...), custom_call_target="tpu_custom_call" | custom-call | tf_op jit(solution)/shard_map/expert/pallas_call | solution.py:124
  43.7 0.0 collective-permute-done.11
  43.7 0.2 collective-permute-start.12
  44.0 0.4 collective-permute-start.18
  44.4 2.0 %collective-permute-done.12 = bf16[128,4096]{1,0:T(8,128)(2,1)S(1)} collective-permute-done((bf16[128,4096]{1,0:T(8,128)(2,1)S(1)}, bf16[128,4096]{1,0:T(8,128)(2,1)S(1)}, u32[]{:S(2)}, u32[]{:S(2)}) %collective-permute-start.12) | collective-permute-done | bytes 1048608 | tf_op jit(solution)/shard_map/ppermute | solution.py:150
  46.5 0.2 convert_add_fusion.1
  46.7 0.5 collective-permute-start.14
  47.2 0.2 collective-permute-done.18.refs_3_
  47.4 7.1 %expert.3 = (bf16[64,4096]{1,0:T(8,128)(2,1)S(1)}, bf16[64,4096]{1,0:T(8,128)(2,1)S(1)}, bf16[128,4096]{1,0:T(8,128)(2,1)S(1)}) custom-call(s32[16]{0:T(128)S(1)} %copy-done, bf16[4096,768]{1,0:T(8,128)(2,1)S(1)} %get-tuple-element.46.gate_ref, bf16[4096,768]{1,0:T(8,128)(2,1)S(1)} %get-tuple-element.47.up_ref, bf16[768,4096]{1,0:T(8,128)(2,1)S(1)} %load_weights.3.down_ref, ...), custom_call_target="tpu_custom_call" | custom-call | tf_op jit(solution)/shard_map/expert/pallas_call | solution.py:124
  54.5 0.6 collective-permute-done.14
  55.1 0.0 collective-permute-start.19
  55.1 0.9 %collective-permute-start.13 = (bf16[32,4096]{1,0:T(8,128)(2,1)S(1)}, bf16[32,4096]{1,0:T(8,128)(2,1)S(1)}, u32[]{:S(2)}, u32[]{:S(2)}) collective-permute-start(bf16[32,4096]{1,0:T(8,128)(2,1)S(1)} %get-tuple-element.83), channel_id=1, source_target_pairs={{0,2},{1,3},{2,0},{3,1},{4,6},{5,7},{6,4},{7,5},{8,10},{9,11},{10,... | collective-permute-start | bytes 786440 | tf_op jit(solution)/shard_map/ppermute | solution.py:153
  56.1 7.7 %collective-permute-done.13 = bf16[32,4096]{1,0:T(8,128)(2,1)S(1)} collective-permute-done((bf16[32,4096]{1,0:T(8,128)(2,1)S(1)}, bf16[32,4096]{1,0:T(8,128)(2,1)S(1)}, u32[]{:S(2)}, u32[]{:S(2)}) %collective-permute-start.13) | collective-permute-done | bytes 262176 | tf_op jit(solution)/shard_map/ppermute | solution.py:153
  63.9 0.0 collective-permute-done.19
  63.9 0.2 add_convert_fusion
  64.2 0.9 %collective-permute-start.20 = (bf16[32,4096]{1,0:T(8,128)(2,1)S(1)}, bf16[32,4096]{1,0:T(8,128)(2,1)S(1)}, u32[]{:S(2)}, u32[]{:S(2)}) collective-permute-start(bf16[32,4096]{1,0:T(8,128)(2,1)S(1)} %get-tuple-element.86), channel_id=1, source_target_pairs={{0,2},{1,3},{2,0},{3,1},{4,6},{5,7},{6,4},{7,5},{8,10},{9,11},{10,... | collective-permute-start | bytes 786440 | tf_op jit(solution)/shard_map/ppermute | solution.py:153
  65.2 2.1 %collective-permute-start.15 = (bf16[16,4096]{1,0:T(8,128)(2,1)S(1)}, bf16[16,4096]{1,0:T(8,128)(2,1)S(1)}, u32[]{:S(2)}, u32[]{:S(2)}) collective-permute-start(bf16[16,4096]{1,0:T(8,128)(2,1)S(1)} %slice.147), channel_id=1, source_target_pairs={{0,4},{1,5},{2,6},{3,7},{4,0},{5,1},{6,2},{7,3},{8,12},{9,13},{10,... | collective-permute-start | bytes 393224 | tf_op jit(solution)/shard_map/ppermute | solution.py:156
  67.3 0.1 collective-permute-start.16
  67.4 4.8 %collective-permute-done.20 = bf16[32,4096]{1,0:T(8,128)(2,1)S(1)} collective-permute-done((bf16[32,4096]{1,0:T(8,128)(2,1)S(1)}, bf16[32,4096]{1,0:T(8,128)(2,1)S(1)}, u32[]{:S(2)}, u32[]{:S(2)}) %collective-permute-start.20) | collective-permute-done | bytes 262176 | tf_op jit(solution)/shard_map/ppermute | solution.py:153
  72.2 2.1 %collective-permute-start.23 = (bf16[16,4096]{1,0:T(8,128)(2,1)S(1)}, bf16[16,4096]{1,0:T(8,128)(2,1)S(1)}, u32[]{:S(2)}, u32[]{:S(2)}) collective-permute-start(bf16[16,4096]{1,0:T(8,128)(2,1)S(1)} %slice.144), channel_id=1, source_target_pairs={{0,4},{1,5},{2,6},{3,7},{4,0},{5,1},{6,2},{7,3},{8,12},{9,13},{10,... | collective-permute-start | bytes 393224 | tf_op jit(solution)/shard_map/ppermute | solution.py:156
  74.3 0.0 collective-permute-done.16
  74.4 1.2 %collective-permute-start.17 = (bf16[16,4096]{1,0:T(8,128)(2,1)S(1)}, bf16[16,4096]{1,0:T(8,128)(2,1)S(1)}, u32[]{:S(2)}, u32[]{:S(2)}) collective-permute-start(bf16[16,4096]{1,0:T(8,128)(2,1)S(1)} %fusion.3), channel_id=1, source_target_pairs={{0,8},{1,9},{2,10},{3,11},{4,12},{5,13},{6,14},{7,15},{8,0},{9,1},... | collective-permute-start | bytes 393224 | tf_op jit(solution)/shard_map/ppermute | solution.py:156
  75.5 1.2 %collective-permute-start.21 = (bf16[32,4096]{1,0:T(8,128)(2,1)S(1)}, bf16[32,4096]{1,0:T(8,128)(2,1)S(1)}, u32[]{:S(2)}, u32[]{:S(2)}) collective-permute-start(bf16[32,4096]{1,0:T(8,128)(2,1)S(1)} %get-tuple-element.77), channel_id=1, source_target_pairs={{0,2},{1,3},{2,0},{3,1},{4,6},{5,7},{6,4},{7,5},{8,10},{9,11},{10,... | collective-permute-start | bytes 786440 | tf_op jit(solution)/shard_map/ppermute | solution.py:153
  76.7 1.3 %collective-permute-done.23 = bf16[16,4096]{1,0:T(8,128)(2,1)S(1)} collective-permute-done((bf16[16,4096]{1,0:T(8,128)(2,1)S(1)}, bf16[16,4096]{1,0:T(8,128)(2,1)S(1)}, u32[]{:S(2)}, u32[]{:S(2)}) %collective-permute-start.23) | collective-permute-done | bytes 131104 | tf_op jit(solution)/shard_map/ppermute | solution.py:156
  78.1 2.5 %collective-permute-start.24 = (bf16[16,4096]{1,0:T(8,128)(2,1)S(1)}, bf16[16,4096]{1,0:T(8,128)(2,1)S(1)}, u32[]{:S(2)}, u32[]{:S(2)}) collective-permute-start(bf16[16,4096]{1,0:T(8,128)(2,1)S(1)} %fusion), channel_id=1, source_target_pairs={{0,8},{1,9},{2,10},{3,11},{4,12},{5,13},{6,14},{7,15},{8,0},{9,1},... | collective-permute-start | bytes 393224 | tf_op jit(solution)/shard_map/ppermute | solution.py:156
  80.6 1.3 %collective-permute-done.21 = bf16[32,4096]{1,0:T(8,128)(2,1)S(1)} collective-permute-done((bf16[32,4096]{1,0:T(8,128)(2,1)S(1)}, bf16[32,4096]{1,0:T(8,128)(2,1)S(1)}, u32[]{:S(2)}, u32[]{:S(2)}) %collective-permute-start.21) | collective-permute-done | bytes 262176 | tf_op jit(solution)/shard_map/ppermute | solution.py:153
  82.0 1.6 %collective-permute-start.22 = (bf16[16,4096]{1,0:T(8,128)(2,1)S(1)}, bf16[16,4096]{1,0:T(8,128)(2,1)S(1)}, u32[]{:S(2)}, u32[]{:S(2)}) collective-permute-start(bf16[16,4096]{1,0:T(8,128)(2,1)S(1)} %slice.145), channel_id=1, source_target_pairs={{0,4},{1,5},{2,6},{3,7},{4,0},{5,1},{6,2},{7,3},{8,12},{9,13},{10,... | collective-permute-start | bytes 393224 | tf_op jit(solution)/shard_map/ppermute | solution.py:156
  83.6 0.0 collective-permute-done.15
  83.6 1.9 %collective-permute-done.17 = bf16[16,4096]{1,0:T(8,128)(2,1)S(1)} collective-permute-done((bf16[16,4096]{1,0:T(8,128)(2,1)S(1)}, bf16[16,4096]{1,0:T(8,128)(2,1)S(1)}, u32[]{:S(2)}, u32[]{:S(2)}) %collective-permute-start.17) | collective-permute-done | bytes 131104 | tf_op jit(solution)/shard_map/ppermute | solution.py:156
  85.6 2.2 %collective-permute-done.24 = bf16[16,4096]{1,0:T(8,128)(2,1)S(1)} collective-permute-done((bf16[16,4096]{1,0:T(8,128)(2,1)S(1)}, bf16[16,4096]{1,0:T(8,128)(2,1)S(1)}, u32[]{:S(2)}, u32[]{:S(2)}) %collective-permute-start.24) | collective-permute-done | bytes 131104 | tf_op jit(solution)/shard_map/ppermute | solution.py:156
  87.9 0.7 collective-permute-done.22
  88.6 0.7 pad_maximum_fusion.2
  (24 shorter events, 0.7 us)
Async XLA Ops:
  1.2 12.4 %collective-permute-start = (bf16[32,4224]{1,0:T(8,128)(2,1)S(1)}, bf16[32,4224]{1,0:T(8,128)(2,1)S(1)}, u32[]{:S(2)}, u32[]{:S(2)}) collective-permute-start(bf16[32,4224]{1,0:T(8,128)(2,1)S(1)} %get-tuple-element.42), channel_id=1, source_target_pairs={{0,4},{1,5},{2,6},{3,7},{4,0},{5,1},{6,2},{7,3},{8,12},{9,13},{10,... | collective-permute-start | bytes 811016 | tf_op jit(solution)/shard_map/ppermute | solution.py:156
  4.3 9.4 %collective-permute-start.2 = (bf16[32,4224]{1,0:T(8,128)(2,1)S(1)}, bf16[32,4224]{1,0:T(8,128)(2,1)S(1)}, u32[]{:S(2)}, u32[]{:S(2)}) collective-permute-start(bf16[32,4224]{1,0:T(8,128)(2,1)S(1)} %get-tuple-element.42), channel_id=1, source_target_pairs={{0,2},{1,3},{2,0},{3,1},{4,6},{5,7},{6,4},{7,5},{8,10},{9,11},{10,... | collective-permute-start | bytes 811016 | tf_op jit(solution)/shard_map/ppermute | solution.py:153
  5.8 7.2 %collective-permute-start.1 = (bf16[16,4224]{1,0:T(8,128)(2,1)S(1)}, bf16[16,4224]{1,0:T(8,128)(2,1)S(1)}, u32[]{:S(2)}, u32[]{:S(2)}) collective-permute-start(bf16[16,4224]{1,0:T(8,128)(2,1)S(1)} %get-tuple-element.43), channel_id=1, source_target_pairs={{0,8},{1,9},{2,10},{3,11},{4,12},{5,13},{6,14},{7,15},{8,0},{9,1},... | collective-permute-start | bytes 405512 | tf_op jit(solution)/shard_map/ppermute | solution.py:156
  13.6 8.9 %collective-permute-start.3 = (bf16[16,4224]{1,0:T(8,128)(2,1)S(1)}, bf16[16,4224]{1,0:T(8,128)(2,1)S(1)}, u32[]{:S(2)}, u32[]{:S(2)}) collective-permute-start(bf16[16,4224]{1,0:T(8,128)(2,1)S(1)} %collective-permute-done.1), channel_id=1, source_target_pairs={{0,4},{1,5},{2,6},{3,7},{4,0},{5,1},{6,2},{7,3},{8,12},{9,13},{10,... | collective-permute-start | bytes 405512 | tf_op jit(solution)/shard_map/ppermute | solution.py:156
  16.4 6.1 %collective-permute-start.4 = (bf16[16,4224]{1,0:T(8,128)(2,1)S(1)}, bf16[16,4224]{1,0:T(8,128)(2,1)S(1)}, u32[]{:S(2)}, u32[]{:S(2)}) collective-permute-start(bf16[16,4224]{1,0:T(8,128)(2,1)S(1)} %get-tuple-element.88), channel_id=1, source_target_pairs={{0,2},{1,3},{2,0},{3,1},{4,6},{5,7},{6,4},{7,5},{8,10},{9,11},{10,... | collective-permute-start | bytes 405512 | tf_op jit(solution)/shard_map/ppermute | solution.py:153
  18.0 7.6 %collective-permute-start.6 = (bf16[16,4224]{1,0:T(8,128)(2,1)S(1)}, bf16[16,4224]{1,0:T(8,128)(2,1)S(1)}, u32[]{:S(2)}, u32[]{:S(2)}) collective-permute-start(bf16[16,4224]{1,0:T(8,128)(2,1)S(1)} %get-tuple-element.56), channel_id=1, source_target_pairs={{0,8},{1,9},{2,10},{3,11},{4,12},{5,13},{6,14},{7,15},{8,0},{9,1},... | collective-permute-start | bytes 405512 | tf_op jit(solution)/shard_map/ppermute | solution.py:156
  19.7 16.9 %copy-start = (s32[16]{0:T(128)S(1)}, s32[16]{0:T(128)}, u32[]{:S(2)}) copy-start(s32[16]{0:T(128)} %flags_ref.3) | copy-start | bytes 196
  25.6 5.0 %collective-permute-start.10 = (bf16[16,4224]{1,0:T(8,128)(2,1)S(1)}, bf16[16,4224]{1,0:T(8,128)(2,1)S(1)}, u32[]{:S(2)}, u32[]{:S(2)}) collective-permute-start(bf16[16,4224]{1,0:T(8,128)(2,1)S(1)} %collective-permute-done.6), channel_id=1, source_target_pairs={{0,4},{1,5},{2,6},{3,7},{4,0},{5,1},{6,2},{7,3},{8,12},{9,13},{10,... | collective-permute-start | bytes 405512 | tf_op jit(solution)/shard_map/ppermute | solution.py:156
  25.6 11.0 %collective-permute-start.5 = (bf16[112,4224]{1,0:T(8,128)(2,1)S(1)}, bf16[112,4224]{1,0:T(8,128)(2,1)S(1)}, u32[]{:S(2)}, u32[]{:S(2)}) collective-permute-start(bf16[112,4224]{1,0:T(8,128)(2,1)S(1)} %constant_dynamic-update-slice_fusion.refs_0_), channel_id=1, source_target_pairs={{0,1},{1,0},{2,3},{3,2},{4,5},{5,4},{6,7},{7,6},{8,9},{9,8},{10,11... | collective-permute-start | bytes 2838536 | tf_op jit(solution)/shard_map/ppermute | solution.py:150
  25.7 9.3 %collective-permute-start.8 = (bf16[32,4224]{1,0:T(8,128)(2,1)S(1)}, bf16[32,4224]{1,0:T(8,128)(2,1)S(1)}, u32[]{:S(2)}, u32[]{:S(2)}) collective-permute-start(bf16[32,4224]{1,0:T(8,128)(2,1)S(1)} %pad_maximum_fusion.1.refs_2_), channel_id=1, source_target_pairs={{0,2},{1,3},{2,0},{3,1},{4,6},{5,7},{6,4},{7,5},{8,10},{9,11},{10,... | collective-permute-start | bytes 811016 | tf_op jit(solution)/shard_map/ppermute | solution.py:153
  26.2 8.9 %collective-permute-start.7 = (bf16[32,4224]{1,0:T(8,128)(2,1)S(1)}, bf16[32,4224]{1,0:T(8,128)(2,1)S(1)}, u32[]{:S(2)}, u32[]{:S(2)}) collective-permute-start(bf16[32,4224]{1,0:T(8,128)(2,1)S(1)} %pad_maximum_fusion.1.refs_2_), channel_id=1, source_target_pairs={{0,1},{1,0},{2,3},{3,2},{4,5},{5,4},{6,7},{7,6},{8,9},{9,8},{10,11... | collective-permute-start | bytes 811016 | tf_op jit(solution)/shard_map/ppermute | solution.py:150
  30.7 13.1 %collective-permute-start.11 = (bf16[48,4224]{1,0:T(8,128)(2,1)S(1)}, bf16[48,4224]{1,0:T(8,128)(2,1)S(1)}, u32[]{:S(2)}, u32[]{:S(2)}) collective-permute-start(bf16[48,4224]{1,0:T(8,128)(2,1)S(1)} %pad_maximum_fusion), channel_id=1, source_target_pairs={{0,2},{1,3},{2,0},{3,1},{4,6},{5,7},{6,4},{7,5},{8,10},{9,11},{10,... | collective-permute-start | bytes 1216520 | tf_op jit(solution)/shard_map/ppermute | solution.py:153
  35.1 1.5 %collective-permute-start.9 = (bf16[32,4224]{1,0:T(8,128)(2,1)S(1)}, bf16[32,4224]{1,0:T(8,128)(2,1)S(1)}, u32[]{:S(2)}, u32[]{:S(2)}) collective-permute-start(bf16[32,4224]{1,0:T(8,128)(2,1)S(1)} %collective-permute-done.8.refs_4_), channel_id=1, source_target_pairs={{0,1},{1,0},{2,3},{3,2},{4,5},{5,4},{6,7},{7,6},{8,9},{9,8},{10,11... | collective-permute-start | bytes 811016 | tf_op jit(solution)/shard_map/ppermute | solution.py:150
  43.7 2.7 %collective-permute-start.12 = (bf16[128,4096]{1,0:T(8,128)(2,1)S(1)}, bf16[128,4096]{1,0:T(8,128)(2,1)S(1)}, u32[]{:S(2)}, u32[]{:S(2)}) collective-permute-start(bf16[128,4096]{1,0:T(8,128)(2,1)S(1)} %get-tuple-element.66), channel_id=1, source_target_pairs={{0,1},{1,0},{2,3},{3,2},{4,5},{5,4},{6,7},{7,6},{8,9},{9,8},{10,11... | collective-permute-start | bytes 3145736 | tf_op jit(solution)/shard_map/ppermute | solution.py:150
  44.0 3.4 %collective-permute-start.18 = (bf16[80,4224]{1,0:T(8,128)(2,1)S(1)}, bf16[80,4224]{1,0:T(8,128)(2,1)S(1)}, u32[]{:S(2)}, u32[]{:S(2)}) collective-permute-start(bf16[80,4224]{1,0:T(8,128)(2,1)S(1)} %constant_dynamic-update-slice_fusion.4.refs_2_), channel_id=1, source_target_pairs={{0,1},{1,0},{2,3},{3,2},{4,5},{5,4},{6,7},{7,6},{8,9},{9,8},{10,11... | collective-permute-start | bytes 2027528 | tf_op jit(solution)/shard_map/ppermute | solution.py:150
  46.7 8.4 %collective-permute-start.14 = (bf16[32,4096]{1,0:T(8,128)(2,1)S(1)}, bf16[32,4096]{1,0:T(8,128)(2,1)S(1)}, u32[]{:S(2)}, u32[]{:S(2)}) collective-permute-start(bf16[32,4096]{1,0:T(8,128)(2,1)S(1)} %get-tuple-element.84), channel_id=1, source_target_pairs={{0,2},{1,3},{2,0},{3,1},{4,6},{5,7},{6,4},{7,5},{8,10},{9,11},{10,... | collective-permute-start | bytes 786440 | tf_op jit(solution)/shard_map/ppermute | solution.py:153
  55.1 8.7 %collective-permute-start.19 = (bf16[128,4096]{1,0:T(8,128)(2,1)S(1)}, bf16[128,4096]{1,0:T(8,128)(2,1)S(1)}, u32[]{:S(2)}, u32[]{:S(2)}) collective-permute-start(bf16[128,4096]{1,0:T(8,128)(2,1)S(1)} %get-tuple-element.75), channel_id=1, source_target_pairs={{0,1},{1,0},{2,3},{3,2},{4,5},{5,4},{6,7},{7,6},{8,9},{9,8},{10,11... | collective-permute-start | bytes 3145736 | tf_op jit(solution)/shard_map/ppermute | solution.py:150
  55.1 8.7 %collective-permute-start.13 = (bf16[32,4096]{1,0:T(8,128)(2,1)S(1)}, bf16[32,4096]{1,0:T(8,128)(2,1)S(1)}, u32[]{:S(2)}, u32[]{:S(2)}) collective-permute-start(bf16[32,4096]{1,0:T(8,128)(2,1)S(1)} %get-tuple-element.83), channel_id=1, source_target_pairs={{0,2},{1,3},{2,0},{3,1},{4,6},{5,7},{6,4},{7,5},{8,10},{9,11},{10,... | collective-permute-start | bytes 786440 | tf_op jit(solution)/shard_map/ppermute | solution.py:153
  64.2 8.0 %collective-permute-start.20 = (bf16[32,4096]{1,0:T(8,128)(2,1)S(1)}, bf16[32,4096]{1,0:T(8,128)(2,1)S(1)}, u32[]{:S(2)}, u32[]{:S(2)}) collective-permute-start(bf16[32,4096]{1,0:T(8,128)(2,1)S(1)} %get-tuple-element.86), channel_id=1, source_target_pairs={{0,2},{1,3},{2,0},{3,1},{4,6},{5,7},{6,4},{7,5},{8,10},{9,11},{10,... | collective-permute-start | bytes 786440 | tf_op jit(solution)/shard_map/ppermute | solution.py:153
  65.2 18.4 %collective-permute-start.15 = (bf16[16,4096]{1,0:T(8,128)(2,1)S(1)}, bf16[16,4096]{1,0:T(8,128)(2,1)S(1)}, u32[]{:S(2)}, u32[]{:S(2)}) collective-permute-start(bf16[16,4096]{1,0:T(8,128)(2,1)S(1)} %slice.147), channel_id=1, source_target_pairs={{0,4},{1,5},{2,6},{3,7},{4,0},{5,1},{6,2},{7,3},{8,12},{9,13},{10,... | collective-permute-start | bytes 393224 | tf_op jit(solution)/shard_map/ppermute | solution.py:156
  67.3 7.0 %collective-permute-start.16 = (bf16[16,4096]{1,0:T(8,128)(2,1)S(1)}, bf16[16,4096]{1,0:T(8,128)(2,1)S(1)}, u32[]{:S(2)}, u32[]{:S(2)}) collective-permute-start(bf16[16,4096]{1,0:T(8,128)(2,1)S(1)} %slice.146), channel_id=1, source_target_pairs={{0,4},{1,5},{2,6},{3,7},{4,0},{5,1},{6,2},{7,3},{8,12},{9,13},{10,... | collective-permute-start | bytes 393224 | tf_op jit(solution)/shard_map/ppermute | solution.py:156
  72.2 5.8 %collective-permute-start.23 = (bf16[16,4096]{1,0:T(8,128)(2,1)S(1)}, bf16[16,4096]{1,0:T(8,128)(2,1)S(1)}, u32[]{:S(2)}, u32[]{:S(2)}) collective-permute-start(bf16[16,4096]{1,0:T(8,128)(2,1)S(1)} %slice.144), channel_id=1, source_target_pairs={{0,4},{1,5},{2,6},{3,7},{4,0},{5,1},{6,2},{7,3},{8,12},{9,13},{10,... | collective-permute-start | bytes 393224 | tf_op jit(solution)/shard_map/ppermute | solution.py:156
  74.4 11.2 %collective-permute-start.17 = (bf16[16,4096]{1,0:T(8,128)(2,1)S(1)}, bf16[16,4096]{1,0:T(8,128)(2,1)S(1)}, u32[]{:S(2)}, u32[]{:S(2)}) collective-permute-start(bf16[16,4096]{1,0:T(8,128)(2,1)S(1)} %fusion.3), channel_id=1, source_target_pairs={{0,8},{1,9},{2,10},{3,11},{4,12},{5,13},{6,14},{7,15},{8,0},{9,1},... | collective-permute-start | bytes 393224 | tf_op jit(solution)/shard_map/ppermute | solution.py:156
  75.5 6.4 %collective-permute-start.21 = (bf16[32,4096]{1,0:T(8,128)(2,1)S(1)}, bf16[32,4096]{1,0:T(8,128)(2,1)S(1)}, u32[]{:S(2)}, u32[]{:S(2)}) collective-permute-start(bf16[32,4096]{1,0:T(8,128)(2,1)S(1)} %get-tuple-element.77), channel_id=1, source_target_pairs={{0,2},{1,3},{2,0},{3,1},{4,6},{5,7},{6,4},{7,5},{8,10},{9,11},{10,... | collective-permute-start | bytes 786440 | tf_op jit(solution)/shard_map/ppermute | solution.py:153
  78.1 9.8 %collective-permute-start.24 = (bf16[16,4096]{1,0:T(8,128)(2,1)S(1)}, bf16[16,4096]{1,0:T(8,128)(2,1)S(1)}, u32[]{:S(2)}, u32[]{:S(2)}) collective-permute-start(bf16[16,4096]{1,0:T(8,128)(2,1)S(1)} %fusion), channel_id=1, source_target_pairs={{0,8},{1,9},{2,10},{3,11},{4,12},{5,13},{6,14},{7,15},{8,0},{9,1},... | collective-permute-start | bytes 393224 | tf_op jit(solution)/shard_map/ppermute | solution.py:156
  82.0 6.6 %collective-permute-start.22 = (bf16[16,4096]{1,0:T(8,128)(2,1)S(1)}, bf16[16,4096]{1,0:T(8,128)(2,1)S(1)}, u32[]{:S(2)}, u32[]{:S(2)}) collective-permute-start(bf16[16,4096]{1,0:T(8,128)(2,1)S(1)} %slice.145), channel_id=1, source_target_pairs={{0,4},{1,5},{2,6},{3,7},{4,0},{5,1},{6,2},{7,3},{8,12},{9,13},{10,... | collective-permute-start | bytes 393224 | tf_op jit(solution)/shard_map/ppermute | solution.py:156

commit v7 on v6

--- a/solution.py
+++ b/solution.py
@@ -84,7 +84,7 @@
 
 
 def expert_kernel(swapped, count, plan, flags_ref, gate_ref, up_ref, down_ref, *refs):
-    *sources, own_ref, near_ref, other_ref, rows, hidden = refs
+    *sources, own_ref, near_ref, low_ref, high_ref, rows, hidden = refs
     width, units = gate_ref.shape
     tail = rows.shape[1] - width
     owner = lax.axis_index("expert")
@@ -110,7 +110,10 @@
         out = out.astype(jnp.bfloat16)
         own_ref[:, at] = out[:count]
         near_ref[:, at] = out[count : 2 * count]
-        other_ref[:, at] = out[2 * count :]
+        for side in range(2):
+            low, part = (2 + side) * count, slice(side * count // 2, (side + 1) * count // 2)
+            low_ref[part, at] = out[low : low + count // 2]
+            high_ref[part, at] = out[low + count // 2 : low + count]
         return 0
 
     lax.fori_loop(0, width // 512, columns, 0)
@@ -123,17 +126,35 @@
     weights = [pltpu.with_memory_space_constraint(w, pltpu.VMEM) for w in weights]
     return pl.pallas_call(
         functools.partial(expert_kernel, swapped, count, plan),
-        out_shape=[jax.ShapeDtypeStruct((k * count, width), jnp.bfloat16) for k in (1, 1, 2)],
+        out_shape=[jax.ShapeDtypeStruct((count, width), jnp.bfloat16)] * 4,
         in_specs=[pl.BlockSpec(memory_space=pltpu.SMEM)] + [in_vmem()] * (3 + len(parts)),
-        out_specs=[in_vmem()] * 3,
+        out_specs=[in_vmem()] * 4,
         scratch_shapes=[
             pltpu.VMEM((total, parts[0].shape[1]), jnp.bfloat16),
             pltpu.VMEM((total, units), jnp.bfloat16),
         ],
         compiler_params=pltpu.CompilerParams(vmem_limit_bytes=16 * MIB),
-        cost_estimate=pl.CostEstimate(flops=0, bytes_accessed=0, transcendentals=0),
+        cost_estimate=pl.CostEstimate(
+            flops=total * width * units * 6, bytes_accessed=4 * total * width, transcendentals=0
+        ),
         name="expert",
     )(flags, *weights, *parts)
+
+
+def add_kernel(first_ref, second_ref, sum_ref):
+    sum_ref[...] = first_ref[...] + second_ref[...].astype(jnp.float32)
+
+
+def add(first, second):
+    return pl.pallas_call(
+        add_kernel,
+        out_shape=jax.ShapeDtypeStruct(first.shape, jnp.float32),
+        in_specs=[in_vmem()] * 2,
+        out_specs=in_vmem(),
+        compiler_params=pltpu.CompilerParams(vmem_limit_bytes=4 * MIB),
+        cost_estimate=pl.CostEstimate(flops=1 << 34, bytes_accessed=0, transcendentals=0),
+        name="add",
+    )(first, second)
 
 
 def on_device(states, ids, probs, flags, w_gate, w_up, w_down):
@@ -203,12 +224,10 @@
             if steps > 1:
                 crossed = swap_far(after(own_messages[1], cross), middle)
             far.append(grow(cross))
-            w_down = after(w_down, cross)
-            last = load_weights(w_down)
-            far[0], near, last = lax.optimization_barrier((far[0], near, last))
+            near_far.append(swap_near(far[0]))
+            last = load_weights(after(w_down, far[0]))
+            crossed, near_close, last = lax.optimization_barrier((crossed, near, last))
             loaded += last
-            near_close = near
-            near_far.append(swap_near(far[0]))
     shared = jnp.concatenate([close, near_message, near_close])
     shared = [shared, swap_core(shared)]
     outputs, ready = [], far
@@ -230,19 +249,30 @@
             plan.append((2 * (step > 0) + core, at, at + head - tokens))
             at = head if step else 0
             plan.append(((2 if step else 4) + core, at, at + head))
-        own, peer, other = run_expert(step > 0, flags, loaded, after(parts, ready), tuple(plan))
-        other = swap_core(after(other, near_high if step else near_far[1]))
-        own = own.astype(jnp.float32) + other[:half].astype(jnp.float32)
-        peer = (peer.astype(jnp.float32) + other[half:].astype(jnp.float32)).astype(jnp.bfloat16)
-        ready = peer
-        near_high, near_low = swap_near(peer[head:]), peer[:head]
-        if step + 1 == steps:
-            near_low = after(near_low, near_high)
-        high = own[head:] + near_high.astype(jnp.float32)
-        low = own[:head] + after(swap_near(near_low), high).astype(jnp.float32)
-        high = swap_far(collapse(high).astype(jnp.bfloat16), middle)
-        outputs.append((collapse(low) + high.astype(jnp.float32)).astype(jnp.bfloat16))
-    return jnp.stack(outputs)
+        own, peer, other_low, other_high = run_expert(step > 0, flags, loaded, after(parts, ready), tuple(plan))
+        other_high = swap_core(other_high if step else after(other_high, near_far[1])).astype(jnp.float32)
+        other_low = swap_core(after(other_low, near) if step else other_low)
+        to_high = (peer[head:].astype(jnp.float32) + other_high[head:]).astype(jnp.bfloat16)
+        other_low = after(other_low, to_high).astype(jnp.float32)
+        to_low = (peer[:head].astype(jnp.float32) + other_low[head:]).astype(jnp.bfloat16)
+        ready = to_high, to_low
+        if step:
+            near = after(near, to_high).astype(jnp.float32)
+            high += near[head:]
+            low += after(near[:head], high)
+            high = swap_far(collapse(high).astype(jnp.bfloat16), middle)
+            outputs.append((collapse(low), high))
+        high = own[head:].astype(jnp.float32) + other_high[:head]
+        low = own[:head].astype(jnp.float32) + other_low[:head]
+        if step + 1 < steps:
+            near = swap_near(jnp.concatenate([to_low, to_high]))
+    near = swap_near(to_low)
+    outputs = [low + after(high, near).astype(jnp.float32) for low, high in outputs]
+    high = collapse(high + swap_near(to_high).astype(jnp.float32))
+    low += after(near, high).astype(jnp.float32)
+    first = add(low[:tokens], swap_far(high.astype(jnp.bfloat16), middle))
+    outputs.append(collapse(jnp.concatenate([first, low[tokens:]])))
+    return jnp.stack(outputs).astype(jnp.bfloat16)
 
 
 def solution(mesh):

time: 89.5 us -> 91.2 us (1.019)
  waiting for transfers between devices: 36.2 us -> 38.3 us
    ppermute x11, waiting for transfers between devices: 14.1 us -> 19.6 us  [swap_far(): lax.ppermute(x, 'expert', [(index(z, y, c), index(z ^ by, y, c)) for z, y...]
    ppermute x8 -> x7, waiting for transfers between devices: 18.3 us -> 13.5 us  [swap_near(): lax.ppermute(x, 'expert', [(index(z, y, c), index(z, 1 - y, c)) for z, y,...]
    ppermute x6 -> x8, waiting for transfers between devices: 3.74 us -> 5.15 us  [swap_core(): lax.ppermute(x, 'expert', [(index(z, y, c), index(z, y, 1 - c)) for z, y,...]
    ppermute x11, starting transfers between devices: 19.6 us -> 18.3 us  [swap_far(): lax.ppermute(x, 'expert', [(index(z, y, c), index(z ^ by, y, c)) for z, y...]
    ppermute x8 -> x7, starting transfers between devices: 7.73 us -> 7.63 us  [swap_near(): lax.ppermute(x, 'expert', [(index(z, y, c), index(z, 1 - y, c)) for z, y,...]
  transfers between devices with their start and end apart: 25 -> 26, of which waited for: 15 -> 15; matrix products, arithmetic and copies ran while one was open for 1% -> 2% of each run, Pallas kernels for 24% -> 16%
where the time goes in v7:
time: 91.2 us; the launch traced here: 91 us
  waiting for transfers between devices  38.3 us (42%)
  starting transfers between devices  27.6 us (30%)
  Pallas kernels  22.7 us (25%)
  other arithmetic  1.86 us (2%)
    ppermute x11, waiting for transfers between devices, swap_far(): lax.ppermute(x, 'expert', [(index(z, y, c), index(z ^ by, y, c)) for z, y...  19.6 us
    ppermute x11, starting transfers between devices, swap_far(): lax.ppermute(x, 'expert', [(index(z, y, c), index(z ^ by, y, c)) for z, y...  18.3 us
    pallas_call x2, Pallas kernels, run_expert(): pl.pallas_call(functools.partial(expert_kernel, swapped, count, plan), ou...  14 us
    ppermute x7, waiting for transfers between devices, swap_near(): lax.ppermute(x, 'expert', [(index(z, y, c), index(z, 1 - y, c)) for z, y,...  13.5 us
    ppermute x7, starting transfers between devices, swap_near(): lax.ppermute(x, 'expert', [(index(z, y, c), index(z, 1 - y, c)) for z, y,...  7.63 us
    pallas_call x2, Pallas kernels, load_weights(): pl.pallas_call(load_kernel, out_shape=[pltpu.VMEM(x.shape, x.dtype) for x...  7.43 us
    ppermute x8, waiting for transfers between devices, swap_core(): lax.ppermute(x, 'expert', [(index(z, y, c), index(z, y, 1 - c)) for z, y,...  5.15 us
  transfers between devices with their start and end apart: 26, of which 15 were waited for; matrix products, arithmetic and copies ran while one was open for 2% of the time, Pallas kernels for 16%

profile of v7, /device:TPU:0, one launch (start us, length us, event | category | flops | bytes accessed | tf_op | source)
XLA Modules:
  0.0 91.0 jit_solution(17349234383542617353)
XLA Ops:
  0.0 1.2 %messages.1 = (bf16[32,4224]{1,0:T(8,128)(2,1)S(1)}, bf16[16,4224]{1,0:T(8,128)(2,1)S(1)}, bf16[16,4224]{1,0:T(8,128)(2,1)S(1)}) custom-call(bf16[2,16,4096]{2,1,0:T(8,128)(2,1)} %states_ref.1, s32[2,8,16]{2,1,0:T(8,128)} %bitcast.12, f32[2,8,16]{2,1,0:T(8,128)} %bitcast.13), custom_call_target="tpu_custom_call" | custom-call | tf_op jit(solution)/shard_map/messages/pallas_call | solution.py:50
  1.2 3.0 %collective-permute-start.2 = (bf16[32,4224]{1,0:T(8,128)(2,1)S(1)}, bf16[32,4224]{1,0:T(8,128)(2,1)S(1)}, u32[]{:S(2)}, u32[]{:S(2)}) collective-permute-start(bf16[32,4224]{1,0:T(8,128)(2,1)S(1)} %get-tuple-element.47), channel_id=1, source_target_pairs={{0,2},{1,3},{2,0},{3,1},{4,6},{5,7},{6,4},{7,5},{8,10},{9,11},{10,... | collective-permute-start | bytes 811016 | tf_op jit(solution)/shard_map/ppermute | solution.py:174
  4.2 1.6 %collective-permute-start = (bf16[32,4224]{1,0:T(8,128)(2,1)S(1)}, bf16[32,4224]{1,0:T(8,128)(2,1)S(1)}, u32[]{:S(2)}, u32[]{:S(2)}) collective-permute-start(bf16[32,4224]{1,0:T(8,128)(2,1)S(1)} %get-tuple-element.47), channel_id=1, source_target_pairs={{0,4},{1,5},{2,6},{3,7},{4,0},{5,1},{6,2},{7,3},{8,12},{9,13},{10,... | collective-permute-start | bytes 811016 | tf_op jit(solution)/shard_map/ppermute | solution.py:177
  5.8 2.6 %collective-permute-start.1 = (bf16[16,4224]{1,0:T(8,128)(2,1)S(1)}, bf16[16,4224]{1,0:T(8,128)(2,1)S(1)}, u32[]{:S(2)}, u32[]{:S(2)}) collective-permute-start(bf16[16,4224]{1,0:T(8,128)(2,1)S(1)} %get-tuple-element.48), channel_id=1, source_target_pairs={{0,8},{1,9},{2,10},{3,11},{4,12},{5,13},{6,14},{7,15},{8,0},{9,1},... | collective-permute-start | bytes 405512 | tf_op jit(solution)/shard_map/ppermute | solution.py:177
  8.4 4.6 %load_weights.2 = (bf16[4096,768]{1,0:T(8,128)(2,1)S(1)}, bf16[4096,768]{1,0:T(8,128)(2,1)S(1)}) custom-call(bf16[4096,768]{1,0:T(8,128)(2,1)} %bitcast.9, bf16[4096,768]{1,0:T(8,128)(2,1)} %bitcast.10), custom_call_target="tpu_custom_call" | custom-call | tf_op jit(solution)/shard_map/load_weights/pallas_call | solution.py:74
  13.0 1.1 %collective-permute-done.1 = bf16[16,4224]{1,0:T(8,128)(2,1)S(1)} collective-permute-done((bf16[16,4224]{1,0:T(8,128)(2,1)S(1)}, bf16[16,4224]{1,0:T(8,128)(2,1)S(1)}, u32[]{:S(2)}, u32[]{:S(2)}) %collective-permute-start.1) | collective-permute-done | bytes 135200 | tf_op jit(solution)/shard_map/ppermute | solution.py:177
  14.1 0.9 collective-permute-done
  15.1 2.7 %collective-permute-start.5 = (bf16[16,4224]{1,0:T(8,128)(2,1)S(1)}, bf16[16,4224]{1,0:T(8,128)(2,1)S(1)}, u32[]{:S(2)}, u32[]{:S(2)}) collective-permute-start(bf16[16,4224]{1,0:T(8,128)(2,1)S(1)} %collective-permute-done.1), channel_id=1, source_target_pairs={{0,4},{1,5},{2,6},{3,7},{4,0},{5,1},{6,2},{7,3},{8,12},{9,13},{10,... | collective-permute-start | bytes 405512 | tf_op jit(solution)/shard_map/ppermute | solution.py:177
  17.8 1.6 %collective-permute-start.3 = (bf16[16,4224]{1,0:T(8,128)(2,1)S(1)}, bf16[16,4224]{1,0:T(8,128)(2,1)S(1)}, u32[]{:S(2)}, u32[]{:S(2)}) collective-permute-start(bf16[16,4224]{1,0:T(8,128)(2,1)S(1)} %get-tuple-element.55), channel_id=1, source_target_pairs={{0,8},{1,9},{2,10},{3,11},{4,12},{5,13},{6,14},{7,15},{8,0},{9,1},... | collective-permute-start | bytes 405512 | tf_op jit(solution)/shard_map/ppermute | solution.py:177
  19.3 0.5 collective-permute-start.4
  19.9 2.2 %collective-permute-done.5 = bf16[16,4224]{1,0:T(8,128)(2,1)S(1)} collective-permute-done((bf16[16,4224]{1,0:T(8,128)(2,1)S(1)}, bf16[16,4224]{1,0:T(8,128)(2,1)S(1)}, u32[]{:S(2)}, u32[]{:S(2)}) %collective-permute-start.5) | collective-permute-done | bytes 135200 | tf_op jit(solution)/shard_map/ppermute | solution.py:177
  22.1 0.6 collective-permute-start.8
  22.6 2.8 %load_weights.3.down_ref = bf16[768,4096]{1,0:T(8,128)(2,1)S(1)} custom-call(bf16[768,4096]{1,0:T(8,128)(2,1)} %bitcast.11), custom_call_target="tpu_custom_call" | custom-call | tf_op jit(solution)/shard_map/load_weights/pallas_call | solution.py:74
  25.5 0.0 collective-permute-done.3
  25.5 0.4 collective-permute-done.4
  25.8 1.1 %collective-permute-start.11 = (bf16[16,4224]{1,0:T(8,128)(2,1)S(1)}, bf16[16,4224]{1,0:T(8,128)(2,1)S(1)}, u32[]{:S(2)}, u32[]{:S(2)}) collective-permute-start(bf16[16,4224]{1,0:T(8,128)(2,1)S(1)} %collective-permute-done.3), channel_id=1, source_target_pairs={{0,4},{1,5},{2,6},{3,7},{4,0},{5,1},{6,2},{7,3},{8,12},{9,13},{10,... | collective-permute-start | bytes 405512 | tf_op jit(solution)/shard_map/ppermute | solution.py:177
  26.9 0.1 collective-permute-start.7
  27.0 0.6 collective-permute-start.6
  27.6 3.3 %collective-permute-done.11 = bf16[16,4224]{1,0:T(8,128)(2,1)S(1)} collective-permute-done((bf16[16,4224]{1,0:T(8,128)(2,1)S(1)}, bf16[16,4224]{1,0:T(8,128)(2,1)S(1)}, u32[]{:S(2)}, u32[]{:S(2)}) %collective-permute-start.11) | collective-permute-done | bytes 135200 | tf_op jit(solution)/shard_map/ppermute | solution.py:177
  30.9 1.3 %collective-permute-start.12 = (bf16[48,4224]{1,0:T(8,128)(2,1)S(1)}, bf16[48,4224]{1,0:T(8,128)(2,1)S(1)}, u32[]{:S(2)}, u32[]{:S(2)}) collective-permute-start(bf16[48,4224]{1,0:T(8,128)(2,1)S(1)} %pad_maximum_fusion.1), channel_id=1, source_target_pairs={{0,2},{1,3},{2,0},{3,1},{4,6},{5,7},{6,4},{7,5},{8,10},{9,11},{10,... | collective-permute-start | bytes 1216520 | tf_op jit(solution)/shard_map/ppermute | solution.py:174
  32.2 0.0 collective-permute-done.8.refs_4_
  32.2 0.0 collective-permute-start.9
  32.2 1.5 %collective-permute-done.9.refs_5_ = bf16[32,4224]{1,0:T(8,128)(2,1)S(1)} collective-permute-done((bf16[32,4224]{1,0:T(8,128)(2,1)S(1)}, bf16[32,4224]{1,0:T(8,128)(2,1)S(1)}, u32[]{:S(2)}, u32[]{:S(2)}) %collective-permute-start.9) | collective-permute-done | bytes 270368 | tf_op jit(solution)/shard_map/ppermute | solution.py:171
  33.7 0.0 collective-permute-done.6.refs_1_
  33.7 7.0 %expert.2 = (bf16[64,4096]{1,0:T(8,128)(2,1)S(1)}, bf16[64,4096]{1,0:T(8,128)(2,1)S(1)}, bf16[64,4096]{1,0:T(8,128)(2,1)S(1)}, bf16[64,4096]{1,0:T(8,128)(2,1)S(1)}) custom-call(s32[16]{0:T(128)S(1)} %copy-done, bf16[4096,768]{1,0:T(8,128)(2,1)S(1)} %get-tuple-element.51.gate_ref, bf16[4096,768]{1,0:T(8,128)(2,1)S(1)} %get-tuple-element.52.up_ref, ...), custom_call_target="tpu_custom_call" | custom-call | flops 4831838208 | bytes 4194304 | tf_op jit(solution)/shard_map/expert/pallas_call | solution.py:127
  40.8 0.2 collective-permute-start.13
  41.0 0.5 collective-permute-start.15
  41.4 0.1 collective-permute-start.10
  41.6 1.2 %collective-permute-done.13 = bf16[64,4096]{1,0:T(8,128)(2,1)S(1)} collective-permute-done((bf16[64,4096]{1,0:T(8,128)(2,1)S(1)}, bf16[64,4096]{1,0:T(8,128)(2,1)S(1)}, u32[]{:S(2)}, u32[]{:S(2)}) %collective-permute-start.13) | collective-permute-done | bytes 524320 | tf_op jit(solution)/shard_map/ppermute | solution.py:171
  42.7 0.1 convert_element_type.85
  42.9 1.6 %collective-permute-done.10 = bf16[64,4096]{1,0:T(8,128)(2,1)S(1)} collective-permute-done((bf16[64,4096]{1,0:T(8,128)(2,1)S(1)}, bf16[64,4096]{1,0:T(8,128)(2,1)S(1)}, u32[]{:S(2)}, u32[]{:S(2)}) %collective-permute-start.10) | collective-permute-done | bytes 524320 | tf_op jit(solution)/shard_map/ppermute | solution.py:171
  44.5 0.1 convert_element_type.87
  44.6 7.0 %expert.3 = (bf16[64,4096]{1,0:T(8,128)(2,1)S(1)}, bf16[64,4096]{1,0:T(8,128)(2,1)S(1)}, bf16[64,4096]{1,0:T(8,128)(2,1)S(1)}, bf16[64,4096]{1,0:T(8,128)(2,1)S(1)}) custom-call(s32[16]{0:T(128)S(1)} %copy-done, bf16[4096,768]{1,0:T(8,128)(2,1)S(1)} %get-tuple-element.51.gate_ref, bf16[4096,768]{1,0:T(8,128)(2,1)S(1)} %get-tuple-element.52.up_ref, ...), custom_call_target="tpu_custom_call" | custom-call | flops 4831838208 | bytes 4194304 | tf_op jit(solution)/shard_map/expert/pallas_call | solution.py:127
  51.6 0.2 collective-permute-start.16
  51.8 0.9 collective-permute-start.14
  52.7 0.9 collective-permute-done.16
  53.6 0.1 convert_element_type.91
  53.6 0.1 fusion.3
  53.7 0.9 collective-permute-start.22
  54.6 12.1 %collective-permute-done.14 = bf16[64,4096]{1,0:T(8,128)(2,1)S(1)} collective-permute-done((bf16[64,4096]{1,0:T(8,128)(2,1)S(1)}, bf16[64,4096]{1,0:T(8,128)(2,1)S(1)}, u32[]{:S(2)}, u32[]{:S(2)}) %collective-permute-start.14) | collective-permute-done | bytes 524320 | tf_op jit(solution)/shard_map/ppermute | solution.py:174
  66.7 0.1 convert_element_type.93
  66.8 0.1 collective-permute-start.20
  66.9 0.1 slice_add_fusion.3
  67.0 1.4 %collective-permute-start.18 = (bf16[16,4096]{1,0:T(8,128)(2,1)S(1)}, bf16[16,4096]{1,0:T(8,128)(2,1)S(1)}, u32[]{:S(2)}, u32[]{:S(2)}) collective-permute-start(bf16[16,4096]{1,0:T(8,128)(2,1)S(1)} %slice.184), channel_id=1, source_target_pairs={{0,4},{1,5},{2,6},{3,7},{4,0},{5,1},{6,2},{7,3},{8,12},{9,13},{10,... | collective-permute-start | bytes 393224 | tf_op jit(solution)/shard_map/ppermute | solution.py:177
  68.4 0.1 fusion.5
  68.5 0.7 collective-permute-start.17
  69.2 4.1 %collective-permute-done.18 = bf16[16,4096]{1,0:T(8,128)(2,1)S(1)} collective-permute-done((bf16[16,4096]{1,0:T(8,128)(2,1)S(1)}, bf16[16,4096]{1,0:T(8,128)(2,1)S(1)}, u32[]{:S(2)}, u32[]{:S(2)}) %collective-permute-start.18) | collective-permute-done | bytes 131104 | tf_op jit(solution)/shard_map/ppermute | solution.py:177
  73.4 2.4 %collective-permute-start.19 = (bf16[16,4096]{1,0:T(8,128)(2,1)S(1)}, bf16[16,4096]{1,0:T(8,128)(2,1)S(1)}, u32[]{:S(2)}, u32[]{:S(2)}) collective-permute-start(bf16[16,4096]{1,0:T(8,128)(2,1)S(1)} %fusion.7), channel_id=1, source_target_pairs={{0,8},{1,9},{2,10},{3,11},{4,12},{5,13},{6,14},{7,15},{8,0},{9,1},... | collective-permute-start | bytes 393224 | tf_op jit(solution)/shard_map/ppermute | solution.py:177
  75.7 0.1 fusion
  75.8 2.0 %collective-permute-start.23 = (bf16[16,4096]{1,0:T(8,128)(2,1)S(1)}, bf16[16,4096]{1,0:T(8,128)(2,1)S(1)}, u32[]{:S(2)}, u32[]{:S(2)}) collective-permute-start(bf16[16,4096]{1,0:T(8,128)(2,1)S(1)} %slice.183), channel_id=1, source_target_pairs={{0,4},{1,5},{2,6},{3,7},{4,0},{5,1},{6,2},{7,3},{8,12},{9,13},{10,... | collective-permute-start | bytes 393224 | tf_op jit(solution)/shard_map/ppermute | solution.py:177
  77.9 0.0 collective-permute-done.20
  77.9 0.1 convert_element_type.99
  77.9 0.1 fusion.2
  78.0 0.6 collective-permute-start.21
  78.6 3.6 %collective-permute-done.23 = bf16[16,4096]{1,0:T(8,128)(2,1)S(1)} collective-permute-done((bf16[16,4096]{1,0:T(8,128)(2,1)S(1)}, bf16[16,4096]{1,0:T(8,128)(2,1)S(1)}, u32[]{:S(2)}, u32[]{:S(2)}) %collective-permute-start.23) | collective-permute-done | bytes 131104 | tf_op jit(solution)/shard_map/ppermute | solution.py:177
  82.2 1.8 %collective-permute-start.24 = (bf16[16,4096]{1,0:T(8,128)(2,1)S(1)}, bf16[16,4096]{1,0:T(8,128)(2,1)S(1)}, u32[]{:S(2)}, u32[]{:S(2)}) collective-permute-start(bf16[16,4096]{1,0:T(8,128)(2,1)S(1)} %slice_add_fusion.9), channel_id=1, source_target_pairs={{0,8},{1,9},{2,10},{3,11},{4,12},{5,13},{6,14},{7,15},{8,0},{9,1},... | collective-permute-start | bytes 393224 | tf_op jit(solution)/shard_map/ppermute | solution.py:177
  84.0 1.0 %collective-permute-done.21 = bf16[32,4096]{1,0:T(8,128)(2,1)S(1)} collective-permute-done((bf16[32,4096]{1,0:T(8,128)(2,1)S(1)}, bf16[32,4096]{1,0:T(8,128)(2,1)S(1)}, u32[]{:S(2)}, u32[]{:S(2)}) %collective-permute-start.21) | collective-permute-done | bytes 262176 | tf_op jit(solution)/shard_map/ppermute | solution.py:174
  85.0 0.1 fusion.1
  85.2 0.6 collective-permute-start.25
  85.7 3.2 %collective-permute-done.24.second_ref = bf16[16,4096]{1,0:T(8,128)(2,1)S(1)} collective-permute-done((bf16[16,4096]{1,0:T(8,128)(2,1)S(1)}, bf16[16,4096]{1,0:T(8,128)(2,1)S(1)}, u32[]{:S(2)}, u32[]{:S(2)}) %collective-permute-start.24) | collective-permute-done | bytes 131104 | tf_op jit(solution)/shard_map/ppermute | solution.py:177
  89.0 0.0 collective-permute-done.19
  89.0 0.1 fusion.11
  89.1 1.2 %collective-permute-done.25 = bf16[16,4096]{1,0:T(8,128)(2,1)S(1)} collective-permute-done((bf16[16,4096]{1,0:T(8,128)(2,1)S(1)}, bf16[16,4096]{1,0:T(8,128)(2,1)S(1)}, u32[]{:S(2)}, u32[]{:S(2)}) %collective-permute-start.25) | collective-permute-done | bytes 131104 | tf_op jit(solution)/shard_map/ppermute | solution.py:177
  90.3 0.7 pad_maximum_fusion.2
  (32 shorter events, 0.6 us)
Async XLA Ops:
  1.2 12.9 %collective-permute-start.2 = (bf16[32,4224]{1,0:T(8,128)(2,1)S(1)}, bf16[32,4224]{1,0:T(8,128)(2,1)S(1)}, u32[]{:S(2)}, u32[]{:S(2)}) collective-permute-start(bf16[32,4224]{1,0:T(8,128)(2,1)S(1)} %get-tuple-element.47), channel_id=1, source_target_pairs={{0,2},{1,3},{2,0},{3,1},{4,6},{5,7},{6,4},{7,5},{8,10},{9,11},{10,... | collective-permute-start | bytes 811016 | tf_op jit(solution)/shard_map/ppermute | solution.py:174
  4.2 10.8 %collective-permute-start = (bf16[32,4224]{1,0:T(8,128)(2,1)S(1)}, bf16[32,4224]{1,0:T(8,128)(2,1)S(1)}, u32[]{:S(2)}, u32[]{:S(2)}) collective-permute-start(bf16[32,4224]{1,0:T(8,128)(2,1)S(1)} %get-tuple-element.47), channel_id=1, source_target_pairs={{0,4},{1,5},{2,6},{3,7},{4,0},{5,1},{6,2},{7,3},{8,12},{9,13},{10,... | collective-permute-start | bytes 811016 | tf_op jit(solution)/shard_map/ppermute | solution.py:177
  5.8 8.4 %collective-permute-start.1 = (bf16[16,4224]{1,0:T(8,128)(2,1)S(1)}, bf16[16,4224]{1,0:T(8,128)(2,1)S(1)}, u32[]{:S(2)}, u32[]{:S(2)}) collective-permute-start(bf16[16,4224]{1,0:T(8,128)(2,1)S(1)} %get-tuple-element.48), channel_id=1, source_target_pairs={{0,8},{1,9},{2,10},{3,11},{4,12},{5,13},{6,14},{7,15},{8,0},{9,1},... | collective-permute-start | bytes 405512 | tf_op jit(solution)/shard_map/ppermute | solution.py:177
  15.1 7.0 %collective-permute-start.5 = (bf16[16,4224]{1,0:T(8,128)(2,1)S(1)}, bf16[16,4224]{1,0:T(8,128)(2,1)S(1)}, u32[]{:S(2)}, u32[]{:S(2)}) collective-permute-start(bf16[16,4224]{1,0:T(8,128)(2,1)S(1)} %collective-permute-done.1), channel_id=1, source_target_pairs={{0,4},{1,5},{2,6},{3,7},{4,0},{5,1},{6,2},{7,3},{8,12},{9,13},{10,... | collective-permute-start | bytes 405512 | tf_op jit(solution)/shard_map/ppermute | solution.py:177
  17.8 7.7 %collective-permute-start.3 = (bf16[16,4224]{1,0:T(8,128)(2,1)S(1)}, bf16[16,4224]{1,0:T(8,128)(2,1)S(1)}, u32[]{:S(2)}, u32[]{:S(2)}) collective-permute-start(bf16[16,4224]{1,0:T(8,128)(2,1)S(1)} %get-tuple-element.55), channel_id=1, source_target_pairs={{0,8},{1,9},{2,10},{3,11},{4,12},{5,13},{6,14},{7,15},{8,0},{9,1},... | collective-permute-start | bytes 405512 | tf_op jit(solution)/shard_map/ppermute | solution.py:177
  19.3 6.5 %collective-permute-start.4 = (bf16[16,4224]{1,0:T(8,128)(2,1)S(1)}, bf16[16,4224]{1,0:T(8,128)(2,1)S(1)}, u32[]{:S(2)}, u32[]{:S(2)}) collective-permute-start(bf16[16,4224]{1,0:T(8,128)(2,1)S(1)} %get-tuple-element.90), channel_id=1, source_target_pairs={{0,2},{1,3},{2,0},{3,1},{4,6},{5,7},{6,4},{7,5},{8,10},{9,11},{10,... | collective-permute-start | bytes 405512 | tf_op jit(solution)/shard_map/ppermute | solution.py:174
  22.1 10.1 %collective-permute-start.8 = (bf16[32,4224]{1,0:T(8,128)(2,1)S(1)}, bf16[32,4224]{1,0:T(8,128)(2,1)S(1)}, u32[]{:S(2)}, u32[]{:S(2)}) collective-permute-start(bf16[32,4224]{1,0:T(8,128)(2,1)S(1)} %constant_dynamic-update-slice_fusion.refs_2_), channel_id=1, source_target_pairs={{0,2},{1,3},{2,0},{3,1},{4,6},{5,7},{6,4},{7,5},{8,10},{9,11},{10,... | collective-permute-start | bytes 811016 | tf_op jit(solution)/shard_map/ppermute | solution.py:174
  22.6 11.1 %copy-start = (s32[16]{0:T(128)S(1)}, s32[16]{0:T(128)}, u32[]{:S(2)}) copy-start(s32[16]{0:T(128)} %flags_ref.3) | copy-start | bytes 196
  25.8 5.0 %collective-permute-start.11 = (bf16[16,4224]{1,0:T(8,128)(2,1)S(1)}, bf16[16,4224]{1,0:T(8,128)(2,1)S(1)}, u32[]{:S(2)}, u32[]{:S(2)}) collective-permute-start(bf16[16,4224]{1,0:T(8,128)(2,1)S(1)} %collective-permute-done.3), channel_id=1, source_target_pairs={{0,4},{1,5},{2,6},{3,7},{4,0},{5,1},{6,2},{7,3},{8,12},{9,13},{10,... | collective-permute-start | bytes 405512 | tf_op jit(solution)/shard_map/ppermute | solution.py:177
  26.9 5.3 %collective-permute-start.7 = (bf16[32,4224]{1,0:T(8,128)(2,1)S(1)}, bf16[32,4224]{1,0:T(8,128)(2,1)S(1)}, u32[]{:S(2)}, u32[]{:S(2)}) collective-permute-start(bf16[32,4224]{1,0:T(8,128)(2,1)S(1)} %constant_dynamic-update-slice_fusion.refs_2_), channel_id=1, source_target_pairs={{0,1},{1,0},{2,3},{3,2},{4,5},{5,4},{6,7},{7,6},{8,9},{9,8},{10,11... | collective-permute-start | bytes 811016 | tf_op jit(solution)/shard_map/ppermute | solution.py:171
  27.0 6.7 %collective-permute-start.6 = (bf16[112,4224]{1,0:T(8,128)(2,1)S(1)}, bf16[112,4224]{1,0:T(8,128)(2,1)S(1)}, u32[]{:S(2)}, u32[]{:S(2)}) collective-permute-start(bf16[112,4224]{1,0:T(8,128)(2,1)S(1)} %constant_dynamic-update-slice_fusion.2.refs_0_), channel_id=1, source_target_pairs={{0,1},{1,0},{2,3},{3,2},{4,5},{5,4},{6,7},{7,6},{8,9},{9,8},{10,11... | collective-permute-start | bytes 2838536 | tf_op jit(solution)/shard_map/ppermute | solution.py:171
  30.9 9.9 %collective-permute-start.12 = (bf16[48,4224]{1,0:T(8,128)(2,1)S(1)}, bf16[48,4224]{1,0:T(8,128)(2,1)S(1)}, u32[]{:S(2)}, u32[]{:S(2)}) collective-permute-start(bf16[48,4224]{1,0:T(8,128)(2,1)S(1)} %pad_maximum_fusion.1), channel_id=1, source_target_pairs={{0,2},{1,3},{2,0},{3,1},{4,6},{5,7},{6,4},{7,5},{8,10},{9,11},{10,... | collective-permute-start | bytes 1216520 | tf_op jit(solution)/shard_map/ppermute | solution.py:174
  32.2 1.5 %collective-permute-start.9 = (bf16[32,4224]{1,0:T(8,128)(2,1)S(1)}, bf16[32,4224]{1,0:T(8,128)(2,1)S(1)}, u32[]{:S(2)}, u32[]{:S(2)}) collective-permute-start(bf16[32,4224]{1,0:T(8,128)(2,1)S(1)} %collective-permute-done.8.refs_4_), channel_id=1, source_target_pairs={{0,1},{1,0},{2,3},{3,2},{4,5},{5,4},{6,7},{7,6},{8,9},{9,8},{10,11... | collective-permute-start | bytes 811016 | tf_op jit(solution)/shard_map/ppermute | solution.py:171
  40.8 2.0 %collective-permute-start.13 = (bf16[64,4096]{1,0:T(8,128)(2,1)S(1)}, bf16[64,4096]{1,0:T(8,128)(2,1)S(1)}, u32[]{:S(2)}, u32[]{:S(2)}) collective-permute-start(bf16[64,4096]{1,0:T(8,128)(2,1)S(1)} %get-tuple-element.73), channel_id=1, source_target_pairs={{0,1},{1,0},{2,3},{3,2},{4,5},{5,4},{6,7},{7,6},{8,9},{9,8},{10,11... | collective-permute-start | bytes 1572872 | tf_op jit(solution)/shard_map/ppermute | solution.py:171
  41.0 3.6 %collective-permute-start.15 = (bf16[80,4224]{1,0:T(8,128)(2,1)S(1)}, bf16[80,4224]{1,0:T(8,128)(2,1)S(1)}, u32[]{:S(2)}, u32[]{:S(2)}) collective-permute-start(bf16[80,4224]{1,0:T(8,128)(2,1)S(1)} %constant_dynamic-update-slice_fusion.6.refs_2_), channel_id=1, source_target_pairs={{0,1},{1,0},{2,3},{3,2},{4,5},{5,4},{6,7},{7,6},{8,9},{9,8},{10,11... | collective-permute-start | bytes 2027528 | tf_op jit(solution)/shard_map/ppermute | solution.py:171
  41.4 3.0 %collective-permute-start.10 = (bf16[64,4096]{1,0:T(8,128)(2,1)S(1)}, bf16[64,4096]{1,0:T(8,128)(2,1)S(1)}, u32[]{:S(2)}, u32[]{:S(2)}) collective-permute-start(bf16[64,4096]{1,0:T(8,128)(2,1)S(1)} %get-tuple-element.70), channel_id=1, source_target_pairs={{0,1},{1,0},{2,3},{3,2},{4,5},{5,4},{6,7},{7,6},{8,9},{9,8},{10,11... | collective-permute-start | bytes 1572872 | tf_op jit(solution)/shard_map/ppermute | solution.py:171
  51.6 2.0 %collective-permute-start.16 = (bf16[64,4096]{1,0:T(8,128)(2,1)S(1)}, bf16[64,4096]{1,0:T(8,128)(2,1)S(1)}, u32[]{:S(2)}, u32[]{:S(2)}) collective-permute-start(bf16[64,4096]{1,0:T(8,128)(2,1)S(1)} %get-tuple-element.80), channel_id=1, source_target_pairs={{0,1},{1,0},{2,3},{3,2},{4,5},{5,4},{6,7},{7,6},{8,9},{9,8},{10,11... | collective-permute-start | bytes 1572872 | tf_op jit(solution)/shard_map/ppermute | solution.py:171
  51.8 14.8 %collective-permute-start.14 = (bf16[64,4096]{1,0:T(8,128)(2,1)S(1)}, bf16[64,4096]{1,0:T(8,128)(2,1)S(1)}, u32[]{:S(2)}, u32[]{:S(2)}) collective-permute-start(bf16[64,4096]{1,0:T(8,128)(2,1)S(1)} %pad_maximum_fusion), channel_id=1, source_target_pairs={{0,2},{1,3},{2,0},{3,1},{4,6},{5,7},{6,4},{7,5},{8,10},{9,11},{10,... | collective-permute-start | bytes 1572872 | tf_op jit(solution)/shard_map/ppermute | solution.py:174
  53.7 22.0 %collective-permute-start.22 = (bf16[32,4096]{1,0:T(8,128)(2,1)S(1)}, bf16[32,4096]{1,0:T(8,128)(2,1)S(1)}, u32[]{:S(2)}, u32[]{:S(2)}) collective-permute-start(bf16[32,4096]{1,0:T(8,128)(2,1)S(1)} %fusion.3), channel_id=1, source_target_pairs={{0,2},{1,3},{2,0},{3,1},{4,6},{5,7},{6,4},{7,5},{8,10},{9,11},{10,... | collective-permute-start | bytes 786440 | tf_op jit(solution)/shard_map/ppermute | solution.py:174
  66.8 11.1 %collective-permute-start.20 = (bf16[64,4096]{1,0:T(8,128)(2,1)S(1)}, bf16[64,4096]{1,0:T(8,128)(2,1)S(1)}, u32[]{:S(2)}, u32[]{:S(2)}) collective-permute-start(bf16[64,4096]{1,0:T(8,128)(2,1)S(1)} %get-tuple-element.84), channel_id=1, source_target_pairs={{0,1},{1,0},{2,3},{3,2},{4,5},{5,4},{6,7},{7,6},{8,9},{9,8},{10,11... | collective-permute-start | bytes 1572872 | tf_op jit(solution)/shard_map/ppermute | solution.py:171
  67.0 6.4 %collective-permute-start.18 = (bf16[16,4096]{1,0:T(8,128)(2,1)S(1)}, bf16[16,4096]{1,0:T(8,128)(2,1)S(1)}, u32[]{:S(2)}, u32[]{:S(2)}) collective-permute-start(bf16[16,4096]{1,0:T(8,128)(2,1)S(1)} %slice.184), channel_id=1, source_target_pairs={{0,4},{1,5},{2,6},{3,7},{4,0},{5,1},{6,2},{7,3},{8,12},{9,13},{10,... | collective-permute-start | bytes 393224 | tf_op jit(solution)/shard_map/ppermute | solution.py:177
  68.5 20.5 %collective-permute-start.17 = (bf16[16,4096]{1,0:T(8,128)(2,1)S(1)}, bf16[16,4096]{1,0:T(8,128)(2,1)S(1)}, u32[]{:S(2)}, u32[]{:S(2)}) collective-permute-start(bf16[16,4096]{1,0:T(8,128)(2,1)S(1)} %slice.185), channel_id=1, source_target_pairs={{0,4},{1,5},{2,6},{3,7},{4,0},{5,1},{6,2},{7,3},{8,12},{9,13},{10,... | collective-permute-start | bytes 393224 | tf_op jit(solution)/shard_map/ppermute | solution.py:177
  73.4 15.6 %collective-permute-start.19 = (bf16[16,4096]{1,0:T(8,128)(2,1)S(1)}, bf16[16,4096]{1,0:T(8,128)(2,1)S(1)}, u32[]{:S(2)}, u32[]{:S(2)}) collective-permute-start(bf16[16,4096]{1,0:T(8,128)(2,1)S(1)} %fusion.7), channel_id=1, source_target_pairs={{0,8},{1,9},{2,10},{3,11},{4,12},{5,13},{6,14},{7,15},{8,0},{9,1},... | collective-permute-start | bytes 393224 | tf_op jit(solution)/shard_map/ppermute | solution.py:177
  75.8 6.4 %collective-permute-start.23 = (bf16[16,4096]{1,0:T(8,128)(2,1)S(1)}, bf16[16,4096]{1,0:T(8,128)(2,1)S(1)}, u32[]{:S(2)}, u32[]{:S(2)}) collective-permute-start(bf16[16,4096]{1,0:T(8,128)(2,1)S(1)} %slice.183), channel_id=1, source_target_pairs={{0,4},{1,5},{2,6},{3,7},{4,0},{5,1},{6,2},{7,3},{8,12},{9,13},{10,... | collective-permute-start | bytes 393224 | tf_op jit(solution)/shard_map/ppermute | solution.py:177
  78.0 7.0 %collective-permute-start.21 = (bf16[32,4096]{1,0:T(8,128)(2,1)S(1)}, bf16[32,4096]{1,0:T(8,128)(2,1)S(1)}, u32[]{:S(2)}, u32[]{:S(2)}) collective-permute-start(bf16[32,4096]{1,0:T(8,128)(2,1)S(1)} %fusion.2), channel_id=1, source_target_pairs={{0,2},{1,3},{2,0},{3,1},{4,6},{5,7},{6,4},{7,5},{8,10},{9,11},{10,... | collective-permute-start | bytes 786440 | tf_op jit(solution)/shard_map/ppermute | solution.py:174
  82.2 6.7 %collective-permute-start.24 = (bf16[16,4096]{1,0:T(8,128)(2,1)S(1)}, bf16[16,4096]{1,0:T(8,128)(2,1)S(1)}, u32[]{:S(2)}, u32[]{:S(2)}) collective-permute-start(bf16[16,4096]{1,0:T(8,128)(2,1)S(1)} %slice_add_fusion.9), channel_id=1, source_target_pairs={{0,8},{1,9},{2,10},{3,11},{4,12},{5,13},{6,14},{7,15},{8,0},{9,1},... | collective-permute-start | bytes 393224 | tf_op jit(solution)/shard_map/ppermute | solution.py:177
  85.2 5.1 %collective-permute-start.25 = (bf16[16,4096]{1,0:T(8,128)(2,1)S(1)}, bf16[16,4096]{1,0:T(8,128)(2,1)S(1)}, u32[]{:S(2)}, u32[]{:S(2)}) collective-permute-start(bf16[16,4096]{1,0:T(8,128)(2,1)S(1)} %slice.182), channel_id=1, source_target_pairs={{0,4},{1,5},{2,6},{3,7},{4,0},{5,1},{6,2},{7,3},{8,12},{9,13},{10,... | collective-permute-start | bytes 393224 | tf_op jit(solution)/shard_map/ppermute | solution.py:177

commit v8 on v7

--- a/solution.py
+++ b/solution.py
@@ -34,9 +34,8 @@
         terms = jnp.where(place < half, high, dense - high).astype(jnp.bfloat16)
         upright = lax.dot_general(one, terms, (((1,), (1,)), ((), ())), preferred_element_type=jnp.float32)
         upright = upright.astype(jnp.bfloat16)
-        for message_ref, at in ((message_refs[0], step * tokens), (message_refs[step + 1], 0)):
-            message_ref[at : at + tokens, :width] = states_ref[step]
-            message_ref[at : at + tokens, width:] = upright
+        message_refs[step][:, :width] = states_ref[step]
+        message_refs[step][:, width:] = upright
 
 
 def make_messages(states, ids, probs, tail):
@@ -46,7 +45,7 @@
     def whole(shape):
         return pl.BlockSpec(shape, lambda i: (0,) * len(shape))
 
-    shapes = [(steps * tokens, width + tail)] + [(tokens, width + tail)] * steps
+    shapes = [(tokens, width + tail)] * steps
     return pl.pallas_call(
         message_kernel,
         grid=(1,),
@@ -183,10 +182,16 @@
     strides = [middle >> shift for shift in range(1, middle.bit_length())]
     head, half = middle * tokens, lines * tokens
 
-    def grow(block):
+    def grow(block, strides):
         for by in strides:
             block = jnp.concatenate([block, swap_far(block, by)])
         return block
+
+    def places(strides):
+        found = [0]
+        for by in strides:
+            found += [place ^ by for place in found]
+        return found
 
     def collapse(block):
         for by in strides[::-1]:
@@ -197,61 +202,49 @@
     def after(x, *events):
         return lax.optimization_barrier((x, events))[0]
 
-    def of_step(x, step):
-        return jnp.concatenate([x[at : at + tokens] for at in range(step * tokens, x.shape[0], steps * tokens)])
-
     w_gate, w_up, w_down = w_gate[0], w_up[0], w_down[0]
-    message, *own_messages = make_messages(states, ids, probs, tail)
-    near_message = swap_near(message)
-    close = message
-    received = []
-    for by in strides:
-        received.append(swap_far(close, by))
-        close = jnp.concatenate([close, received[-1]])
-    cross = swap_far(own_messages[0], middle)
+    messages = make_messages(states, ids, probs, tail)
+    far = swap_far(messages[0], middle)
+    close = [messages[0], *[swap_far(messages[0], by) for by in places(strides)[1:]]]
+    near_close = [swap_near(messages[0])]
     loaded = load_weights(w_gate, w_up)
-    received, cross, near_message, loaded = lax.optimization_barrier((received, cross, near_message, loaded))
-    close = jnp.concatenate([message, *received])
-    far, near_far = [], []
+    far, close, near_close, loaded = lax.optimization_barrier((far, close, near_close, loaded))
+    others = close[1:]
+    near_close += [swap_near(block) for block in others]
+    crossed = [swap_far(after(message, far), middle) for message in messages[1:]]
+    far = grow(far, strides)
+    near_far = swap_near(far)
+    last = load_weights(after(w_down, far))
+    near_own = [swap_near(after(message, others)) for message in messages[1:]]
+    crossed, near_close, near_own, last = lax.optimization_barrier((crossed, near_close, near_own, last))
+    loaded += last
+    line = jnp.concatenate([*close, far, *near_close])
+    sources = [[line, swap_core(line), near_far, swap_core(near_far)]]
+    wanted = places(strides)
+    wanted += [middle ^ place for place in wanted]
+    found = places([middle] + strides)
+    for message, block, near in zip(messages[1:], crossed, near_own):
+        line = grow(jnp.concatenate([message, block]), strides)
+        near_line = swap_near(line[tokens:])
+        line = jnp.concatenate([line, near])
+        sources.append([line, swap_core(line), near_line, swap_core(near_line)])
+    outputs, ready = [], [source[0] for source in sources]
     for step in range(steps):
-        if step:
-            far.append(grow(crossed))
-            near_far.append(swap_near(jnp.concatenate([far[step], of_step(close, step)[tokens:]])))
-            if step + 1 < steps:
-                crossed = swap_far(after(own_messages[step + 1], crossed), middle)
-        else:
-            near = swap_near(of_step(close, step)[tokens:])
-            if steps > 1:
-                crossed = swap_far(after(own_messages[1], cross), middle)
-            far.append(grow(cross))
-            near_far.append(swap_near(far[0]))
-            last = load_weights(after(w_down, far[0]))
-            crossed, near_close, last = lax.optimization_barrier((crossed, near, last))
-            loaded += last
-    shared = jnp.concatenate([close, near_message, near_close])
-    shared = [shared, swap_core(shared)]
-    outputs, ready = [], far
-    for step in range(steps):
-        if step:
-            rest = jnp.concatenate([far[step], near_far[step]])
-            parts = [*shared, rest, swap_core(rest)]
-        else:
-            parts = [*shared, far[0], swap_core(after(far[0], crossed)), near_far[0], swap_core(near_far[0])]
         plan = []
         for core in range(2):
-            for by in range(middle):
-                at = (by * steps + step) * tokens
-                plan.append((core, at, at + tokens))
-            plan.append((2 + core, 0, head))
-            at = (middle * steps + step) * tokens
-            plan.append((core, at, at + tokens))
-            at = 2 * head if step else (middle + 1) * steps * tokens
-            plan.append((2 * (step > 0) + core, at, at + head - tokens))
-            at = head if step else 0
-            plan.append(((2 if step else 4) + core, at, at + head))
+            if step:
+                at = [found.index(place) * tokens for place in wanted]
+                plan += [(core, low, low + tokens) for low in at] + [(core, half, half + tokens)]
+                plan += [(2 + core, low - tokens, low) for low in at[1:]]
+            else:
+                plan += [(core, 0, half + head), (2 + core, 0, head)]
+        parts = sources[step]
         own, peer, other_low, other_high = run_expert(step > 0, flags, loaded, after(parts, ready), tuple(plan))
-        other_high = swap_core(other_high if step else after(other_high, near_far[1])).astype(jnp.float32)
-        other_low = swap_core(after(other_low, near) if step else other_low)
+        other_high = swap_core(other_high if step else after(other_high, sources[1][2]))
+        if step:
+            other_high = after(other_high, near)
+        other_high = other_high.astype(jnp.float32)
+        other_low = swap_core(after(other_low, near if step else sources[1][2]))
         to_high = (peer[head:].astype(jnp.float32) + other_high[head:]).astype(jnp.bfloat16)
         other_low = after(other_low, to_high).astype(jnp.float32)
         to_low = (peer[:head].astype(jnp.float32) + other_low[head:]).astype(jnp.bfloat16)

time: 91.2 us -> 84.1 us (0.922)
  waiting for transfers between devices: 38.3 us -> 31.1 us
    ppermute x7 -> x8, waiting for transfers between devices: 13.5 us -> 6.78 us  [swap_near(): lax.ppermute(x, 'expert', [(index(z, y, c), index(z, 1 - y, c)) for z, y,...]
    ppermute x7 -> x8, starting transfers between devices: 7.63 us -> 9.86 us  [swap_near(): lax.ppermute(x, 'expert', [(index(z, y, c), index(z, 1 - y, c)) for z, y,...]
    ppermute x11, starting transfers between devices: 18.3 us -> 16.4 us  [swap_far(): lax.ppermute(x, 'expert', [(index(z, y, c), index(z ^ by, y, c)) for z, y...]
  transfers between devices with their start and end apart: 26 -> 27, of which waited for: 15 -> 12; matrix products, arithmetic and copies ran while one was open for 2% -> 2% of each run, Pallas kernels for 16% -> 26%
where the time goes in v8:
time: 84.1 us; the launch traced here: 83.9 us
  waiting for transfers between devices  31.1 us (37%)
  starting transfers between devices  27.6 us (33%)
  Pallas kernels  22.7 us (27%)
  other arithmetic  1.91 us (2%)
    ppermute x11, waiting for transfers between devices, swap_far(): lax.ppermute(x, 'expert', [(index(z, y, c), index(z ^ by, y, c)) for z, y...  19.8 us
    ppermute x11, starting transfers between devices, swap_far(): lax.ppermute(x, 'expert', [(index(z, y, c), index(z ^ by, y, c)) for z, y...  16.4 us
    pallas_call x2, Pallas kernels, run_expert(): pl.pallas_call(functools.partial(expert_kernel, swapped, count, plan), ou...  14 us
    ppermute x8, starting transfers between devices, swap_near(): lax.ppermute(x, 'expert', [(index(z, y, c), index(z, 1 - y, c)) for z, y,...  9.86 us
    pallas_call x2, Pallas kernels, load_weights(): pl.pallas_call(load_kernel, out_shape=[pltpu.VMEM(x.shape, x.dtype) for x...  7.43 us
    ppermute x8, waiting for transfers between devices, swap_near(): lax.ppermute(x, 'expert', [(index(z, y, c), index(z, 1 - y, c)) for z, y,...  6.78 us
    ppermute x8, waiting for transfers between devices, swap_core(): lax.ppermute(x, 'expert', [(index(z, y, c), index(z, y, 1 - c)) for z, y,...  4.55 us
  transfers between devices with their start and end apart: 27, of which 12 were waited for; matrix products, arithmetic and copies ran while one was open for 2% of the time, Pallas kernels for 26%

profile of v8, /device:TPU:0, one launch (start us, length us, event | category | flops | bytes accessed | tf_op | source)
XLA Modules:
  0.0 83.9 jit_solution(12715478644316070163)
XLA Ops:
  0.0 1.2 %messages.1 = (bf16[16,4224]{1,0:T(8,128)(2,1)S(1)}, bf16[16,4224]{1,0:T(8,128)(2,1)S(1)}) custom-call(bf16[2,16,4096]{2,1,0:T(8,128)(2,1)} %states_ref.1, s32[2,8,16]{2,1,0:T(8,128)} %bitcast.12, f32[2,8,16]{2,1,0:T(8,128)} %bitcast.13), custom_call_target="tpu_custom_call" | custom-call | tf_op jit(solution)/shard_map/messages/pallas_call | solution.py:49
  1.2 3.0 %collective-permute-start.2 = (bf16[16,4224]{1,0:T(8,128)(2,1)S(1)}, bf16[16,4224]{1,0:T(8,128)(2,1)S(1)}, u32[]{:S(2)}, u32[]{:S(2)}) collective-permute-start(bf16[16,4224]{1,0:T(8,128)(2,1)S(1)} %get-tuple-element.62), channel_id=1, source_target_pairs={{0,2},{1,3},{2,0},{3,1},{4,6},{5,7},{6,4},{7,5},{8,10},{9,11},{10,... | collective-permute-start | bytes 405512 | tf_op jit(solution)/shard_map/ppermute | solution.py:173
  4.2 1.6 %collective-permute-start.1 = (bf16[16,4224]{1,0:T(8,128)(2,1)S(1)}, bf16[16,4224]{1,0:T(8,128)(2,1)S(1)}, u32[]{:S(2)}, u32[]{:S(2)}) collective-permute-start(bf16[16,4224]{1,0:T(8,128)(2,1)S(1)} %get-tuple-element.62), channel_id=1, source_target_pairs={{0,4},{1,5},{2,6},{3,7},{4,0},{5,1},{6,2},{7,3},{8,12},{9,13},{10,... | collective-permute-start | bytes 405512 | tf_op jit(solution)/shard_map/ppermute | solution.py:176
  5.8 2.6 %collective-permute-start = (bf16[16,4224]{1,0:T(8,128)(2,1)S(1)}, bf16[16,4224]{1,0:T(8,128)(2,1)S(1)}, u32[]{:S(2)}, u32[]{:S(2)}) collective-permute-start(bf16[16,4224]{1,0:T(8,128)(2,1)S(1)} %get-tuple-element.62), channel_id=1, source_target_pairs={{0,8},{1,9},{2,10},{3,11},{4,12},{5,13},{6,14},{7,15},{8,0},{9,1},... | collective-permute-start | bytes 405512 | tf_op jit(solution)/shard_map/ppermute | solution.py:176
  8.4 4.6 %load_weights.2 = (bf16[4096,768]{1,0:T(8,128)(2,1)S(1)}, bf16[4096,768]{1,0:T(8,128)(2,1)S(1)}) custom-call(bf16[4096,768]{1,0:T(8,128)(2,1)} %bitcast.9, bf16[4096,768]{1,0:T(8,128)(2,1)} %bitcast.10), custom_call_target="tpu_custom_call" | custom-call | tf_op jit(solution)/shard_map/load_weights/pallas_call | solution.py:73
  13.0 1.3 %collective-permute-done = bf16[16,4224]{1,0:T(8,128)(2,1)S(1)} collective-permute-done((bf16[16,4224]{1,0:T(8,128)(2,1)S(1)}, bf16[16,4224]{1,0:T(8,128)(2,1)S(1)}, u32[]{:S(2)}, u32[]{:S(2)}) %collective-permute-start) | collective-permute-done | bytes 135200 | tf_op jit(solution)/shard_map/ppermute | solution.py:176
  14.4 0.3 collective-permute-start.6
  14.7 0.5 collective-permute-start.4
  15.2 1.5 %collective-permute-start.5 = (bf16[16,4224]{1,0:T(8,128)(2,1)S(1)}, bf16[16,4224]{1,0:T(8,128)(2,1)S(1)}, u32[]{:S(2)}, u32[]{:S(2)}) collective-permute-start(bf16[16,4224]{1,0:T(8,128)(2,1)S(1)} %get-tuple-element.59), channel_id=1, source_target_pairs={{0,2},{1,3},{2,0},{3,1},{4,6},{5,7},{6,4},{7,5},{8,10},{9,11},{10,... | collective-permute-start | bytes 405512 | tf_op jit(solution)/shard_map/ppermute | solution.py:173
  16.8 2.8 %collective-permute-start.3 = (bf16[16,4224]{1,0:T(8,128)(2,1)S(1)}, bf16[16,4224]{1,0:T(8,128)(2,1)S(1)}, u32[]{:S(2)}, u32[]{:S(2)}) collective-permute-start(bf16[16,4224]{1,0:T(8,128)(2,1)S(1)} %get-tuple-element.59), channel_id=1, source_target_pairs={{0,8},{1,9},{2,10},{3,11},{4,12},{5,13},{6,14},{7,15},{8,0},{9,1},... | collective-permute-start | bytes 405512 | tf_op jit(solution)/shard_map/ppermute | solution.py:176
  19.6 1.0 %collective-permute-done.6 = bf16[16,4224]{1,0:T(8,128)(2,1)S(1)} collective-permute-done((bf16[16,4224]{1,0:T(8,128)(2,1)S(1)}, bf16[16,4224]{1,0:T(8,128)(2,1)S(1)}, u32[]{:S(2)}, u32[]{:S(2)}) %collective-permute-start.6) | collective-permute-done | bytes 135200 | tf_op jit(solution)/shard_map/ppermute | solution.py:176
  20.7 0.6 collective-permute-start.8
  21.3 2.8 %load_weights.3.down_ref = bf16[768,4096]{1,0:T(8,128)(2,1)S(1)} custom-call(bf16[768,4096]{1,0:T(8,128)(2,1)} %bitcast.11), custom_call_target="tpu_custom_call" | custom-call | tf_op jit(solution)/shard_map/load_weights/pallas_call | solution.py:73
  24.1 0.0 collective-permute-done.3
  24.2 1.4 %collective-permute-start.10 = (bf16[32,4224]{1,0:T(8,128)(2,1)S(1)}, bf16[32,4224]{1,0:T(8,128)(2,1)S(1)}, u32[]{:S(2)}, u32[]{:S(2)}) collective-permute-start(bf16[32,4224]{1,0:T(8,128)(2,1)S(1)} %pad_maximum_fusion.2), channel_id=1, source_target_pairs={{0,4},{1,5},{2,6},{3,7},{4,0},{5,1},{6,2},{7,3},{8,12},{9,13},{10,... | collective-permute-start | bytes 811016 | tf_op jit(solution)/shard_map/ppermute | solution.py:176
  25.6 0.1 collective-permute-start.7
  25.7 5.0 %collective-permute-done.10 = bf16[32,4224]{1,0:T(8,128)(2,1)S(1)} collective-permute-done((bf16[32,4224]{1,0:T(8,128)(2,1)S(1)}, bf16[32,4224]{1,0:T(8,128)(2,1)S(1)}, u32[]{:S(2)}, u32[]{:S(2)}) %collective-permute-start.10) | collective-permute-done | bytes 270368 | tf_op jit(solution)/shard_map/ppermute | solution.py:176
  30.7 1.6 %collective-permute-start.11 = (bf16[48,4224]{1,0:T(8,128)(2,1)S(1)}, bf16[48,4224]{1,0:T(8,128)(2,1)S(1)}, u32[]{:S(2)}, u32[]{:S(2)}) collective-permute-start(bf16[48,4224]{1,0:T(8,128)(2,1)S(1)} %pad_maximum_fusion.1), channel_id=1, source_target_pairs={{0,2},{1,3},{2,0},{3,1},{4,6},{5,7},{6,4},{7,5},{8,10},{9,11},{10,... | collective-permute-start | bytes 1216520 | tf_op jit(solution)/shard_map/ppermute | solution.py:173
  32.4 1.5 %collective-permute-done.9.refs_3_ = bf16[32,4224]{1,0:T(8,128)(2,1)S(1)} collective-permute-done((bf16[32,4224]{1,0:T(8,128)(2,1)S(1)}, bf16[32,4224]{1,0:T(8,128)(2,1)S(1)}, u32[]{:S(2)}, u32[]{:S(2)}) %collective-permute-start.9) | collective-permute-done | bytes 270368 | tf_op jit(solution)/shard_map/ppermute | solution.py:170
  33.9 7.0 %expert.2 = (bf16[64,4096]{1,0:T(8,128)(2,1)S(1)}, bf16[64,4096]{1,0:T(8,128)(2,1)S(1)}, bf16[64,4096]{1,0:T(8,128)(2,1)S(1)}, bf16[64,4096]{1,0:T(8,128)(2,1)S(1)}) custom-call(s32[16]{0:T(128)S(1)} %copy-done, bf16[4096,768]{1,0:T(8,128)(2,1)S(1)} %get-tuple-element.52.gate_ref, bf16[4096,768]{1,0:T(8,128)(2,1)S(1)} %get-tuple-element.53.up_ref, ...), custom_call_target="tpu_custom_call" | custom-call | flops 4831838208 | bytes 4194304 | tf_op jit(solution)/shard_map/expert/pallas_call | solution.py:126
  40.9 0.0 collective-permute-done.11.refs_2_
  40.9 0.2 collective-permute-start.13
  41.1 0.4 collective-permute-start.15
  41.5 0.1 collective-permute-start.16
  41.6 0.4 collective-permute-start.12
  42.0 0.9 %collective-permute-done.13 = bf16[64,4096]{1,0:T(8,128)(2,1)S(1)} collective-permute-done((bf16[64,4096]{1,0:T(8,128)(2,1)S(1)}, bf16[64,4096]{1,0:T(8,128)(2,1)S(1)}, u32[]{:S(2)}, u32[]{:S(2)}) %collective-permute-start.13) | collective-permute-done | bytes 524320 | tf_op jit(solution)/shard_map/ppermute | solution.py:170
  42.9 0.1 convert_element_type.85
  42.9 0.1 fusion.6
  43.0 2.2 %collective-permute-done.12 = bf16[64,4096]{1,0:T(8,128)(2,1)S(1)} collective-permute-done((bf16[64,4096]{1,0:T(8,128)(2,1)S(1)}, bf16[64,4096]{1,0:T(8,128)(2,1)S(1)}, u32[]{:S(2)}, u32[]{:S(2)}) %collective-permute-start.12) | collective-permute-done | bytes 524320 | tf_op jit(solution)/shard_map/ppermute | solution.py:170
  45.2 0.1 convert_element_type.87
  45.2 0.1 fusion.4
  45.4 0.0 collective-permute-done.16.refs_3_
  45.4 0.6 collective-permute-start.14
  45.9 7.0 %expert.3 = (bf16[64,4096]{1,0:T(8,128)(2,1)S(1)}, bf16[64,4096]{1,0:T(8,128)(2,1)S(1)}, bf16[64,4096]{1,0:T(8,128)(2,1)S(1)}, bf16[64,4096]{1,0:T(8,128)(2,1)S(1)}) custom-call(s32[16]{0:T(128)S(1)} %copy-done, bf16[4096,768]{1,0:T(8,128)(2,1)S(1)} %get-tuple-element.52.gate_ref, bf16[4096,768]{1,0:T(8,128)(2,1)S(1)} %get-tuple-element.53.up_ref, ...), custom_call_target="tpu_custom_call" | custom-call | flops 4831838208 | bytes 4194304 | tf_op jit(solution)/shard_map/expert/pallas_call | solution.py:126
  53.0 0.1 collective-permute-start.17
  53.0 6.4 %collective-permute-done.14 = bf16[64,4096]{1,0:T(8,128)(2,1)S(1)} collective-permute-done((bf16[64,4096]{1,0:T(8,128)(2,1)S(1)}, bf16[64,4096]{1,0:T(8,128)(2,1)S(1)}, u32[]{:S(2)}, u32[]{:S(2)}) %collective-permute-start.14) | collective-permute-done | bytes 524320 | tf_op jit(solution)/shard_map/ppermute | solution.py:173
  59.4 0.1 convert_element_type.91
  59.5 0.1 fusion.3
  59.5 0.6 collective-permute-start.23
  60.1 0.1 convert_element_type.93
  60.2 0.1 collective-permute-start.21
  60.3 0.1 slice_add_fusion.3
  60.4 1.4 %collective-permute-start.19 = (bf16[16,4096]{1,0:T(8,128)(2,1)S(1)}, bf16[16,4096]{1,0:T(8,128)(2,1)S(1)}, u32[]{:S(2)}, u32[]{:S(2)}) collective-permute-start(bf16[16,4096]{1,0:T(8,128)(2,1)S(1)} %slice.178), channel_id=1, source_target_pairs={{0,4},{1,5},{2,6},{3,7},{4,0},{5,1},{6,2},{7,3},{8,12},{9,13},{10,... | collective-permute-start | bytes 393224 | tf_op jit(solution)/shard_map/ppermute | solution.py:176
  61.8 0.1 fusion.5
  61.9 0.8 collective-permute-start.18
  62.7 4.1 %collective-permute-done.19 = bf16[16,4096]{1,0:T(8,128)(2,1)S(1)} collective-permute-done((bf16[16,4096]{1,0:T(8,128)(2,1)S(1)}, bf16[16,4096]{1,0:T(8,128)(2,1)S(1)}, u32[]{:S(2)}, u32[]{:S(2)}) %collective-permute-start.19) | collective-permute-done | bytes 131104 | tf_op jit(solution)/shard_map/ppermute | solution.py:176
  66.8 2.0 %collective-permute-start.20 = (bf16[16,4096]{1,0:T(8,128)(2,1)S(1)}, bf16[16,4096]{1,0:T(8,128)(2,1)S(1)}, u32[]{:S(2)}, u32[]{:S(2)}) collective-permute-start(bf16[16,4096]{1,0:T(8,128)(2,1)S(1)} %fusion.7), channel_id=1, source_target_pairs={{0,8},{1,9},{2,10},{3,11},{4,12},{5,13},{6,14},{7,15},{8,0},{9,1},... | collective-permute-start | bytes 393224 | tf_op jit(solution)/shard_map/ppermute | solution.py:176
  68.8 0.0 collective-permute-done.23
  68.8 0.1 fusion
  69.0 1.2 %collective-permute-start.24 = (bf16[16,4096]{1,0:T(8,128)(2,1)S(1)}, bf16[16,4096]{1,0:T(8,128)(2,1)S(1)}, u32[]{:S(2)}, u32[]{:S(2)}) collective-permute-start(bf16[16,4096]{1,0:T(8,128)(2,1)S(1)} %slice.177), channel_id=1, source_target_pairs={{0,4},{1,5},{2,6},{3,7},{4,0},{5,1},{6,2},{7,3},{8,12},{9,13},{10,... | collective-permute-start | bytes 393224 | tf_op jit(solution)/shard_map/ppermute | solution.py:176
  70.1 0.0 collective-permute-done.21
  70.2 0.1 convert_element_type.99
  70.3 1.6 %collective-permute-start.22 = (bf16[32,4096]{1,0:T(8,128)(2,1)S(1)}, bf16[32,4096]{1,0:T(8,128)(2,1)S(1)}, u32[]{:S(2)}, u32[]{:S(2)}) collective-permute-start(bf16[32,4096]{1,0:T(8,128)(2,1)S(1)} %fusion.2), channel_id=1, source_target_pairs={{0,2},{1,3},{2,0},{3,1},{4,6},{5,7},{6,4},{7,5},{8,10},{9,11},{10,... | collective-permute-start | bytes 786440 | tf_op jit(solution)/shard_map/ppermute | solution.py:173
  71.9 3.6 %collective-permute-done.24 = bf16[16,4096]{1,0:T(8,128)(2,1)S(1)} collective-permute-done((bf16[16,4096]{1,0:T(8,128)(2,1)S(1)}, bf16[16,4096]{1,0:T(8,128)(2,1)S(1)}, u32[]{:S(2)}, u32[]{:S(2)}) %collective-permute-start.24) | collective-permute-done | bytes 131104 | tf_op jit(solution)/shard_map/ppermute | solution.py:176
  75.5 1.4 %collective-permute-start.25 = (bf16[16,4096]{1,0:T(8,128)(2,1)S(1)}, bf16[16,4096]{1,0:T(8,128)(2,1)S(1)}, u32[]{:S(2)}, u32[]{:S(2)}) collective-permute-start(bf16[16,4096]{1,0:T(8,128)(2,1)S(1)} %slice_add_fusion.9), channel_id=1, source_target_pairs={{0,8},{1,9},{2,10},{3,11},{4,12},{5,13},{6,14},{7,15},{8,0},{9,1},... | collective-permute-start | bytes 393224 | tf_op jit(solution)/shard_map/ppermute | solution.py:176
  76.9 0.4 collective-permute-done.22
  77.3 0.1 fusion.1
  77.5 1.0 %collective-permute-start.26 = (bf16[16,4096]{1,0:T(8,128)(2,1)S(1)}, bf16[16,4096]{1,0:T(8,128)(2,1)S(1)}, u32[]{:S(2)}, u32[]{:S(2)}) collective-permute-start(bf16[16,4096]{1,0:T(8,128)(2,1)S(1)} %slice.176), channel_id=1, source_target_pairs={{0,4},{1,5},{2,6},{3,7},{4,0},{5,1},{6,2},{7,3},{8,12},{9,13},{10,... | collective-permute-start | bytes 393224 | tf_op jit(solution)/shard_map/ppermute | solution.py:176
  78.4 4.6 %collective-permute-done.25.second_ref = bf16[16,4096]{1,0:T(8,128)(2,1)S(1)} collective-permute-done((bf16[16,4096]{1,0:T(8,128)(2,1)S(1)}, bf16[16,4096]{1,0:T(8,128)(2,1)S(1)}, u32[]{:S(2)}, u32[]{:S(2)}) %collective-permute-start.25) | collective-permute-done | bytes 131104 | tf_op jit(solution)/shard_map/ppermute | solution.py:176
  83.0 0.0 collective-permute-done.20
  83.0 0.0 collective-permute-done.18
  83.0 0.1 fusion.11
  83.1 0.1 collective-permute-done.26
  83.2 0.7 pad_maximum_fusion.3
  (35 shorter events, 0.6 us)
Async XLA Ops:
  1.2 11.8 %collective-permute-start.2 = (bf16[16,4224]{1,0:T(8,128)(2,1)S(1)}, bf16[16,4224]{1,0:T(8,128)(2,1)S(1)}, u32[]{:S(2)}, u32[]{:S(2)}) collective-permute-start(bf16[16,4224]{1,0:T(8,128)(2,1)S(1)} %get-tuple-element.62), channel_id=1, source_target_pairs={{0,2},{1,3},{2,0},{3,1},{4,6},{5,7},{6,4},{7,5},{8,10},{9,11},{10,... | collective-permute-start | bytes 405512 | tf_op jit(solution)/shard_map/ppermute | solution.py:173
  4.2 8.8 %collective-permute-start.1 = (bf16[16,4224]{1,0:T(8,128)(2,1)S(1)}, bf16[16,4224]{1,0:T(8,128)(2,1)S(1)}, u32[]{:S(2)}, u32[]{:S(2)}) collective-permute-start(bf16[16,4224]{1,0:T(8,128)(2,1)S(1)} %get-tuple-element.62), channel_id=1, source_target_pairs={{0,4},{1,5},{2,6},{3,7},{4,0},{5,1},{6,2},{7,3},{8,12},{9,13},{10,... | collective-permute-start | bytes 405512 | tf_op jit(solution)/shard_map/ppermute | solution.py:176
  5.8 8.6 %collective-permute-start = (bf16[16,4224]{1,0:T(8,128)(2,1)S(1)}, bf16[16,4224]{1,0:T(8,128)(2,1)S(1)}, u32[]{:S(2)}, u32[]{:S(2)}) collective-permute-start(bf16[16,4224]{1,0:T(8,128)(2,1)S(1)} %get-tuple-element.62), channel_id=1, source_target_pairs={{0,8},{1,9},{2,10},{3,11},{4,12},{5,13},{6,14},{7,15},{8,0},{9,1},... | collective-permute-start | bytes 405512 | tf_op jit(solution)/shard_map/ppermute | solution.py:176
  14.4 6.3 %collective-permute-start.6 = (bf16[16,4224]{1,0:T(8,128)(2,1)S(1)}, bf16[16,4224]{1,0:T(8,128)(2,1)S(1)}, u32[]{:S(2)}, u32[]{:S(2)}) collective-permute-start(bf16[16,4224]{1,0:T(8,128)(2,1)S(1)} %collective-permute-done), channel_id=1, source_target_pairs={{0,4},{1,5},{2,6},{3,7},{4,0},{5,1},{6,2},{7,3},{8,12},{9,13},{10,... | collective-permute-start | bytes 405512 | tf_op jit(solution)/shard_map/ppermute | solution.py:176
  14.7 9.4 %collective-permute-start.4 = (bf16[16,4224]{1,0:T(8,128)(2,1)S(1)}, bf16[16,4224]{1,0:T(8,128)(2,1)S(1)}, u32[]{:S(2)}, u32[]{:S(2)}) collective-permute-start(bf16[16,4224]{1,0:T(8,128)(2,1)S(1)} %collective-permute-done.1), channel_id=1, source_target_pairs={{0,2},{1,3},{2,0},{3,1},{4,6},{5,7},{6,4},{7,5},{8,10},{9,11},{10,... | collective-permute-start | bytes 405512 | tf_op jit(solution)/shard_map/ppermute | solution.py:173
  15.2 8.8 %collective-permute-start.5 = (bf16[16,4224]{1,0:T(8,128)(2,1)S(1)}, bf16[16,4224]{1,0:T(8,128)(2,1)S(1)}, u32[]{:S(2)}, u32[]{:S(2)}) collective-permute-start(bf16[16,4224]{1,0:T(8,128)(2,1)S(1)} %get-tuple-element.59), channel_id=1, source_target_pairs={{0,2},{1,3},{2,0},{3,1},{4,6},{5,7},{6,4},{7,5},{8,10},{9,11},{10,... | collective-permute-start | bytes 405512 | tf_op jit(solution)/shard_map/ppermute | solution.py:173
  16.8 7.3 %collective-permute-start.3 = (bf16[16,4224]{1,0:T(8,128)(2,1)S(1)}, bf16[16,4224]{1,0:T(8,128)(2,1)S(1)}, u32[]{:S(2)}, u32[]{:S(2)}) collective-permute-start(bf16[16,4224]{1,0:T(8,128)(2,1)S(1)} %get-tuple-element.59), channel_id=1, source_target_pairs={{0,8},{1,9},{2,10},{3,11},{4,12},{5,13},{6,14},{7,15},{8,0},{9,1},... | collective-permute-start | bytes 405512 | tf_op jit(solution)/shard_map/ppermute | solution.py:176
  20.7 11.6 %collective-permute-start.8 = (bf16[32,4224]{1,0:T(8,128)(2,1)S(1)}, bf16[32,4224]{1,0:T(8,128)(2,1)S(1)}, u32[]{:S(2)}, u32[]{:S(2)}) collective-permute-start(bf16[32,4224]{1,0:T(8,128)(2,1)S(1)} %get-tuple-element.94), channel_id=1, source_target_pairs={{0,2},{1,3},{2,0},{3,1},{4,6},{5,7},{6,4},{7,5},{8,10},{9,11},{10,... | collective-permute-start | bytes 811016 | tf_op jit(solution)/shard_map/ppermute | solution.py:173
  21.3 12.6 %copy-start = (s32[16]{0:T(128)S(1)}, s32[16]{0:T(128)}, u32[]{:S(2)}) copy-start(s32[16]{0:T(128)} %flags_ref.3) | copy-start | bytes 196
  24.2 6.5 %collective-permute-start.10 = (bf16[32,4224]{1,0:T(8,128)(2,1)S(1)}, bf16[32,4224]{1,0:T(8,128)(2,1)S(1)}, u32[]{:S(2)}, u32[]{:S(2)}) collective-permute-start(bf16[32,4224]{1,0:T(8,128)(2,1)S(1)} %pad_maximum_fusion.2), channel_id=1, source_target_pairs={{0,4},{1,5},{2,6},{3,7},{4,0},{5,1},{6,2},{7,3},{8,12},{9,13},{10,... | collective-permute-start | bytes 811016 | tf_op jit(solution)/shard_map/ppermute | solution.py:176
  25.6 8.3 %collective-permute-start.7 = (bf16[96,4224]{1,0:T(8,128)(2,1)S(1)}, bf16[96,4224]{1,0:T(8,128)(2,1)S(1)}, u32[]{:S(2)}, u32[]{:S(2)}) collective-permute-start(bf16[96,4224]{1,0:T(8,128)(2,1)S(1)} %constant_dynamic-update-slice_fusion.2.refs_0_), channel_id=1, source_target_pairs={{0,1},{1,0},{2,3},{3,2},{4,5},{5,4},{6,7},{7,6},{8,9},{9,8},{10,11... | collective-permute-start | bytes 2433032 | tf_op jit(solution)/shard_map/ppermute | solution.py:170
  30.7 10.2 %collective-permute-start.11 = (bf16[48,4224]{1,0:T(8,128)(2,1)S(1)}, bf16[48,4224]{1,0:T(8,128)(2,1)S(1)}, u32[]{:S(2)}, u32[]{:S(2)}) collective-permute-start(bf16[48,4224]{1,0:T(8,128)(2,1)S(1)} %pad_maximum_fusion.1), channel_id=1, source_target_pairs={{0,2},{1,3},{2,0},{3,1},{4,6},{5,7},{6,4},{7,5},{8,10},{9,11},{10,... | collective-permute-start | bytes 1216520 | tf_op jit(solution)/shard_map/ppermute | solution.py:173
  32.3 1.5 %collective-permute-start.9 = (bf16[32,4224]{1,0:T(8,128)(2,1)S(1)}, bf16[32,4224]{1,0:T(8,128)(2,1)S(1)}, u32[]{:S(2)}, u32[]{:S(2)}) collective-permute-start(bf16[32,4224]{1,0:T(8,128)(2,1)S(1)} %collective-permute-done.8.refs_2_), channel_id=1, source_target_pairs={{0,1},{1,0},{2,3},{3,2},{4,5},{5,4},{6,7},{7,6},{8,9},{9,8},{10,11... | collective-permute-start | bytes 811016 | tf_op jit(solution)/shard_map/ppermute | solution.py:170
  40.9 2.0 %collective-permute-start.13 = (bf16[64,4096]{1,0:T(8,128)(2,1)S(1)}, bf16[64,4096]{1,0:T(8,128)(2,1)S(1)}, u32[]{:S(2)}, u32[]{:S(2)}) collective-permute-start(bf16[64,4096]{1,0:T(8,128)(2,1)S(1)} %get-tuple-element.76), channel_id=1, source_target_pairs={{0,1},{1,0},{2,3},{3,2},{4,5},{5,4},{6,7},{7,6},{8,9},{9,8},{10,11... | collective-permute-start | bytes 1572872 | tf_op jit(solution)/shard_map/ppermute | solution.py:170
  41.1 4.3 %collective-permute-start.15 = (bf16[80,4224]{1,0:T(8,128)(2,1)S(1)}, bf16[80,4224]{1,0:T(8,128)(2,1)S(1)}, u32[]{:S(2)}, u32[]{:S(2)}) collective-permute-start(bf16[80,4224]{1,0:T(8,128)(2,1)S(1)} %constant_dynamic-update-slice_fusion.8.refs_0_), channel_id=1, source_target_pairs={{0,1},{1,0},{2,3},{3,2},{4,5},{5,4},{6,7},{7,6},{8,9},{9,8},{10,11... | collective-permute-start | bytes 2027528 | tf_op jit(solution)/shard_map/ppermute | solution.py:170
  41.5 3.9 %collective-permute-start.16 = (bf16[48,4224]{1,0:T(8,128)(2,1)S(1)}, bf16[48,4224]{1,0:T(8,128)(2,1)S(1)}, u32[]{:S(2)}, u32[]{:S(2)}) collective-permute-start(bf16[48,4224]{1,0:T(8,128)(2,1)S(1)} %collective-permute-done.11.refs_2_), channel_id=1, source_target_pairs={{0,1},{1,0},{2,3},{3,2},{4,5},{5,4},{6,7},{7,6},{8,9},{9,8},{10,11... | collective-permute-start | bytes 1216520 | tf_op jit(solution)/shard_map/ppermute | solution.py:170
  41.6 3.6 %collective-permute-start.12 = (bf16[64,4096]{1,0:T(8,128)(2,1)S(1)}, bf16[64,4096]{1,0:T(8,128)(2,1)S(1)}, u32[]{:S(2)}, u32[]{:S(2)}) collective-permute-start(bf16[64,4096]{1,0:T(8,128)(2,1)S(1)} %get-tuple-element.73), channel_id=1, source_target_pairs={{0,1},{1,0},{2,3},{3,2},{4,5},{5,4},{6,7},{7,6},{8,9},{9,8},{10,11... | collective-permute-start | bytes 1572872 | tf_op jit(solution)/shard_map/ppermute | solution.py:170
  45.4 14.0 %collective-permute-start.14 = (bf16[64,4096]{1,0:T(8,128)(2,1)S(1)}, bf16[64,4096]{1,0:T(8,128)(2,1)S(1)}, u32[]{:S(2)}, u32[]{:S(2)}) collective-permute-start(bf16[64,4096]{1,0:T(8,128)(2,1)S(1)} %pad_maximum_fusion), channel_id=1, source_target_pairs={{0,2},{1,3},{2,0},{3,1},{4,6},{5,7},{6,4},{7,5},{8,10},{9,11},{10,... | collective-permute-start | bytes 1572872 | tf_op jit(solution)/shard_map/ppermute | solution.py:173
  53.0 6.4 %collective-permute-start.17 = (bf16[64,4096]{1,0:T(8,128)(2,1)S(1)}, bf16[64,4096]{1,0:T(8,128)(2,1)S(1)}, u32[]{:S(2)}, u32[]{:S(2)}) collective-permute-start(bf16[64,4096]{1,0:T(8,128)(2,1)S(1)} %get-tuple-element.83), channel_id=1, source_target_pairs={{0,1},{1,0},{2,3},{3,2},{4,5},{5,4},{6,7},{7,6},{8,9},{9,8},{10,11... | collective-permute-start | bytes 1572872 | tf_op jit(solution)/shard_map/ppermute | solution.py:170
  59.5 9.3 %collective-permute-start.23 = (bf16[32,4096]{1,0:T(8,128)(2,1)S(1)}, bf16[32,4096]{1,0:T(8,128)(2,1)S(1)}, u32[]{:S(2)}, u32[]{:S(2)}) collective-permute-start(bf16[32,4096]{1,0:T(8,128)(2,1)S(1)} %fusion.3), channel_id=1, source_target_pairs={{0,2},{1,3},{2,0},{3,1},{4,6},{5,7},{6,4},{7,5},{8,10},{9,11},{10,... | collective-permute-start | bytes 786440 | tf_op jit(solution)/shard_map/ppermute | solution.py:173
  60.2 9.9 %collective-permute-start.21 = (bf16[64,4096]{1,0:T(8,128)(2,1)S(1)}, bf16[64,4096]{1,0:T(8,128)(2,1)S(1)}, u32[]{:S(2)}, u32[]{:S(2)}) collective-permute-start(bf16[64,4096]{1,0:T(8,128)(2,1)S(1)} %get-tuple-element.88), channel_id=1, source_target_pairs={{0,1},{1,0},{2,3},{3,2},{4,5},{5,4},{6,7},{7,6},{8,9},{9,8},{10,11... | collective-permute-start | bytes 1572872 | tf_op jit(solution)/shard_map/ppermute | solution.py:170
  60.4 6.4 %collective-permute-start.19 = (bf16[16,4096]{1,0:T(8,128)(2,1)S(1)}, bf16[16,4096]{1,0:T(8,128)(2,1)S(1)}, u32[]{:S(2)}, u32[]{:S(2)}) collective-permute-start(bf16[16,4096]{1,0:T(8,128)(2,1)S(1)} %slice.178), channel_id=1, source_target_pairs={{0,4},{1,5},{2,6},{3,7},{4,0},{5,1},{6,2},{7,3},{8,12},{9,13},{10,... | collective-permute-start | bytes 393224 | tf_op jit(solution)/shard_map/ppermute | solution.py:176
  61.9 21.1 %collective-permute-start.18 = (bf16[16,4096]{1,0:T(8,128)(2,1)S(1)}, bf16[16,4096]{1,0:T(8,128)(2,1)S(1)}, u32[]{:S(2)}, u32[]{:S(2)}) collective-permute-start(bf16[16,4096]{1,0:T(8,128)(2,1)S(1)} %slice.179), channel_id=1, source_target_pairs={{0,4},{1,5},{2,6},{3,7},{4,0},{5,1},{6,2},{7,3},{8,12},{9,13},{10,... | collective-permute-start | bytes 393224 | tf_op jit(solution)/shard_map/ppermute | solution.py:176
  66.8 16.2 %collective-permute-start.20 = (bf16[16,4096]{1,0:T(8,128)(2,1)S(1)}, bf16[16,4096]{1,0:T(8,128)(2,1)S(1)}, u32[]{:S(2)}, u32[]{:S(2)}) collective-permute-start(bf16[16,4096]{1,0:T(8,128)(2,1)S(1)} %fusion.7), channel_id=1, source_target_pairs={{0,8},{1,9},{2,10},{3,11},{4,12},{5,13},{6,14},{7,15},{8,0},{9,1},... | collective-permute-start | bytes 393224 | tf_op jit(solution)/shard_map/ppermute | solution.py:176
  69.0 6.6 %collective-permute-start.24 = (bf16[16,4096]{1,0:T(8,128)(2,1)S(1)}, bf16[16,4096]{1,0:T(8,128)(2,1)S(1)}, u32[]{:S(2)}, u32[]{:S(2)}) collective-permute-start(bf16[16,4096]{1,0:T(8,128)(2,1)S(1)} %slice.177), channel_id=1, source_target_pairs={{0,4},{1,5},{2,6},{3,7},{4,0},{5,1},{6,2},{7,3},{8,12},{9,13},{10,... | collective-permute-start | bytes 393224 | tf_op jit(solution)/shard_map/ppermute | solution.py:176
  70.3 7.0 %collective-permute-start.22 = (bf16[32,4096]{1,0:T(8,128)(2,1)S(1)}, bf16[32,4096]{1,0:T(8,128)(2,1)S(1)}, u32[]{:S(2)}, u32[]{:S(2)}) collective-permute-start(bf16[32,4096]{1,0:T(8,128)(2,1)S(1)} %fusion.2), channel_id=1, source_target_pairs={{0,2},{1,3},{2,0},{3,1},{4,6},{5,7},{6,4},{7,5},{8,10},{9,11},{10,... | collective-permute-start | bytes 786440 | tf_op jit(solution)/shard_map/ppermute | solution.py:173
  75.5 7.4 %collective-permute-start.25 = (bf16[16,4096]{1,0:T(8,128)(2,1)S(1)}, bf16[16,4096]{1,0:T(8,128)(2,1)S(1)}, u32[]{:S(2)}, u32[]{:S(2)}) collective-permute-start(bf16[16,4096]{1,0:T(8,128)(2,1)S(1)} %slice_add_fusion.9), channel_id=1, source_target_pairs={{0,8},{1,9},{2,10},{3,11},{4,12},{5,13},{6,14},{7,15},{8,0},{9,1},... | collective-permute-start | bytes 393224 | tf_op jit(solution)/shard_map/ppermute | solution.py:176
  77.5 5.7 %collective-permute-start.26 = (bf16[16,4096]{1,0:T(8,128)(2,1)S(1)}, bf16[16,4096]{1,0:T(8,128)(2,1)S(1)}, u32[]{:S(2)}, u32[]{:S(2)}) collective-permute-start(bf16[16,4096]{1,0:T(8,128)(2,1)S(1)} %slice.176), channel_id=1, source_target_pairs={{0,4},{1,5},{2,6},{3,7},{4,0},{5,1},{6,2},{7,3},{8,12},{9,13},{10,... | collective-permute-start | bytes 393224 | tf_op jit(solution)/shard_map/ppermute | solution.py:176

commit v9 on v8

--- a/solution.py
+++ b/solution.py
@@ -103,19 +103,16 @@
         value = gate / (1.0 + jnp.exp(-gate)) * up
         hidden[:, at : at + step] = (value * weight).astype(jnp.bfloat16)
 
-    def columns(index, _):
-        at = pl.ds(pl.multiple_of(index * 512, 512), 512)
-        out = jnp.dot(hidden[...], down_ref[:, at], preferred_element_type=jnp.float32)
+    for at in range(0, width, 512):
+        part = slice(at, at + 512)
+        out = jnp.dot(hidden[...], down_ref[:, part], preferred_element_type=jnp.float32)
         out = out.astype(jnp.bfloat16)
-        own_ref[:, at] = out[:count]
-        near_ref[:, at] = out[count : 2 * count]
+        own_ref[:, part] = out[:count]
+        near_ref[:, part] = out[count : 2 * count]
         for side in range(2):
-            low, part = (2 + side) * count, slice(side * count // 2, (side + 1) * count // 2)
-            low_ref[part, at] = out[low : low + count // 2]
-            high_ref[part, at] = out[low + count // 2 : low + count]
-        return 0
-
-    lax.fori_loop(0, width // 512, columns, 0)
+            low, rows_of = (2 + side) * count, slice(side * count // 2, (side + 1) * count // 2)
+            low_ref[rows_of, part] = out[low : low + count // 2]
+            high_ref[rows_of, part] = out[low + count // 2 : low + count]
 
 
 def run_expert(swapped, flags, weights, parts, plan):
@@ -208,7 +205,7 @@
     close = [messages[0], *[swap_far(messages[0], by) for by in places(strides)[1:]]]
     near_close = [swap_near(messages[0])]
     loaded = load_weights(w_gate, w_up)
-    far, close, near_close, loaded = lax.optimization_barrier((far, close, near_close, loaded))
+    loaded, near_close, close, far = lax.optimization_barrier((loaded, near_close, close, far))
     others = close[1:]
     near_close += [swap_near(block) for block in others]
     crossed = [swap_far(after(message, far), middle) for message in messages[1:]]
@@ -224,7 +221,7 @@
     wanted += [middle ^ place for place in wanted]
     found = places([middle] + strides)
     for message, block, near in zip(messages[1:], crossed, near_own):
-        line = grow(jnp.concatenate([message, block]), strides)
+        line = after(grow(jnp.concatenate([message, block]), strides), near_far)
         near_line = swap_near(line[tokens:])
         line = jnp.concatenate([line, near])
         sources.append([line, swap_core(line), near_line, swap_core(near_line)])
@@ -240,7 +237,7 @@
                 plan += [(core, 0, half + head), (2 + core, 0, head)]
         parts = sources[step]
         own, peer, other_low, other_high = run_expert(step > 0, flags, loaded, after(parts, ready), tuple(plan))
-        other_high = swap_core(other_high if step else after(other_high, sources[1][2]))
+        other_high = swap_core(other_high if step else after(other_high, sources[1][1:3]))
         if step:
             other_high = after(other_high, near)
         other_high = other_high.astype(jnp.float32)
@@ -251,9 +248,9 @@
         ready = to_high, to_low
         if step:
             near = after(near, to_high).astype(jnp.float32)
-            high += near[head:]
+            high = collapse(high + near[head:])
             low += after(near[:head], high)
-            high = swap_far(collapse(high).astype(jnp.bfloat16), middle)
+            high = swap_far(high.astype(jnp.bfloat16), middle)
             outputs.append((collapse(low), high))
         high = own[head:].astype(jnp.float32) + other_high[:head]
         low = own[:head].astype(jnp.float32) + other_low[:head]

time: 84.1 us -> 85.2 us (1.013)
  Pallas kernels: 22.7 us -> 19.9 us
  starting transfers between devices: 27.6 us -> 30 us
  waiting for transfers between devices: 31.1 us -> 32.5 us
    ppermute x8, waiting for transfers between devices: 6.78 us -> 10.4 us  [swap_near(): lax.ppermute(x, 'expert', [(index(z, y, c), index(z, 1 - y, c)) for z, y,...]
    pallas_call x2, Pallas kernels: 14 us -> 11.3 us  [run_expert(): pl.pallas_call(functools.partial(expert_kernel, swapped, count, plan), ou...]
    ppermute x8, starting transfers between devices: 9.86 us -> 11.9 us  [swap_near(): lax.ppermute(x, 'expert', [(index(z, y, c), index(z, 1 - y, c)) for z, y,...]
    ppermute x8, waiting for transfers between devices: 4.55 us -> 2.6 us  [swap_core(): lax.ppermute(x, 'expert', [(index(z, y, c), index(z, y, 1 - c)) for z, y,...]
  transfers between devices with their start and end apart: 27 -> 27, of which waited for: 12 -> 10; matrix products, arithmetic and copies ran while one was open for 2% -> 1% of each run, Pallas kernels for 26% -> 22%
where the time goes in v9:
time: 85.2 us; the launch traced here: 85 us
  waiting for transfers between devices  32.5 us (38%)
  starting transfers between devices  30 us (35%)
  Pallas kernels  19.9 us (23%)
  other arithmetic  1.9 us (2%)
    ppermute x11, waiting for transfers between devices, swap_far(): lax.ppermute(x, 'expert', [(index(z, y, c), index(z ^ by, y, c)) for z, y...  19.5 us
    ppermute x11, starting transfers between devices, swap_far(): lax.ppermute(x, 'expert', [(index(z, y, c), index(z ^ by, y, c)) for z, y...  16.7 us
    ppermute x8, starting transfers between devices, swap_near(): lax.ppermute(x, 'expert', [(index(z, y, c), index(z, 1 - y, c)) for z, y,...  11.9 us
    pallas_call x2, Pallas kernels, run_expert(): pl.pallas_call(functools.partial(expert_kernel, swapped, count, plan), ou...  11.3 us
    ppermute x8, waiting for transfers between devices, swap_near(): lax.ppermute(x, 'expert', [(index(z, y, c), index(z, 1 - y, c)) for z, y,...  10.4 us
    pallas_call x2, Pallas kernels, load_weights(): pl.pallas_call(load_kernel, out_shape=[pltpu.VMEM(x.shape, x.dtype) for x...  7.43 us
    ppermute x8, waiting for transfers between devices, swap_core(): lax.ppermute(x, 'expert', [(index(z, y, c), index(z, y, 1 - c)) for z, y,...  2.6 us
  transfers between devices with their start and end apart: 27, of which 10 were waited for; matrix products, arithmetic and copies ran while one was open for 1% of the time, Pallas kernels for 22%

profile of v9, /device:TPU:0, one launch (start us, length us, event | category | flops | bytes accessed | tf_op | source)
XLA Modules:
  0.0 85.0 jit_solution(9406356266359306900)
XLA Ops:
  0.0 1.2 %messages.1 = (bf16[16,4224]{1,0:T(8,128)(2,1)S(1)}, bf16[16,4224]{1,0:T(8,128)(2,1)S(1)}) custom-call(bf16[2,16,4096]{2,1,0:T(8,128)(2,1)} %states_ref.1, s32[2,8,16]{2,1,0:T(8,128)} %bitcast.12, f32[2,8,16]{2,1,0:T(8,128)} %bitcast.13), custom_call_target="tpu_custom_call" | custom-call | tf_op jit(solution)/shard_map/messages/pallas_call | solution.py:49
  1.2 4.0 %collective-permute-start.2 = (bf16[16,4224]{1,0:T(8,128)(2,1)S(1)}, bf16[16,4224]{1,0:T(8,128)(2,1)S(1)}, u32[]{:S(2)}, u32[]{:S(2)}) collective-permute-start(bf16[16,4224]{1,0:T(8,128)(2,1)S(1)} %get-tuple-element.63), channel_id=1, source_target_pairs={{0,8},{1,9},{2,10},{3,11},{4,12},{5,13},{6,14},{7,15},{8,0},{9,1},... | collective-permute-start | bytes 405512 | tf_op jit(solution)/shard_map/ppermute | solution.py:173
  5.3 1.6 %collective-permute-start.1 = (bf16[16,4224]{1,0:T(8,128)(2,1)S(1)}, bf16[16,4224]{1,0:T(8,128)(2,1)S(1)}, u32[]{:S(2)}, u32[]{:S(2)}) collective-permute-start(bf16[16,4224]{1,0:T(8,128)(2,1)S(1)} %get-tuple-element.63), channel_id=1, source_target_pairs={{0,4},{1,5},{2,6},{3,7},{4,0},{5,1},{6,2},{7,3},{8,12},{9,13},{10,... | collective-permute-start | bytes 405512 | tf_op jit(solution)/shard_map/ppermute | solution.py:173
  6.8 1.5 %collective-permute-start = (bf16[16,4224]{1,0:T(8,128)(2,1)S(1)}, bf16[16,4224]{1,0:T(8,128)(2,1)S(1)}, u32[]{:S(2)}, u32[]{:S(2)}) collective-permute-start(bf16[16,4224]{1,0:T(8,128)(2,1)S(1)} %get-tuple-element.63), channel_id=1, source_target_pairs={{0,2},{1,3},{2,0},{3,1},{4,6},{5,7},{6,4},{7,5},{8,10},{9,11},{10,... | collective-permute-start | bytes 405512 | tf_op jit(solution)/shard_map/ppermute | solution.py:170
  8.4 4.6 %load_weights.2 = (bf16[4096,768]{1,0:T(8,128)(2,1)S(1)}, bf16[4096,768]{1,0:T(8,128)(2,1)S(1)}) custom-call(bf16[4096,768]{1,0:T(8,128)(2,1)} %bitcast.9, bf16[4096,768]{1,0:T(8,128)(2,1)} %bitcast.10), custom_call_target="tpu_custom_call" | custom-call | tf_op jit(solution)/shard_map/load_weights/pallas_call | solution.py:73
  13.0 0.0 collective-permute-done.1
  13.0 0.0 collective-permute-done
  13.0 0.5 collective-permute-start.6
  13.5 1.5 %collective-permute-start.4 = (bf16[16,4224]{1,0:T(8,128)(2,1)S(1)}, bf16[16,4224]{1,0:T(8,128)(2,1)S(1)}, u32[]{:S(2)}, u32[]{:S(2)}) collective-permute-start(bf16[16,4224]{1,0:T(8,128)(2,1)S(1)} %collective-permute-done.1), channel_id=1, source_target_pairs={{0,2},{1,3},{2,0},{3,1},{4,6},{5,7},{6,4},{7,5},{8,10},{9,11},{10,... | collective-permute-start | bytes 405512 | tf_op jit(solution)/shard_map/ppermute | solution.py:170
  15.0 0.5 collective-permute-start.5
  15.6 2.3 %collective-permute-start.3 = (bf16[16,4224]{1,0:T(8,128)(2,1)S(1)}, bf16[16,4224]{1,0:T(8,128)(2,1)S(1)}, u32[]{:S(2)}, u32[]{:S(2)}) collective-permute-start(bf16[16,4224]{1,0:T(8,128)(2,1)S(1)} %get-tuple-element.60), channel_id=1, source_target_pairs={{0,8},{1,9},{2,10},{3,11},{4,12},{5,13},{6,14},{7,15},{8,0},{9,1},... | collective-permute-start | bytes 405512 | tf_op jit(solution)/shard_map/ppermute | solution.py:173
  18.0 0.9 %collective-permute-done.6 = bf16[16,4224]{1,0:T(8,128)(2,1)S(1)} collective-permute-done((bf16[16,4224]{1,0:T(8,128)(2,1)S(1)}, bf16[16,4224]{1,0:T(8,128)(2,1)S(1)}, u32[]{:S(2)}, u32[]{:S(2)}) %collective-permute-start.6) | collective-permute-done | bytes 135200 | tf_op jit(solution)/shard_map/ppermute | solution.py:173
  18.8 0.7 collective-permute-start.8
  19.6 2.8 %load_weights.3.down_ref = bf16[768,4096]{1,0:T(8,128)(2,1)S(1)} custom-call(bf16[768,4096]{1,0:T(8,128)(2,1)} %bitcast.11), custom_call_target="tpu_custom_call" | custom-call | tf_op jit(solution)/shard_map/load_weights/pallas_call | solution.py:73
  22.4 1.3 %collective-permute-done.3 = bf16[16,4224]{1,0:T(8,128)(2,1)S(1)} collective-permute-done((bf16[16,4224]{1,0:T(8,128)(2,1)S(1)}, bf16[16,4224]{1,0:T(8,128)(2,1)S(1)}, u32[]{:S(2)}, u32[]{:S(2)}) %collective-permute-start.3) | collective-permute-done | bytes 135200 | tf_op jit(solution)/shard_map/ppermute | solution.py:173
  23.7 0.9 %collective-permute-start.10 = (bf16[32,4224]{1,0:T(8,128)(2,1)S(1)}, bf16[32,4224]{1,0:T(8,128)(2,1)S(1)}, u32[]{:S(2)}, u32[]{:S(2)}) collective-permute-start(bf16[32,4224]{1,0:T(8,128)(2,1)S(1)} %pad_maximum_fusion.2), channel_id=1, source_target_pairs={{0,4},{1,5},{2,6},{3,7},{4,0},{5,1},{6,2},{7,3},{8,12},{9,13},{10,... | collective-permute-start | bytes 811016 | tf_op jit(solution)/shard_map/ppermute | solution.py:173
  24.6 0.1 collective-permute-start.7
  24.7 5.5 %collective-permute-done.10 = bf16[32,4224]{1,0:T(8,128)(2,1)S(1)} collective-permute-done((bf16[32,4224]{1,0:T(8,128)(2,1)S(1)}, bf16[32,4224]{1,0:T(8,128)(2,1)S(1)}, u32[]{:S(2)}, u32[]{:S(2)}) %collective-permute-start.10) | collective-permute-done | bytes 270368 | tf_op jit(solution)/shard_map/ppermute | solution.py:173
  30.3 0.1 pad_maximum_fusion
  30.3 0.0 collective-permute-done.8.refs_2_
  30.4 0.1 collective-permute-start.9
  30.5 0.6 collective-permute-start.13
  31.1 2.3 %collective-permute-start.11 = (bf16[48,4224]{1,0:T(8,128)(2,1)S(1)}, bf16[48,4224]{1,0:T(8,128)(2,1)S(1)}, u32[]{:S(2)}, u32[]{:S(2)}) collective-permute-start(bf16[48,4224]{1,0:T(8,128)(2,1)S(1)} %slice.86), channel_id=1, source_target_pairs={{0,2},{1,3},{2,0},{3,1},{4,6},{5,7},{6,4},{7,5},{8,10},{9,11},{10,... | collective-permute-start | bytes 1216520 | tf_op jit(solution)/shard_map/ppermute | solution.py:170
  33.4 0.0 collective-permute-done.9.refs_3_
  33.4 0.0 collective-permute-done.7.refs_1_
  33.4 5.6 %expert.2 = (bf16[64,4096]{1,0:T(8,128)(2,1)S(1)}, bf16[64,4096]{1,0:T(8,128)(2,1)S(1)}, bf16[64,4096]{1,0:T(8,128)(2,1)S(1)}, bf16[64,4096]{1,0:T(8,128)(2,1)S(1)}) custom-call(s32[16]{0:T(128)S(1)} %copy-done, bf16[4096,768]{1,0:T(8,128)(2,1)S(1)} %get-tuple-element.53.gate_ref, bf16[4096,768]{1,0:T(8,128)(2,1)S(1)} %get-tuple-element.54.up_ref, ...), custom_call_target="tpu_custom_call" | custom-call | flops 4831838208 | bytes 4194304 | tf_op jit(solution)/shard_map/expert/pallas_call | solution.py:123
  39.0 3.9 %collective-permute-done.11.refs_2_ = bf16[48,4224]{1,0:T(8,128)(2,1)S(1)} collective-permute-done((bf16[48,4224]{1,0:T(8,128)(2,1)S(1)}, bf16[48,4224]{1,0:T(8,128)(2,1)S(1)}, u32[]{:S(2)}, u32[]{:S(2)}) %collective-permute-start.11) | collective-permute-done | bytes 405536 | tf_op jit(solution)/shard_map/ppermute | solution.py:170
  42.9 0.5 collective-permute-start.16
  43.5 0.0 collective-permute-start.12
  43.5 1.4 %collective-permute-done.14 = bf16[64,4096]{1,0:T(8,128)(2,1)S(1)} collective-permute-done((bf16[64,4096]{1,0:T(8,128)(2,1)S(1)}, bf16[64,4096]{1,0:T(8,128)(2,1)S(1)}, u32[]{:S(2)}, u32[]{:S(2)}) %collective-permute-start.14) | collective-permute-done | bytes 524320 | tf_op jit(solution)/shard_map/ppermute | solution.py:167
  44.9 0.1 convert_element_type.85
  44.9 0.1 fusion.6
  45.0 1.2 %collective-permute-done.12 = bf16[64,4096]{1,0:T(8,128)(2,1)S(1)} collective-permute-done((bf16[64,4096]{1,0:T(8,128)(2,1)S(1)}, bf16[64,4096]{1,0:T(8,128)(2,1)S(1)}, u32[]{:S(2)}, u32[]{:S(2)}) %collective-permute-start.12) | collective-permute-done | bytes 524320 | tf_op jit(solution)/shard_map/ppermute | solution.py:167
  46.2 0.1 convert_element_type.87
  46.3 0.1 fusion.4
  46.4 1.8 %collective-permute-start.15 = (bf16[64,4096]{1,0:T(8,128)(2,1)S(1)}, bf16[64,4096]{1,0:T(8,128)(2,1)S(1)}, u32[]{:S(2)}, u32[]{:S(2)}) collective-permute-start(bf16[64,4096]{1,0:T(8,128)(2,1)S(1)} %pad_maximum_fusion.1), channel_id=1, source_target_pairs={{0,2},{1,3},{2,0},{3,1},{4,6},{5,7},{6,4},{7,5},{8,10},{9,11},{10,... | collective-permute-start | bytes 1572872 | tf_op jit(solution)/shard_map/ppermute | solution.py:170
  48.2 5.6 %expert.3 = (bf16[64,4096]{1,0:T(8,128)(2,1)S(1)}, bf16[64,4096]{1,0:T(8,128)(2,1)S(1)}, bf16[64,4096]{1,0:T(8,128)(2,1)S(1)}, bf16[64,4096]{1,0:T(8,128)(2,1)S(1)}) custom-call(s32[16]{0:T(128)S(1)} %copy-done, bf16[4096,768]{1,0:T(8,128)(2,1)S(1)} %get-tuple-element.53.gate_ref, bf16[4096,768]{1,0:T(8,128)(2,1)S(1)} %get-tuple-element.54.up_ref, ...), custom_call_target="tpu_custom_call" | custom-call | flops 4831838208 | bytes 4194304 | tf_op jit(solution)/shard_map/expert/pallas_call | solution.py:123
  53.8 0.1 collective-permute-start.17
  53.9 6.5 %collective-permute-done.15 = bf16[64,4096]{1,0:T(8,128)(2,1)S(1)} collective-permute-done((bf16[64,4096]{1,0:T(8,128)(2,1)S(1)}, bf16[64,4096]{1,0:T(8,128)(2,1)S(1)}, u32[]{:S(2)}, u32[]{:S(2)}) %collective-permute-start.15) | collective-permute-done | bytes 524320 | tf_op jit(solution)/shard_map/ppermute | solution.py:170
  60.4 0.1 convert_element_type.91
  60.5 0.1 fusion.3
  60.6 0.1 convert_element_type.93
  60.6 0.1 slice_add_fusion.3
  60.7 0.4 collective-permute-start.18
  61.1 1.7 %collective-permute-start.23 = (bf16[32,4096]{1,0:T(8,128)(2,1)S(1)}, bf16[32,4096]{1,0:T(8,128)(2,1)S(1)}, u32[]{:S(2)}, u32[]{:S(2)}) collective-permute-start(bf16[32,4096]{1,0:T(8,128)(2,1)S(1)} %fusion.3), channel_id=1, source_target_pairs={{0,2},{1,3},{2,0},{3,1},{4,6},{5,7},{6,4},{7,5},{8,10},{9,11},{10,... | collective-permute-start | bytes 786440 | tf_op jit(solution)/shard_map/ppermute | solution.py:170
  62.9 0.1 collective-permute-start.21
  62.9 2.8 %collective-permute-done.18 = bf16[16,4096]{1,0:T(8,128)(2,1)S(1)} collective-permute-done((bf16[16,4096]{1,0:T(8,128)(2,1)S(1)}, bf16[16,4096]{1,0:T(8,128)(2,1)S(1)}, u32[]{:S(2)}, u32[]{:S(2)}) %collective-permute-start.18) | collective-permute-done | bytes 131104 | tf_op jit(solution)/shard_map/ppermute | solution.py:173
  65.8 1.7 %collective-permute-start.20 = (bf16[16,4096]{1,0:T(8,128)(2,1)S(1)}, bf16[16,4096]{1,0:T(8,128)(2,1)S(1)}, u32[]{:S(2)}, u32[]{:S(2)}) collective-permute-start(bf16[16,4096]{1,0:T(8,128)(2,1)S(1)} %slice_add_fusion.11), channel_id=1, source_target_pairs={{0,8},{1,9},{2,10},{3,11},{4,12},{5,13},{6,14},{7,15},{8,0},{9,1},... | collective-permute-start | bytes 393224 | tf_op jit(solution)/shard_map/ppermute | solution.py:173
  67.5 0.1 fusion.5
  67.6 1.8 %collective-permute-start.19 = (bf16[16,4096]{1,0:T(8,128)(2,1)S(1)}, bf16[16,4096]{1,0:T(8,128)(2,1)S(1)}, u32[]{:S(2)}, u32[]{:S(2)}) collective-permute-start(bf16[16,4096]{1,0:T(8,128)(2,1)S(1)} %slice.178), channel_id=1, source_target_pairs={{0,4},{1,5},{2,6},{3,7},{4,0},{5,1},{6,2},{7,3},{8,12},{9,13},{10,... | collective-permute-start | bytes 393224 | tf_op jit(solution)/shard_map/ppermute | solution.py:173
  69.4 0.1 fusion
  69.5 0.8 collective-permute-start.24
  70.3 0.0 collective-permute-done.21
  70.3 0.1 convert_element_type.99
  70.4 1.8 %collective-permute-start.22 = (bf16[32,4096]{1,0:T(8,128)(2,1)S(1)}, bf16[32,4096]{1,0:T(8,128)(2,1)S(1)}, u32[]{:S(2)}, u32[]{:S(2)}) collective-permute-start(bf16[32,4096]{1,0:T(8,128)(2,1)S(1)} %fusion.2), channel_id=1, source_target_pairs={{0,2},{1,3},{2,0},{3,1},{4,6},{5,7},{6,4},{7,5},{8,10},{9,11},{10,... | collective-permute-start | bytes 786440 | tf_op jit(solution)/shard_map/ppermute | solution.py:170
  72.2 4.3 %collective-permute-done.24 = bf16[16,4096]{1,0:T(8,128)(2,1)S(1)} collective-permute-done((bf16[16,4096]{1,0:T(8,128)(2,1)S(1)}, bf16[16,4096]{1,0:T(8,128)(2,1)S(1)}, u32[]{:S(2)}, u32[]{:S(2)}) %collective-permute-start.24) | collective-permute-done | bytes 131104 | tf_op jit(solution)/shard_map/ppermute | solution.py:173
  76.5 0.8 collective-permute-start.25
  77.4 0.0 collective-permute-done.22
  77.4 0.1 fusion.1
  77.5 2.0 %collective-permute-start.26 = (bf16[16,4096]{1,0:T(8,128)(2,1)S(1)}, bf16[16,4096]{1,0:T(8,128)(2,1)S(1)}, u32[]{:S(2)}, u32[]{:S(2)}) collective-permute-start(bf16[16,4096]{1,0:T(8,128)(2,1)S(1)} %slice.176), channel_id=1, source_target_pairs={{0,4},{1,5},{2,6},{3,7},{4,0},{5,1},{6,2},{7,3},{8,12},{9,13},{10,... | collective-permute-start | bytes 393224 | tf_op jit(solution)/shard_map/ppermute | solution.py:173
  79.5 4.7 %collective-permute-done.25.second_ref = bf16[16,4096]{1,0:T(8,128)(2,1)S(1)} collective-permute-done((bf16[16,4096]{1,0:T(8,128)(2,1)S(1)}, bf16[16,4096]{1,0:T(8,128)(2,1)S(1)}, u32[]{:S(2)}, u32[]{:S(2)}) %collective-permute-start.25) | collective-permute-done | bytes 131104 | tf_op jit(solution)/shard_map/ppermute | solution.py:173
  84.2 0.1 fusion.10
  84.2 0.0 collective-permute-done.26
  84.3 0.7 pad_maximum_fusion.3
  (34 shorter events, 0.6 us)
Async XLA Ops:
  1.2 11.8 %collective-permute-start.2 = (bf16[16,4224]{1,0:T(8,128)(2,1)S(1)}, bf16[16,4224]{1,0:T(8,128)(2,1)S(1)}, u32[]{:S(2)}, u32[]{:S(2)}) collective-permute-start(bf16[16,4224]{1,0:T(8,128)(2,1)S(1)} %get-tuple-element.63), channel_id=1, source_target_pairs={{0,8},{1,9},{2,10},{3,11},{4,12},{5,13},{6,14},{7,15},{8,0},{9,1},... | collective-permute-start | bytes 405512 | tf_op jit(solution)/shard_map/ppermute | solution.py:173
  5.3 7.7 %collective-permute-start.1 = (bf16[16,4224]{1,0:T(8,128)(2,1)S(1)}, bf16[16,4224]{1,0:T(8,128)(2,1)S(1)}, u32[]{:S(2)}, u32[]{:S(2)}) collective-permute-start(bf16[16,4224]{1,0:T(8,128)(2,1)S(1)} %get-tuple-element.63), channel_id=1, source_target_pairs={{0,4},{1,5},{2,6},{3,7},{4,0},{5,1},{6,2},{7,3},{8,12},{9,13},{10,... | collective-permute-start | bytes 405512 | tf_op jit(solution)/shard_map/ppermute | solution.py:173
  6.8 6.2 %collective-permute-start = (bf16[16,4224]{1,0:T(8,128)(2,1)S(1)}, bf16[16,4224]{1,0:T(8,128)(2,1)S(1)}, u32[]{:S(2)}, u32[]{:S(2)}) collective-permute-start(bf16[16,4224]{1,0:T(8,128)(2,1)S(1)} %get-tuple-element.63), channel_id=1, source_target_pairs={{0,2},{1,3},{2,0},{3,1},{4,6},{5,7},{6,4},{7,5},{8,10},{9,11},{10,... | collective-permute-start | bytes 405512 | tf_op jit(solution)/shard_map/ppermute | solution.py:170
  13.0 5.8 %collective-permute-start.6 = (bf16[16,4224]{1,0:T(8,128)(2,1)S(1)}, bf16[16,4224]{1,0:T(8,128)(2,1)S(1)}, u32[]{:S(2)}, u32[]{:S(2)}) collective-permute-start(bf16[16,4224]{1,0:T(8,128)(2,1)S(1)} %collective-permute-done.2), channel_id=1, source_target_pairs={{0,4},{1,5},{2,6},{3,7},{4,0},{5,1},{6,2},{7,3},{8,12},{9,13},{10,... | collective-permute-start | bytes 405512 | tf_op jit(solution)/shard_map/ppermute | solution.py:173
  13.5 10.2 %collective-permute-start.4 = (bf16[16,4224]{1,0:T(8,128)(2,1)S(1)}, bf16[16,4224]{1,0:T(8,128)(2,1)S(1)}, u32[]{:S(2)}, u32[]{:S(2)}) collective-permute-start(bf16[16,4224]{1,0:T(8,128)(2,1)S(1)} %collective-permute-done.1), channel_id=1, source_target_pairs={{0,2},{1,3},{2,0},{3,1},{4,6},{5,7},{6,4},{7,5},{8,10},{9,11},{10,... | collective-permute-start | bytes 405512 | tf_op jit(solution)/shard_map/ppermute | solution.py:170
  15.0 7.4 %collective-permute-start.5 = (bf16[16,4224]{1,0:T(8,128)(2,1)S(1)}, bf16[16,4224]{1,0:T(8,128)(2,1)S(1)}, u32[]{:S(2)}, u32[]{:S(2)}) collective-permute-start(bf16[16,4224]{1,0:T(8,128)(2,1)S(1)} %get-tuple-element.60), channel_id=1, source_target_pairs={{0,2},{1,3},{2,0},{3,1},{4,6},{5,7},{6,4},{7,5},{8,10},{9,11},{10,... | collective-permute-start | bytes 405512 | tf_op jit(solution)/shard_map/ppermute | solution.py:170
  15.6 8.1 %collective-permute-start.3 = (bf16[16,4224]{1,0:T(8,128)(2,1)S(1)}, bf16[16,4224]{1,0:T(8,128)(2,1)S(1)}, u32[]{:S(2)}, u32[]{:S(2)}) collective-permute-start(bf16[16,4224]{1,0:T(8,128)(2,1)S(1)} %get-tuple-element.60), channel_id=1, source_target_pairs={{0,8},{1,9},{2,10},{3,11},{4,12},{5,13},{6,14},{7,15},{8,0},{9,1},... | collective-permute-start | bytes 405512 | tf_op jit(solution)/shard_map/ppermute | solution.py:173
  18.8 11.5 %collective-permute-start.8 = (bf16[32,4224]{1,0:T(8,128)(2,1)S(1)}, bf16[32,4224]{1,0:T(8,128)(2,1)S(1)}, u32[]{:S(2)}, u32[]{:S(2)}) collective-permute-start(bf16[32,4224]{1,0:T(8,128)(2,1)S(1)} %get-tuple-element.96), channel_id=1, source_target_pairs={{0,2},{1,3},{2,0},{3,1},{4,6},{5,7},{6,4},{7,5},{8,10},{9,11},{10,... | collective-permute-start | bytes 811016 | tf_op jit(solution)/shard_map/ppermute | solution.py:170
  19.6 13.8 %copy-start = (s32[16]{0:T(128)S(1)}, s32[16]{0:T(128)}, u32[]{:S(2)}) copy-start(s32[16]{0:T(128)} %flags_ref.3) | copy-start | bytes 196
  23.7 6.5 %collective-permute-start.10 = (bf16[32,4224]{1,0:T(8,128)(2,1)S(1)}, bf16[32,4224]{1,0:T(8,128)(2,1)S(1)}, u32[]{:S(2)}, u32[]{:S(2)}) collective-permute-start(bf16[32,4224]{1,0:T(8,128)(2,1)S(1)} %pad_maximum_fusion.2), channel_id=1, source_target_pairs={{0,4},{1,5},{2,6},{3,7},{4,0},{5,1},{6,2},{7,3},{8,12},{9,13},{10,... | collective-permute-start | bytes 811016 | tf_op jit(solution)/shard_map/ppermute | solution.py:173
  24.6 8.7 %collective-permute-start.7 = (bf16[96,4224]{1,0:T(8,128)(2,1)S(1)}, bf16[96,4224]{1,0:T(8,128)(2,1)S(1)}, u32[]{:S(2)}, u32[]{:S(2)}) collective-permute-start(bf16[96,4224]{1,0:T(8,128)(2,1)S(1)} %constant_dynamic-update-slice_fusion.2.refs_0_), channel_id=1, source_target_pairs={{0,1},{1,0},{2,3},{3,2},{4,5},{5,4},{6,7},{7,6},{8,9},{9,8},{10,11... | collective-permute-start | bytes 2433032 | tf_op jit(solution)/shard_map/ppermute | solution.py:167
  30.4 3.0 %collective-permute-start.9 = (bf16[32,4224]{1,0:T(8,128)(2,1)S(1)}, bf16[32,4224]{1,0:T(8,128)(2,1)S(1)}, u32[]{:S(2)}, u32[]{:S(2)}) collective-permute-start(bf16[32,4224]{1,0:T(8,128)(2,1)S(1)} %collective-permute-done.8.refs_2_), channel_id=1, source_target_pairs={{0,1},{1,0},{2,3},{3,2},{4,5},{5,4},{6,7},{7,6},{8,9},{9,8},{10,11... | collective-permute-start | bytes 811016 | tf_op jit(solution)/shard_map/ppermute | solution.py:167
  30.5 12.5 %collective-permute-start.13 = (bf16[80,4224]{1,0:T(8,128)(2,1)S(1)}, bf16[80,4224]{1,0:T(8,128)(2,1)S(1)}, u32[]{:S(2)}, u32[]{:S(2)}) collective-permute-start(bf16[80,4224]{1,0:T(8,128)(2,1)S(1)} %constant_dynamic-update-slice_fusion.8.refs_0_), channel_id=1, source_target_pairs={{0,1},{1,0},{2,3},{3,2},{4,5},{5,4},{6,7},{7,6},{8,9},{9,8},{10,11... | collective-permute-start | bytes 2027528 | tf_op jit(solution)/shard_map/ppermute | solution.py:167
  31.1 11.9 %collective-permute-start.11 = (bf16[48,4224]{1,0:T(8,128)(2,1)S(1)}, bf16[48,4224]{1,0:T(8,128)(2,1)S(1)}, u32[]{:S(2)}, u32[]{:S(2)}) collective-permute-start(bf16[48,4224]{1,0:T(8,128)(2,1)S(1)} %slice.86), channel_id=1, source_target_pairs={{0,2},{1,3},{2,0},{3,1},{4,6},{5,7},{6,4},{7,5},{8,10},{9,11},{10,... | collective-permute-start | bytes 1216520 | tf_op jit(solution)/shard_map/ppermute | solution.py:170
  42.9 1.9 %collective-permute-start.14 = (bf16[64,4096]{1,0:T(8,128)(2,1)S(1)}, bf16[64,4096]{1,0:T(8,128)(2,1)S(1)}, u32[]{:S(2)}, u32[]{:S(2)}) collective-permute-start(bf16[64,4096]{1,0:T(8,128)(2,1)S(1)} %get-tuple-element.78), channel_id=1, source_target_pairs={{0,1},{1,0},{2,3},{3,2},{4,5},{5,4},{6,7},{7,6},{8,9},{9,8},{10,11... | collective-permute-start | bytes 1572872 | tf_op jit(solution)/shard_map/ppermute | solution.py:167
  42.9 3.4 %collective-permute-start.16 = (bf16[48,4224]{1,0:T(8,128)(2,1)S(1)}, bf16[48,4224]{1,0:T(8,128)(2,1)S(1)}, u32[]{:S(2)}, u32[]{:S(2)}) collective-permute-start(bf16[48,4224]{1,0:T(8,128)(2,1)S(1)} %collective-permute-done.11.refs_2_), channel_id=1, source_target_pairs={{0,1},{1,0},{2,3},{3,2},{4,5},{5,4},{6,7},{7,6},{8,9},{9,8},{10,11... | collective-permute-start | bytes 1216520 | tf_op jit(solution)/shard_map/ppermute | solution.py:167
  43.5 2.7 %collective-permute-start.12 = (bf16[64,4096]{1,0:T(8,128)(2,1)S(1)}, bf16[64,4096]{1,0:T(8,128)(2,1)S(1)}, u32[]{:S(2)}, u32[]{:S(2)}) collective-permute-start(bf16[64,4096]{1,0:T(8,128)(2,1)S(1)} %get-tuple-element.75), channel_id=1, source_target_pairs={{0,1},{1,0},{2,3},{3,2},{4,5},{5,4},{6,7},{7,6},{8,9},{9,8},{10,11... | collective-permute-start | bytes 1572872 | tf_op jit(solution)/shard_map/ppermute | solution.py:167
  46.4 14.0 %collective-permute-start.15 = (bf16[64,4096]{1,0:T(8,128)(2,1)S(1)}, bf16[64,4096]{1,0:T(8,128)(2,1)S(1)}, u32[]{:S(2)}, u32[]{:S(2)}) collective-permute-start(bf16[64,4096]{1,0:T(8,128)(2,1)S(1)} %pad_maximum_fusion.1), channel_id=1, source_target_pairs={{0,2},{1,3},{2,0},{3,1},{4,6},{5,7},{6,4},{7,5},{8,10},{9,11},{10,... | collective-permute-start | bytes 1572872 | tf_op jit(solution)/shard_map/ppermute | solution.py:170
  53.8 6.6 %collective-permute-start.17 = (bf16[64,4096]{1,0:T(8,128)(2,1)S(1)}, bf16[64,4096]{1,0:T(8,128)(2,1)S(1)}, u32[]{:S(2)}, u32[]{:S(2)}) collective-permute-start(bf16[64,4096]{1,0:T(8,128)(2,1)S(1)} %get-tuple-element.85), channel_id=1, source_target_pairs={{0,1},{1,0},{2,3},{3,2},{4,5},{5,4},{6,7},{7,6},{8,9},{9,8},{10,11... | collective-permute-start | bytes 1572872 | tf_op jit(solution)/shard_map/ppermute | solution.py:167
  60.7 5.0 %collective-permute-start.18 = (bf16[16,4096]{1,0:T(8,128)(2,1)S(1)}, bf16[16,4096]{1,0:T(8,128)(2,1)S(1)}, u32[]{:S(2)}, u32[]{:S(2)}) collective-permute-start(bf16[16,4096]{1,0:T(8,128)(2,1)S(1)} %slice.179), channel_id=1, source_target_pairs={{0,4},{1,5},{2,6},{3,7},{4,0},{5,1},{6,2},{7,3},{8,12},{9,13},{10,... | collective-permute-start | bytes 393224 | tf_op jit(solution)/shard_map/ppermute | solution.py:173
  61.1 8.3 %collective-permute-start.23 = (bf16[32,4096]{1,0:T(8,128)(2,1)S(1)}, bf16[32,4096]{1,0:T(8,128)(2,1)S(1)}, u32[]{:S(2)}, u32[]{:S(2)}) collective-permute-start(bf16[32,4096]{1,0:T(8,128)(2,1)S(1)} %fusion.3), channel_id=1, source_target_pairs={{0,2},{1,3},{2,0},{3,1},{4,6},{5,7},{6,4},{7,5},{8,10},{9,11},{10,... | collective-permute-start | bytes 786440 | tf_op jit(solution)/shard_map/ppermute | solution.py:170
  62.9 7.4 %collective-permute-start.21 = (bf16[64,4096]{1,0:T(8,128)(2,1)S(1)}, bf16[64,4096]{1,0:T(8,128)(2,1)S(1)}, u32[]{:S(2)}, u32[]{:S(2)}) collective-permute-start(bf16[64,4096]{1,0:T(8,128)(2,1)S(1)} %get-tuple-element.90), channel_id=1, source_target_pairs={{0,1},{1,0},{2,3},{3,2},{4,5},{5,4},{6,7},{7,6},{8,9},{9,8},{10,11... | collective-permute-start | bytes 1572872 | tf_op jit(solution)/shard_map/ppermute | solution.py:167
  65.8 18.4 %collective-permute-start.20 = (bf16[16,4096]{1,0:T(8,128)(2,1)S(1)}, bf16[16,4096]{1,0:T(8,128)(2,1)S(1)}, u32[]{:S(2)}, u32[]{:S(2)}) collective-permute-start(bf16[16,4096]{1,0:T(8,128)(2,1)S(1)} %slice_add_fusion.11), channel_id=1, source_target_pairs={{0,8},{1,9},{2,10},{3,11},{4,12},{5,13},{6,14},{7,15},{8,0},{9,1},... | collective-permute-start | bytes 393224 | tf_op jit(solution)/shard_map/ppermute | solution.py:173
  67.6 16.6 %collective-permute-start.19 = (bf16[16,4096]{1,0:T(8,128)(2,1)S(1)}, bf16[16,4096]{1,0:T(8,128)(2,1)S(1)}, u32[]{:S(2)}, u32[]{:S(2)}) collective-permute-start(bf16[16,4096]{1,0:T(8,128)(2,1)S(1)} %slice.178), channel_id=1, source_target_pairs={{0,4},{1,5},{2,6},{3,7},{4,0},{5,1},{6,2},{7,3},{8,12},{9,13},{10,... | collective-permute-start | bytes 393224 | tf_op jit(solution)/shard_map/ppermute | solution.py:173
  69.5 7.0 %collective-permute-start.24 = (bf16[16,4096]{1,0:T(8,128)(2,1)S(1)}, bf16[16,4096]{1,0:T(8,128)(2,1)S(1)}, u32[]{:S(2)}, u32[]{:S(2)}) collective-permute-start(bf16[16,4096]{1,0:T(8,128)(2,1)S(1)} %slice.177), channel_id=1, source_target_pairs={{0,4},{1,5},{2,6},{3,7},{4,0},{5,1},{6,2},{7,3},{8,12},{9,13},{10,... | collective-permute-start | bytes 393224 | tf_op jit(solution)/shard_map/ppermute | solution.py:173
  70.4 7.0 %collective-permute-start.22 = (bf16[32,4096]{1,0:T(8,128)(2,1)S(1)}, bf16[32,4096]{1,0:T(8,128)(2,1)S(1)}, u32[]{:S(2)}, u32[]{:S(2)}) collective-permute-start(bf16[32,4096]{1,0:T(8,128)(2,1)S(1)} %fusion.2), channel_id=1, source_target_pairs={{0,2},{1,3},{2,0},{3,1},{4,6},{5,7},{6,4},{7,5},{8,10},{9,11},{10,... | collective-permute-start | bytes 786440 | tf_op jit(solution)/shard_map/ppermute | solution.py:170
  76.5 7.6 %collective-permute-start.25 = (bf16[16,4096]{1,0:T(8,128)(2,1)S(1)}, bf16[16,4096]{1,0:T(8,128)(2,1)S(1)}, u32[]{:S(2)}, u32[]{:S(2)}) collective-permute-start(bf16[16,4096]{1,0:T(8,128)(2,1)S(1)} %slice_add_fusion.9), channel_id=1, source_target_pairs={{0,8},{1,9},{2,10},{3,11},{4,12},{5,13},{6,14},{7,15},{8,0},{9,1},... | collective-permute-start | bytes 393224 | tf_op jit(solution)/shard_map/ppermute | solution.py:173
  77.5 6.7 %collective-permute-start.26 = (bf16[16,4096]{1,0:T(8,128)(2,1)S(1)}, bf16[16,4096]{1,0:T(8,128)(2,1)S(1)}, u32[]{:S(2)}, u32[]{:S(2)}) collective-permute-start(bf16[16,4096]{1,0:T(8,128)(2,1)S(1)} %slice.176), channel_id=1, source_target_pairs={{0,4},{1,5},{2,6},{3,7},{4,0},{5,1},{6,2},{7,3},{8,12},{9,13},{10,... | collective-permute-start | bytes 393224 | tf_op jit(solution)/shard_map/ppermute | solution.py:173

commit v10 on v9

--- a/solution.py
+++ b/solution.py
@@ -202,40 +202,49 @@
     w_gate, w_up, w_down = w_gate[0], w_up[0], w_down[0]
     messages = make_messages(states, ids, probs, tail)
     far = swap_far(messages[0], middle)
-    close = [messages[0], *[swap_far(messages[0], by) for by in places(strides)[1:]]]
-    near_close = [swap_near(messages[0])]
+    others = [swap_far(messages[0], by) for by in places(strides)[1:]]
+    near_own = [swap_near(message) for message in messages]
     loaded = load_weights(w_gate, w_up)
-    loaded, near_close, close, far = lax.optimization_barrier((loaded, near_close, close, far))
-    others = close[1:]
-    near_close += [swap_near(block) for block in others]
+    loaded, near_own, others, far = lax.optimization_barrier((loaded, near_own, others, far))
+    near_close = [swap_near(block) for block in others]
     crossed = [swap_far(after(message, far), middle) for message in messages[1:]]
     far = grow(far, strides)
     near_far = swap_near(far)
     last = load_weights(after(w_down, far))
-    near_own = [swap_near(after(message, others)) for message in messages[1:]]
-    crossed, near_close, near_own, last = lax.optimization_barrier((crossed, near_close, near_own, last))
+    last, near_close, crossed = lax.optimization_barrier((last, near_close, crossed))
     loaded += last
-    line = jnp.concatenate([*close, far, *near_close])
+    line = jnp.concatenate([messages[0], *others, far, near_own[0], *near_close])
     sources = [[line, swap_core(line), near_far, swap_core(near_far)]]
     wanted = places(strides)
     wanted += [middle ^ place for place in wanted]
     found = places([middle] + strides)
-    for message, block, near in zip(messages[1:], crossed, near_own):
-        line = after(grow(jnp.concatenate([message, block]), strides), near_far)
-        near_line = swap_near(line[tokens:])
-        line = jnp.concatenate([line, near])
-        sources.append([line, swap_core(line), near_line, swap_core(near_line)])
+    for step in range(1, steps):
+        block = crossed[step - 1]
+        near_block = swap_near(block)
+        line = jnp.concatenate([messages[step], block])
+        rest = []
+        for by in strides:
+            rest.append(after(swap_far(line, by), sources[0][3]))
+            line = jnp.concatenate([line, rest[-1]])
+        near_rest = swap_near(jnp.concatenate(rest))
+        line = jnp.concatenate([messages[step], block, *rest, near_own[step], near_block])
+        sources.append([line, swap_core(line), near_rest])
     outputs, ready = [], [source[0] for source in sources]
     for step in range(steps):
         plan = []
         for core in range(2):
             if step:
                 at = [found.index(place) * tokens for place in wanted]
-                plan += [(core, low, low + tokens) for low in at] + [(core, half, half + tokens)]
-                plan += [(2 + core, low - tokens, low) for low in at[1:]]
+                plan += [(core, row, row + tokens) for row in at]
+                for row in at:
+                    early = row < 2 * tokens
+                    row += half if early else -2 * tokens
+                    plan.append((core if early else 2 + core, row, row + tokens))
             else:
                 plan += [(core, 0, half + head), (2 + core, 0, head)]
         parts = sources[step]
+        if step:
+            parts = [*parts, swap_core(after(parts[2], ready))]
         own, peer, other_low, other_high = run_expert(step > 0, flags, loaded, after(parts, ready), tuple(plan))
         other_high = swap_core(other_high if step else after(other_high, sources[1][1:3]))
         if step:

time: 85.2 us -> 85.7 us (level)
  waiting for transfers between devices: 32.5 us -> 38.1 us
  starting transfers between devices: 30 us -> 25.1 us
    ppermute x8 -> x9, waiting for transfers between devices: 10.4 us -> 15 us  [swap_near(): lax.ppermute(x, 'expert', [(index(z, y, c), index(z, 1 - y, c)) for z, y,...]
    ppermute x11, starting transfers between devices: 16.7 us -> 14 us  [swap_far(): lax.ppermute(x, 'expert', [(index(z, y, c), index(z ^ by, y, c)) for z, y...]
    ppermute x8 -> x9, starting transfers between devices: 11.9 us -> 9.58 us  [swap_near(): lax.ppermute(x, 'expert', [(index(z, y, c), index(z, 1 - y, c)) for z, y,...]
    ppermute x11, waiting for transfers between devices: 19.5 us -> 20.4 us  [swap_far(): lax.ppermute(x, 'expert', [(index(z, y, c), index(z ^ by, y, c)) for z, y...]
  transfers between devices with their start and end apart: 27 -> 28, of which waited for: 10 -> 15; matrix products, arithmetic and copies ran while one was open for 1% -> 1% of each run, Pallas kernels for 22% -> 22%
where the time goes in v10:
time: 85.7 us; the launch traced here: 85.5 us
  waiting for transfers between devices  38.1 us (44%)
  starting transfers between devices  25.1 us (29%)
  Pallas kernels  19.9 us (23%)
  other arithmetic  1.87 us (2%)
    ppermute x11, waiting for transfers between devices, swap_far(): lax.ppermute(x, 'expert', [(index(z, y, c), index(z ^ by, y, c)) for z, y...  20.4 us
    ppermute x9, waiting for transfers between devices, swap_near(): lax.ppermute(x, 'expert', [(index(z, y, c), index(z, 1 - y, c)) for z, y,...  15 us
    ppermute x11, starting transfers between devices, swap_far(): lax.ppermute(x, 'expert', [(index(z, y, c), index(z ^ by, y, c)) for z, y...  14 us
    pallas_call x2, Pallas kernels, run_expert(): pl.pallas_call(functools.partial(expert_kernel, swapped, count, plan), ou...  11.3 us
    ppermute x9, starting transfers between devices, swap_near(): lax.ppermute(x, 'expert', [(index(z, y, c), index(z, 1 - y, c)) for z, y,...  9.58 us
    pallas_call x2, Pallas kernels, load_weights(): pl.pallas_call(load_kernel, out_shape=[pltpu.VMEM(x.shape, x.dtype) for x...  7.43 us
    ppermute x8, waiting for transfers between devices, swap_core(): lax.ppermute(x, 'expert', [(index(z, y, c), index(z, y, 1 - c)) for z, y,...  2.66 us
  transfers between devices with their start and end apart: 28, of which 15 were waited for; matrix products, arithmetic and copies ran while one was open for 1% of the time, Pallas kernels for 22%

profile of v10, /device:TPU:0, one launch (start us, length us, event | category | flops | bytes accessed | tf_op | source)
XLA Modules:
  0.0 85.5 jit_solution(17724881860620408303)
XLA Ops:
  0.0 1.2 %messages.1 = (bf16[16,4224]{1,0:T(8,128)(2,1)S(1)}, bf16[16,4224]{1,0:T(8,128)(2,1)S(1)}) custom-call(bf16[2,16,4096]{2,1,0:T(8,128)(2,1)} %states_ref.1, s32[2,8,16]{2,1,0:T(8,128)} %bitcast.12, f32[2,8,16]{2,1,0:T(8,128)} %bitcast.13), custom_call_target="tpu_custom_call" | custom-call | tf_op jit(solution)/shard_map/messages/pallas_call | solution.py:49
  1.2 4.0 %collective-permute-start.3 = (bf16[16,4224]{1,0:T(8,128)(2,1)S(1)}, bf16[16,4224]{1,0:T(8,128)(2,1)S(1)}, u32[]{:S(2)}, u32[]{:S(2)}) collective-permute-start(bf16[16,4224]{1,0:T(8,128)(2,1)S(1)} %get-tuple-element.50), channel_id=1, source_target_pairs={{0,8},{1,9},{2,10},{3,11},{4,12},{5,13},{6,14},{7,15},{8,0},{9,1},... | collective-permute-start | bytes 405512 | tf_op jit(solution)/shard_map/ppermute | solution.py:173
  5.3 1.6 %collective-permute-start.2 = (bf16[16,4224]{1,0:T(8,128)(2,1)S(1)}, bf16[16,4224]{1,0:T(8,128)(2,1)S(1)}, u32[]{:S(2)}, u32[]{:S(2)}) collective-permute-start(bf16[16,4224]{1,0:T(8,128)(2,1)S(1)} %get-tuple-element.50), channel_id=1, source_target_pairs={{0,4},{1,5},{2,6},{3,7},{4,0},{5,1},{6,2},{7,3},{8,12},{9,13},{10,... | collective-permute-start | bytes 405512 | tf_op jit(solution)/shard_map/ppermute | solution.py:173
  6.8 1.5 %collective-permute-start = (bf16[16,4224]{1,0:T(8,128)(2,1)S(1)}, bf16[16,4224]{1,0:T(8,128)(2,1)S(1)}, u32[]{:S(2)}, u32[]{:S(2)}) collective-permute-start(bf16[16,4224]{1,0:T(8,128)(2,1)S(1)} %get-tuple-element.50), channel_id=1, source_target_pairs={{0,2},{1,3},{2,0},{3,1},{4,6},{5,7},{6,4},{7,5},{8,10},{9,11},{10,... | collective-permute-start | bytes 405512 | tf_op jit(solution)/shard_map/ppermute | solution.py:170
  8.4 0.5 collective-permute-start.1
  8.9 4.6 %load_weights.2 = (bf16[4096,768]{1,0:T(8,128)(2,1)S(1)}, bf16[4096,768]{1,0:T(8,128)(2,1)S(1)}) custom-call(bf16[4096,768]{1,0:T(8,128)(2,1)} %bitcast.9, bf16[4096,768]{1,0:T(8,128)(2,1)} %bitcast.10), custom_call_target="tpu_custom_call" | custom-call | tf_op jit(solution)/shard_map/load_weights/pallas_call | solution.py:73
  13.5 0.0 collective-permute-done.3
  13.6 0.0 collective-permute-done.2
  13.6 0.9 %collective-permute-done.1 = bf16[16,4224]{1,0:T(8,128)(2,1)S(1)} collective-permute-done((bf16[16,4224]{1,0:T(8,128)(2,1)S(1)}, bf16[16,4224]{1,0:T(8,128)(2,1)S(1)}, u32[]{:S(2)}, u32[]{:S(2)}) %collective-permute-start.1) | collective-permute-done | bytes 135200 | tf_op jit(solution)/shard_map/ppermute | solution.py:170
  14.5 0.4 collective-permute-start.4
  15.0 1.5 %collective-permute-start.5 = (bf16[16,4224]{1,0:T(8,128)(2,1)S(1)}, bf16[16,4224]{1,0:T(8,128)(2,1)S(1)}, u32[]{:S(2)}, u32[]{:S(2)}) collective-permute-start(bf16[16,4224]{1,0:T(8,128)(2,1)S(1)} %collective-permute-done.2), channel_id=1, source_target_pairs={{0,2},{1,3},{2,0},{3,1},{4,6},{5,7},{6,4},{7,5},{8,10},{9,11},{10,... | collective-permute-start | bytes 405512 | tf_op jit(solution)/shard_map/ppermute | solution.py:170
  16.5 1.0 %collective-permute-start.6 = (bf16[16,4224]{1,0:T(8,128)(2,1)S(1)}, bf16[16,4224]{1,0:T(8,128)(2,1)S(1)}, u32[]{:S(2)}, u32[]{:S(2)}) collective-permute-start(bf16[16,4224]{1,0:T(8,128)(2,1)S(1)} %get-tuple-element.57), channel_id=1, source_target_pairs={{0,8},{1,9},{2,10},{3,11},{4,12},{5,13},{6,14},{7,15},{8,0},{9,1},... | collective-permute-start | bytes 405512 | tf_op jit(solution)/shard_map/ppermute | solution.py:173
  17.6 3.2 %collective-permute-done.4 = bf16[16,4224]{1,0:T(8,128)(2,1)S(1)} collective-permute-done((bf16[16,4224]{1,0:T(8,128)(2,1)S(1)}, bf16[16,4224]{1,0:T(8,128)(2,1)S(1)}, u32[]{:S(2)}, u32[]{:S(2)}) %collective-permute-start.4) | collective-permute-done | bytes 135200 | tf_op jit(solution)/shard_map/ppermute | solution.py:173
  20.8 0.7 collective-permute-start.8
  21.5 2.8 %load_weights.3.down_ref = bf16[768,4096]{1,0:T(8,128)(2,1)S(1)} custom-call(bf16[768,4096]{1,0:T(8,128)(2,1)} %bitcast.11), custom_call_target="tpu_custom_call" | custom-call | tf_op jit(solution)/shard_map/load_weights/pallas_call | solution.py:73
  24.3 0.0 collective-permute-done.5
  24.3 1.4 %collective-permute-start.11 = (bf16[16,4224]{1,0:T(8,128)(2,1)S(1)}, bf16[16,4224]{1,0:T(8,128)(2,1)S(1)}, u32[]{:S(2)}, u32[]{:S(2)}) collective-permute-start(bf16[16,4224]{1,0:T(8,128)(2,1)S(1)} %collective-permute-done.6), channel_id=1, source_target_pairs={{0,2},{1,3},{2,0},{3,1},{4,6},{5,7},{6,4},{7,5},{8,10},{9,11},{10,... | collective-permute-start | bytes 405512 | tf_op jit(solution)/shard_map/ppermute | solution.py:170
  25.8 0.2 collective-permute-start.10
  26.0 1.9 %collective-permute-done.8.refs_2_ = bf16[32,4224]{1,0:T(8,128)(2,1)S(1)} collective-permute-done((bf16[32,4224]{1,0:T(8,128)(2,1)S(1)}, bf16[32,4224]{1,0:T(8,128)(2,1)S(1)}, u32[]{:S(2)}, u32[]{:S(2)}) %collective-permute-start.8) | collective-permute-done | bytes 270368 | tf_op jit(solution)/shard_map/ppermute | solution.py:170
  28.0 0.6 collective-permute-start.7
  28.5 3.8 %collective-permute-done.10 = bf16[32,4224]{1,0:T(8,128)(2,1)S(1)} collective-permute-done((bf16[32,4224]{1,0:T(8,128)(2,1)S(1)}, bf16[32,4224]{1,0:T(8,128)(2,1)S(1)}, u32[]{:S(2)}, u32[]{:S(2)}) %collective-permute-start.10) | collective-permute-done | bytes 270368 | tf_op jit(solution)/shard_map/ppermute | solution.py:173
  32.4 0.1 collective-permute-start.14
  32.5 0.7 collective-permute-start.12
  33.2 0.0 collective-permute-done.7.refs_1_
  33.2 5.6 %expert.2 = (bf16[64,4096]{1,0:T(8,128)(2,1)S(1)}, bf16[64,4096]{1,0:T(8,128)(2,1)S(1)}, bf16[64,4096]{1,0:T(8,128)(2,1)S(1)}, bf16[64,4096]{1,0:T(8,128)(2,1)S(1)}) custom-call(s32[16]{0:T(128)S(1)} %copy-done, bf16[4096,768]{1,0:T(8,128)(2,1)S(1)} %get-tuple-element.52.gate_ref, bf16[4096,768]{1,0:T(8,128)(2,1)S(1)} %get-tuple-element.53.up_ref, ...), custom_call_target="tpu_custom_call" | custom-call | flops 4831838208 | bytes 4194304 | tf_op jit(solution)/shard_map/expert/pallas_call | solution.py:123
  38.8 2.5 %collective-permute-done.12.refs_2_ = bf16[32,4224]{1,0:T(8,128)(2,1)S(1)} collective-permute-done((bf16[32,4224]{1,0:T(8,128)(2,1)S(1)}, bf16[32,4224]{1,0:T(8,128)(2,1)S(1)}, u32[]{:S(2)}, u32[]{:S(2)}) %collective-permute-start.12) | collective-permute-done | bytes 270368 | tf_op jit(solution)/shard_map/ppermute | solution.py:170
  41.4 0.5 collective-permute-start.13
  41.9 1.4 %collective-permute-done.15 = bf16[64,4096]{1,0:T(8,128)(2,1)S(1)} collective-permute-done((bf16[64,4096]{1,0:T(8,128)(2,1)S(1)}, bf16[64,4096]{1,0:T(8,128)(2,1)S(1)}, u32[]{:S(2)}, u32[]{:S(2)}) %collective-permute-start.15) | collective-permute-done | bytes 524320 | tf_op jit(solution)/shard_map/ppermute | solution.py:167
  43.3 0.1 convert_element_type.85
  43.4 0.1 fusion.6
  43.4 0.6 collective-permute-done.13
  44.0 0.1 convert_element_type.87
  44.1 0.1 fusion.4
  44.2 0.2 collective-permute-start.17
  44.4 0.7 collective-permute-start.16
  45.2 0.6 collective-permute-done.17.refs_3_
  45.8 5.6 %expert.3 = (bf16[64,4096]{1,0:T(8,128)(2,1)S(1)}, bf16[64,4096]{1,0:T(8,128)(2,1)S(1)}, bf16[64,4096]{1,0:T(8,128)(2,1)S(1)}, bf16[64,4096]{1,0:T(8,128)(2,1)S(1)}) custom-call(s32[16]{0:T(128)S(1)} %copy-done, bf16[4096,768]{1,0:T(8,128)(2,1)S(1)} %get-tuple-element.52.gate_ref, bf16[4096,768]{1,0:T(8,128)(2,1)S(1)} %get-tuple-element.53.up_ref, ...), custom_call_target="tpu_custom_call" | custom-call | flops 4831838208 | bytes 4194304 | tf_op jit(solution)/shard_map/expert/pallas_call | solution.py:123
  51.4 0.2 collective-permute-start.18
  51.6 7.1 %collective-permute-done.16 = bf16[64,4096]{1,0:T(8,128)(2,1)S(1)} collective-permute-done((bf16[64,4096]{1,0:T(8,128)(2,1)S(1)}, bf16[64,4096]{1,0:T(8,128)(2,1)S(1)}, u32[]{:S(2)}, u32[]{:S(2)}) %collective-permute-start.16) | collective-permute-done | bytes 524320 | tf_op jit(solution)/shard_map/ppermute | solution.py:170
  58.7 0.1 convert_element_type.91
  58.8 0.1 fusion.3
  58.8 0.1 convert_element_type.93
  58.9 0.1 slice_add_fusion.3
  59.0 0.5 collective-permute-start.19
  59.5 1.7 %collective-permute-start.24 = (bf16[32,4096]{1,0:T(8,128)(2,1)S(1)}, bf16[32,4096]{1,0:T(8,128)(2,1)S(1)}, u32[]{:S(2)}, u32[]{:S(2)}) collective-permute-start(bf16[32,4096]{1,0:T(8,128)(2,1)S(1)} %fusion.3), channel_id=1, source_target_pairs={{0,2},{1,3},{2,0},{3,1},{4,6},{5,7},{6,4},{7,5},{8,10},{9,11},{10,... | collective-permute-start | bytes 786440 | tf_op jit(solution)/shard_map/ppermute | solution.py:170
  61.3 2.8 %collective-permute-done.19 = bf16[16,4096]{1,0:T(8,128)(2,1)S(1)} collective-permute-done((bf16[16,4096]{1,0:T(8,128)(2,1)S(1)}, bf16[16,4096]{1,0:T(8,128)(2,1)S(1)}, u32[]{:S(2)}, u32[]{:S(2)}) %collective-permute-start.19) | collective-permute-done | bytes 131104 | tf_op jit(solution)/shard_map/ppermute | solution.py:173
  64.1 1.3 %collective-permute-start.21 = (bf16[16,4096]{1,0:T(8,128)(2,1)S(1)}, bf16[16,4096]{1,0:T(8,128)(2,1)S(1)}, u32[]{:S(2)}, u32[]{:S(2)}) collective-permute-start(bf16[16,4096]{1,0:T(8,128)(2,1)S(1)} %slice_add_fusion.11), channel_id=1, source_target_pairs={{0,8},{1,9},{2,10},{3,11},{4,12},{5,13},{6,14},{7,15},{8,0},{9,1},... | collective-permute-start | bytes 393224 | tf_op jit(solution)/shard_map/ppermute | solution.py:173
  65.4 0.1 fusion.5
  65.5 1.8 %collective-permute-start.20 = (bf16[16,4096]{1,0:T(8,128)(2,1)S(1)}, bf16[16,4096]{1,0:T(8,128)(2,1)S(1)}, u32[]{:S(2)}, u32[]{:S(2)}) collective-permute-start(bf16[16,4096]{1,0:T(8,128)(2,1)S(1)} %slice.174), channel_id=1, source_target_pairs={{0,4},{1,5},{2,6},{3,7},{4,0},{5,1},{6,2},{7,3},{8,12},{9,13},{10,... | collective-permute-start | bytes 393224 | tf_op jit(solution)/shard_map/ppermute | solution.py:173
  67.3 0.1 convert_element_type.99
  67.4 0.9 %collective-permute-done.24 = bf16[32,4096]{1,0:T(8,128)(2,1)S(1)} collective-permute-done((bf16[32,4096]{1,0:T(8,128)(2,1)S(1)}, bf16[32,4096]{1,0:T(8,128)(2,1)S(1)}, u32[]{:S(2)}, u32[]{:S(2)}) %collective-permute-start.24) | collective-permute-done | bytes 262176 | tf_op jit(solution)/shard_map/ppermute | solution.py:170
  68.2 0.1 fusion
  68.4 1.7 %collective-permute-start.25 = (bf16[16,4096]{1,0:T(8,128)(2,1)S(1)}, bf16[16,4096]{1,0:T(8,128)(2,1)S(1)}, u32[]{:S(2)}, u32[]{:S(2)}) collective-permute-start(bf16[16,4096]{1,0:T(8,128)(2,1)S(1)} %slice.173), channel_id=1, source_target_pairs={{0,4},{1,5},{2,6},{3,7},{4,0},{5,1},{6,2},{7,3},{8,12},{9,13},{10,... | collective-permute-start | bytes 393224 | tf_op jit(solution)/shard_map/ppermute | solution.py:173
  70.1 0.7 collective-permute-start.23
  70.8 4.4 %collective-permute-done.25 = bf16[16,4096]{1,0:T(8,128)(2,1)S(1)} collective-permute-done((bf16[16,4096]{1,0:T(8,128)(2,1)S(1)}, bf16[16,4096]{1,0:T(8,128)(2,1)S(1)}, u32[]{:S(2)}, u32[]{:S(2)}) %collective-permute-start.25) | collective-permute-done | bytes 131104 | tf_op jit(solution)/shard_map/ppermute | solution.py:173
  75.2 0.9 %collective-permute-start.26 = (bf16[16,4096]{1,0:T(8,128)(2,1)S(1)}, bf16[16,4096]{1,0:T(8,128)(2,1)S(1)}, u32[]{:S(2)}, u32[]{:S(2)}) collective-permute-start(bf16[16,4096]{1,0:T(8,128)(2,1)S(1)} %slice_add_fusion.9), channel_id=1, source_target_pairs={{0,8},{1,9},{2,10},{3,11},{4,12},{5,13},{6,14},{7,15},{8,0},{9,1},... | collective-permute-start | bytes 393224 | tf_op jit(solution)/shard_map/ppermute | solution.py:173
  76.2 1.6 %collective-permute-done.23 = bf16[32,4096]{1,0:T(8,128)(2,1)S(1)} collective-permute-done((bf16[32,4096]{1,0:T(8,128)(2,1)S(1)}, bf16[32,4096]{1,0:T(8,128)(2,1)S(1)}, u32[]{:S(2)}, u32[]{:S(2)}) %collective-permute-start.23) | collective-permute-done | bytes 262176 | tf_op jit(solution)/shard_map/ppermute | solution.py:170
  77.8 0.1 fusion.1
  77.9 0.5 collective-permute-start.27
  78.4 0.0 collective-permute-done.21
  78.4 0.0 collective-permute-done.20
  78.5 5.0 %collective-permute-done.26.second_ref = bf16[16,4096]{1,0:T(8,128)(2,1)S(1)} collective-permute-done((bf16[16,4096]{1,0:T(8,128)(2,1)S(1)}, bf16[16,4096]{1,0:T(8,128)(2,1)S(1)}, u32[]{:S(2)}, u32[]{:S(2)}) %collective-permute-start.26) | collective-permute-done | bytes 131104 | tf_op jit(solution)/shard_map/ppermute | solution.py:173
  83.6 1.2 %collective-permute-done.27 = bf16[16,4096]{1,0:T(8,128)(2,1)S(1)} collective-permute-done((bf16[16,4096]{1,0:T(8,128)(2,1)S(1)}, bf16[16,4096]{1,0:T(8,128)(2,1)S(1)}, u32[]{:S(2)}, u32[]{:S(2)}) %collective-permute-start.27) | collective-permute-done | bytes 131104 | tf_op jit(solution)/shard_map/ppermute | solution.py:173
  84.8 0.7 pad_maximum_fusion.2
  (37 shorter events, 0.6 us)
Async XLA Ops:
  1.2 12.3 %collective-permute-start.3 = (bf16[16,4224]{1,0:T(8,128)(2,1)S(1)}, bf16[16,4224]{1,0:T(8,128)(2,1)S(1)}, u32[]{:S(2)}, u32[]{:S(2)}) collective-permute-start(bf16[16,4224]{1,0:T(8,128)(2,1)S(1)} %get-tuple-element.50), channel_id=1, source_target_pairs={{0,8},{1,9},{2,10},{3,11},{4,12},{5,13},{6,14},{7,15},{8,0},{9,1},... | collective-permute-start | bytes 405512 | tf_op jit(solution)/shard_map/ppermute | solution.py:173
  5.3 8.3 %collective-permute-start.2 = (bf16[16,4224]{1,0:T(8,128)(2,1)S(1)}, bf16[16,4224]{1,0:T(8,128)(2,1)S(1)}, u32[]{:S(2)}, u32[]{:S(2)}) collective-permute-start(bf16[16,4224]{1,0:T(8,128)(2,1)S(1)} %get-tuple-element.50), channel_id=1, source_target_pairs={{0,4},{1,5},{2,6},{3,7},{4,0},{5,1},{6,2},{7,3},{8,12},{9,13},{10,... | collective-permute-start | bytes 405512 | tf_op jit(solution)/shard_map/ppermute | solution.py:173
  6.8 6.7 %collective-permute-start = (bf16[16,4224]{1,0:T(8,128)(2,1)S(1)}, bf16[16,4224]{1,0:T(8,128)(2,1)S(1)}, u32[]{:S(2)}, u32[]{:S(2)}) collective-permute-start(bf16[16,4224]{1,0:T(8,128)(2,1)S(1)} %get-tuple-element.50), channel_id=1, source_target_pairs={{0,2},{1,3},{2,0},{3,1},{4,6},{5,7},{6,4},{7,5},{8,10},{9,11},{10,... | collective-permute-start | bytes 405512 | tf_op jit(solution)/shard_map/ppermute | solution.py:170
  8.4 6.1 %collective-permute-start.1 = (bf16[16,4224]{1,0:T(8,128)(2,1)S(1)}, bf16[16,4224]{1,0:T(8,128)(2,1)S(1)}, u32[]{:S(2)}, u32[]{:S(2)}) collective-permute-start(bf16[16,4224]{1,0:T(8,128)(2,1)S(1)} %get-tuple-element.57), channel_id=1, source_target_pairs={{0,2},{1,3},{2,0},{3,1},{4,6},{5,7},{6,4},{7,5},{8,10},{9,11},{10,... | collective-permute-start | bytes 405512 | tf_op jit(solution)/shard_map/ppermute | solution.py:170
  14.5 6.2 %collective-permute-start.4 = (bf16[16,4224]{1,0:T(8,128)(2,1)S(1)}, bf16[16,4224]{1,0:T(8,128)(2,1)S(1)}, u32[]{:S(2)}, u32[]{:S(2)}) collective-permute-start(bf16[16,4224]{1,0:T(8,128)(2,1)S(1)} %collective-permute-done.3), channel_id=1, source_target_pairs={{0,4},{1,5},{2,6},{3,7},{4,0},{5,1},{6,2},{7,3},{8,12},{9,13},{10,... | collective-permute-start | bytes 405512 | tf_op jit(solution)/shard_map/ppermute | solution.py:173
  15.0 9.3 %collective-permute-start.5 = (bf16[16,4224]{1,0:T(8,128)(2,1)S(1)}, bf16[16,4224]{1,0:T(8,128)(2,1)S(1)}, u32[]{:S(2)}, u32[]{:S(2)}) collective-permute-start(bf16[16,4224]{1,0:T(8,128)(2,1)S(1)} %collective-permute-done.2), channel_id=1, source_target_pairs={{0,2},{1,3},{2,0},{3,1},{4,6},{5,7},{6,4},{7,5},{8,10},{9,11},{10,... | collective-permute-start | bytes 405512 | tf_op jit(solution)/shard_map/ppermute | solution.py:170
  16.5 7.8 %collective-permute-start.6 = (bf16[16,4224]{1,0:T(8,128)(2,1)S(1)}, bf16[16,4224]{1,0:T(8,128)(2,1)S(1)}, u32[]{:S(2)}, u32[]{:S(2)}) collective-permute-start(bf16[16,4224]{1,0:T(8,128)(2,1)S(1)} %get-tuple-element.57), channel_id=1, source_target_pairs={{0,8},{1,9},{2,10},{3,11},{4,12},{5,13},{6,14},{7,15},{8,0},{9,1},... | collective-permute-start | bytes 405512 | tf_op jit(solution)/shard_map/ppermute | solution.py:173
  20.8 7.2 %collective-permute-start.8 = (bf16[32,4224]{1,0:T(8,128)(2,1)S(1)}, bf16[32,4224]{1,0:T(8,128)(2,1)S(1)}, u32[]{:S(2)}, u32[]{:S(2)}) collective-permute-start(bf16[32,4224]{1,0:T(8,128)(2,1)S(1)} %get-tuple-element.92), channel_id=1, source_target_pairs={{0,2},{1,3},{2,0},{3,1},{4,6},{5,7},{6,4},{7,5},{8,10},{9,11},{10,... | collective-permute-start | bytes 811016 | tf_op jit(solution)/shard_map/ppermute | solution.py:170
  21.5 11.7 %copy-start = (s32[16]{0:T(128)S(1)}, s32[16]{0:T(128)}, u32[]{:S(2)}) copy-start(s32[16]{0:T(128)} %flags_ref.3) | copy-start | bytes 196
  24.3 8.0 %collective-permute-start.11 = (bf16[16,4224]{1,0:T(8,128)(2,1)S(1)}, bf16[16,4224]{1,0:T(8,128)(2,1)S(1)}, u32[]{:S(2)}, u32[]{:S(2)}) collective-permute-start(bf16[16,4224]{1,0:T(8,128)(2,1)S(1)} %collective-permute-done.6), channel_id=1, source_target_pairs={{0,2},{1,3},{2,0},{3,1},{4,6},{5,7},{6,4},{7,5},{8,10},{9,11},{10,... | collective-permute-start | bytes 405512 | tf_op jit(solution)/shard_map/ppermute | solution.py:170
  25.8 6.5 %collective-permute-start.10 = (bf16[32,4224]{1,0:T(8,128)(2,1)S(1)}, bf16[32,4224]{1,0:T(8,128)(2,1)S(1)}, u32[]{:S(2)}, u32[]{:S(2)}) collective-permute-start(bf16[32,4224]{1,0:T(8,128)(2,1)S(1)} %pad_maximum_fusion.1), channel_id=1, source_target_pairs={{0,4},{1,5},{2,6},{3,7},{4,0},{5,1},{6,2},{7,3},{8,12},{9,13},{10,... | collective-permute-start | bytes 811016 | tf_op jit(solution)/shard_map/ppermute | solution.py:173
  27.9 4.4 %collective-permute-start.9 = (bf16[32,4224]{1,0:T(8,128)(2,1)S(1)}, bf16[32,4224]{1,0:T(8,128)(2,1)S(1)}, u32[]{:S(2)}, u32[]{:S(2)}) collective-permute-start(bf16[32,4224]{1,0:T(8,128)(2,1)S(1)} %collective-permute-done.8.refs_2_), channel_id=1, source_target_pairs={{0,1},{1,0},{2,3},{3,2},{4,5},{5,4},{6,7},{7,6},{8,9},{9,8},{10,11... | collective-permute-start | bytes 811016 | tf_op jit(solution)/shard_map/ppermute | solution.py:167
  28.0 5.2 %collective-permute-start.7 = (bf16[96,4224]{1,0:T(8,128)(2,1)S(1)}, bf16[96,4224]{1,0:T(8,128)(2,1)S(1)}, u32[]{:S(2)}, u32[]{:S(2)}) collective-permute-start(bf16[96,4224]{1,0:T(8,128)(2,1)S(1)} %constant_dynamic-update-slice_fusion.2.refs_0_), channel_id=1, source_target_pairs={{0,1},{1,0},{2,3},{3,2},{4,5},{5,4},{6,7},{7,6},{8,9},{9,8},{10,11... | collective-permute-start | bytes 2433032 | tf_op jit(solution)/shard_map/ppermute | solution.py:167
  32.4 9.0 %collective-permute-start.14 = (bf16[96,4224]{1,0:T(8,128)(2,1)S(1)}, bf16[96,4224]{1,0:T(8,128)(2,1)S(1)}, u32[]{:S(2)}, u32[]{:S(2)}) collective-permute-start(bf16[96,4224]{1,0:T(8,128)(2,1)S(1)} %constant_dynamic-update-slice_fusion.8.refs_0_), channel_id=1, source_target_pairs={{0,1},{1,0},{2,3},{3,2},{4,5},{5,4},{6,7},{7,6},{8,9},{9,8},{10,11... | collective-permute-start | bytes 2433032 | tf_op jit(solution)/shard_map/ppermute | solution.py:167
  32.5 8.9 %collective-permute-start.12 = (bf16[32,4224]{1,0:T(8,128)(2,1)S(1)}, bf16[32,4224]{1,0:T(8,128)(2,1)S(1)}, u32[]{:S(2)}, u32[]{:S(2)}) collective-permute-start(bf16[32,4224]{1,0:T(8,128)(2,1)S(1)} %collective-permute-done.10), channel_id=1, source_target_pairs={{0,2},{1,3},{2,0},{3,1},{4,6},{5,7},{6,4},{7,5},{8,10},{9,11},{10,... | collective-permute-start | bytes 811016 | tf_op jit(solution)/shard_map/ppermute | solution.py:170
  41.4 1.9 %collective-permute-start.15 = (bf16[64,4096]{1,0:T(8,128)(2,1)S(1)}, bf16[64,4096]{1,0:T(8,128)(2,1)S(1)}, u32[]{:S(2)}, u32[]{:S(2)}) collective-permute-start(bf16[64,4096]{1,0:T(8,128)(2,1)S(1)} %get-tuple-element.73), channel_id=1, source_target_pairs={{0,1},{1,0},{2,3},{3,2},{4,5},{5,4},{6,7},{7,6},{8,9},{9,8},{10,11... | collective-permute-start | bytes 1572872 | tf_op jit(solution)/shard_map/ppermute | solution.py:167
  41.4 2.7 %collective-permute-start.13 = (bf16[64,4096]{1,0:T(8,128)(2,1)S(1)}, bf16[64,4096]{1,0:T(8,128)(2,1)S(1)}, u32[]{:S(2)}, u32[]{:S(2)}) collective-permute-start(bf16[64,4096]{1,0:T(8,128)(2,1)S(1)} %get-tuple-element.70), channel_id=1, source_target_pairs={{0,1},{1,0},{2,3},{3,2},{4,5},{5,4},{6,7},{7,6},{8,9},{9,8},{10,11... | collective-permute-start | bytes 1572872 | tf_op jit(solution)/shard_map/ppermute | solution.py:167
  44.2 1.6 %collective-permute-start.17 = (bf16[32,4224]{1,0:T(8,128)(2,1)S(1)}, bf16[32,4224]{1,0:T(8,128)(2,1)S(1)}, u32[]{:S(2)}, u32[]{:S(2)}) collective-permute-start(bf16[32,4224]{1,0:T(8,128)(2,1)S(1)} %collective-permute-done.12.refs_2_), channel_id=1, source_target_pairs={{0,1},{1,0},{2,3},{3,2},{4,5},{5,4},{6,7},{7,6},{8,9},{9,8},{10,11... | collective-permute-start | bytes 811016 | tf_op jit(solution)/shard_map/ppermute | solution.py:167
  44.4 14.3 %collective-permute-start.16 = (bf16[64,4096]{1,0:T(8,128)(2,1)S(1)}, bf16[64,4096]{1,0:T(8,128)(2,1)S(1)}, u32[]{:S(2)}, u32[]{:S(2)}) collective-permute-start(bf16[64,4096]{1,0:T(8,128)(2,1)S(1)} %pad_maximum_fusion), channel_id=1, source_target_pairs={{0,2},{1,3},{2,0},{3,1},{4,6},{5,7},{6,4},{7,5},{8,10},{9,11},{10,... | collective-permute-start | bytes 1572872 | tf_op jit(solution)/shard_map/ppermute | solution.py:170
  51.4 7.3 %collective-permute-start.18 = (bf16[64,4096]{1,0:T(8,128)(2,1)S(1)}, bf16[64,4096]{1,0:T(8,128)(2,1)S(1)}, u32[]{:S(2)}, u32[]{:S(2)}) collective-permute-start(bf16[64,4096]{1,0:T(8,128)(2,1)S(1)} %get-tuple-element.81), channel_id=1, source_target_pairs={{0,1},{1,0},{2,3},{3,2},{4,5},{5,4},{6,7},{7,6},{8,9},{9,8},{10,11... | collective-permute-start | bytes 1572872 | tf_op jit(solution)/shard_map/ppermute | solution.py:167
  59.0 5.0 %collective-permute-start.19 = (bf16[16,4096]{1,0:T(8,128)(2,1)S(1)}, bf16[16,4096]{1,0:T(8,128)(2,1)S(1)}, u32[]{:S(2)}, u32[]{:S(2)}) collective-permute-start(bf16[16,4096]{1,0:T(8,128)(2,1)S(1)} %slice.175), channel_id=1, source_target_pairs={{0,4},{1,5},{2,6},{3,7},{4,0},{5,1},{6,2},{7,3},{8,12},{9,13},{10,... | collective-permute-start | bytes 393224 | tf_op jit(solution)/shard_map/ppermute | solution.py:173
  59.5 7.8 %collective-permute-start.22 = (bf16[64,4096]{1,0:T(8,128)(2,1)S(1)}, bf16[64,4096]{1,0:T(8,128)(2,1)S(1)}, u32[]{:S(2)}, u32[]{:S(2)}) collective-permute-start(bf16[64,4096]{1,0:T(8,128)(2,1)S(1)} %get-tuple-element.86), channel_id=1, source_target_pairs={{0,1},{1,0},{2,3},{3,2},{4,5},{5,4},{6,7},{7,6},{8,9},{9,8},{10,11... | collective-permute-start | bytes 1572872 | tf_op jit(solution)/shard_map/ppermute | solution.py:167
  59.5 8.7 %collective-permute-start.24 = (bf16[32,4096]{1,0:T(8,128)(2,1)S(1)}, bf16[32,4096]{1,0:T(8,128)(2,1)S(1)}, u32[]{:S(2)}, u32[]{:S(2)}) collective-permute-start(bf16[32,4096]{1,0:T(8,128)(2,1)S(1)} %fusion.3), channel_id=1, source_target_pairs={{0,2},{1,3},{2,0},{3,1},{4,6},{5,7},{6,4},{7,5},{8,10},{9,11},{10,... | collective-permute-start | bytes 786440 | tf_op jit(solution)/shard_map/ppermute | solution.py:170
  64.1 14.3 %collective-permute-start.21 = (bf16[16,4096]{1,0:T(8,128)(2,1)S(1)}, bf16[16,4096]{1,0:T(8,128)(2,1)S(1)}, u32[]{:S(2)}, u32[]{:S(2)}) collective-permute-start(bf16[16,4096]{1,0:T(8,128)(2,1)S(1)} %slice_add_fusion.11), channel_id=1, source_target_pairs={{0,8},{1,9},{2,10},{3,11},{4,12},{5,13},{6,14},{7,15},{8,0},{9,1},... | collective-permute-start | bytes 393224 | tf_op jit(solution)/shard_map/ppermute | solution.py:173
  65.5 12.9 %collective-permute-start.20 = (bf16[16,4096]{1,0:T(8,128)(2,1)S(1)}, bf16[16,4096]{1,0:T(8,128)(2,1)S(1)}, u32[]{:S(2)}, u32[]{:S(2)}) collective-permute-start(bf16[16,4096]{1,0:T(8,128)(2,1)S(1)} %slice.174), channel_id=1, source_target_pairs={{0,4},{1,5},{2,6},{3,7},{4,0},{5,1},{6,2},{7,3},{8,12},{9,13},{10,... | collective-permute-start | bytes 393224 | tf_op jit(solution)/shard_map/ppermute | solution.py:173
  68.4 6.8 %collective-permute-start.25 = (bf16[16,4096]{1,0:T(8,128)(2,1)S(1)}, bf16[16,4096]{1,0:T(8,128)(2,1)S(1)}, u32[]{:S(2)}, u32[]{:S(2)}) collective-permute-start(bf16[16,4096]{1,0:T(8,128)(2,1)S(1)} %slice.173), channel_id=1, source_target_pairs={{0,4},{1,5},{2,6},{3,7},{4,0},{5,1},{6,2},{7,3},{8,12},{9,13},{10,... | collective-permute-start | bytes 393224 | tf_op jit(solution)/shard_map/ppermute | solution.py:173
  70.1 7.7 %collective-permute-start.23 = (bf16[32,4096]{1,0:T(8,128)(2,1)S(1)}, bf16[32,4096]{1,0:T(8,128)(2,1)S(1)}, u32[]{:S(2)}, u32[]{:S(2)}) collective-permute-start(bf16[32,4096]{1,0:T(8,128)(2,1)S(1)} %fusion.2), channel_id=1, source_target_pairs={{0,2},{1,3},{2,0},{3,1},{4,6},{5,7},{6,4},{7,5},{8,10},{9,11},{10,... | collective-permute-start | bytes 786440 | tf_op jit(solution)/shard_map/ppermute | solution.py:170
  75.2 8.3 %collective-permute-start.26 = (bf16[16,4096]{1,0:T(8,128)(2,1)S(1)}, bf16[16,4096]{1,0:T(8,128)(2,1)S(1)}, u32[]{:S(2)}, u32[]{:S(2)}) collective-permute-start(bf16[16,4096]{1,0:T(8,128)(2,1)S(1)} %slice_add_fusion.9), channel_id=1, source_target_pairs={{0,8},{1,9},{2,10},{3,11},{4,12},{5,13},{6,14},{7,15},{8,0},{9,1},... | collective-permute-start | bytes 393224 | tf_op jit(solution)/shard_map/ppermute | solution.py:173
  77.9 6.8 %collective-permute-start.27 = (bf16[16,4096]{1,0:T(8,128)(2,1)S(1)}, bf16[16,4096]{1,0:T(8,128)(2,1)S(1)}, u32[]{:S(2)}, u32[]{:S(2)}) collective-permute-start(bf16[16,4096]{1,0:T(8,128)(2,1)S(1)} %slice.172), channel_id=1, source_target_pairs={{0,4},{1,5},{2,6},{3,7},{4,0},{5,1},{6,2},{7,3},{8,12},{9,13},{10,... | collective-permute-start | bytes 393224 | tf_op jit(solution)/shard_map/ppermute | solution.py:173

commit v11 on v10

--- a/solution.py
+++ b/solution.py
@@ -214,60 +214,60 @@
     last, near_close, crossed = lax.optimization_barrier((last, near_close, crossed))
     loaded += last
     line = jnp.concatenate([messages[0], *others, far, near_own[0], *near_close])
-    sources = [[line, swap_core(line), near_far, swap_core(near_far)]]
+    parts = [line, swap_core(line), near_far, swap_core(near_far)]
+    near_crossed = [swap_near(block) for block in crossed]
     wanted = places(strides)
     wanted += [middle ^ place for place in wanted]
     found = places([middle] + strides)
-    for step in range(1, steps):
-        block = crossed[step - 1]
-        near_block = swap_near(block)
-        line = jnp.concatenate([messages[step], block])
-        rest = []
-        for by in strides:
-            rest.append(after(swap_far(line, by), sources[0][3]))
-            line = jnp.concatenate([line, rest[-1]])
-        near_rest = swap_near(jnp.concatenate(rest))
-        line = jnp.concatenate([messages[step], block, *rest, near_own[step], near_block])
-        sources.append([line, swap_core(line), near_rest])
-    outputs, ready = [], [source[0] for source in sources]
+    outputs, ready = [], far
     for step in range(steps):
         plan = []
+        if step:
+            rest = jnp.concatenate(arrived)
+            line = jnp.concatenate([messages[step], crossed[step - 1], rest, near_own[step], near_crossed[step - 1], after(near_rest, ready)])
+            parts = [line, swap_core(line)]
         for core in range(2):
             if step:
-                at = [found.index(place) * tokens for place in wanted]
-                plan += [(core, row, row + tokens) for row in at]
-                for row in at:
-                    early = row < 2 * tokens
-                    row += half if early else -2 * tokens
-                    plan.append((core if early else 2 + core, row, row + tokens))
+                for side in range(2):
+                    at = [side * half + found.index(place) * tokens for place in wanted]
+                    plan += [(core, row, row + tokens) for row in at]
             else:
                 plan += [(core, 0, half + head), (2 + core, 0, head)]
-        parts = sources[step]
+        own, peer, other_low, other_high = run_expert(step > 0, flags, loaded, after(parts, ready), tuple(plan))
         if step:
-            parts = [*parts, swap_core(after(parts[2], ready))]
-        own, peer, other_low, other_high = run_expert(step > 0, flags, loaded, after(parts, ready), tuple(plan))
-        other_high = swap_core(other_high if step else after(other_high, sources[1][1:3]))
-        if step:
-            other_high = after(other_high, near)
-        other_high = other_high.astype(jnp.float32)
-        other_low = swap_core(after(other_low, near if step else sources[1][2]))
+            other_high = after(swap_core(other_high), near).astype(jnp.float32)
+            other_low = swap_core(after(other_low, near))
+        else:
+            arrived, line = [], jnp.concatenate([messages[1], crossed[0]])
+            for by in strides:
+                arrived.append(after(swap_far(line, by), other_low))
+                line = jnp.concatenate([line, arrived[-1]])
+            near_rest = swap_near(jnp.concatenate(arrived))
+            other_high, other_low = after((other_high, other_low), arrived)
+            other_high = swap_core(other_high).astype(jnp.float32)
+            other_low = swap_core(other_low)
         to_high = (peer[head:].astype(jnp.float32) + other_high[head:]).astype(jnp.bfloat16)
         other_low = after(other_low, to_high).astype(jnp.float32)
         to_low = (peer[:head].astype(jnp.float32) + other_low[head:]).astype(jnp.bfloat16)
         ready = to_high, to_low
         if step:
-            near = after(near, to_high).astype(jnp.float32)
-            high = collapse(high + near[head:])
-            low += after(near[:head], high)
-            high = swap_far(high.astype(jnp.bfloat16), middle)
-            outputs.append((collapse(low), high))
+            near = after(near, other_low).astype(jnp.float32)
+            high += near[head:]
+            low += near[:head]
+            for by in strides[::-1]:
+                keep = high.shape[0] // 2
+                sent = jnp.concatenate([low[keep:], high[keep:]]).astype(jnp.bfloat16)
+                sent = swap_far(sent, by).astype(jnp.float32)
+                low, high = low[:keep] + sent[:keep], high[:keep] + sent[keep:]
+            outputs.append((low, swap_far(high.astype(jnp.bfloat16), middle)))
         high = own[head:].astype(jnp.float32) + other_high[:head]
         low = own[:head].astype(jnp.float32) + other_low[:head]
         if step + 1 < steps:
             near = swap_near(jnp.concatenate([to_low, to_high]))
-    near = swap_near(to_low)
+    near_high = swap_near(to_high)
+    near = swap_near(after(to_low, near_high))
     outputs = [low + after(high, near).astype(jnp.float32) for low, high in outputs]
-    high = collapse(high + swap_near(to_high).astype(jnp.float32))
+    high = collapse(high + near_high.astype(jnp.float32))
     low += after(near, high).astype(jnp.float32)
     first = add(low[:tokens], swap_far(high.astype(jnp.bfloat16), middle))
     outputs.append(collapse(jnp.concatenate([first, low[tokens:]])))

time: 85.7 us -> 86.5 us (level)
    ppermute x11 -> x10, waiting for transfers between devices: 20.4 us -> 12.8 us  [swap_far(): lax.ppermute(x, 'expert', [(index(z, y, c), index(z ^ by, y, c)) for z, y...]
    ppermute x8 -> x7, waiting for transfers between devices: 2.66 us -> 6.43 us  [swap_core(): lax.ppermute(x, 'expert', [(index(z, y, c), index(z, y, 1 - c)) for z, y,...]
    ppermute x9, waiting for transfers between devices: 15 us -> 18.7 us  [swap_near(): lax.ppermute(x, 'expert', [(index(z, y, c), index(z, 1 - y, c)) for z, y,...]
    ppermute x11 -> x10, starting transfers between devices: 14 us -> 15.5 us  [swap_far(): lax.ppermute(x, 'expert', [(index(z, y, c), index(z ^ by, y, c)) for z, y...]
  transfers between devices with their start and end apart: 28 -> 26, of which waited for: 15 -> 16; matrix products, arithmetic and copies ran while one was open for 1% -> 2% of each run, Pallas kernels for 22% -> 22%
where the time goes in v11:
time: 86.5 us; the launch traced here: 86.3 us
  waiting for transfers between devices  37.9 us (44%)
  starting transfers between devices  25.9 us (30%)
  Pallas kernels  19.9 us (23%)
  other arithmetic  1.97 us (2%)
    ppermute x9, waiting for transfers between devices, swap_near(): lax.ppermute(x, 'expert', [(index(z, y, c), index(z, 1 - y, c)) for z, y,...  18.7 us
    ppermute x10, starting transfers between devices, swap_far(): lax.ppermute(x, 'expert', [(index(z, y, c), index(z ^ by, y, c)) for z, y...  15.5 us
    ppermute x10, waiting for transfers between devices, swap_far(): lax.ppermute(x, 'expert', [(index(z, y, c), index(z ^ by, y, c)) for z, y...  12.8 us
    pallas_call x2, Pallas kernels, run_expert(): pl.pallas_call(functools.partial(expert_kernel, swapped, count, plan), ou...  11.2 us
    ppermute x9, starting transfers between devices, swap_near(): lax.ppermute(x, 'expert', [(index(z, y, c), index(z, 1 - y, c)) for z, y,...  9.5 us
    pallas_call x2, Pallas kernels, load_weights(): pl.pallas_call(load_kernel, out_shape=[pltpu.VMEM(x.shape, x.dtype) for x...  7.42 us
    ppermute x7, waiting for transfers between devices, swap_core(): lax.ppermute(x, 'expert', [(index(z, y, c), index(z, y, 1 - c)) for z, y,...  6.43 us
  transfers between devices with their start and end apart: 26, of which 16 were waited for; matrix products, arithmetic and copies ran while one was open for 2% of the time, Pallas kernels for 22%

profile of v11, /device:TPU:0, one launch (start us, length us, event | category | flops | bytes accessed | tf_op | source)
XLA Modules:
  0.0 86.3 jit_solution(16681200215319901121)
XLA Ops:
  0.0 1.2 %messages.1 = (bf16[16,4224]{1,0:T(8,128)(2,1)S(1)}, bf16[16,4224]{1,0:T(8,128)(2,1)S(1)}) custom-call(bf16[2,16,4096]{2,1,0:T(8,128)(2,1)} %states_ref.1, s32[2,8,16]{2,1,0:T(8,128)} %bitcast.12, f32[2,8,16]{2,1,0:T(8,128)} %bitcast.13), custom_call_target="tpu_custom_call" | custom-call | tf_op jit(solution)/shard_map/messages/pallas_call | solution.py:49
  1.2 4.0 %collective-permute-start.3 = (bf16[16,4224]{1,0:T(8,128)(2,1)S(1)}, bf16[16,4224]{1,0:T(8,128)(2,1)S(1)}, u32[]{:S(2)}, u32[]{:S(2)}) collective-permute-start(bf16[16,4224]{1,0:T(8,128)(2,1)S(1)} %get-tuple-element.48), channel_id=1, source_target_pairs={{0,8},{1,9},{2,10},{3,11},{4,12},{5,13},{6,14},{7,15},{8,0},{9,1},... | collective-permute-start | bytes 405512 | tf_op jit(solution)/shard_map/ppermute | solution.py:173
  5.3 1.6 %collective-permute-start.2 = (bf16[16,4224]{1,0:T(8,128)(2,1)S(1)}, bf16[16,4224]{1,0:T(8,128)(2,1)S(1)}, u32[]{:S(2)}, u32[]{:S(2)}) collective-permute-start(bf16[16,4224]{1,0:T(8,128)(2,1)S(1)} %get-tuple-element.48), channel_id=1, source_target_pairs={{0,4},{1,5},{2,6},{3,7},{4,0},{5,1},{6,2},{7,3},{8,12},{9,13},{10,... | collective-permute-start | bytes 405512 | tf_op jit(solution)/shard_map/ppermute | solution.py:173
  6.8 1.5 %collective-permute-start = (bf16[16,4224]{1,0:T(8,128)(2,1)S(1)}, bf16[16,4224]{1,0:T(8,128)(2,1)S(1)}, u32[]{:S(2)}, u32[]{:S(2)}) collective-permute-start(bf16[16,4224]{1,0:T(8,128)(2,1)S(1)} %get-tuple-element.48), channel_id=1, source_target_pairs={{0,2},{1,3},{2,0},{3,1},{4,6},{5,7},{6,4},{7,5},{8,10},{9,11},{10,... | collective-permute-start | bytes 405512 | tf_op jit(solution)/shard_map/ppermute | solution.py:170
  8.4 0.5 collective-permute-start.1
  8.9 4.6 %load_weights.2 = (bf16[4096,768]{1,0:T(8,128)(2,1)S(1)}, bf16[4096,768]{1,0:T(8,128)(2,1)S(1)}) custom-call(bf16[4096,768]{1,0:T(8,128)(2,1)} %bitcast.9, bf16[4096,768]{1,0:T(8,128)(2,1)} %bitcast.10), custom_call_target="tpu_custom_call" | custom-call | tf_op jit(solution)/shard_map/load_weights/pallas_call | solution.py:73
  13.6 0.0 collective-permute-done.2
  13.6 0.0 collective-permute-done
  13.6 0.9 %collective-permute-done.1 = bf16[16,4224]{1,0:T(8,128)(2,1)S(1)} collective-permute-done((bf16[16,4224]{1,0:T(8,128)(2,1)S(1)}, bf16[16,4224]{1,0:T(8,128)(2,1)S(1)}, u32[]{:S(2)}, u32[]{:S(2)}) %collective-permute-start.1) | collective-permute-done | bytes 135200 | tf_op jit(solution)/shard_map/ppermute | solution.py:170
  14.5 0.4 collective-permute-start.4
  15.0 1.5 %collective-permute-start.5 = (bf16[16,4224]{1,0:T(8,128)(2,1)S(1)}, bf16[16,4224]{1,0:T(8,128)(2,1)S(1)}, u32[]{:S(2)}, u32[]{:S(2)}) collective-permute-start(bf16[16,4224]{1,0:T(8,128)(2,1)S(1)} %collective-permute-done.2), channel_id=1, source_target_pairs={{0,2},{1,3},{2,0},{3,1},{4,6},{5,7},{6,4},{7,5},{8,10},{9,11},{10,... | collective-permute-start | bytes 405512 | tf_op jit(solution)/shard_map/ppermute | solution.py:170
  16.5 1.0 %collective-permute-start.6 = (bf16[16,4224]{1,0:T(8,128)(2,1)S(1)}, bf16[16,4224]{1,0:T(8,128)(2,1)S(1)}, u32[]{:S(2)}, u32[]{:S(2)}) collective-permute-start(bf16[16,4224]{1,0:T(8,128)(2,1)S(1)} %get-tuple-element.55), channel_id=1, source_target_pairs={{0,8},{1,9},{2,10},{3,11},{4,12},{5,13},{6,14},{7,15},{8,0},{9,1},... | collective-permute-start | bytes 405512 | tf_op jit(solution)/shard_map/ppermute | solution.py:173
  17.6 3.2 %collective-permute-done.4 = bf16[16,4224]{1,0:T(8,128)(2,1)S(1)} collective-permute-done((bf16[16,4224]{1,0:T(8,128)(2,1)S(1)}, bf16[16,4224]{1,0:T(8,128)(2,1)S(1)}, u32[]{:S(2)}, u32[]{:S(2)}) %collective-permute-start.4) | collective-permute-done | bytes 135200 | tf_op jit(solution)/shard_map/ppermute | solution.py:173
  20.8 0.7 collective-permute-start.8
  21.5 2.8 %load_weights.3.down_ref = bf16[768,4096]{1,0:T(8,128)(2,1)S(1)} custom-call(bf16[768,4096]{1,0:T(8,128)(2,1)} %bitcast.11), custom_call_target="tpu_custom_call" | custom-call | tf_op jit(solution)/shard_map/load_weights/pallas_call | solution.py:73
  24.3 0.0 copy-start
  24.3 0.0 collective-permute-done.6
  24.3 0.0 collective-permute-done.5
  24.3 0.1 collective-permute-start.7
  24.5 1.4 %collective-permute-start.14 = (bf16[16,4224]{1,0:T(8,128)(2,1)S(1)}, bf16[16,4224]{1,0:T(8,128)(2,1)S(1)}, u32[]{:S(2)}, u32[]{:S(2)}) collective-permute-start(bf16[16,4224]{1,0:T(8,128)(2,1)S(1)} %collective-permute-done.6), channel_id=1, source_target_pairs={{0,2},{1,3},{2,0},{3,1},{4,6},{5,7},{6,4},{7,5},{8,10},{9,11},{10,... | collective-permute-start | bytes 405512 | tf_op jit(solution)/shard_map/ppermute | solution.py:170
  25.9 1.4 %collective-permute-done.8.refs_2_ = bf16[32,4224]{1,0:T(8,128)(2,1)S(1)} collective-permute-done((bf16[32,4224]{1,0:T(8,128)(2,1)S(1)}, bf16[32,4224]{1,0:T(8,128)(2,1)S(1)}, u32[]{:S(2)}, u32[]{:S(2)}) %collective-permute-start.8) | collective-permute-done | bytes 270368 | tf_op jit(solution)/shard_map/ppermute | solution.py:170
  27.3 0.2 collective-permute-start.10
  27.5 1.3 %collective-permute-done.9.refs_3_ = bf16[32,4224]{1,0:T(8,128)(2,1)S(1)} collective-permute-done((bf16[32,4224]{1,0:T(8,128)(2,1)S(1)}, bf16[32,4224]{1,0:T(8,128)(2,1)S(1)}, u32[]{:S(2)}, u32[]{:S(2)}) %collective-permute-start.9) | collective-permute-done | bytes 270368 | tf_op jit(solution)/shard_map/ppermute | solution.py:167
  28.8 5.6 %expert.2 = (bf16[64,4096]{1,0:T(8,128)(2,1)S(1)}, bf16[64,4096]{1,0:T(8,128)(2,1)S(1)}, bf16[64,4096]{1,0:T(8,128)(2,1)S(1)}, bf16[64,4096]{1,0:T(8,128)(2,1)S(1)}) custom-call(s32[16]{0:T(128)S(1)} %copy-done, bf16[4096,768]{1,0:T(8,128)(2,1)S(1)} %get-tuple-element.50.gate_ref, bf16[4096,768]{1,0:T(8,128)(2,1)S(1)} %get-tuple-element.51.up_ref, ...), custom_call_target="tpu_custom_call" | custom-call | flops 4831838208 | bytes 4194304 | tf_op jit(solution)/shard_map/expert/pallas_call | solution.py:123
  34.5 1.8 %collective-permute-done.10 = bf16[32,4224]{1,0:T(8,128)(2,1)S(1)} collective-permute-done((bf16[32,4224]{1,0:T(8,128)(2,1)S(1)}, bf16[32,4224]{1,0:T(8,128)(2,1)S(1)}, u32[]{:S(2)}, u32[]{:S(2)}) %collective-permute-start.10) | collective-permute-done | bytes 270368 | tf_op jit(solution)/shard_map/ppermute | solution.py:173
  36.3 0.6 collective-permute-start.15
  36.9 0.1 collective-permute-start.11
  37.0 0.5 collective-permute-start.12
  37.6 2.1 %collective-permute-done.12 = bf16[64,4096]{1,0:T(8,128)(2,1)S(1)} collective-permute-done((bf16[64,4096]{1,0:T(8,128)(2,1)S(1)}, bf16[64,4096]{1,0:T(8,128)(2,1)S(1)}, u32[]{:S(2)}, u32[]{:S(2)}) %collective-permute-start.12) | collective-permute-done | bytes 524320 | tf_op jit(solution)/shard_map/ppermute | solution.py:167
  39.7 0.1 convert_element_type.81
  39.7 0.1 fusion.5
  39.8 0.1 convert_element_type.83
  39.9 0.1 fusion.4
  39.9 4.4 %collective-permute-done.15 = bf16[32,4224]{1,0:T(8,128)(2,1)S(1)} collective-permute-done((bf16[32,4224]{1,0:T(8,128)(2,1)S(1)}, bf16[32,4224]{1,0:T(8,128)(2,1)S(1)}, u32[]{:S(2)}, u32[]{:S(2)}) %collective-permute-start.15) | collective-permute-done | bytes 270368 | tf_op jit(solution)/shard_map/ppermute | solution.py:170
  44.4 0.1 collective-permute-start.16
  44.5 0.7 collective-permute-start.13
  45.2 1.9 %collective-permute-done.16.refs_1_ = bf16[128,4224]{1,0:T(8,128)(2,1)S(1)} collective-permute-done((bf16[128,4224]{1,0:T(8,128)(2,1)S(1)}, bf16[128,4224]{1,0:T(8,128)(2,1)S(1)}, u32[]{:S(2)}, u32[]{:S(2)}) %collective-permute-start.16) | collective-permute-done | bytes 1081376 | tf_op jit(solution)/shard_map/ppermute | solution.py:167
  47.2 5.6 %expert.3 = (bf16[64,4096]{1,0:T(8,128)(2,1)S(1)}, bf16[64,4096]{1,0:T(8,128)(2,1)S(1)}, bf16[64,4096]{1,0:T(8,128)(2,1)S(1)}, bf16[64,4096]{1,0:T(8,128)(2,1)S(1)}) custom-call(s32[16]{0:T(128)S(1)} %copy-done, bf16[4096,768]{1,0:T(8,128)(2,1)S(1)} %get-tuple-element.50.gate_ref, bf16[4096,768]{1,0:T(8,128)(2,1)S(1)} %get-tuple-element.51.up_ref, ...), custom_call_target="tpu_custom_call" | custom-call | flops 4831838208 | bytes 4194304 | tf_op jit(solution)/shard_map/expert/pallas_call | solution.py:123
  52.8 0.2 collective-permute-start.18
  53.0 5.9 %collective-permute-done.13 = bf16[64,4096]{1,0:T(8,128)(2,1)S(1)} collective-permute-done((bf16[64,4096]{1,0:T(8,128)(2,1)S(1)}, bf16[64,4096]{1,0:T(8,128)(2,1)S(1)}, u32[]{:S(2)}, u32[]{:S(2)}) %collective-permute-start.13) | collective-permute-done | bytes 524320 | tf_op jit(solution)/shard_map/ppermute | solution.py:170
  58.9 0.0 collective-permute-start.17
  58.9 0.1 convert_element_type.87
  59.0 0.1 fusion.3
  59.1 0.7 collective-permute-start.21
  59.8 1.1 %collective-permute-done.17 = bf16[64,4096]{1,0:T(8,128)(2,1)S(1)} collective-permute-done((bf16[64,4096]{1,0:T(8,128)(2,1)S(1)}, bf16[64,4096]{1,0:T(8,128)(2,1)S(1)}, u32[]{:S(2)}, u32[]{:S(2)}) %collective-permute-start.17) | collective-permute-done | bytes 524320 | tf_op jit(solution)/shard_map/ppermute | solution.py:167
  60.8 0.1 convert_element_type.89
  60.9 0.1 fusion.2
  61.0 0.1 convert_element_type.90
  61.0 0.2 slice_add_fusion.5
  61.3 0.5 collective-permute-start.19
  61.8 6.0 %collective-permute-done.21 = bf16[32,4096]{1,0:T(8,128)(2,1)S(1)} collective-permute-done((bf16[32,4096]{1,0:T(8,128)(2,1)S(1)}, bf16[32,4096]{1,0:T(8,128)(2,1)S(1)}, u32[]{:S(2)}, u32[]{:S(2)}) %collective-permute-start.21) | collective-permute-done | bytes 262176 | tf_op jit(solution)/shard_map/ppermute | solution.py:170
  67.8 0.1 fusion
  68.0 0.5 collective-permute-start.23
  68.4 1.7 %collective-permute-start.22 = (bf16[32,4096]{1,0:T(8,128)(2,1)S(1)}, bf16[32,4096]{1,0:T(8,128)(2,1)S(1)}, u32[]{:S(2)}, u32[]{:S(2)}) collective-permute-start(bf16[32,4096]{1,0:T(8,128)(2,1)S(1)} %fusion.2), channel_id=1, source_target_pairs={{0,2},{1,3},{2,0},{3,1},{4,6},{5,7},{6,4},{7,5},{8,10},{9,11},{10,... | collective-permute-start | bytes 786440 | tf_op jit(solution)/shard_map/ppermute | solution.py:170
  70.3 2.8 %collective-permute-start.20 = (bf16[16,4096]{1,0:T(8,128)(2,1)S(1)}, bf16[16,4096]{1,0:T(8,128)(2,1)S(1)}, u32[]{:S(2)}, u32[]{:S(2)}) collective-permute-start(bf16[16,4096]{1,0:T(8,128)(2,1)S(1)} %fusion.6), channel_id=1, source_target_pairs={{0,8},{1,9},{2,10},{3,11},{4,12},{5,13},{6,14},{7,15},{8,0},{9,1},... | collective-permute-start | bytes 393224 | tf_op jit(solution)/shard_map/ppermute | solution.py:173
  73.0 0.2 collective-permute-done.23
  73.3 2.7 %collective-permute-start.24 = (bf16[16,4096]{1,0:T(8,128)(2,1)S(1)}, bf16[16,4096]{1,0:T(8,128)(2,1)S(1)}, u32[]{:S(2)}, u32[]{:S(2)}) collective-permute-start(bf16[16,4096]{1,0:T(8,128)(2,1)S(1)} %slice_add_fusion.10), channel_id=1, source_target_pairs={{0,8},{1,9},{2,10},{3,11},{4,12},{5,13},{6,14},{7,15},{8,0},{9,1},... | collective-permute-start | bytes 393224 | tf_op jit(solution)/shard_map/ppermute | solution.py:173
  76.0 0.1 collective-permute-done.22
  76.1 0.1 fusion.1
  76.2 1.7 %collective-permute-start.25 = (bf16[16,4096]{1,0:T(8,128)(2,1)S(1)}, bf16[16,4096]{1,0:T(8,128)(2,1)S(1)}, u32[]{:S(2)}, u32[]{:S(2)}) collective-permute-start(bf16[16,4096]{1,0:T(8,128)(2,1)S(1)} %slice.189), channel_id=1, source_target_pairs={{0,4},{1,5},{2,6},{3,7},{4,0},{5,1},{6,2},{7,3},{8,12},{9,13},{10,... | collective-permute-start | bytes 393224 | tf_op jit(solution)/shard_map/ppermute | solution.py:173
  77.9 4.6 %collective-permute-done.20 = bf16[16,4096]{1,0:T(8,128)(2,1)S(1)} collective-permute-done((bf16[16,4096]{1,0:T(8,128)(2,1)S(1)}, bf16[16,4096]{1,0:T(8,128)(2,1)S(1)}, u32[]{:S(2)}, u32[]{:S(2)}) %collective-permute-start.20) | collective-permute-done | bytes 131104 | tf_op jit(solution)/shard_map/ppermute | solution.py:173
  82.5 1.9 %collective-permute-done.24.second_ref = bf16[16,4096]{1,0:T(8,128)(2,1)S(1)} collective-permute-done((bf16[16,4096]{1,0:T(8,128)(2,1)S(1)}, bf16[16,4096]{1,0:T(8,128)(2,1)S(1)}, u32[]{:S(2)}, u32[]{:S(2)}) %collective-permute-start.24) | collective-permute-done | bytes 131104 | tf_op jit(solution)/shard_map/ppermute | solution.py:173
  84.4 1.1 %collective-permute-done.25 = bf16[16,4096]{1,0:T(8,128)(2,1)S(1)} collective-permute-done((bf16[16,4096]{1,0:T(8,128)(2,1)S(1)}, bf16[16,4096]{1,0:T(8,128)(2,1)S(1)}, u32[]{:S(2)}, u32[]{:S(2)}) %collective-permute-start.25) | collective-permute-done | bytes 131104 | tf_op jit(solution)/shard_map/ppermute | solution.py:173
  85.6 0.7 pad_maximum_fusion.3
  (34 shorter events, 0.6 us)
Async XLA Ops:
  1.2 12.3 %collective-permute-start.3 = (bf16[16,4224]{1,0:T(8,128)(2,1)S(1)}, bf16[16,4224]{1,0:T(8,128)(2,1)S(1)}, u32[]{:S(2)}, u32[]{:S(2)}) collective-permute-start(bf16[16,4224]{1,0:T(8,128)(2,1)S(1)} %get-tuple-element.48), channel_id=1, source_target_pairs={{0,8},{1,9},{2,10},{3,11},{4,12},{5,13},{6,14},{7,15},{8,0},{9,1},... | collective-permute-start | bytes 405512 | tf_op jit(solution)/shard_map/ppermute | solution.py:173
  5.3 8.3 %collective-permute-start.2 = (bf16[16,4224]{1,0:T(8,128)(2,1)S(1)}, bf16[16,4224]{1,0:T(8,128)(2,1)S(1)}, u32[]{:S(2)}, u32[]{:S(2)}) collective-permute-start(bf16[16,4224]{1,0:T(8,128)(2,1)S(1)} %get-tuple-element.48), channel_id=1, source_target_pairs={{0,4},{1,5},{2,6},{3,7},{4,0},{5,1},{6,2},{7,3},{8,12},{9,13},{10,... | collective-permute-start | bytes 405512 | tf_op jit(solution)/shard_map/ppermute | solution.py:173
  6.8 6.7 %collective-permute-start = (bf16[16,4224]{1,0:T(8,128)(2,1)S(1)}, bf16[16,4224]{1,0:T(8,128)(2,1)S(1)}, u32[]{:S(2)}, u32[]{:S(2)}) collective-permute-start(bf16[16,4224]{1,0:T(8,128)(2,1)S(1)} %get-tuple-element.48), channel_id=1, source_target_pairs={{0,2},{1,3},{2,0},{3,1},{4,6},{5,7},{6,4},{7,5},{8,10},{9,11},{10,... | collective-permute-start | bytes 405512 | tf_op jit(solution)/shard_map/ppermute | solution.py:170
  8.4 6.1 %collective-permute-start.1 = (bf16[16,4224]{1,0:T(8,128)(2,1)S(1)}, bf16[16,4224]{1,0:T(8,128)(2,1)S(1)}, u32[]{:S(2)}, u32[]{:S(2)}) collective-permute-start(bf16[16,4224]{1,0:T(8,128)(2,1)S(1)} %get-tuple-element.55), channel_id=1, source_target_pairs={{0,2},{1,3},{2,0},{3,1},{4,6},{5,7},{6,4},{7,5},{8,10},{9,11},{10,... | collective-permute-start | bytes 405512 | tf_op jit(solution)/shard_map/ppermute | solution.py:170
  14.5 6.2 %collective-permute-start.4 = (bf16[16,4224]{1,0:T(8,128)(2,1)S(1)}, bf16[16,4224]{1,0:T(8,128)(2,1)S(1)}, u32[]{:S(2)}, u32[]{:S(2)}) collective-permute-start(bf16[16,4224]{1,0:T(8,128)(2,1)S(1)} %collective-permute-done.3), channel_id=1, source_target_pairs={{0,4},{1,5},{2,6},{3,7},{4,0},{5,1},{6,2},{7,3},{8,12},{9,13},{10,... | collective-permute-start | bytes 405512 | tf_op jit(solution)/shard_map/ppermute | solution.py:173
  15.0 9.3 %collective-permute-start.5 = (bf16[16,4224]{1,0:T(8,128)(2,1)S(1)}, bf16[16,4224]{1,0:T(8,128)(2,1)S(1)}, u32[]{:S(2)}, u32[]{:S(2)}) collective-permute-start(bf16[16,4224]{1,0:T(8,128)(2,1)S(1)} %collective-permute-done.2), channel_id=1, source_target_pairs={{0,2},{1,3},{2,0},{3,1},{4,6},{5,7},{6,4},{7,5},{8,10},{9,11},{10,... | collective-permute-start | bytes 405512 | tf_op jit(solution)/shard_map/ppermute | solution.py:170
  16.5 7.8 %collective-permute-start.6 = (bf16[16,4224]{1,0:T(8,128)(2,1)S(1)}, bf16[16,4224]{1,0:T(8,128)(2,1)S(1)}, u32[]{:S(2)}, u32[]{:S(2)}) collective-permute-start(bf16[16,4224]{1,0:T(8,128)(2,1)S(1)} %get-tuple-element.55), channel_id=1, source_target_pairs={{0,8},{1,9},{2,10},{3,11},{4,12},{5,13},{6,14},{7,15},{8,0},{9,1},... | collective-permute-start | bytes 405512 | tf_op jit(solution)/shard_map/ppermute | solution.py:173
  20.8 6.5 %collective-permute-start.8 = (bf16[32,4224]{1,0:T(8,128)(2,1)S(1)}, bf16[32,4224]{1,0:T(8,128)(2,1)S(1)}, u32[]{:S(2)}, u32[]{:S(2)}) collective-permute-start(bf16[32,4224]{1,0:T(8,128)(2,1)S(1)} %get-tuple-element.90), channel_id=1, source_target_pairs={{0,2},{1,3},{2,0},{3,1},{4,6},{5,7},{6,4},{7,5},{8,10},{9,11},{10,... | collective-permute-start | bytes 811016 | tf_op jit(solution)/shard_map/ppermute | solution.py:170
  24.3 4.6 %copy-start = (s32[16]{0:T(128)S(1)}, s32[16]{0:T(128)}, u32[]{:S(2)}) copy-start(s32[16]{0:T(128)} %flags_ref.3) | copy-start | bytes 196
  24.3 4.5 %collective-permute-start.7 = (bf16[96,4224]{1,0:T(8,128)(2,1)S(1)}, bf16[96,4224]{1,0:T(8,128)(2,1)S(1)}, u32[]{:S(2)}, u32[]{:S(2)}) collective-permute-start(bf16[96,4224]{1,0:T(8,128)(2,1)S(1)} %constant_dynamic-update-slice_fusion.2.refs_0_), channel_id=1, source_target_pairs={{0,1},{1,0},{2,3},{3,2},{4,5},{5,4},{6,7},{7,6},{8,9},{9,8},{10,11... | collective-permute-start | bytes 2433032 | tf_op jit(solution)/shard_map/ppermute | solution.py:167
  24.5 13.1 %collective-permute-start.14 = (bf16[16,4224]{1,0:T(8,128)(2,1)S(1)}, bf16[16,4224]{1,0:T(8,128)(2,1)S(1)}, u32[]{:S(2)}, u32[]{:S(2)}) collective-permute-start(bf16[16,4224]{1,0:T(8,128)(2,1)S(1)} %collective-permute-done.6), channel_id=1, source_target_pairs={{0,2},{1,3},{2,0},{3,1},{4,6},{5,7},{6,4},{7,5},{8,10},{9,11},{10,... | collective-permute-start | bytes 405512 | tf_op jit(solution)/shard_map/ppermute | solution.py:170
  27.3 1.5 %collective-permute-start.9 = (bf16[32,4224]{1,0:T(8,128)(2,1)S(1)}, bf16[32,4224]{1,0:T(8,128)(2,1)S(1)}, u32[]{:S(2)}, u32[]{:S(2)}) collective-permute-start(bf16[32,4224]{1,0:T(8,128)(2,1)S(1)} %collective-permute-done.8.refs_2_), channel_id=1, source_target_pairs={{0,1},{1,0},{2,3},{3,2},{4,5},{5,4},{6,7},{7,6},{8,9},{9,8},{10,11... | collective-permute-start | bytes 811016 | tf_op jit(solution)/shard_map/ppermute | solution.py:167
  27.3 9.0 %collective-permute-start.10 = (bf16[32,4224]{1,0:T(8,128)(2,1)S(1)}, bf16[32,4224]{1,0:T(8,128)(2,1)S(1)}, u32[]{:S(2)}, u32[]{:S(2)}) collective-permute-start(bf16[32,4224]{1,0:T(8,128)(2,1)S(1)} %pad_maximum_fusion.1), channel_id=1, source_target_pairs={{0,4},{1,5},{2,6},{3,7},{4,0},{5,1},{6,2},{7,3},{8,12},{9,13},{10,... | collective-permute-start | bytes 811016 | tf_op jit(solution)/shard_map/ppermute | solution.py:173
  36.3 8.1 %collective-permute-start.15 = (bf16[32,4224]{1,0:T(8,128)(2,1)S(1)}, bf16[32,4224]{1,0:T(8,128)(2,1)S(1)}, u32[]{:S(2)}, u32[]{:S(2)}) collective-permute-start(bf16[32,4224]{1,0:T(8,128)(2,1)S(1)} %collective-permute-done.10), channel_id=1, source_target_pairs={{0,2},{1,3},{2,0},{3,1},{4,6},{5,7},{6,4},{7,5},{8,10},{9,11},{10,... | collective-permute-start | bytes 811016 | tf_op jit(solution)/shard_map/ppermute | solution.py:170
  36.9 2.9 %collective-permute-start.11 = (bf16[64,4096]{1,0:T(8,128)(2,1)S(1)}, bf16[64,4096]{1,0:T(8,128)(2,1)S(1)}, u32[]{:S(2)}, u32[]{:S(2)}) collective-permute-start(bf16[64,4096]{1,0:T(8,128)(2,1)S(1)} %get-tuple-element.68), channel_id=1, source_target_pairs={{0,1},{1,0},{2,3},{3,2},{4,5},{5,4},{6,7},{7,6},{8,9},{9,8},{10,11... | collective-permute-start | bytes 1572872 | tf_op jit(solution)/shard_map/ppermute | solution.py:167
  37.0 2.6 %collective-permute-start.12 = (bf16[64,4096]{1,0:T(8,128)(2,1)S(1)}, bf16[64,4096]{1,0:T(8,128)(2,1)S(1)}, u32[]{:S(2)}, u32[]{:S(2)}) collective-permute-start(bf16[64,4096]{1,0:T(8,128)(2,1)S(1)} %get-tuple-element.70), channel_id=1, source_target_pairs={{0,1},{1,0},{2,3},{3,2},{4,5},{5,4},{6,7},{7,6},{8,9},{9,8},{10,11... | collective-permute-start | bytes 1572872 | tf_op jit(solution)/shard_map/ppermute | solution.py:167
  44.4 2.8 %collective-permute-start.16 = (bf16[128,4224]{1,0:T(8,128)(2,1)S(1)}, bf16[128,4224]{1,0:T(8,128)(2,1)S(1)}, u32[]{:S(2)}, u32[]{:S(2)}) collective-permute-start(bf16[128,4224]{1,0:T(8,128)(2,1)S(1)} %constant_dynamic-update-slice_fusion.8.refs_0_), channel_id=1, source_target_pairs={{0,1},{1,0},{2,3},{3,2},{4,5},{5,4},{6,7},{7,6},{8,9},{9,8},{10,11... | collective-permute-start | bytes 3244040 | tf_op jit(solution)/shard_map/ppermute | solution.py:167
  44.5 14.4 %collective-permute-start.13 = (bf16[64,4096]{1,0:T(8,128)(2,1)S(1)}, bf16[64,4096]{1,0:T(8,128)(2,1)S(1)}, u32[]{:S(2)}, u32[]{:S(2)}) collective-permute-start(bf16[64,4096]{1,0:T(8,128)(2,1)S(1)} %pad_maximum_fusion), channel_id=1, source_target_pairs={{0,2},{1,3},{2,0},{3,1},{4,6},{5,7},{6,4},{7,5},{8,10},{9,11},{10,... | collective-permute-start | bytes 1572872 | tf_op jit(solution)/shard_map/ppermute | solution.py:170
  52.8 6.1 %collective-permute-start.18 = (bf16[64,4096]{1,0:T(8,128)(2,1)S(1)}, bf16[64,4096]{1,0:T(8,128)(2,1)S(1)}, u32[]{:S(2)}, u32[]{:S(2)}) collective-permute-start(bf16[64,4096]{1,0:T(8,128)(2,1)S(1)} %get-tuple-element.79), channel_id=1, source_target_pairs={{0,1},{1,0},{2,3},{3,2},{4,5},{5,4},{6,7},{7,6},{8,9},{9,8},{10,11... | collective-permute-start | bytes 1572872 | tf_op jit(solution)/shard_map/ppermute | solution.py:167
  58.9 1.9 %collective-permute-start.17 = (bf16[64,4096]{1,0:T(8,128)(2,1)S(1)}, bf16[64,4096]{1,0:T(8,128)(2,1)S(1)}, u32[]{:S(2)}, u32[]{:S(2)}) collective-permute-start(bf16[64,4096]{1,0:T(8,128)(2,1)S(1)} %get-tuple-element.77), channel_id=1, source_target_pairs={{0,1},{1,0},{2,3},{3,2},{4,5},{5,4},{6,7},{7,6},{8,9},{9,8},{10,11... | collective-permute-start | bytes 1572872 | tf_op jit(solution)/shard_map/ppermute | solution.py:167
  59.1 8.8 %collective-permute-start.21 = (bf16[32,4096]{1,0:T(8,128)(2,1)S(1)}, bf16[32,4096]{1,0:T(8,128)(2,1)S(1)}, u32[]{:S(2)}, u32[]{:S(2)}) collective-permute-start(bf16[32,4096]{1,0:T(8,128)(2,1)S(1)} %fusion.3), channel_id=1, source_target_pairs={{0,2},{1,3},{2,0},{3,1},{4,6},{5,7},{6,4},{7,5},{8,10},{9,11},{10,... | collective-permute-start | bytes 786440 | tf_op jit(solution)/shard_map/ppermute | solution.py:170
  61.3 8.9 %collective-permute-start.19 = (bf16[32,4096]{1,0:T(8,128)(2,1)S(1)}, bf16[32,4096]{1,0:T(8,128)(2,1)S(1)}, u32[]{:S(2)}, u32[]{:S(2)}) collective-permute-start(bf16[32,4096]{1,0:T(8,128)(2,1)S(1)} %pad_maximum_fusion.2), channel_id=1, source_target_pairs={{0,4},{1,5},{2,6},{3,7},{4,0},{5,1},{6,2},{7,3},{8,12},{9,13},{10,... | collective-permute-start | bytes 786440 | tf_op jit(solution)/shard_map/ppermute | solution.py:173
  68.0 5.3 %collective-permute-start.23 = (bf16[16,4096]{1,0:T(8,128)(2,1)S(1)}, bf16[16,4096]{1,0:T(8,128)(2,1)S(1)}, u32[]{:S(2)}, u32[]{:S(2)}) collective-permute-start(bf16[16,4096]{1,0:T(8,128)(2,1)S(1)} %slice.190), channel_id=1, source_target_pairs={{0,4},{1,5},{2,6},{3,7},{4,0},{5,1},{6,2},{7,3},{8,12},{9,13},{10,... | collective-permute-start | bytes 393224 | tf_op jit(solution)/shard_map/ppermute | solution.py:173
  68.4 7.7 %collective-permute-start.22 = (bf16[32,4096]{1,0:T(8,128)(2,1)S(1)}, bf16[32,4096]{1,0:T(8,128)(2,1)S(1)}, u32[]{:S(2)}, u32[]{:S(2)}) collective-permute-start(bf16[32,4096]{1,0:T(8,128)(2,1)S(1)} %fusion.2), channel_id=1, source_target_pairs={{0,2},{1,3},{2,0},{3,1},{4,6},{5,7},{6,4},{7,5},{8,10},{9,11},{10,... | collective-permute-start | bytes 786440 | tf_op jit(solution)/shard_map/ppermute | solution.py:170
  70.3 12.2 %collective-permute-start.20 = (bf16[16,4096]{1,0:T(8,128)(2,1)S(1)}, bf16[16,4096]{1,0:T(8,128)(2,1)S(1)}, u32[]{:S(2)}, u32[]{:S(2)}) collective-permute-start(bf16[16,4096]{1,0:T(8,128)(2,1)S(1)} %fusion.6), channel_id=1, source_target_pairs={{0,8},{1,9},{2,10},{3,11},{4,12},{5,13},{6,14},{7,15},{8,0},{9,1},... | collective-permute-start | bytes 393224 | tf_op jit(solution)/shard_map/ppermute | solution.py:173
  73.3 11.1 %collective-permute-start.24 = (bf16[16,4096]{1,0:T(8,128)(2,1)S(1)}, bf16[16,4096]{1,0:T(8,128)(2,1)S(1)}, u32[]{:S(2)}, u32[]{:S(2)}) collective-permute-start(bf16[16,4096]{1,0:T(8,128)(2,1)S(1)} %slice_add_fusion.10), channel_id=1, source_target_pairs={{0,8},{1,9},{2,10},{3,11},{4,12},{5,13},{6,14},{7,15},{8,0},{9,1},... | collective-permute-start | bytes 393224 | tf_op jit(solution)/shard_map/ppermute | solution.py:173
  76.2 9.3 %collective-permute-start.25 = (bf16[16,4096]{1,0:T(8,128)(2,1)S(1)}, bf16[16,4096]{1,0:T(8,128)(2,1)S(1)}, u32[]{:S(2)}, u32[]{:S(2)}) collective-permute-start(bf16[16,4096]{1,0:T(8,128)(2,1)S(1)} %slice.189), channel_id=1, source_target_pairs={{0,4},{1,5},{2,6},{3,7},{4,0},{5,1},{6,2},{7,3},{8,12},{9,13},{10,... | collective-permute-start | bytes 393224 | tf_op jit(solution)/shard_map/ppermute | solution.py:173

commit v12 on v11

--- a/solution.py
+++ b/solution.py
@@ -205,7 +205,8 @@
     others = [swap_far(messages[0], by) for by in places(strides)[1:]]
     near_own = [swap_near(message) for message in messages]
     loaded = load_weights(w_gate, w_up)
-    loaded, near_own, others, far = lax.optimization_barrier((loaded, near_own, others, far))
+    later = [[swap_far(message, by) for by in places(strides)[1:]] for message in messages[1:]]
+    near_own, later, loaded, others, far = lax.optimization_barrier((near_own, later, loaded, others, far))
     near_close = [swap_near(block) for block in others]
     crossed = [swap_far(after(message, far), middle) for message in messages[1:]]
     far = grow(far, strides)
@@ -215,35 +216,34 @@
     loaded += last
     line = jnp.concatenate([messages[0], *others, far, near_own[0], *near_close])
     parts = [line, swap_core(line), near_far, swap_core(near_far)]
-    near_crossed = [swap_near(block) for block in crossed]
-    wanted = places(strides)
-    wanted += [middle ^ place for place in wanted]
-    found = places([middle] + strides)
+    next_line, next_near = [], []
+    for step in range(1, steps):
+        block, rest = crossed[step - 1], []
+        near_block = swap_near(block)
+        for by in strides:
+            rest.append(after(swap_far(block, by), near_far))
+            block = jnp.concatenate([block, rest[-1]])
+        near_rest = swap_near(jnp.concatenate([*later[step - 1], *rest]))
+        next_line.append([messages[step], *later[step - 1], block])
+        next_near.append([near_own[step], near_block, near_rest])
     outputs, ready = [], far
     for step in range(steps):
         plan = []
         if step:
-            rest = jnp.concatenate(arrived)
-            line = jnp.concatenate([messages[step], crossed[step - 1], rest, near_own[step], near_crossed[step - 1], after(near_rest, ready)])
+            near_first, near_block, near_rest = next_near[step - 1]
+            near_rest = after(near_rest, ready)
+            cut = head - tokens
+            line = [*next_line[step - 1], near_first, near_rest[:cut], near_block, near_rest[cut:]]
+            line = jnp.concatenate(line)
             parts = [line, swap_core(line)]
         for core in range(2):
-            if step:
-                for side in range(2):
-                    at = [side * half + found.index(place) * tokens for place in wanted]
-                    plan += [(core, row, row + tokens) for row in at]
-            else:
-                plan += [(core, 0, half + head), (2 + core, 0, head)]
+            plan += [(core, 0, 2 * half)] if step else [(core, 0, half + head), (2 + core, 0, head)]
         own, peer, other_low, other_high = run_expert(step > 0, flags, loaded, after(parts, ready), tuple(plan))
         if step:
             other_high = after(swap_core(other_high), near).astype(jnp.float32)
             other_low = swap_core(after(other_low, near))
         else:
-            arrived, line = [], jnp.concatenate([messages[1], crossed[0]])
-            for by in strides:
-                arrived.append(after(swap_far(line, by), other_low))
-                line = jnp.concatenate([line, arrived[-1]])
-            near_rest = swap_near(jnp.concatenate(arrived))
-            other_high, other_low = after((other_high, other_low), arrived)
+            other_high, other_low = after((other_high, other_low), next_near[0][2])
             other_high = swap_core(other_high).astype(jnp.float32)
             other_low = swap_core(other_low)
         to_high = (peer[head:].astype(jnp.float32) + other_high[head:]).astype(jnp.bfloat16)

time: 86.5 us -> 85.8 us (level)
  waiting for transfers between devices: 37.9 us -> 30.9 us
  starting transfers between devices: 25.9 us -> 32.2 us
    ppermute x9, waiting for transfers between devices: 18.7 us -> 14.5 us  [swap_near(): lax.ppermute(x, 'expert', [(index(z, y, c), index(z, 1 - y, c)) for z, y,...]
    ppermute x9, starting transfers between devices: 9.5 us -> 13.2 us  [swap_near(): lax.ppermute(x, 'expert', [(index(z, y, c), index(z, 1 - y, c)) for z, y,...]
    ppermute x7, waiting for transfers between devices: 6.43 us -> 2.8 us  [swap_core(): lax.ppermute(x, 'expert', [(index(z, y, c), index(z, y, 1 - c)) for z, y,...]
    ppermute x10 -> x11, starting transfers between devices: 15.5 us -> 17.9 us  [swap_far(): lax.ppermute(x, 'expert', [(index(z, y, c), index(z ^ by, y, c)) for z, y...]
    ppermute x10 -> x11, waiting for transfers between devices: 12.8 us -> 13.6 us  [swap_far(): lax.ppermute(x, 'expert', [(index(z, y, c), index(z ^ by, y, c)) for z, y...]
  transfers between devices with their start and end apart: 26 -> 27, of which waited for: 16 -> 14; matrix products, arithmetic and copies ran while one was open for 2% -> 2% of each run, Pallas kernels for 22% -> 22%
where the time goes in v12:
time: 85.8 us; the launch traced here: 85.6 us
  starting transfers between devices  32.2 us (38%)
  waiting for transfers between devices  30.9 us (36%)
  Pallas kernels  19.9 us (23%)
  other arithmetic  1.95 us (2%)
    ppermute x11, starting transfers between devices, swap_far(): lax.ppermute(x, 'expert', [(index(z, y, c), index(z ^ by, y, c)) for z, y...  17.9 us
    ppermute x9, waiting for transfers between devices, swap_near(): lax.ppermute(x, 'expert', [(index(z, y, c), index(z, 1 - y, c)) for z, y,...  14.5 us
    ppermute x11, waiting for transfers between devices, swap_far(): lax.ppermute(x, 'expert', [(index(z, y, c), index(z ^ by, y, c)) for z, y...  13.6 us
    ppermute x9, starting transfers between devices, swap_near(): lax.ppermute(x, 'expert', [(index(z, y, c), index(z, 1 - y, c)) for z, y,...  13.2 us
    pallas_call x2, Pallas kernels, run_expert(): pl.pallas_call(functools.partial(expert_kernel, swapped, count, plan), ou...  11.2 us
    pallas_call x2, Pallas kernels, load_weights(): pl.pallas_call(load_kernel, out_shape=[pltpu.VMEM(x.shape, x.dtype) for x...  7.42 us
    ppermute x7, waiting for transfers between devices, swap_core(): lax.ppermute(x, 'expert', [(index(z, y, c), index(z, y, 1 - c)) for z, y,...  2.8 us
  transfers between devices with their start and end apart: 27, of which 14 were waited for; matrix products, arithmetic and copies ran while one was open for 2% of the time, Pallas kernels for 22%

profile of v12, /device:TPU:0, one launch (start us, length us, event | category | flops | bytes accessed | tf_op | source)
XLA Modules:
  0.0 85.6 jit_solution(2534713851749768979)
XLA Ops:
  0.0 1.2 %messages.1 = (bf16[16,4224]{1,0:T(8,128)(2,1)S(1)}, bf16[16,4224]{1,0:T(8,128)(2,1)S(1)}) custom-call(bf16[2,16,4096]{2,1,0:T(8,128)(2,1)} %states_ref.1, s32[2,8,16]{2,1,0:T(8,128)} %bitcast.12, f32[2,8,16]{2,1,0:T(8,128)} %bitcast.13), custom_call_target="tpu_custom_call" | custom-call | tf_op jit(solution)/shard_map/messages/pallas_call | solution.py:49
  1.2 4.0 %collective-permute-start.4 = (bf16[16,4224]{1,0:T(8,128)(2,1)S(1)}, bf16[16,4224]{1,0:T(8,128)(2,1)S(1)}, u32[]{:S(2)}, u32[]{:S(2)}) collective-permute-start(bf16[16,4224]{1,0:T(8,128)(2,1)S(1)} %get-tuple-element.47), channel_id=1, source_target_pairs={{0,8},{1,9},{2,10},{3,11},{4,12},{5,13},{6,14},{7,15},{8,0},{9,1},... | collective-permute-start | bytes 405512 | tf_op jit(solution)/shard_map/ppermute | solution.py:173
  5.3 1.6 %collective-permute-start.3 = (bf16[16,4224]{1,0:T(8,128)(2,1)S(1)}, bf16[16,4224]{1,0:T(8,128)(2,1)S(1)}, u32[]{:S(2)}, u32[]{:S(2)}) collective-permute-start(bf16[16,4224]{1,0:T(8,128)(2,1)S(1)} %get-tuple-element.47), channel_id=1, source_target_pairs={{0,4},{1,5},{2,6},{3,7},{4,0},{5,1},{6,2},{7,3},{8,12},{9,13},{10,... | collective-permute-start | bytes 405512 | tf_op jit(solution)/shard_map/ppermute | solution.py:173
  6.8 1.5 %collective-permute-start = (bf16[16,4224]{1,0:T(8,128)(2,1)S(1)}, bf16[16,4224]{1,0:T(8,128)(2,1)S(1)}, u32[]{:S(2)}, u32[]{:S(2)}) collective-permute-start(bf16[16,4224]{1,0:T(8,128)(2,1)S(1)} %get-tuple-element.47), channel_id=1, source_target_pairs={{0,2},{1,3},{2,0},{3,1},{4,6},{5,7},{6,4},{7,5},{8,10},{9,11},{10,... | collective-permute-start | bytes 405512 | tf_op jit(solution)/shard_map/ppermute | solution.py:170
  8.4 0.4 collective-permute-start.2
  8.8 0.5 collective-permute-start.1
  9.4 4.6 %load_weights.2 = (bf16[4096,768]{1,0:T(8,128)(2,1)S(1)}, bf16[4096,768]{1,0:T(8,128)(2,1)S(1)}) custom-call(bf16[4096,768]{1,0:T(8,128)(2,1)} %bitcast.9, bf16[4096,768]{1,0:T(8,128)(2,1)} %bitcast.10), custom_call_target="tpu_custom_call" | custom-call | tf_op jit(solution)/shard_map/load_weights/pallas_call | solution.py:73
  14.0 0.0 collective-permute-done.4
  14.0 0.9 %collective-permute-done.2 = bf16[16,4224]{1,0:T(8,128)(2,1)S(1)} collective-permute-done((bf16[16,4224]{1,0:T(8,128)(2,1)S(1)}, bf16[16,4224]{1,0:T(8,128)(2,1)S(1)}, u32[]{:S(2)}, u32[]{:S(2)}) %collective-permute-start.2) | collective-permute-done | bytes 135200 | tf_op jit(solution)/shard_map/ppermute | solution.py:173
  14.9 0.0 collective-permute-done.1
  14.9 1.5 %collective-permute-start.5 = (bf16[16,4224]{1,0:T(8,128)(2,1)S(1)}, bf16[16,4224]{1,0:T(8,128)(2,1)S(1)}, u32[]{:S(2)}, u32[]{:S(2)}) collective-permute-start(bf16[16,4224]{1,0:T(8,128)(2,1)S(1)} %collective-permute-done.4), channel_id=1, source_target_pairs={{0,4},{1,5},{2,6},{3,7},{4,0},{5,1},{6,2},{7,3},{8,12},{9,13},{10,... | collective-permute-start | bytes 405512 | tf_op jit(solution)/shard_map/ppermute | solution.py:173
  16.4 1.5 %collective-permute-start.6 = (bf16[16,4224]{1,0:T(8,128)(2,1)S(1)}, bf16[16,4224]{1,0:T(8,128)(2,1)S(1)}, u32[]{:S(2)}, u32[]{:S(2)}) collective-permute-start(bf16[16,4224]{1,0:T(8,128)(2,1)S(1)} %collective-permute-done.3), channel_id=1, source_target_pairs={{0,2},{1,3},{2,0},{3,1},{4,6},{5,7},{6,4},{7,5},{8,10},{9,11},{10,... | collective-permute-start | bytes 405512 | tf_op jit(solution)/shard_map/ppermute | solution.py:170
  17.9 1.7 %collective-permute-start.7 = (bf16[16,4224]{1,0:T(8,128)(2,1)S(1)}, bf16[16,4224]{1,0:T(8,128)(2,1)S(1)}, u32[]{:S(2)}, u32[]{:S(2)}) collective-permute-start(bf16[16,4224]{1,0:T(8,128)(2,1)S(1)} %get-tuple-element.56), channel_id=1, source_target_pairs={{0,8},{1,9},{2,10},{3,11},{4,12},{5,13},{6,14},{7,15},{8,0},{9,1},... | collective-permute-start | bytes 405512 | tf_op jit(solution)/shard_map/ppermute | solution.py:173
  19.7 0.4 collective-permute-done.5
  20.1 2.8 %collective-permute-start.9 = (bf16[32,4224]{1,0:T(8,128)(2,1)S(1)}, bf16[32,4224]{1,0:T(8,128)(2,1)S(1)}, u32[]{:S(2)}, u32[]{:S(2)}) collective-permute-start(bf16[32,4224]{1,0:T(8,128)(2,1)S(1)} %get-tuple-element.92), channel_id=1, source_target_pairs={{0,2},{1,3},{2,0},{3,1},{4,6},{5,7},{6,4},{7,5},{8,10},{9,11},{10,... | collective-permute-start | bytes 811016 | tf_op jit(solution)/shard_map/ppermute | solution.py:170
  22.9 2.8 %load_weights.3.down_ref = bf16[768,4096]{1,0:T(8,128)(2,1)S(1)} custom-call(bf16[768,4096]{1,0:T(8,128)(2,1)} %bitcast.11), custom_call_target="tpu_custom_call" | custom-call | tf_op jit(solution)/shard_map/load_weights/pallas_call | solution.py:73
  25.7 0.0 copy-start
  25.8 0.0 collective-permute-done.6
  25.8 0.4 collective-permute-start.16
  26.2 1.4 %collective-permute-start.11 = (bf16[16,4224]{1,0:T(8,128)(2,1)S(1)}, bf16[16,4224]{1,0:T(8,128)(2,1)S(1)}, u32[]{:S(2)}, u32[]{:S(2)}) collective-permute-start(bf16[16,4224]{1,0:T(8,128)(2,1)S(1)} %collective-permute-done.7), channel_id=1, source_target_pairs={{0,4},{1,5},{2,6},{3,7},{4,0},{5,1},{6,2},{7,3},{8,12},{9,13},{10,... | collective-permute-start | bytes 405512 | tf_op jit(solution)/shard_map/ppermute | solution.py:173
  27.6 0.1 collective-permute-start.8
  27.7 3.5 %collective-permute-done.11 = bf16[16,4224]{1,0:T(8,128)(2,1)S(1)} collective-permute-done((bf16[16,4224]{1,0:T(8,128)(2,1)S(1)}, bf16[16,4224]{1,0:T(8,128)(2,1)S(1)}, u32[]{:S(2)}, u32[]{:S(2)}) %collective-permute-start.11) | collective-permute-done | bytes 135200 | tf_op jit(solution)/shard_map/ppermute | solution.py:173
  31.2 0.1 collective-permute-start.10
  31.3 1.7 %collective-permute-start.12 = (bf16[32,4224]{1,0:T(8,128)(2,1)S(1)}, bf16[32,4224]{1,0:T(8,128)(2,1)S(1)}, u32[]{:S(2)}, u32[]{:S(2)}) collective-permute-start(bf16[32,4224]{1,0:T(8,128)(2,1)S(1)} %pad_maximum_fusion.1), channel_id=1, source_target_pairs={{0,2},{1,3},{2,0},{3,1},{4,6},{5,7},{6,4},{7,5},{8,10},{9,11},{10,... | collective-permute-start | bytes 811016 | tf_op jit(solution)/shard_map/ppermute | solution.py:170
  33.1 5.6 %expert.2 = (bf16[64,4096]{1,0:T(8,128)(2,1)S(1)}, bf16[64,4096]{1,0:T(8,128)(2,1)S(1)}, bf16[64,4096]{1,0:T(8,128)(2,1)S(1)}, bf16[64,4096]{1,0:T(8,128)(2,1)S(1)}) custom-call(s32[16]{0:T(128)S(1)} %copy-done, bf16[4096,768]{1,0:T(8,128)(2,1)S(1)} %get-tuple-element.51.gate_ref, bf16[4096,768]{1,0:T(8,128)(2,1)S(1)} %get-tuple-element.52.up_ref, ...), custom_call_target="tpu_custom_call" | custom-call | flops 4831838208 | bytes 4194304 | tf_op jit(solution)/shard_map/expert/pallas_call | solution.py:123
  38.7 1.6 %collective-permute-done.12 = bf16[32,4224]{1,0:T(8,128)(2,1)S(1)} collective-permute-done((bf16[32,4224]{1,0:T(8,128)(2,1)S(1)}, bf16[32,4224]{1,0:T(8,128)(2,1)S(1)}, u32[]{:S(2)}, u32[]{:S(2)}) %collective-permute-start.12) | collective-permute-done | bytes 270368 | tf_op jit(solution)/shard_map/ppermute | solution.py:170
  40.3 0.0 collective-permute-start.14
  40.3 0.6 collective-permute-start.13
  40.9 1.3 %collective-permute-done.14 = bf16[64,4096]{1,0:T(8,128)(2,1)S(1)} collective-permute-done((bf16[64,4096]{1,0:T(8,128)(2,1)S(1)}, bf16[64,4096]{1,0:T(8,128)(2,1)S(1)}, u32[]{:S(2)}, u32[]{:S(2)}) %collective-permute-start.14) | collective-permute-done | bytes 524320 | tf_op jit(solution)/shard_map/ppermute | solution.py:167
  42.2 0.1 convert_element_type.81
  42.3 0.1 fusion.5
  42.3 0.6 collective-permute-done.13
  43.0 0.1 convert_element_type.83
  43.0 0.1 fusion.4
  43.1 0.0 collective-permute-done.16
  43.2 0.2 collective-permute-start.17
  43.4 1.7 %collective-permute-start.15 = (bf16[64,4096]{1,0:T(8,128)(2,1)S(1)}, bf16[64,4096]{1,0:T(8,128)(2,1)S(1)}, u32[]{:S(2)}, u32[]{:S(2)}) collective-permute-start(bf16[64,4096]{1,0:T(8,128)(2,1)S(1)} %pad_maximum_fusion), channel_id=1, source_target_pairs={{0,2},{1,3},{2,0},{3,1},{4,6},{5,7},{6,4},{7,5},{8,10},{9,11},{10,... | collective-permute-start | bytes 1572872 | tf_op jit(solution)/shard_map/ppermute | solution.py:170
  45.1 0.8 collective-permute-done.17.refs_1_
  45.9 5.6 %expert.3 = (bf16[64,4096]{1,0:T(8,128)(2,1)S(1)}, bf16[64,4096]{1,0:T(8,128)(2,1)S(1)}, bf16[64,4096]{1,0:T(8,128)(2,1)S(1)}, bf16[64,4096]{1,0:T(8,128)(2,1)S(1)}) custom-call(s32[16]{0:T(128)S(1)} %copy-done, bf16[4096,768]{1,0:T(8,128)(2,1)S(1)} %get-tuple-element.51.gate_ref, bf16[4096,768]{1,0:T(8,128)(2,1)S(1)} %get-tuple-element.52.up_ref, ...), custom_call_target="tpu_custom_call" | custom-call | flops 4831838208 | bytes 4194304 | tf_op jit(solution)/shard_map/expert/pallas_call | solution.py:123
  51.6 0.2 collective-permute-start.19
  51.8 5.9 %collective-permute-done.15 = bf16[64,4096]{1,0:T(8,128)(2,1)S(1)} collective-permute-done((bf16[64,4096]{1,0:T(8,128)(2,1)S(1)}, bf16[64,4096]{1,0:T(8,128)(2,1)S(1)}, u32[]{:S(2)}, u32[]{:S(2)}) %collective-permute-start.15) | collective-permute-done | bytes 524320 | tf_op jit(solution)/shard_map/ppermute | solution.py:170
  57.7 0.1 convert_element_type.87
  57.8 0.1 fusion.3
  57.8 1.7 %collective-permute-start.22 = (bf16[32,4096]{1,0:T(8,128)(2,1)S(1)}, bf16[32,4096]{1,0:T(8,128)(2,1)S(1)}, u32[]{:S(2)}, u32[]{:S(2)}) collective-permute-start(bf16[32,4096]{1,0:T(8,128)(2,1)S(1)} %fusion.3), channel_id=1, source_target_pairs={{0,2},{1,3},{2,0},{3,1},{4,6},{5,7},{6,4},{7,5},{8,10},{9,11},{10,... | collective-permute-start | bytes 786440 | tf_op jit(solution)/shard_map/ppermute | solution.py:170
  59.5 0.1 collective-permute-done.18
  59.6 0.1 convert_element_type.89
  59.7 0.1 fusion.2
  59.7 0.1 convert_element_type.90
  59.8 0.2 slice_add_fusion.5
  60.1 1.4 %collective-permute-start.20 = (bf16[32,4096]{1,0:T(8,128)(2,1)S(1)}, bf16[32,4096]{1,0:T(8,128)(2,1)S(1)}, u32[]{:S(2)}, u32[]{:S(2)}) collective-permute-start(bf16[32,4096]{1,0:T(8,128)(2,1)S(1)} %pad_maximum_fusion.2), channel_id=1, source_target_pairs={{0,4},{1,5},{2,6},{3,7},{4,0},{5,1},{6,2},{7,3},{8,12},{9,13},{10,... | collective-permute-start | bytes 786440 | tf_op jit(solution)/shard_map/ppermute | solution.py:173
  61.5 5.1 %collective-permute-done.22 = bf16[32,4096]{1,0:T(8,128)(2,1)S(1)} collective-permute-done((bf16[32,4096]{1,0:T(8,128)(2,1)S(1)}, bf16[32,4096]{1,0:T(8,128)(2,1)S(1)}, u32[]{:S(2)}, u32[]{:S(2)}) %collective-permute-start.22) | collective-permute-done | bytes 262176 | tf_op jit(solution)/shard_map/ppermute | solution.py:170
  66.6 0.1 fusion
  66.7 1.4 %collective-permute-start.24 = (bf16[16,4096]{1,0:T(8,128)(2,1)S(1)}, bf16[16,4096]{1,0:T(8,128)(2,1)S(1)}, u32[]{:S(2)}, u32[]{:S(2)}) collective-permute-start(bf16[16,4096]{1,0:T(8,128)(2,1)S(1)} %slice.200), channel_id=1, source_target_pairs={{0,4},{1,5},{2,6},{3,7},{4,0},{5,1},{6,2},{7,3},{8,12},{9,13},{10,... | collective-permute-start | bytes 393224 | tf_op jit(solution)/shard_map/ppermute | solution.py:173
  68.2 1.3 %collective-permute-start.23 = (bf16[32,4096]{1,0:T(8,128)(2,1)S(1)}, bf16[32,4096]{1,0:T(8,128)(2,1)S(1)}, u32[]{:S(2)}, u32[]{:S(2)}) collective-permute-start(bf16[32,4096]{1,0:T(8,128)(2,1)S(1)} %fusion.2), channel_id=1, source_target_pairs={{0,2},{1,3},{2,0},{3,1},{4,6},{5,7},{6,4},{7,5},{8,10},{9,11},{10,... | collective-permute-start | bytes 786440 | tf_op jit(solution)/shard_map/ppermute | solution.py:170
  69.5 1.8 %collective-permute-start.21 = (bf16[16,4096]{1,0:T(8,128)(2,1)S(1)}, bf16[16,4096]{1,0:T(8,128)(2,1)S(1)}, u32[]{:S(2)}, u32[]{:S(2)}) collective-permute-start(bf16[16,4096]{1,0:T(8,128)(2,1)S(1)} %fusion.6), channel_id=1, source_target_pairs={{0,8},{1,9},{2,10},{3,11},{4,12},{5,13},{6,14},{7,15},{8,0},{9,1},... | collective-permute-start | bytes 393224 | tf_op jit(solution)/shard_map/ppermute | solution.py:173
  71.3 0.6 collective-permute-done.24
  71.9 1.9 %collective-permute-start.25 = (bf16[16,4096]{1,0:T(8,128)(2,1)S(1)}, bf16[16,4096]{1,0:T(8,128)(2,1)S(1)}, u32[]{:S(2)}, u32[]{:S(2)}) collective-permute-start(bf16[16,4096]{1,0:T(8,128)(2,1)S(1)} %slice_add_fusion.10), channel_id=1, source_target_pairs={{0,8},{1,9},{2,10},{3,11},{4,12},{5,13},{6,14},{7,15},{8,0},{9,1},... | collective-permute-start | bytes 393224 | tf_op jit(solution)/shard_map/ppermute | solution.py:173
  73.9 1.9 %collective-permute-done.23 = bf16[32,4096]{1,0:T(8,128)(2,1)S(1)} collective-permute-done((bf16[32,4096]{1,0:T(8,128)(2,1)S(1)}, bf16[32,4096]{1,0:T(8,128)(2,1)S(1)}, u32[]{:S(2)}, u32[]{:S(2)}) %collective-permute-start.23) | collective-permute-done | bytes 262176 | tf_op jit(solution)/shard_map/ppermute | solution.py:170
  75.8 0.1 fusion.1
  75.9 0.7 collective-permute-start.26
  76.7 5.0 %collective-permute-done.21 = bf16[16,4096]{1,0:T(8,128)(2,1)S(1)} collective-permute-done((bf16[16,4096]{1,0:T(8,128)(2,1)S(1)}, bf16[16,4096]{1,0:T(8,128)(2,1)S(1)}, u32[]{:S(2)}, u32[]{:S(2)}) %collective-permute-start.21) | collective-permute-done | bytes 131104 | tf_op jit(solution)/shard_map/ppermute | solution.py:173
  81.6 1.9 %collective-permute-done.25.second_ref = bf16[16,4096]{1,0:T(8,128)(2,1)S(1)} collective-permute-done((bf16[16,4096]{1,0:T(8,128)(2,1)S(1)}, bf16[16,4096]{1,0:T(8,128)(2,1)S(1)}, u32[]{:S(2)}, u32[]{:S(2)}) %collective-permute-start.25) | collective-permute-done | bytes 131104 | tf_op jit(solution)/shard_map/ppermute | solution.py:173
  83.6 1.2 %collective-permute-done.26 = bf16[16,4096]{1,0:T(8,128)(2,1)S(1)} collective-permute-done((bf16[16,4096]{1,0:T(8,128)(2,1)S(1)}, bf16[16,4096]{1,0:T(8,128)(2,1)S(1)}, u32[]{:S(2)}, u32[]{:S(2)}) %collective-permute-start.26) | collective-permute-done | bytes 131104 | tf_op jit(solution)/shard_map/ppermute | solution.py:173
  84.9 0.7 pad_maximum_fusion.3
  (38 shorter events, 0.6 us)
Async XLA Ops:
  1.2 12.8 %collective-permute-start.4 = (bf16[16,4224]{1,0:T(8,128)(2,1)S(1)}, bf16[16,4224]{1,0:T(8,128)(2,1)S(1)}, u32[]{:S(2)}, u32[]{:S(2)}) collective-permute-start(bf16[16,4224]{1,0:T(8,128)(2,1)S(1)} %get-tuple-element.47), channel_id=1, source_target_pairs={{0,8},{1,9},{2,10},{3,11},{4,12},{5,13},{6,14},{7,15},{8,0},{9,1},... | collective-permute-start | bytes 405512 | tf_op jit(solution)/shard_map/ppermute | solution.py:173
  5.3 8.7 %collective-permute-start.3 = (bf16[16,4224]{1,0:T(8,128)(2,1)S(1)}, bf16[16,4224]{1,0:T(8,128)(2,1)S(1)}, u32[]{:S(2)}, u32[]{:S(2)}) collective-permute-start(bf16[16,4224]{1,0:T(8,128)(2,1)S(1)} %get-tuple-element.47), channel_id=1, source_target_pairs={{0,4},{1,5},{2,6},{3,7},{4,0},{5,1},{6,2},{7,3},{8,12},{9,13},{10,... | collective-permute-start | bytes 405512 | tf_op jit(solution)/shard_map/ppermute | solution.py:173
  6.8 7.2 %collective-permute-start = (bf16[16,4224]{1,0:T(8,128)(2,1)S(1)}, bf16[16,4224]{1,0:T(8,128)(2,1)S(1)}, u32[]{:S(2)}, u32[]{:S(2)}) collective-permute-start(bf16[16,4224]{1,0:T(8,128)(2,1)S(1)} %get-tuple-element.47), channel_id=1, source_target_pairs={{0,2},{1,3},{2,0},{3,1},{4,6},{5,7},{6,4},{7,5},{8,10},{9,11},{10,... | collective-permute-start | bytes 405512 | tf_op jit(solution)/shard_map/ppermute | solution.py:170
  8.4 6.6 %collective-permute-start.2 = (bf16[16,4224]{1,0:T(8,128)(2,1)S(1)}, bf16[16,4224]{1,0:T(8,128)(2,1)S(1)}, u32[]{:S(2)}, u32[]{:S(2)}) collective-permute-start(bf16[16,4224]{1,0:T(8,128)(2,1)S(1)} %get-tuple-element.56), channel_id=1, source_target_pairs={{0,4},{1,5},{2,6},{3,7},{4,0},{5,1},{6,2},{7,3},{8,12},{9,13},{10,... | collective-permute-start | bytes 405512 | tf_op jit(solution)/shard_map/ppermute | solution.py:173
  8.8 6.1 %collective-permute-start.1 = (bf16[16,4224]{1,0:T(8,128)(2,1)S(1)}, bf16[16,4224]{1,0:T(8,128)(2,1)S(1)}, u32[]{:S(2)}, u32[]{:S(2)}) collective-permute-start(bf16[16,4224]{1,0:T(8,128)(2,1)S(1)} %get-tuple-element.56), channel_id=1, source_target_pairs={{0,2},{1,3},{2,0},{3,1},{4,6},{5,7},{6,4},{7,5},{8,10},{9,11},{10,... | collective-permute-start | bytes 405512 | tf_op jit(solution)/shard_map/ppermute | solution.py:170
  14.9 5.1 %collective-permute-start.5 = (bf16[16,4224]{1,0:T(8,128)(2,1)S(1)}, bf16[16,4224]{1,0:T(8,128)(2,1)S(1)}, u32[]{:S(2)}, u32[]{:S(2)}) collective-permute-start(bf16[16,4224]{1,0:T(8,128)(2,1)S(1)} %collective-permute-done.4), channel_id=1, source_target_pairs={{0,4},{1,5},{2,6},{3,7},{4,0},{5,1},{6,2},{7,3},{8,12},{9,13},{10,... | collective-permute-start | bytes 405512 | tf_op jit(solution)/shard_map/ppermute | solution.py:173
  16.4 9.3 %collective-permute-start.6 = (bf16[16,4224]{1,0:T(8,128)(2,1)S(1)}, bf16[16,4224]{1,0:T(8,128)(2,1)S(1)}, u32[]{:S(2)}, u32[]{:S(2)}) collective-permute-start(bf16[16,4224]{1,0:T(8,128)(2,1)S(1)} %collective-permute-done.3), channel_id=1, source_target_pairs={{0,2},{1,3},{2,0},{3,1},{4,6},{5,7},{6,4},{7,5},{8,10},{9,11},{10,... | collective-permute-start | bytes 405512 | tf_op jit(solution)/shard_map/ppermute | solution.py:170
  17.9 7.8 %collective-permute-start.7 = (bf16[16,4224]{1,0:T(8,128)(2,1)S(1)}, bf16[16,4224]{1,0:T(8,128)(2,1)S(1)}, u32[]{:S(2)}, u32[]{:S(2)}) collective-permute-start(bf16[16,4224]{1,0:T(8,128)(2,1)S(1)} %get-tuple-element.56), channel_id=1, source_target_pairs={{0,8},{1,9},{2,10},{3,11},{4,12},{5,13},{6,14},{7,15},{8,0},{9,1},... | collective-permute-start | bytes 405512 | tf_op jit(solution)/shard_map/ppermute | solution.py:173
  20.1 11.1 %collective-permute-start.9 = (bf16[32,4224]{1,0:T(8,128)(2,1)S(1)}, bf16[32,4224]{1,0:T(8,128)(2,1)S(1)}, u32[]{:S(2)}, u32[]{:S(2)}) collective-permute-start(bf16[32,4224]{1,0:T(8,128)(2,1)S(1)} %get-tuple-element.92), channel_id=1, source_target_pairs={{0,2},{1,3},{2,0},{3,1},{4,6},{5,7},{6,4},{7,5},{8,10},{9,11},{10,... | collective-permute-start | bytes 811016 | tf_op jit(solution)/shard_map/ppermute | solution.py:170
  25.7 7.3 %copy-start = (s32[16]{0:T(128)S(1)}, s32[16]{0:T(128)}, u32[]{:S(2)}) copy-start(s32[16]{0:T(128)} %flags_ref.3) | copy-start | bytes 196
  25.8 17.4 %collective-permute-start.16 = (bf16[16,4224]{1,0:T(8,128)(2,1)S(1)}, bf16[16,4224]{1,0:T(8,128)(2,1)S(1)}, u32[]{:S(2)}, u32[]{:S(2)}) collective-permute-start(bf16[16,4224]{1,0:T(8,128)(2,1)S(1)} %collective-permute-done.7), channel_id=1, source_target_pairs={{0,2},{1,3},{2,0},{3,1},{4,6},{5,7},{6,4},{7,5},{8,10},{9,11},{10,... | collective-permute-start | bytes 405512 | tf_op jit(solution)/shard_map/ppermute | solution.py:170
  26.2 5.0 %collective-permute-start.11 = (bf16[16,4224]{1,0:T(8,128)(2,1)S(1)}, bf16[16,4224]{1,0:T(8,128)(2,1)S(1)}, u32[]{:S(2)}, u32[]{:S(2)}) collective-permute-start(bf16[16,4224]{1,0:T(8,128)(2,1)S(1)} %collective-permute-done.7), channel_id=1, source_target_pairs={{0,4},{1,5},{2,6},{3,7},{4,0},{5,1},{6,2},{7,3},{8,12},{9,13},{10,... | collective-permute-start | bytes 405512 | tf_op jit(solution)/shard_map/ppermute | solution.py:173
  27.6 5.4 %collective-permute-start.8 = (bf16[96,4224]{1,0:T(8,128)(2,1)S(1)}, bf16[96,4224]{1,0:T(8,128)(2,1)S(1)}, u32[]{:S(2)}, u32[]{:S(2)}) collective-permute-start(bf16[96,4224]{1,0:T(8,128)(2,1)S(1)} %constant_dynamic-update-slice_fusion.2.refs_0_), channel_id=1, source_target_pairs={{0,1},{1,0},{2,3},{3,2},{4,5},{5,4},{6,7},{7,6},{8,9},{9,8},{10,11... | collective-permute-start | bytes 2433032 | tf_op jit(solution)/shard_map/ppermute | solution.py:167
  31.2 1.8 %collective-permute-start.10 = (bf16[32,4224]{1,0:T(8,128)(2,1)S(1)}, bf16[32,4224]{1,0:T(8,128)(2,1)S(1)}, u32[]{:S(2)}, u32[]{:S(2)}) collective-permute-start(bf16[32,4224]{1,0:T(8,128)(2,1)S(1)} %collective-permute-done.9.refs_2_), channel_id=1, source_target_pairs={{0,1},{1,0},{2,3},{3,2},{4,5},{5,4},{6,7},{7,6},{8,9},{9,8},{10,11... | collective-permute-start | bytes 811016 | tf_op jit(solution)/shard_map/ppermute | solution.py:167
  31.3 8.9 %collective-permute-start.12 = (bf16[32,4224]{1,0:T(8,128)(2,1)S(1)}, bf16[32,4224]{1,0:T(8,128)(2,1)S(1)}, u32[]{:S(2)}, u32[]{:S(2)}) collective-permute-start(bf16[32,4224]{1,0:T(8,128)(2,1)S(1)} %pad_maximum_fusion.1), channel_id=1, source_target_pairs={{0,2},{1,3},{2,0},{3,1},{4,6},{5,7},{6,4},{7,5},{8,10},{9,11},{10,... | collective-permute-start | bytes 811016 | tf_op jit(solution)/shard_map/ppermute | solution.py:170
  40.3 1.9 %collective-permute-start.14 = (bf16[64,4096]{1,0:T(8,128)(2,1)S(1)}, bf16[64,4096]{1,0:T(8,128)(2,1)S(1)}, u32[]{:S(2)}, u32[]{:S(2)}) collective-permute-start(bf16[64,4096]{1,0:T(8,128)(2,1)S(1)} %get-tuple-element.72), channel_id=1, source_target_pairs={{0,1},{1,0},{2,3},{3,2},{4,5},{5,4},{6,7},{7,6},{8,9},{9,8},{10,11... | collective-permute-start | bytes 1572872 | tf_op jit(solution)/shard_map/ppermute | solution.py:167
  40.3 2.6 %collective-permute-start.13 = (bf16[64,4096]{1,0:T(8,128)(2,1)S(1)}, bf16[64,4096]{1,0:T(8,128)(2,1)S(1)}, u32[]{:S(2)}, u32[]{:S(2)}) collective-permute-start(bf16[64,4096]{1,0:T(8,128)(2,1)S(1)} %get-tuple-element.70), channel_id=1, source_target_pairs={{0,1},{1,0},{2,3},{3,2},{4,5},{5,4},{6,7},{7,6},{8,9},{9,8},{10,11... | collective-permute-start | bytes 1572872 | tf_op jit(solution)/shard_map/ppermute | solution.py:167
  43.2 2.8 %collective-permute-start.17 = (bf16[128,4224]{1,0:T(8,128)(2,1)S(1)}, bf16[128,4224]{1,0:T(8,128)(2,1)S(1)}, u32[]{:S(2)}, u32[]{:S(2)}) collective-permute-start(bf16[128,4224]{1,0:T(8,128)(2,1)S(1)} %slice_dynamic-update-slice_fusion.refs_0_), channel_id=1, source_target_pairs={{0,1},{1,0},{2,3},{3,2},{4,5},{5,4},{6,7},{7,6},{8,9},{9,8},{10,11... | collective-permute-start | bytes 3244040 | tf_op jit(solution)/shard_map/ppermute | solution.py:167
  43.4 14.3 %collective-permute-start.15 = (bf16[64,4096]{1,0:T(8,128)(2,1)S(1)}, bf16[64,4096]{1,0:T(8,128)(2,1)S(1)}, u32[]{:S(2)}, u32[]{:S(2)}) collective-permute-start(bf16[64,4096]{1,0:T(8,128)(2,1)S(1)} %pad_maximum_fusion), channel_id=1, source_target_pairs={{0,2},{1,3},{2,0},{3,1},{4,6},{5,7},{6,4},{7,5},{8,10},{9,11},{10,... | collective-permute-start | bytes 1572872 | tf_op jit(solution)/shard_map/ppermute | solution.py:170
  51.6 6.1 %collective-permute-start.19 = (bf16[64,4096]{1,0:T(8,128)(2,1)S(1)}, bf16[64,4096]{1,0:T(8,128)(2,1)S(1)}, u32[]{:S(2)}, u32[]{:S(2)}) collective-permute-start(bf16[64,4096]{1,0:T(8,128)(2,1)S(1)} %get-tuple-element.81), channel_id=1, source_target_pairs={{0,1},{1,0},{2,3},{3,2},{4,5},{5,4},{6,7},{7,6},{8,9},{9,8},{10,11... | collective-permute-start | bytes 1572872 | tf_op jit(solution)/shard_map/ppermute | solution.py:167
  57.7 1.9 %collective-permute-start.18 = (bf16[64,4096]{1,0:T(8,128)(2,1)S(1)}, bf16[64,4096]{1,0:T(8,128)(2,1)S(1)}, u32[]{:S(2)}, u32[]{:S(2)}) collective-permute-start(bf16[64,4096]{1,0:T(8,128)(2,1)S(1)} %get-tuple-element.79), channel_id=1, source_target_pairs={{0,1},{1,0},{2,3},{3,2},{4,5},{5,4},{6,7},{7,6},{8,9},{9,8},{10,11... | collective-permute-start | bytes 1572872 | tf_op jit(solution)/shard_map/ppermute | solution.py:167
  57.8 8.8 %collective-permute-start.22 = (bf16[32,4096]{1,0:T(8,128)(2,1)S(1)}, bf16[32,4096]{1,0:T(8,128)(2,1)S(1)}, u32[]{:S(2)}, u32[]{:S(2)}) collective-permute-start(bf16[32,4096]{1,0:T(8,128)(2,1)S(1)} %fusion.3), channel_id=1, source_target_pairs={{0,2},{1,3},{2,0},{3,1},{4,6},{5,7},{6,4},{7,5},{8,10},{9,11},{10,... | collective-permute-start | bytes 786440 | tf_op jit(solution)/shard_map/ppermute | solution.py:170
  60.1 9.3 %collective-permute-start.20 = (bf16[32,4096]{1,0:T(8,128)(2,1)S(1)}, bf16[32,4096]{1,0:T(8,128)(2,1)S(1)}, u32[]{:S(2)}, u32[]{:S(2)}) collective-permute-start(bf16[32,4096]{1,0:T(8,128)(2,1)S(1)} %pad_maximum_fusion.2), channel_id=1, source_target_pairs={{0,4},{1,5},{2,6},{3,7},{4,0},{5,1},{6,2},{7,3},{8,12},{9,13},{10,... | collective-permute-start | bytes 786440 | tf_op jit(solution)/shard_map/ppermute | solution.py:173
  66.7 5.2 %collective-permute-start.24 = (bf16[16,4096]{1,0:T(8,128)(2,1)S(1)}, bf16[16,4096]{1,0:T(8,128)(2,1)S(1)}, u32[]{:S(2)}, u32[]{:S(2)}) collective-permute-start(bf16[16,4096]{1,0:T(8,128)(2,1)S(1)} %slice.200), channel_id=1, source_target_pairs={{0,4},{1,5},{2,6},{3,7},{4,0},{5,1},{6,2},{7,3},{8,12},{9,13},{10,... | collective-permute-start | bytes 393224 | tf_op jit(solution)/shard_map/ppermute | solution.py:173
  68.2 7.7 %collective-permute-start.23 = (bf16[32,4096]{1,0:T(8,128)(2,1)S(1)}, bf16[32,4096]{1,0:T(8,128)(2,1)S(1)}, u32[]{:S(2)}, u32[]{:S(2)}) collective-permute-start(bf16[32,4096]{1,0:T(8,128)(2,1)S(1)} %fusion.2), channel_id=1, source_target_pairs={{0,2},{1,3},{2,0},{3,1},{4,6},{5,7},{6,4},{7,5},{8,10},{9,11},{10,... | collective-permute-start | bytes 786440 | tf_op jit(solution)/shard_map/ppermute | solution.py:170
  69.5 12.1 %collective-permute-start.21 = (bf16[16,4096]{1,0:T(8,128)(2,1)S(1)}, bf16[16,4096]{1,0:T(8,128)(2,1)S(1)}, u32[]{:S(2)}, u32[]{:S(2)}) collective-permute-start(bf16[16,4096]{1,0:T(8,128)(2,1)S(1)} %fusion.6), channel_id=1, source_target_pairs={{0,8},{1,9},{2,10},{3,11},{4,12},{5,13},{6,14},{7,15},{8,0},{9,1},... | collective-permute-start | bytes 393224 | tf_op jit(solution)/shard_map/ppermute | solution.py:173
  71.9 11.6 %collective-permute-start.25 = (bf16[16,4096]{1,0:T(8,128)(2,1)S(1)}, bf16[16,4096]{1,0:T(8,128)(2,1)S(1)}, u32[]{:S(2)}, u32[]{:S(2)}) collective-permute-start(bf16[16,4096]{1,0:T(8,128)(2,1)S(1)} %slice_add_fusion.10), channel_id=1, source_target_pairs={{0,8},{1,9},{2,10},{3,11},{4,12},{5,13},{6,14},{7,15},{8,0},{9,1},... | collective-permute-start | bytes 393224 | tf_op jit(solution)/shard_map/ppermute | solution.py:173
  75.9 8.9 %collective-permute-start.26 = (bf16[16,4096]{1,0:T(8,128)(2,1)S(1)}, bf16[16,4096]{1,0:T(8,128)(2,1)S(1)}, u32[]{:S(2)}, u32[]{:S(2)}) collective-permute-start(bf16[16,4096]{1,0:T(8,128)(2,1)S(1)} %slice.199), channel_id=1, source_target_pairs={{0,4},{1,5},{2,6},{3,7},{4,0},{5,1},{6,2},{7,3},{8,12},{9,13},{10,... | collective-permute-start | bytes 393224 | tf_op jit(solution)/shard_map/ppermute | solution.py:173

commit v13 on v12

--- a/solution.py
+++ b/solution.py
@@ -207,14 +207,15 @@
     loaded = load_weights(w_gate, w_up)
     later = [[swap_far(message, by) for by in places(strides)[1:]] for message in messages[1:]]
     near_own, later, loaded, others, far = lax.optimization_barrier((near_own, later, loaded, others, far))
-    near_close = [swap_near(block) for block in others]
+    near_close = swap_near(jnp.concatenate(sum(later, others)))
     crossed = [swap_far(after(message, far), middle) for message in messages[1:]]
     far = grow(far, strides)
     near_far = swap_near(far)
     last = load_weights(after(w_down, far))
     last, near_close, crossed = lax.optimization_barrier((last, near_close, crossed))
     loaded += last
-    line = jnp.concatenate([messages[0], *others, far, near_own[0], *near_close])
+    cut = head - tokens
+    line = jnp.concatenate([messages[0], *others, far, near_own[0], near_close[:cut]])
     parts = [line, swap_core(line), near_far, swap_core(near_far)]
     next_line, next_near = [], []
     for step in range(1, steps):
@@ -223,18 +224,15 @@
         for by in strides:
             rest.append(after(swap_far(block, by), near_far))
             block = jnp.concatenate([block, rest[-1]])
-        near_rest = swap_near(jnp.concatenate([*later[step - 1], *rest]))
-        next_line.append([messages[step], *later[step - 1], block])
-        next_near.append([near_own[step], near_block, near_rest])
+        near_rest = swap_near(jnp.concatenate(rest))
+        next_line.append([messages[step], *later[step - 1], block, near_own[step]])
+        next_line[-1] += [near_close[step * cut : (step + 1) * cut], near_block]
+        next_near.append(near_rest)
     outputs, ready = [], far
     for step in range(steps):
         plan = []
         if step:
-            near_first, near_block, near_rest = next_near[step - 1]
-            near_rest = after(near_rest, ready)
-            cut = head - tokens
-            line = [*next_line[step - 1], near_first, near_rest[:cut], near_block, near_rest[cut:]]
-            line = jnp.concatenate(line)
+            line = jnp.concatenate([*next_line[step - 1], after(next_near[step - 1], ready)])
             parts = [line, swap_core(line)]
         for core in range(2):
             plan += [(core, 0, 2 * half)] if step else [(core, 0, half + head), (2 + core, 0, head)]
@@ -243,7 +241,7 @@
             other_high = after(swap_core(other_high), near).astype(jnp.float32)
             other_low = swap_core(after(other_low, near))
         else:
-            other_high, other_low = after((other_high, other_low), next_near[0][2])
+            other_high, other_low = after((other_high, other_low), next_near[0])
             other_high = swap_core(other_high).astype(jnp.float32)
             other_low = swap_core(other_low)
         to_high = (peer[head:].astype(jnp.float32) + other_high[head:]).astype(jnp.bfloat16)
@@ -252,14 +250,9 @@
         ready = to_high, to_low
         if step:
             near = after(near, other_low).astype(jnp.float32)
-            high += near[head:]
-            low += near[:head]
-            for by in strides[::-1]:
-                keep = high.shape[0] // 2
-                sent = jnp.concatenate([low[keep:], high[keep:]]).astype(jnp.bfloat16)
-                sent = swap_far(sent, by).astype(jnp.float32)
-                low, high = low[:keep] + sent[:keep], high[:keep] + sent[keep:]
-            outputs.append((low, swap_far(high.astype(jnp.bfloat16), middle)))
+            hop = collapse(high + near[head:])
+            low += after(near[:head], hop)
+            outputs.append((collapse(low), swap_far(hop.astype(jnp.bfloat16), middle)))
         high = own[head:].astype(jnp.float32) + other_high[:head]
         low = own[:head].astype(jnp.float32) + other_low[:head]
         if step + 1 < steps:
@@ -267,7 +260,7 @@
     near_high = swap_near(to_high)
     near = swap_near(after(to_low, near_high))
     outputs = [low + after(high, near).astype(jnp.float32) for low, high in outputs]
-    high = collapse(high + near_high.astype(jnp.float32))
+    high = collapse(high + after(near_high, hop).astype(jnp.float32))
     low += after(near, high).astype(jnp.float32)
     first = add(low[:tokens], swap_far(high.astype(jnp.bfloat16), middle))
     outputs.append(collapse(jnp.concatenate([first, low[tokens:]])))

time: 85.8 us -> 85.6 us (level)
  starting transfers between devices: 32.2 us -> 29.4 us
  waiting for transfers between devices: 30.9 us -> 33.7 us
    ppermute x11 -> x12, waiting for transfers between devices: 13.6 us -> 18.7 us  [swap_far(): lax.ppermute(x, 'expert', [(index(z, y, c), index(z ^ by, y, c)) for z, y...]
    ppermute x9, waiting for transfers between devices: 14.5 us -> 11.8 us  [swap_near(): lax.ppermute(x, 'expert', [(index(z, y, c), index(z, 1 - y, c)) for z, y,...]
    ppermute x9, starting transfers between devices: 13.2 us -> 11.5 us  [swap_near(): lax.ppermute(x, 'expert', [(index(z, y, c), index(z, 1 - y, c)) for z, y,...]
    ppermute x11 -> x12, starting transfers between devices: 17.9 us -> 16.3 us  [swap_far(): lax.ppermute(x, 'expert', [(index(z, y, c), index(z ^ by, y, c)) for z, y...]
  transfers between devices with their start and end apart: 27 -> 28, of which waited for: 14 -> 17; matrix products, arithmetic and copies ran while one was open for 2% -> 1% of each run, Pallas kernels for 22% -> 22%
where the time goes in v13:
time: 85.6 us; the launch traced here: 85.5 us
  waiting for transfers between devices  33.7 us (39%)
  starting transfers between devices  29.4 us (34%)
  Pallas kernels  19.9 us (23%)
  other arithmetic  1.83 us (2%)
    ppermute x12, waiting for transfers between devices, swap_far(): lax.ppermute(x, 'expert', [(index(z, y, c), index(z ^ by, y, c)) for z, y...  18.7 us
    ppermute x12, starting transfers between devices, swap_far(): lax.ppermute(x, 'expert', [(index(z, y, c), index(z ^ by, y, c)) for z, y...  16.3 us
    ppermute x9, waiting for transfers between devices, swap_near(): lax.ppermute(x, 'expert', [(index(z, y, c), index(z, 1 - y, c)) for z, y,...  11.8 us
    ppermute x9, starting transfers between devices, swap_near(): lax.ppermute(x, 'expert', [(index(z, y, c), index(z, 1 - y, c)) for z, y,...  11.5 us
    pallas_call x2, Pallas kernels, run_expert(): pl.pallas_call(functools.partial(expert_kernel, swapped, count, plan), ou...  11.3 us
    pallas_call x2, Pallas kernels, load_weights(): pl.pallas_call(load_kernel, out_shape=[pltpu.VMEM(x.shape, x.dtype) for x...  7.42 us
    ppermute x7, waiting for transfers between devices, swap_core(): lax.ppermute(x, 'expert', [(index(z, y, c), index(z, y, 1 - c)) for z, y,...  3.22 us
  transfers between devices with their start and end apart: 28, of which 17 were waited for; matrix products, arithmetic and copies ran while one was open for 1% of the time, Pallas kernels for 22%

profile of v13, /device:TPU:0, one launch (start us, length us, event | category | flops | bytes accessed | tf_op | source)
XLA Modules:
  0.0 85.5 jit_solution(8856486625885057165)
XLA Ops:
  0.0 1.2 %messages.1 = (bf16[16,4224]{1,0:T(8,128)(2,1)S(1)}, bf16[16,4224]{1,0:T(8,128)(2,1)S(1)}) custom-call(bf16[2,16,4096]{2,1,0:T(8,128)(2,1)} %states_ref.1, s32[2,8,16]{2,1,0:T(8,128)} %bitcast.12, f32[2,8,16]{2,1,0:T(8,128)} %bitcast.13), custom_call_target="tpu_custom_call" | custom-call | tf_op jit(solution)/shard_map/messages/pallas_call | solution.py:49
  1.2 4.0 %collective-permute-start.4 = (bf16[16,4224]{1,0:T(8,128)(2,1)S(1)}, bf16[16,4224]{1,0:T(8,128)(2,1)S(1)}, u32[]{:S(2)}, u32[]{:S(2)}) collective-permute-start(bf16[16,4224]{1,0:T(8,128)(2,1)S(1)} %get-tuple-element.49), channel_id=1, source_target_pairs={{0,8},{1,9},{2,10},{3,11},{4,12},{5,13},{6,14},{7,15},{8,0},{9,1},... | collective-permute-start | bytes 405512 | tf_op jit(solution)/shard_map/ppermute | solution.py:173
  5.3 1.6 %collective-permute-start.3 = (bf16[16,4224]{1,0:T(8,128)(2,1)S(1)}, bf16[16,4224]{1,0:T(8,128)(2,1)S(1)}, u32[]{:S(2)}, u32[]{:S(2)}) collective-permute-start(bf16[16,4224]{1,0:T(8,128)(2,1)S(1)} %get-tuple-element.49), channel_id=1, source_target_pairs={{0,4},{1,5},{2,6},{3,7},{4,0},{5,1},{6,2},{7,3},{8,12},{9,13},{10,... | collective-permute-start | bytes 405512 | tf_op jit(solution)/shard_map/ppermute | solution.py:173
  6.8 1.5 %collective-permute-start = (bf16[16,4224]{1,0:T(8,128)(2,1)S(1)}, bf16[16,4224]{1,0:T(8,128)(2,1)S(1)}, u32[]{:S(2)}, u32[]{:S(2)}) collective-permute-start(bf16[16,4224]{1,0:T(8,128)(2,1)S(1)} %get-tuple-element.49), channel_id=1, source_target_pairs={{0,2},{1,3},{2,0},{3,1},{4,6},{5,7},{6,4},{7,5},{8,10},{9,11},{10,... | collective-permute-start | bytes 405512 | tf_op jit(solution)/shard_map/ppermute | solution.py:170
  8.4 0.4 collective-permute-start.2
  8.8 0.5 collective-permute-start.1
  9.4 4.6 %load_weights.2 = (bf16[4096,768]{1,0:T(8,128)(2,1)S(1)}, bf16[4096,768]{1,0:T(8,128)(2,1)S(1)}) custom-call(bf16[4096,768]{1,0:T(8,128)(2,1)} %bitcast.9, bf16[4096,768]{1,0:T(8,128)(2,1)} %bitcast.10), custom_call_target="tpu_custom_call" | custom-call | tf_op jit(solution)/shard_map/load_weights/pallas_call | solution.py:73
  14.0 0.0 collective-permute-done
  14.0 0.9 %collective-permute-done.2 = bf16[16,4224]{1,0:T(8,128)(2,1)S(1)} collective-permute-done((bf16[16,4224]{1,0:T(8,128)(2,1)S(1)}, bf16[16,4224]{1,0:T(8,128)(2,1)S(1)}, u32[]{:S(2)}, u32[]{:S(2)}) %collective-permute-start.2) | collective-permute-done | bytes 135200 | tf_op jit(solution)/shard_map/ppermute | solution.py:173
  14.9 1.5 %collective-permute-start.5 = (bf16[16,4224]{1,0:T(8,128)(2,1)S(1)}, bf16[16,4224]{1,0:T(8,128)(2,1)S(1)}, u32[]{:S(2)}, u32[]{:S(2)}) collective-permute-start(bf16[16,4224]{1,0:T(8,128)(2,1)S(1)} %collective-permute-done.4), channel_id=1, source_target_pairs={{0,4},{1,5},{2,6},{3,7},{4,0},{5,1},{6,2},{7,3},{8,12},{9,13},{10,... | collective-permute-start | bytes 405512 | tf_op jit(solution)/shard_map/ppermute | solution.py:173
  16.5 1.7 %collective-permute-start.7 = (bf16[16,4224]{1,0:T(8,128)(2,1)S(1)}, bf16[16,4224]{1,0:T(8,128)(2,1)S(1)}, u32[]{:S(2)}, u32[]{:S(2)}) collective-permute-start(bf16[16,4224]{1,0:T(8,128)(2,1)S(1)} %get-tuple-element.59), channel_id=1, source_target_pairs={{0,8},{1,9},{2,10},{3,11},{4,12},{5,13},{6,14},{7,15},{8,0},{9,1},... | collective-permute-start | bytes 405512 | tf_op jit(solution)/shard_map/ppermute | solution.py:173
  18.2 1.6 %collective-permute-start.6 = (bf16[32,4224]{1,0:T(8,128)(2,1)S(1)}, bf16[32,4224]{1,0:T(8,128)(2,1)S(1)}, u32[]{:S(2)}, u32[]{:S(2)}) collective-permute-start(bf16[32,4224]{1,0:T(8,128)(2,1)S(1)} %pad_maximum_fusion.1), channel_id=1, source_target_pairs={{0,2},{1,3},{2,0},{3,1},{4,6},{5,7},{6,4},{7,5},{8,10},{9,11},{10,... | collective-permute-start | bytes 811016 | tf_op jit(solution)/shard_map/ppermute | solution.py:170
  19.8 1.4 %collective-permute-done.5 = bf16[16,4224]{1,0:T(8,128)(2,1)S(1)} collective-permute-done((bf16[16,4224]{1,0:T(8,128)(2,1)S(1)}, bf16[16,4224]{1,0:T(8,128)(2,1)S(1)}, u32[]{:S(2)}, u32[]{:S(2)}) %collective-permute-start.5) | collective-permute-done | bytes 135200 | tf_op jit(solution)/shard_map/ppermute | solution.py:173
  21.2 1.2 %collective-permute-start.9 = (bf16[32,4224]{1,0:T(8,128)(2,1)S(1)}, bf16[32,4224]{1,0:T(8,128)(2,1)S(1)}, u32[]{:S(2)}, u32[]{:S(2)}) collective-permute-start(bf16[32,4224]{1,0:T(8,128)(2,1)S(1)} %get-tuple-element.96), channel_id=1, source_target_pairs={{0,2},{1,3},{2,0},{3,1},{4,6},{5,7},{6,4},{7,5},{8,10},{9,11},{10,... | collective-permute-start | bytes 811016 | tf_op jit(solution)/shard_map/ppermute | solution.py:170
  22.4 2.8 %load_weights.3.down_ref = bf16[768,4096]{1,0:T(8,128)(2,1)S(1)} custom-call(bf16[768,4096]{1,0:T(8,128)(2,1)} %bitcast.11), custom_call_target="tpu_custom_call" | custom-call | tf_op jit(solution)/shard_map/load_weights/pallas_call | solution.py:73
  25.3 0.0 copy-start
  25.3 2.4 %collective-permute-done.6 = bf16[32,4224]{1,0:T(8,128)(2,1)S(1)} collective-permute-done((bf16[32,4224]{1,0:T(8,128)(2,1)S(1)}, bf16[32,4224]{1,0:T(8,128)(2,1)S(1)}, u32[]{:S(2)}, u32[]{:S(2)}) %collective-permute-start.6) | collective-permute-done | bytes 270368 | tf_op jit(solution)/shard_map/ppermute | solution.py:170
  27.7 0.3 collective-permute-start.11
  28.0 2.6 %collective-permute-done.9.refs_2_ = bf16[32,4224]{1,0:T(8,128)(2,1)S(1)} collective-permute-done((bf16[32,4224]{1,0:T(8,128)(2,1)S(1)}, bf16[32,4224]{1,0:T(8,128)(2,1)S(1)}, u32[]{:S(2)}, u32[]{:S(2)}) %collective-permute-start.9) | collective-permute-done | bytes 270368 | tf_op jit(solution)/shard_map/ppermute | solution.py:170
  30.6 2.1 %collective-permute-done.11 = bf16[16,4224]{1,0:T(8,128)(2,1)S(1)} collective-permute-done((bf16[16,4224]{1,0:T(8,128)(2,1)S(1)}, bf16[16,4224]{1,0:T(8,128)(2,1)S(1)}, u32[]{:S(2)}, u32[]{:S(2)}) %collective-permute-start.11) | collective-permute-done | bytes 135200 | tf_op jit(solution)/shard_map/ppermute | solution.py:173
  32.7 0.1 collective-permute-start.8
  32.8 0.5 collective-permute-start.10
  33.3 1.5 %collective-permute-start.16 = (bf16[16,4224]{1,0:T(8,128)(2,1)S(1)}, bf16[16,4224]{1,0:T(8,128)(2,1)S(1)}, u32[]{:S(2)}, u32[]{:S(2)}) collective-permute-start(bf16[16,4224]{1,0:T(8,128)(2,1)S(1)} %collective-permute-done.7), channel_id=1, source_target_pairs={{0,2},{1,3},{2,0},{3,1},{4,6},{5,7},{6,4},{7,5},{8,10},{9,11},{10,... | collective-permute-start | bytes 405512 | tf_op jit(solution)/shard_map/ppermute | solution.py:170
  34.8 0.5 collective-permute-start.12
  35.3 0.2 collective-permute-done.10.refs_3_
  35.5 5.6 %expert.2 = (bf16[64,4096]{1,0:T(8,128)(2,1)S(1)}, bf16[64,4096]{1,0:T(8,128)(2,1)S(1)}, bf16[64,4096]{1,0:T(8,128)(2,1)S(1)}, bf16[64,4096]{1,0:T(8,128)(2,1)S(1)}) custom-call(s32[16]{0:T(128)S(1)} %copy-done, bf16[4096,768]{1,0:T(8,128)(2,1)S(1)} %get-tuple-element.53.gate_ref, bf16[4096,768]{1,0:T(8,128)(2,1)S(1)} %get-tuple-element.54.up_ref, ...), custom_call_target="tpu_custom_call" | custom-call | flops 4831838208 | bytes 4194304 | tf_op jit(solution)/shard_map/expert/pallas_call | solution.py:123
  41.2 0.6 collective-permute-done.12
  41.8 0.6 collective-permute-start.13
  42.4 1.3 %collective-permute-done.14 = bf16[64,4096]{1,0:T(8,128)(2,1)S(1)} collective-permute-done((bf16[64,4096]{1,0:T(8,128)(2,1)S(1)}, bf16[64,4096]{1,0:T(8,128)(2,1)S(1)}, u32[]{:S(2)}, u32[]{:S(2)}) %collective-permute-start.14) | collective-permute-done | bytes 524320 | tf_op jit(solution)/shard_map/ppermute | solution.py:167
  43.7 0.1 convert_element_type.85
  43.8 0.1 fusion.6
  43.8 0.6 collective-permute-done.13
  44.4 0.1 convert_element_type.87
  44.5 0.1 fusion.4
  44.6 0.2 collective-permute-start.17
  44.8 1.6 %collective-permute-start.15 = (bf16[64,4096]{1,0:T(8,128)(2,1)S(1)}, bf16[64,4096]{1,0:T(8,128)(2,1)S(1)}, u32[]{:S(2)}, u32[]{:S(2)}) collective-permute-start(bf16[64,4096]{1,0:T(8,128)(2,1)S(1)} %pad_maximum_fusion), channel_id=1, source_target_pairs={{0,2},{1,3},{2,0},{3,1},{4,6},{5,7},{6,4},{7,5},{8,10},{9,11},{10,... | collective-permute-start | bytes 1572872 | tf_op jit(solution)/shard_map/ppermute | solution.py:170
  46.4 0.9 %collective-permute-done.17.refs_1_ = bf16[128,4224]{1,0:T(8,128)(2,1)S(1)} collective-permute-done((bf16[128,4224]{1,0:T(8,128)(2,1)S(1)}, bf16[128,4224]{1,0:T(8,128)(2,1)S(1)}, u32[]{:S(2)}, u32[]{:S(2)}) %collective-permute-start.17) | collective-permute-done | bytes 1081376 | tf_op jit(solution)/shard_map/ppermute | solution.py:167
  47.4 5.6 %expert.3 = (bf16[64,4096]{1,0:T(8,128)(2,1)S(1)}, bf16[64,4096]{1,0:T(8,128)(2,1)S(1)}, bf16[64,4096]{1,0:T(8,128)(2,1)S(1)}, bf16[64,4096]{1,0:T(8,128)(2,1)S(1)}) custom-call(s32[16]{0:T(128)S(1)} %copy-done, bf16[4096,768]{1,0:T(8,128)(2,1)S(1)} %get-tuple-element.53.gate_ref, bf16[4096,768]{1,0:T(8,128)(2,1)S(1)} %get-tuple-element.54.up_ref, ...), custom_call_target="tpu_custom_call" | custom-call | flops 4831838208 | bytes 4194304 | tf_op jit(solution)/shard_map/expert/pallas_call | solution.py:123
  53.0 0.2 collective-permute-start.19
  53.2 5.9 %collective-permute-done.15 = bf16[64,4096]{1,0:T(8,128)(2,1)S(1)} collective-permute-done((bf16[64,4096]{1,0:T(8,128)(2,1)S(1)}, bf16[64,4096]{1,0:T(8,128)(2,1)S(1)}, u32[]{:S(2)}, u32[]{:S(2)}) %collective-permute-start.15) | collective-permute-done | bytes 524320 | tf_op jit(solution)/shard_map/ppermute | solution.py:170
  59.1 0.1 convert_element_type.91
  59.2 0.1 fusion.3
  59.3 1.6 %collective-permute-start.23 = (bf16[32,4096]{1,0:T(8,128)(2,1)S(1)}, bf16[32,4096]{1,0:T(8,128)(2,1)S(1)}, u32[]{:S(2)}, u32[]{:S(2)}) collective-permute-start(bf16[32,4096]{1,0:T(8,128)(2,1)S(1)} %fusion.3), channel_id=1, source_target_pairs={{0,2},{1,3},{2,0},{3,1},{4,6},{5,7},{6,4},{7,5},{8,10},{9,11},{10,... | collective-permute-start | bytes 786440 | tf_op jit(solution)/shard_map/ppermute | solution.py:170
  60.8 0.2 collective-permute-done.18
  61.0 0.1 convert_element_type.93
  61.1 0.1 convert_element_type.94
  61.2 0.1 slice_add_fusion.3
  61.3 0.4 collective-permute-start.20
  61.7 0.1 fusion.2
  61.8 5.1 %collective-permute-done.20 = bf16[16,4096]{1,0:T(8,128)(2,1)S(1)} collective-permute-done((bf16[16,4096]{1,0:T(8,128)(2,1)S(1)}, bf16[16,4096]{1,0:T(8,128)(2,1)S(1)}, u32[]{:S(2)}, u32[]{:S(2)}) %collective-permute-start.20) | collective-permute-done | bytes 131104 | tf_op jit(solution)/shard_map/ppermute | solution.py:173
  66.9 1.4 %collective-permute-start.22 = (bf16[16,4096]{1,0:T(8,128)(2,1)S(1)}, bf16[16,4096]{1,0:T(8,128)(2,1)S(1)}, u32[]{:S(2)}, u32[]{:S(2)}) collective-permute-start(bf16[16,4096]{1,0:T(8,128)(2,1)S(1)} %slice_add_fusion.11), channel_id=1, source_target_pairs={{0,8},{1,9},{2,10},{3,11},{4,12},{5,13},{6,14},{7,15},{8,0},{9,1},... | collective-permute-start | bytes 393224 | tf_op jit(solution)/shard_map/ppermute | solution.py:173
  68.3 0.1 fusion
  68.4 0.6 collective-permute-start.25
  69.0 0.1 fusion.5
  69.1 1.5 %collective-permute-start.21 = (bf16[16,4096]{1,0:T(8,128)(2,1)S(1)}, bf16[16,4096]{1,0:T(8,128)(2,1)S(1)}, u32[]{:S(2)}, u32[]{:S(2)}) collective-permute-start(bf16[16,4096]{1,0:T(8,128)(2,1)S(1)} %slice.184), channel_id=1, source_target_pairs={{0,4},{1,5},{2,6},{3,7},{4,0},{5,1},{6,2},{7,3},{8,12},{9,13},{10,... | collective-permute-start | bytes 393224 | tf_op jit(solution)/shard_map/ppermute | solution.py:173
  70.7 1.5 %collective-permute-start.24 = (bf16[32,4096]{1,0:T(8,128)(2,1)S(1)}, bf16[32,4096]{1,0:T(8,128)(2,1)S(1)}, u32[]{:S(2)}, u32[]{:S(2)}) collective-permute-start(bf16[32,4096]{1,0:T(8,128)(2,1)S(1)} %fusion.2), channel_id=1, source_target_pairs={{0,2},{1,3},{2,0},{3,1},{4,6},{5,7},{6,4},{7,5},{8,10},{9,11},{10,... | collective-permute-start | bytes 786440 | tf_op jit(solution)/shard_map/ppermute | solution.py:170
  72.2 4.9 %collective-permute-done.25 = bf16[16,4096]{1,0:T(8,128)(2,1)S(1)} collective-permute-done((bf16[16,4096]{1,0:T(8,128)(2,1)S(1)}, bf16[16,4096]{1,0:T(8,128)(2,1)S(1)}, u32[]{:S(2)}, u32[]{:S(2)}) %collective-permute-start.25) | collective-permute-done | bytes 131104 | tf_op jit(solution)/shard_map/ppermute | solution.py:173
  77.1 0.4 collective-permute-start.26
  77.5 0.3 collective-permute-done.24
  77.8 0.1 fusion.1
  77.9 2.4 %collective-permute-start.27 = (bf16[16,4096]{1,0:T(8,128)(2,1)S(1)}, bf16[16,4096]{1,0:T(8,128)(2,1)S(1)}, u32[]{:S(2)}, u32[]{:S(2)}) collective-permute-start(bf16[16,4096]{1,0:T(8,128)(2,1)S(1)} %slice.182), channel_id=1, source_target_pairs={{0,4},{1,5},{2,6},{3,7},{4,0},{5,1},{6,2},{7,3},{8,12},{9,13},{10,... | collective-permute-start | bytes 393224 | tf_op jit(solution)/shard_map/ppermute | solution.py:173
  80.4 3.8 %collective-permute-done.26.second_ref = bf16[16,4096]{1,0:T(8,128)(2,1)S(1)} collective-permute-done((bf16[16,4096]{1,0:T(8,128)(2,1)S(1)}, bf16[16,4096]{1,0:T(8,128)(2,1)S(1)}, u32[]{:S(2)}, u32[]{:S(2)}) %collective-permute-start.26) | collective-permute-done | bytes 131104 | tf_op jit(solution)/shard_map/ppermute | solution.py:173
  84.3 0.4 collective-permute-done.27
  84.7 0.7 pad_maximum_fusion.2
  (39 shorter events, 0.6 us)
Async XLA Ops:
  1.2 12.8 %collective-permute-start.4 = (bf16[16,4224]{1,0:T(8,128)(2,1)S(1)}, bf16[16,4224]{1,0:T(8,128)(2,1)S(1)}, u32[]{:S(2)}, u32[]{:S(2)}) collective-permute-start(bf16[16,4224]{1,0:T(8,128)(2,1)S(1)} %get-tuple-element.49), channel_id=1, source_target_pairs={{0,8},{1,9},{2,10},{3,11},{4,12},{5,13},{6,14},{7,15},{8,0},{9,1},... | collective-permute-start | bytes 405512 | tf_op jit(solution)/shard_map/ppermute | solution.py:173
  5.3 8.7 %collective-permute-start.3 = (bf16[16,4224]{1,0:T(8,128)(2,1)S(1)}, bf16[16,4224]{1,0:T(8,128)(2,1)S(1)}, u32[]{:S(2)}, u32[]{:S(2)}) collective-permute-start(bf16[16,4224]{1,0:T(8,128)(2,1)S(1)} %get-tuple-element.49), channel_id=1, source_target_pairs={{0,4},{1,5},{2,6},{3,7},{4,0},{5,1},{6,2},{7,3},{8,12},{9,13},{10,... | collective-permute-start | bytes 405512 | tf_op jit(solution)/shard_map/ppermute | solution.py:173
  6.8 7.2 %collective-permute-start = (bf16[16,4224]{1,0:T(8,128)(2,1)S(1)}, bf16[16,4224]{1,0:T(8,128)(2,1)S(1)}, u32[]{:S(2)}, u32[]{:S(2)}) collective-permute-start(bf16[16,4224]{1,0:T(8,128)(2,1)S(1)} %get-tuple-element.49), channel_id=1, source_target_pairs={{0,2},{1,3},{2,0},{3,1},{4,6},{5,7},{6,4},{7,5},{8,10},{9,11},{10,... | collective-permute-start | bytes 405512 | tf_op jit(solution)/shard_map/ppermute | solution.py:170
  8.4 6.6 %collective-permute-start.2 = (bf16[16,4224]{1,0:T(8,128)(2,1)S(1)}, bf16[16,4224]{1,0:T(8,128)(2,1)S(1)}, u32[]{:S(2)}, u32[]{:S(2)}) collective-permute-start(bf16[16,4224]{1,0:T(8,128)(2,1)S(1)} %get-tuple-element.59), channel_id=1, source_target_pairs={{0,4},{1,5},{2,6},{3,7},{4,0},{5,1},{6,2},{7,3},{8,12},{9,13},{10,... | collective-permute-start | bytes 405512 | tf_op jit(solution)/shard_map/ppermute | solution.py:173
  8.8 6.1 %collective-permute-start.1 = (bf16[16,4224]{1,0:T(8,128)(2,1)S(1)}, bf16[16,4224]{1,0:T(8,128)(2,1)S(1)}, u32[]{:S(2)}, u32[]{:S(2)}) collective-permute-start(bf16[16,4224]{1,0:T(8,128)(2,1)S(1)} %get-tuple-element.59), channel_id=1, source_target_pairs={{0,2},{1,3},{2,0},{3,1},{4,6},{5,7},{6,4},{7,5},{8,10},{9,11},{10,... | collective-permute-start | bytes 405512 | tf_op jit(solution)/shard_map/ppermute | solution.py:170
  14.9 6.3 %collective-permute-start.5 = (bf16[16,4224]{1,0:T(8,128)(2,1)S(1)}, bf16[16,4224]{1,0:T(8,128)(2,1)S(1)}, u32[]{:S(2)}, u32[]{:S(2)}) collective-permute-start(bf16[16,4224]{1,0:T(8,128)(2,1)S(1)} %collective-permute-done.4), channel_id=1, source_target_pairs={{0,4},{1,5},{2,6},{3,7},{4,0},{5,1},{6,2},{7,3},{8,12},{9,13},{10,... | collective-permute-start | bytes 405512 | tf_op jit(solution)/shard_map/ppermute | solution.py:173
  16.5 8.8 %collective-permute-start.7 = (bf16[16,4224]{1,0:T(8,128)(2,1)S(1)}, bf16[16,4224]{1,0:T(8,128)(2,1)S(1)}, u32[]{:S(2)}, u32[]{:S(2)}) collective-permute-start(bf16[16,4224]{1,0:T(8,128)(2,1)S(1)} %get-tuple-element.59), channel_id=1, source_target_pairs={{0,8},{1,9},{2,10},{3,11},{4,12},{5,13},{6,14},{7,15},{8,0},{9,1},... | collective-permute-start | bytes 405512 | tf_op jit(solution)/shard_map/ppermute | solution.py:173
  18.2 9.5 %collective-permute-start.6 = (bf16[32,4224]{1,0:T(8,128)(2,1)S(1)}, bf16[32,4224]{1,0:T(8,128)(2,1)S(1)}, u32[]{:S(2)}, u32[]{:S(2)}) collective-permute-start(bf16[32,4224]{1,0:T(8,128)(2,1)S(1)} %pad_maximum_fusion.1), channel_id=1, source_target_pairs={{0,2},{1,3},{2,0},{3,1},{4,6},{5,7},{6,4},{7,5},{8,10},{9,11},{10,... | collective-permute-start | bytes 811016 | tf_op jit(solution)/shard_map/ppermute | solution.py:170
  21.2 9.3 %collective-permute-start.9 = (bf16[32,4224]{1,0:T(8,128)(2,1)S(1)}, bf16[32,4224]{1,0:T(8,128)(2,1)S(1)}, u32[]{:S(2)}, u32[]{:S(2)}) collective-permute-start(bf16[32,4224]{1,0:T(8,128)(2,1)S(1)} %get-tuple-element.96), channel_id=1, source_target_pairs={{0,2},{1,3},{2,0},{3,1},{4,6},{5,7},{6,4},{7,5},{8,10},{9,11},{10,... | collective-permute-start | bytes 811016 | tf_op jit(solution)/shard_map/ppermute | solution.py:170
  25.3 10.3 %copy-start = (s32[16]{0:T(128)S(1)}, s32[16]{0:T(128)}, u32[]{:S(2)}) copy-start(s32[16]{0:T(128)} %flags_ref.3) | copy-start | bytes 196
  27.7 5.0 %collective-permute-start.11 = (bf16[16,4224]{1,0:T(8,128)(2,1)S(1)}, bf16[16,4224]{1,0:T(8,128)(2,1)S(1)}, u32[]{:S(2)}, u32[]{:S(2)}) collective-permute-start(bf16[16,4224]{1,0:T(8,128)(2,1)S(1)} %collective-permute-done.7), channel_id=1, source_target_pairs={{0,4},{1,5},{2,6},{3,7},{4,0},{5,1},{6,2},{7,3},{8,12},{9,13},{10,... | collective-permute-start | bytes 405512 | tf_op jit(solution)/shard_map/ppermute | solution.py:173
  32.7 2.8 %collective-permute-start.8 = (bf16[96,4224]{1,0:T(8,128)(2,1)S(1)}, bf16[96,4224]{1,0:T(8,128)(2,1)S(1)}, u32[]{:S(2)}, u32[]{:S(2)}) collective-permute-start(bf16[96,4224]{1,0:T(8,128)(2,1)S(1)} %get-tuple-element.63.refs_0_), channel_id=1, source_target_pairs={{0,1},{1,0},{2,3},{3,2},{4,5},{5,4},{6,7},{7,6},{8,9},{9,8},{10,11... | collective-permute-start | bytes 2433032 | tf_op jit(solution)/shard_map/ppermute | solution.py:167
  32.8 2.7 %collective-permute-start.10 = (bf16[32,4224]{1,0:T(8,128)(2,1)S(1)}, bf16[32,4224]{1,0:T(8,128)(2,1)S(1)}, u32[]{:S(2)}, u32[]{:S(2)}) collective-permute-start(bf16[32,4224]{1,0:T(8,128)(2,1)S(1)} %collective-permute-done.9.refs_2_), channel_id=1, source_target_pairs={{0,1},{1,0},{2,3},{3,2},{4,5},{5,4},{6,7},{7,6},{8,9},{9,8},{10,11... | collective-permute-start | bytes 811016 | tf_op jit(solution)/shard_map/ppermute | solution.py:167
  33.3 8.5 %collective-permute-start.16 = (bf16[16,4224]{1,0:T(8,128)(2,1)S(1)}, bf16[16,4224]{1,0:T(8,128)(2,1)S(1)}, u32[]{:S(2)}, u32[]{:S(2)}) collective-permute-start(bf16[16,4224]{1,0:T(8,128)(2,1)S(1)} %collective-permute-done.7), channel_id=1, source_target_pairs={{0,2},{1,3},{2,0},{3,1},{4,6},{5,7},{6,4},{7,5},{8,10},{9,11},{10,... | collective-permute-start | bytes 405512 | tf_op jit(solution)/shard_map/ppermute | solution.py:170
  34.8 6.9 %collective-permute-start.12 = (bf16[16,4224]{1,0:T(8,128)(2,1)S(1)}, bf16[16,4224]{1,0:T(8,128)(2,1)S(1)}, u32[]{:S(2)}, u32[]{:S(2)}) collective-permute-start(bf16[16,4224]{1,0:T(8,128)(2,1)S(1)} %collective-permute-done.11), channel_id=1, source_target_pairs={{0,2},{1,3},{2,0},{3,1},{4,6},{5,7},{6,4},{7,5},{8,10},{9,11},{10,... | collective-permute-start | bytes 405512 | tf_op jit(solution)/shard_map/ppermute | solution.py:170
  41.8 1.9 %collective-permute-start.14 = (bf16[64,4096]{1,0:T(8,128)(2,1)S(1)}, bf16[64,4096]{1,0:T(8,128)(2,1)S(1)}, u32[]{:S(2)}, u32[]{:S(2)}) collective-permute-start(bf16[64,4096]{1,0:T(8,128)(2,1)S(1)} %get-tuple-element.74), channel_id=1, source_target_pairs={{0,1},{1,0},{2,3},{3,2},{4,5},{5,4},{6,7},{7,6},{8,9},{9,8},{10,11... | collective-permute-start | bytes 1572872 | tf_op jit(solution)/shard_map/ppermute | solution.py:167
  41.8 2.6 %collective-permute-start.13 = (bf16[64,4096]{1,0:T(8,128)(2,1)S(1)}, bf16[64,4096]{1,0:T(8,128)(2,1)S(1)}, u32[]{:S(2)}, u32[]{:S(2)}) collective-permute-start(bf16[64,4096]{1,0:T(8,128)(2,1)S(1)} %get-tuple-element.72), channel_id=1, source_target_pairs={{0,1},{1,0},{2,3},{3,2},{4,5},{5,4},{6,7},{7,6},{8,9},{9,8},{10,11... | collective-permute-start | bytes 1572872 | tf_op jit(solution)/shard_map/ppermute | solution.py:167
  44.6 2.8 %collective-permute-start.17 = (bf16[128,4224]{1,0:T(8,128)(2,1)S(1)}, bf16[128,4224]{1,0:T(8,128)(2,1)S(1)}, u32[]{:S(2)}, u32[]{:S(2)}) collective-permute-start(bf16[128,4224]{1,0:T(8,128)(2,1)S(1)} %constant_dynamic-update-slice_fusion.7.refs_0_), channel_id=1, source_target_pairs={{0,1},{1,0},{2,3},{3,2},{4,5},{5,4},{6,7},{7,6},{8,9},{9,8},{10,11... | collective-permute-start | bytes 3244040 | tf_op jit(solution)/shard_map/ppermute | solution.py:167
  44.8 14.3 %collective-permute-start.15 = (bf16[64,4096]{1,0:T(8,128)(2,1)S(1)}, bf16[64,4096]{1,0:T(8,128)(2,1)S(1)}, u32[]{:S(2)}, u32[]{:S(2)}) collective-permute-start(bf16[64,4096]{1,0:T(8,128)(2,1)S(1)} %pad_maximum_fusion), channel_id=1, source_target_pairs={{0,2},{1,3},{2,0},{3,1},{4,6},{5,7},{6,4},{7,5},{8,10},{9,11},{10,... | collective-permute-start | bytes 1572872 | tf_op jit(solution)/shard_map/ppermute | solution.py:170
  53.0 6.1 %collective-permute-start.19 = (bf16[64,4096]{1,0:T(8,128)(2,1)S(1)}, bf16[64,4096]{1,0:T(8,128)(2,1)S(1)}, u32[]{:S(2)}, u32[]{:S(2)}) collective-permute-start(bf16[64,4096]{1,0:T(8,128)(2,1)S(1)} %get-tuple-element.83), channel_id=1, source_target_pairs={{0,1},{1,0},{2,3},{3,2},{4,5},{5,4},{6,7},{7,6},{8,9},{9,8},{10,11... | collective-permute-start | bytes 1572872 | tf_op jit(solution)/shard_map/ppermute | solution.py:167
  59.1 1.9 %collective-permute-start.18 = (bf16[64,4096]{1,0:T(8,128)(2,1)S(1)}, bf16[64,4096]{1,0:T(8,128)(2,1)S(1)}, u32[]{:S(2)}, u32[]{:S(2)}) collective-permute-start(bf16[64,4096]{1,0:T(8,128)(2,1)S(1)} %get-tuple-element.81), channel_id=1, source_target_pairs={{0,1},{1,0},{2,3},{3,2},{4,5},{5,4},{6,7},{7,6},{8,9},{9,8},{10,11... | collective-permute-start | bytes 1572872 | tf_op jit(solution)/shard_map/ppermute | solution.py:167
  59.3 9.0 %collective-permute-start.23 = (bf16[32,4096]{1,0:T(8,128)(2,1)S(1)}, bf16[32,4096]{1,0:T(8,128)(2,1)S(1)}, u32[]{:S(2)}, u32[]{:S(2)}) collective-permute-start(bf16[32,4096]{1,0:T(8,128)(2,1)S(1)} %fusion.3), channel_id=1, source_target_pairs={{0,2},{1,3},{2,0},{3,1},{4,6},{5,7},{6,4},{7,5},{8,10},{9,11},{10,... | collective-permute-start | bytes 786440 | tf_op jit(solution)/shard_map/ppermute | solution.py:170
  61.3 5.6 %collective-permute-start.20 = (bf16[16,4096]{1,0:T(8,128)(2,1)S(1)}, bf16[16,4096]{1,0:T(8,128)(2,1)S(1)}, u32[]{:S(2)}, u32[]{:S(2)}) collective-permute-start(bf16[16,4096]{1,0:T(8,128)(2,1)S(1)} %slice.185), channel_id=1, source_target_pairs={{0,4},{1,5},{2,6},{3,7},{4,0},{5,1},{6,2},{7,3},{8,12},{9,13},{10,... | collective-permute-start | bytes 393224 | tf_op jit(solution)/shard_map/ppermute | solution.py:173
  66.9 17.3 %collective-permute-start.22 = (bf16[16,4096]{1,0:T(8,128)(2,1)S(1)}, bf16[16,4096]{1,0:T(8,128)(2,1)S(1)}, u32[]{:S(2)}, u32[]{:S(2)}) collective-permute-start(bf16[16,4096]{1,0:T(8,128)(2,1)S(1)} %slice_add_fusion.11), channel_id=1, source_target_pairs={{0,8},{1,9},{2,10},{3,11},{4,12},{5,13},{6,14},{7,15},{8,0},{9,1},... | collective-permute-start | bytes 393224 | tf_op jit(solution)/shard_map/ppermute | solution.py:173
  68.4 8.7 %collective-permute-start.25 = (bf16[16,4096]{1,0:T(8,128)(2,1)S(1)}, bf16[16,4096]{1,0:T(8,128)(2,1)S(1)}, u32[]{:S(2)}, u32[]{:S(2)}) collective-permute-start(bf16[16,4096]{1,0:T(8,128)(2,1)S(1)} %slice.183), channel_id=1, source_target_pairs={{0,4},{1,5},{2,6},{3,7},{4,0},{5,1},{6,2},{7,3},{8,12},{9,13},{10,... | collective-permute-start | bytes 393224 | tf_op jit(solution)/shard_map/ppermute | solution.py:173
  69.1 15.1 %collective-permute-start.21 = (bf16[16,4096]{1,0:T(8,128)(2,1)S(1)}, bf16[16,4096]{1,0:T(8,128)(2,1)S(1)}, u32[]{:S(2)}, u32[]{:S(2)}) collective-permute-start(bf16[16,4096]{1,0:T(8,128)(2,1)S(1)} %slice.184), channel_id=1, source_target_pairs={{0,4},{1,5},{2,6},{3,7},{4,0},{5,1},{6,2},{7,3},{8,12},{9,13},{10,... | collective-permute-start | bytes 393224 | tf_op jit(solution)/shard_map/ppermute | solution.py:173
  70.7 7.1 %collective-permute-start.24 = (bf16[32,4096]{1,0:T(8,128)(2,1)S(1)}, bf16[32,4096]{1,0:T(8,128)(2,1)S(1)}, u32[]{:S(2)}, u32[]{:S(2)}) collective-permute-start(bf16[32,4096]{1,0:T(8,128)(2,1)S(1)} %fusion.2), channel_id=1, source_target_pairs={{0,2},{1,3},{2,0},{3,1},{4,6},{5,7},{6,4},{7,5},{8,10},{9,11},{10,... | collective-permute-start | bytes 786440 | tf_op jit(solution)/shard_map/ppermute | solution.py:170
  77.1 7.1 %collective-permute-start.26 = (bf16[16,4096]{1,0:T(8,128)(2,1)S(1)}, bf16[16,4096]{1,0:T(8,128)(2,1)S(1)}, u32[]{:S(2)}, u32[]{:S(2)}) collective-permute-start(bf16[16,4096]{1,0:T(8,128)(2,1)S(1)} %slice_add_fusion.9), channel_id=1, source_target_pairs={{0,8},{1,9},{2,10},{3,11},{4,12},{5,13},{6,14},{7,15},{8,0},{9,1},... | collective-permute-start | bytes 393224 | tf_op jit(solution)/shard_map/ppermute | solution.py:173
  77.9 6.8 %collective-permute-start.27 = (bf16[16,4096]{1,0:T(8,128)(2,1)S(1)}, bf16[16,4096]{1,0:T(8,128)(2,1)S(1)}, u32[]{:S(2)}, u32[]{:S(2)}) collective-permute-start(bf16[16,4096]{1,0:T(8,128)(2,1)S(1)} %slice.182), channel_id=1, source_target_pairs={{0,4},{1,5},{2,6},{3,7},{4,0},{5,1},{6,2},{7,3},{8,12},{9,13},{10,... | collective-permute-start | bytes 393224 | tf_op jit(solution)/shard_map/ppermute | solution.py:173

commit v14 on v9

--- a/solution.py
+++ b/solution.py
@@ -205,7 +205,7 @@
     close = [messages[0], *[swap_far(messages[0], by) for by in places(strides)[1:]]]
     near_close = [swap_near(messages[0])]
     loaded = load_weights(w_gate, w_up)
-    loaded, near_close, close, far = lax.optimization_barrier((loaded, near_close, close, far))
+    far, close, near_close, loaded = lax.optimization_barrier((far, close, near_close, loaded))
     others = close[1:]
     near_close += [swap_near(block) for block in others]
     crossed = [swap_far(after(message, far), middle) for message in messages[1:]]
@@ -221,10 +221,10 @@
     wanted += [middle ^ place for place in wanted]
     found = places([middle] + strides)
     for message, block, near in zip(messages[1:], crossed, near_own):
-        line = after(grow(jnp.concatenate([message, block]), strides), near_far)
+        line = grow(jnp.concatenate([message, block]), strides)
         near_line = swap_near(line[tokens:])
         line = jnp.concatenate([line, near])
-        sources.append([line, swap_core(line), near_line, swap_core(near_line)])
+        sources.append([line, near_line])
     outputs, ready = [], [source[0] for source in sources]
     for step in range(steps):
         plan = []
@@ -236,29 +236,33 @@
             else:
                 plan += [(core, 0, half + head), (2 + core, 0, head)]
         parts = sources[step]
+        if step:
+            line, near_line = after(sources[step], ready)
+            parts = [line, swap_core(line), near_line, swap_core(near_line)]
         own, peer, other_low, other_high = run_expert(step > 0, flags, loaded, after(parts, ready), tuple(plan))
-        other_high = swap_core(other_high if step else after(other_high, sources[1][1:3]))
+        other_high = swap_core(other_high if step else after(other_high, sources[1][1]))
         if step:
             other_high = after(other_high, near)
         other_high = other_high.astype(jnp.float32)
-        other_low = swap_core(after(other_low, near if step else sources[1][2]))
+        other_low = swap_core(after(other_low, near if step else sources[1][1]))
         to_high = (peer[head:].astype(jnp.float32) + other_high[head:]).astype(jnp.bfloat16)
         other_low = after(other_low, to_high).astype(jnp.float32)
         to_low = (peer[:head].astype(jnp.float32) + other_low[head:]).astype(jnp.bfloat16)
         ready = to_high, to_low
         if step:
             near = after(near, to_high).astype(jnp.float32)
-            high = collapse(high + near[head:])
+            high += near[head:]
             low += after(near[:head], high)
-            high = swap_far(high.astype(jnp.bfloat16), middle)
+            high = swap_far(collapse(high).astype(jnp.bfloat16), middle)
             outputs.append((collapse(low), high))
         high = own[head:].astype(jnp.float32) + other_high[:head]
         low = own[:head].astype(jnp.float32) + other_low[:head]
         if step + 1 < steps:
             near = swap_near(jnp.concatenate([to_low, to_high]))
-    near = swap_near(to_low)
+    near_high = swap_near(to_high)
+    near = swap_near(after(to_low, near_high))
     outputs = [low + after(high, near).astype(jnp.float32) for low, high in outputs]
-    high = collapse(high + swap_near(to_high).astype(jnp.float32))
+    high = collapse(high + near_high.astype(jnp.float32))
     low += after(near, high).astype(jnp.float32)
     first = add(low[:tokens], swap_far(high.astype(jnp.bfloat16), middle))
     outputs.append(collapse(jnp.concatenate([first, low[tokens:]])))

time: 85.2 us -> 83.6 us (0.981)
  starting transfers between devices: 30 us -> 25.1 us
  waiting for transfers between devices: 32.5 us -> 35.9 us
    ppermute x8, waiting for transfers between devices: 2.6 us -> 5.9 us  [swap_core(): lax.ppermute(x, 'expert', [(index(z, y, c), index(z, y, 1 - c)) for z, y,...]
    ppermute x8, waiting for transfers between devices: 10.4 us -> 13.5 us  [swap_near(): lax.ppermute(x, 'expert', [(index(z, y, c), index(z, 1 - y, c)) for z, y,...]
    ppermute x11, waiting for transfers between devices: 19.5 us -> 16.6 us  [swap_far(): lax.ppermute(x, 'expert', [(index(z, y, c), index(z ^ by, y, c)) for z, y...]
    ppermute x8, starting transfers between devices: 11.9 us -> 9.2 us  [swap_near(): lax.ppermute(x, 'expert', [(index(z, y, c), index(z, 1 - y, c)) for z, y,...]
    ppermute x11, starting transfers between devices: 16.7 us -> 14.4 us  [swap_far(): lax.ppermute(x, 'expert', [(index(z, y, c), index(z ^ by, y, c)) for z, y...]
  transfers between devices with their start and end apart: 27 -> 27, of which waited for: 10 -> 14; matrix products, arithmetic and copies ran while one was open for 1% -> 2% of each run, Pallas kernels for 22% -> 22%
where the time goes in v14:
time: 83.6 us; the launch traced here: 83.5 us
  waiting for transfers between devices  35.9 us (43%)
  starting transfers between devices  25.1 us (30%)
  Pallas kernels  19.9 us (24%)
  other arithmetic  1.92 us (2%)
    ppermute x11, waiting for transfers between devices, swap_far(): lax.ppermute(x, 'expert', [(index(z, y, c), index(z ^ by, y, c)) for z, y...  16.6 us
    ppermute x11, starting transfers between devices, swap_far(): lax.ppermute(x, 'expert', [(index(z, y, c), index(z ^ by, y, c)) for z, y...  14.4 us
    ppermute x8, waiting for transfers between devices, swap_near(): lax.ppermute(x, 'expert', [(index(z, y, c), index(z, 1 - y, c)) for z, y,...  13.5 us
    pallas_call x2, Pallas kernels, run_expert(): pl.pallas_call(functools.partial(expert_kernel, swapped, count, plan), ou...  11.3 us
    ppermute x8, starting transfers between devices, swap_near(): lax.ppermute(x, 'expert', [(index(z, y, c), index(z, 1 - y, c)) for z, y,...  9.2 us
    pallas_call x2, Pallas kernels, load_weights(): pl.pallas_call(load_kernel, out_shape=[pltpu.VMEM(x.shape, x.dtype) for x...  7.43 us
    ppermute x8, waiting for transfers between devices, swap_core(): lax.ppermute(x, 'expert', [(index(z, y, c), index(z, y, 1 - c)) for z, y,...  5.9 us
  transfers between devices with their start and end apart: 27, of which 14 were waited for; matrix products, arithmetic and copies ran while one was open for 2% of the time, Pallas kernels for 22%

profile of v14, /device:TPU:0, one launch (start us, length us, event | category | flops | bytes accessed | tf_op | source)
XLA Modules:
  0.0 83.5 jit_solution(17818256590634229305)
XLA Ops:
  0.0 1.2 %messages.1 = (bf16[16,4224]{1,0:T(8,128)(2,1)S(1)}, bf16[16,4224]{1,0:T(8,128)(2,1)S(1)}) custom-call(bf16[2,16,4096]{2,1,0:T(8,128)(2,1)} %states_ref.1, s32[2,8,16]{2,1,0:T(8,128)} %bitcast.12, f32[2,8,16]{2,1,0:T(8,128)} %bitcast.13), custom_call_target="tpu_custom_call" | custom-call | tf_op jit(solution)/shard_map/messages/pallas_call | solution.py:49
  1.2 3.0 %collective-permute-start.2 = (bf16[16,4224]{1,0:T(8,128)(2,1)S(1)}, bf16[16,4224]{1,0:T(8,128)(2,1)S(1)}, u32[]{:S(2)}, u32[]{:S(2)}) collective-permute-start(bf16[16,4224]{1,0:T(8,128)(2,1)S(1)} %get-tuple-element.65), channel_id=1, source_target_pairs={{0,2},{1,3},{2,0},{3,1},{4,6},{5,7},{6,4},{7,5},{8,10},{9,11},{10,... | collective-permute-start | bytes 405512 | tf_op jit(solution)/shard_map/ppermute | solution.py:170
  4.2 1.6 %collective-permute-start.1 = (bf16[16,4224]{1,0:T(8,128)(2,1)S(1)}, bf16[16,4224]{1,0:T(8,128)(2,1)S(1)}, u32[]{:S(2)}, u32[]{:S(2)}) collective-permute-start(bf16[16,4224]{1,0:T(8,128)(2,1)S(1)} %get-tuple-element.65), channel_id=1, source_target_pairs={{0,4},{1,5},{2,6},{3,7},{4,0},{5,1},{6,2},{7,3},{8,12},{9,13},{10,... | collective-permute-start | bytes 405512 | tf_op jit(solution)/shard_map/ppermute | solution.py:173
  5.8 2.6 %collective-permute-start = (bf16[16,4224]{1,0:T(8,128)(2,1)S(1)}, bf16[16,4224]{1,0:T(8,128)(2,1)S(1)}, u32[]{:S(2)}, u32[]{:S(2)}) collective-permute-start(bf16[16,4224]{1,0:T(8,128)(2,1)S(1)} %get-tuple-element.65), channel_id=1, source_target_pairs={{0,8},{1,9},{2,10},{3,11},{4,12},{5,13},{6,14},{7,15},{8,0},{9,1},... | collective-permute-start | bytes 405512 | tf_op jit(solution)/shard_map/ppermute | solution.py:173
  8.4 4.6 %load_weights.2 = (bf16[4096,768]{1,0:T(8,128)(2,1)S(1)}, bf16[4096,768]{1,0:T(8,128)(2,1)S(1)}) custom-call(bf16[4096,768]{1,0:T(8,128)(2,1)} %bitcast.9, bf16[4096,768]{1,0:T(8,128)(2,1)} %bitcast.10), custom_call_target="tpu_custom_call" | custom-call | tf_op jit(solution)/shard_map/load_weights/pallas_call | solution.py:73
  13.0 0.0 collective-permute-done.2
  13.0 0.0 collective-permute-done.1
  13.0 1.3 %collective-permute-done = bf16[16,4224]{1,0:T(8,128)(2,1)S(1)} collective-permute-done((bf16[16,4224]{1,0:T(8,128)(2,1)S(1)}, bf16[16,4224]{1,0:T(8,128)(2,1)S(1)}, u32[]{:S(2)}, u32[]{:S(2)}) %collective-permute-start) | collective-permute-done | bytes 135200 | tf_op jit(solution)/shard_map/ppermute | solution.py:173
  14.4 0.3 collective-permute-start.6
  14.7 0.5 collective-permute-start.4
  15.2 1.5 %collective-permute-start.5 = (bf16[16,4224]{1,0:T(8,128)(2,1)S(1)}, bf16[16,4224]{1,0:T(8,128)(2,1)S(1)}, u32[]{:S(2)}, u32[]{:S(2)}) collective-permute-start(bf16[16,4224]{1,0:T(8,128)(2,1)S(1)} %get-tuple-element.62), channel_id=1, source_target_pairs={{0,2},{1,3},{2,0},{3,1},{4,6},{5,7},{6,4},{7,5},{8,10},{9,11},{10,... | collective-permute-start | bytes 405512 | tf_op jit(solution)/shard_map/ppermute | solution.py:170
  16.8 2.8 %collective-permute-start.3 = (bf16[16,4224]{1,0:T(8,128)(2,1)S(1)}, bf16[16,4224]{1,0:T(8,128)(2,1)S(1)}, u32[]{:S(2)}, u32[]{:S(2)}) collective-permute-start(bf16[16,4224]{1,0:T(8,128)(2,1)S(1)} %get-tuple-element.62), channel_id=1, source_target_pairs={{0,8},{1,9},{2,10},{3,11},{4,12},{5,13},{6,14},{7,15},{8,0},{9,1},... | collective-permute-start | bytes 405512 | tf_op jit(solution)/shard_map/ppermute | solution.py:173
  19.6 1.0 %collective-permute-done.6 = bf16[16,4224]{1,0:T(8,128)(2,1)S(1)} collective-permute-done((bf16[16,4224]{1,0:T(8,128)(2,1)S(1)}, bf16[16,4224]{1,0:T(8,128)(2,1)S(1)}, u32[]{:S(2)}, u32[]{:S(2)}) %collective-permute-start.6) | collective-permute-done | bytes 135200 | tf_op jit(solution)/shard_map/ppermute | solution.py:173
  20.7 0.6 collective-permute-start.8
  21.3 2.8 %load_weights.3.down_ref = bf16[768,4096]{1,0:T(8,128)(2,1)S(1)} custom-call(bf16[768,4096]{1,0:T(8,128)(2,1)} %bitcast.11), custom_call_target="tpu_custom_call" | custom-call | tf_op jit(solution)/shard_map/load_weights/pallas_call | solution.py:73
  24.1 0.0 collective-permute-done.5
  24.1 0.0 collective-permute-done.4
  24.2 1.4 %collective-permute-start.10 = (bf16[32,4224]{1,0:T(8,128)(2,1)S(1)}, bf16[32,4224]{1,0:T(8,128)(2,1)S(1)}, u32[]{:S(2)}, u32[]{:S(2)}) collective-permute-start(bf16[32,4224]{1,0:T(8,128)(2,1)S(1)} %pad_maximum_fusion.2), channel_id=1, source_target_pairs={{0,4},{1,5},{2,6},{3,7},{4,0},{5,1},{6,2},{7,3},{8,12},{9,13},{10,... | collective-permute-start | bytes 811016 | tf_op jit(solution)/shard_map/ppermute | solution.py:173
  25.6 0.1 collective-permute-start.7
  25.7 5.0 %collective-permute-done.10 = bf16[32,4224]{1,0:T(8,128)(2,1)S(1)} collective-permute-done((bf16[32,4224]{1,0:T(8,128)(2,1)S(1)}, bf16[32,4224]{1,0:T(8,128)(2,1)S(1)}, u32[]{:S(2)}, u32[]{:S(2)}) %collective-permute-start.10) | collective-permute-done | bytes 270368 | tf_op jit(solution)/shard_map/ppermute | solution.py:173
  30.7 1.6 %collective-permute-start.11 = (bf16[48,4224]{1,0:T(8,128)(2,1)S(1)}, bf16[48,4224]{1,0:T(8,128)(2,1)S(1)}, u32[]{:S(2)}, u32[]{:S(2)}) collective-permute-start(bf16[48,4224]{1,0:T(8,128)(2,1)S(1)} %pad_maximum_fusion.1), channel_id=1, source_target_pairs={{0,2},{1,3},{2,0},{3,1},{4,6},{5,7},{6,4},{7,5},{8,10},{9,11},{10,... | collective-permute-start | bytes 1216520 | tf_op jit(solution)/shard_map/ppermute | solution.py:170
  32.3 0.0 collective-permute-done.8.refs_2_
  32.3 0.0 collective-permute-start.9
  32.4 1.5 %collective-permute-done.9.refs_3_ = bf16[32,4224]{1,0:T(8,128)(2,1)S(1)} collective-permute-done((bf16[32,4224]{1,0:T(8,128)(2,1)S(1)}, bf16[32,4224]{1,0:T(8,128)(2,1)S(1)}, u32[]{:S(2)}, u32[]{:S(2)}) %collective-permute-start.9) | collective-permute-done | bytes 270368 | tf_op jit(solution)/shard_map/ppermute | solution.py:167
  33.9 5.6 %expert.2 = (bf16[64,4096]{1,0:T(8,128)(2,1)S(1)}, bf16[64,4096]{1,0:T(8,128)(2,1)S(1)}, bf16[64,4096]{1,0:T(8,128)(2,1)S(1)}, bf16[64,4096]{1,0:T(8,128)(2,1)S(1)}) custom-call(s32[16]{0:T(128)S(1)} %copy-done, bf16[4096,768]{1,0:T(8,128)(2,1)S(1)} %get-tuple-element.55.gate_ref, bf16[4096,768]{1,0:T(8,128)(2,1)S(1)} %get-tuple-element.56.up_ref, ...), custom_call_target="tpu_custom_call" | custom-call | flops 4831838208 | bytes 4194304 | tf_op jit(solution)/shard_map/expert/pallas_call | solution.py:123
  39.5 0.2 collective-permute-start.13
  39.7 0.4 collective-permute-start.12
  40.1 1.4 %collective-permute-done.13 = bf16[64,4096]{1,0:T(8,128)(2,1)S(1)} collective-permute-done((bf16[64,4096]{1,0:T(8,128)(2,1)S(1)}, bf16[64,4096]{1,0:T(8,128)(2,1)S(1)}, u32[]{:S(2)}, u32[]{:S(2)}) %collective-permute-start.13) | collective-permute-done | bytes 524320 | tf_op jit(solution)/shard_map/ppermute | solution.py:167
  41.5 0.1 convert_element_type.85
  41.6 0.1 fusion.6
  41.6 0.6 collective-permute-done.12
  42.2 0.1 convert_element_type.87
  42.3 0.1 fusion.4
  42.4 0.2 collective-permute-start.15
  42.6 0.4 collective-permute-start.16
  43.0 0.7 collective-permute-start.14
  43.7 1.5 %collective-permute-done.16.refs_3_ = bf16[48,4224]{1,0:T(8,128)(2,1)S(1)} collective-permute-done((bf16[48,4224]{1,0:T(8,128)(2,1)S(1)}, bf16[48,4224]{1,0:T(8,128)(2,1)S(1)}, u32[]{:S(2)}, u32[]{:S(2)}) %collective-permute-start.16) | collective-permute-done | bytes 405536 | tf_op jit(solution)/shard_map/ppermute | solution.py:167
  45.2 5.6 %expert.3 = (bf16[64,4096]{1,0:T(8,128)(2,1)S(1)}, bf16[64,4096]{1,0:T(8,128)(2,1)S(1)}, bf16[64,4096]{1,0:T(8,128)(2,1)S(1)}, bf16[64,4096]{1,0:T(8,128)(2,1)S(1)}) custom-call(s32[16]{0:T(128)S(1)} %copy-done, bf16[4096,768]{1,0:T(8,128)(2,1)S(1)} %get-tuple-element.55.gate_ref, bf16[4096,768]{1,0:T(8,128)(2,1)S(1)} %get-tuple-element.56.up_ref, ...), custom_call_target="tpu_custom_call" | custom-call | flops 4831838208 | bytes 4194304 | tf_op jit(solution)/shard_map/expert/pallas_call | solution.py:123
  50.8 0.2 collective-permute-start.17
  51.0 6.0 %collective-permute-done.14 = bf16[64,4096]{1,0:T(8,128)(2,1)S(1)} collective-permute-done((bf16[64,4096]{1,0:T(8,128)(2,1)S(1)}, bf16[64,4096]{1,0:T(8,128)(2,1)S(1)}, u32[]{:S(2)}, u32[]{:S(2)}) %collective-permute-start.14) | collective-permute-done | bytes 524320 | tf_op jit(solution)/shard_map/ppermute | solution.py:170
  57.0 0.1 convert_element_type.91
  57.1 0.1 fusion.3
  57.2 0.7 collective-permute-start.22
  57.9 0.1 convert_element_type.93
  58.0 0.9 %collective-permute-done.21 = bf16[64,4096]{1,0:T(8,128)(2,1)S(1)} collective-permute-done((bf16[64,4096]{1,0:T(8,128)(2,1)S(1)}, bf16[64,4096]{1,0:T(8,128)(2,1)S(1)}, u32[]{:S(2)}, u32[]{:S(2)}) %collective-permute-start.21) | collective-permute-done | bytes 524320 | tf_op jit(solution)/shard_map/ppermute | solution.py:167
  58.9 0.1 convert_element_type.99
  59.0 0.1 slice_add_fusion.3
  59.1 0.1 fusion.5
  59.2 0.1 fusion.2
  59.3 0.5 collective-permute-start.19
  59.8 1.6 %collective-permute-start.18 = (bf16[16,4096]{1,0:T(8,128)(2,1)S(1)}, bf16[16,4096]{1,0:T(8,128)(2,1)S(1)}, u32[]{:S(2)}, u32[]{:S(2)}) collective-permute-start(bf16[16,4096]{1,0:T(8,128)(2,1)S(1)} %slice.179), channel_id=1, source_target_pairs={{0,4},{1,5},{2,6},{3,7},{4,0},{5,1},{6,2},{7,3},{8,12},{9,13},{10,... | collective-permute-start | bytes 393224 | tf_op jit(solution)/shard_map/ppermute | solution.py:173
  61.4 4.6 %collective-permute-done.22 = bf16[32,4096]{1,0:T(8,128)(2,1)S(1)} collective-permute-done((bf16[32,4096]{1,0:T(8,128)(2,1)S(1)}, bf16[32,4096]{1,0:T(8,128)(2,1)S(1)}, u32[]{:S(2)}, u32[]{:S(2)}) %collective-permute-start.22) | collective-permute-done | bytes 262176 | tf_op jit(solution)/shard_map/ppermute | solution.py:170
  66.0 0.1 fusion
  66.1 0.5 collective-permute-start.24
  66.6 2.7 %collective-permute-start.20 = (bf16[16,4096]{1,0:T(8,128)(2,1)S(1)}, bf16[16,4096]{1,0:T(8,128)(2,1)S(1)}, u32[]{:S(2)}, u32[]{:S(2)}) collective-permute-start(bf16[16,4096]{1,0:T(8,128)(2,1)S(1)} %fusion.7), channel_id=1, source_target_pairs={{0,8},{1,9},{2,10},{3,11},{4,12},{5,13},{6,14},{7,15},{8,0},{9,1},... | collective-permute-start | bytes 393224 | tf_op jit(solution)/shard_map/ppermute | solution.py:173
  69.3 0.6 collective-permute-start.23
  70.0 3.8 %collective-permute-done.24 = bf16[16,4096]{1,0:T(8,128)(2,1)S(1)} collective-permute-done((bf16[16,4096]{1,0:T(8,128)(2,1)S(1)}, bf16[16,4096]{1,0:T(8,128)(2,1)S(1)}, u32[]{:S(2)}, u32[]{:S(2)}) %collective-permute-start.24) | collective-permute-done | bytes 131104 | tf_op jit(solution)/shard_map/ppermute | solution.py:173
  73.7 0.1 collective-permute-start.25
  73.8 2.9 %collective-permute-done.23 = bf16[32,4096]{1,0:T(8,128)(2,1)S(1)} collective-permute-done((bf16[32,4096]{1,0:T(8,128)(2,1)S(1)}, bf16[32,4096]{1,0:T(8,128)(2,1)S(1)}, u32[]{:S(2)}, u32[]{:S(2)}) %collective-permute-start.23) | collective-permute-done | bytes 262176 | tf_op jit(solution)/shard_map/ppermute | solution.py:170
  76.7 0.1 fusion.1
  76.8 0.4 collective-permute-start.26
  77.2 3.8 %collective-permute-done.25.second_ref = bf16[16,4096]{1,0:T(8,128)(2,1)S(1)} collective-permute-done((bf16[16,4096]{1,0:T(8,128)(2,1)S(1)}, bf16[16,4096]{1,0:T(8,128)(2,1)S(1)}, u32[]{:S(2)}, u32[]{:S(2)}) %collective-permute-start.25) | collective-permute-done | bytes 131104 | tf_op jit(solution)/shard_map/ppermute | solution.py:173
  81.1 1.6 %collective-permute-done.26 = bf16[16,4096]{1,0:T(8,128)(2,1)S(1)} collective-permute-done((bf16[16,4096]{1,0:T(8,128)(2,1)S(1)}, bf16[16,4096]{1,0:T(8,128)(2,1)S(1)}, u32[]{:S(2)}, u32[]{:S(2)}) %collective-permute-start.26) | collective-permute-done | bytes 131104 | tf_op jit(solution)/shard_map/ppermute | solution.py:173
  82.7 0.7 pad_maximum_fusion.3
  (35 shorter events, 0.6 us)
Async XLA Ops:
  1.2 11.8 %collective-permute-start.2 = (bf16[16,4224]{1,0:T(8,128)(2,1)S(1)}, bf16[16,4224]{1,0:T(8,128)(2,1)S(1)}, u32[]{:S(2)}, u32[]{:S(2)}) collective-permute-start(bf16[16,4224]{1,0:T(8,128)(2,1)S(1)} %get-tuple-element.65), channel_id=1, source_target_pairs={{0,2},{1,3},{2,0},{3,1},{4,6},{5,7},{6,4},{7,5},{8,10},{9,11},{10,... | collective-permute-start | bytes 405512 | tf_op jit(solution)/shard_map/ppermute | solution.py:170
  4.2 8.8 %collective-permute-start.1 = (bf16[16,4224]{1,0:T(8,128)(2,1)S(1)}, bf16[16,4224]{1,0:T(8,128)(2,1)S(1)}, u32[]{:S(2)}, u32[]{:S(2)}) collective-permute-start(bf16[16,4224]{1,0:T(8,128)(2,1)S(1)} %get-tuple-element.65), channel_id=1, source_target_pairs={{0,4},{1,5},{2,6},{3,7},{4,0},{5,1},{6,2},{7,3},{8,12},{9,13},{10,... | collective-permute-start | bytes 405512 | tf_op jit(solution)/shard_map/ppermute | solution.py:173
  5.8 8.6 %collective-permute-start = (bf16[16,4224]{1,0:T(8,128)(2,1)S(1)}, bf16[16,4224]{1,0:T(8,128)(2,1)S(1)}, u32[]{:S(2)}, u32[]{:S(2)}) collective-permute-start(bf16[16,4224]{1,0:T(8,128)(2,1)S(1)} %get-tuple-element.65), channel_id=1, source_target_pairs={{0,8},{1,9},{2,10},{3,11},{4,12},{5,13},{6,14},{7,15},{8,0},{9,1},... | collective-permute-start | bytes 405512 | tf_op jit(solution)/shard_map/ppermute | solution.py:173
  14.4 6.3 %collective-permute-start.6 = (bf16[16,4224]{1,0:T(8,128)(2,1)S(1)}, bf16[16,4224]{1,0:T(8,128)(2,1)S(1)}, u32[]{:S(2)}, u32[]{:S(2)}) collective-permute-start(bf16[16,4224]{1,0:T(8,128)(2,1)S(1)} %collective-permute-done), channel_id=1, source_target_pairs={{0,4},{1,5},{2,6},{3,7},{4,0},{5,1},{6,2},{7,3},{8,12},{9,13},{10,... | collective-permute-start | bytes 405512 | tf_op jit(solution)/shard_map/ppermute | solution.py:173
  14.7 9.4 %collective-permute-start.4 = (bf16[16,4224]{1,0:T(8,128)(2,1)S(1)}, bf16[16,4224]{1,0:T(8,128)(2,1)S(1)}, u32[]{:S(2)}, u32[]{:S(2)}) collective-permute-start(bf16[16,4224]{1,0:T(8,128)(2,1)S(1)} %collective-permute-done.1), channel_id=1, source_target_pairs={{0,2},{1,3},{2,0},{3,1},{4,6},{5,7},{6,4},{7,5},{8,10},{9,11},{10,... | collective-permute-start | bytes 405512 | tf_op jit(solution)/shard_map/ppermute | solution.py:170
  15.2 8.8 %collective-permute-start.5 = (bf16[16,4224]{1,0:T(8,128)(2,1)S(1)}, bf16[16,4224]{1,0:T(8,128)(2,1)S(1)}, u32[]{:S(2)}, u32[]{:S(2)}) collective-permute-start(bf16[16,4224]{1,0:T(8,128)(2,1)S(1)} %get-tuple-element.62), channel_id=1, source_target_pairs={{0,2},{1,3},{2,0},{3,1},{4,6},{5,7},{6,4},{7,5},{8,10},{9,11},{10,... | collective-permute-start | bytes 405512 | tf_op jit(solution)/shard_map/ppermute | solution.py:170
  16.8 7.3 %collective-permute-start.3 = (bf16[16,4224]{1,0:T(8,128)(2,1)S(1)}, bf16[16,4224]{1,0:T(8,128)(2,1)S(1)}, u32[]{:S(2)}, u32[]{:S(2)}) collective-permute-start(bf16[16,4224]{1,0:T(8,128)(2,1)S(1)} %get-tuple-element.62), channel_id=1, source_target_pairs={{0,8},{1,9},{2,10},{3,11},{4,12},{5,13},{6,14},{7,15},{8,0},{9,1},... | collective-permute-start | bytes 405512 | tf_op jit(solution)/shard_map/ppermute | solution.py:173
  20.7 11.6 %collective-permute-start.8 = (bf16[32,4224]{1,0:T(8,128)(2,1)S(1)}, bf16[32,4224]{1,0:T(8,128)(2,1)S(1)}, u32[]{:S(2)}, u32[]{:S(2)}) collective-permute-start(bf16[32,4224]{1,0:T(8,128)(2,1)S(1)} %get-tuple-element.100), channel_id=1, source_target_pairs={{0,2},{1,3},{2,0},{3,1},{4,6},{5,7},{6,4},{7,5},{8,10},{9,11},{10,... | collective-permute-start | bytes 811016 | tf_op jit(solution)/shard_map/ppermute | solution.py:170
  21.3 12.6 %copy-start = (s32[16]{0:T(128)S(1)}, s32[16]{0:T(128)}, u32[]{:S(2)}) copy-start(s32[16]{0:T(128)} %flags_ref.3) | copy-start | bytes 196
  24.2 6.5 %collective-permute-start.10 = (bf16[32,4224]{1,0:T(8,128)(2,1)S(1)}, bf16[32,4224]{1,0:T(8,128)(2,1)S(1)}, u32[]{:S(2)}, u32[]{:S(2)}) collective-permute-start(bf16[32,4224]{1,0:T(8,128)(2,1)S(1)} %pad_maximum_fusion.2), channel_id=1, source_target_pairs={{0,4},{1,5},{2,6},{3,7},{4,0},{5,1},{6,2},{7,3},{8,12},{9,13},{10,... | collective-permute-start | bytes 811016 | tf_op jit(solution)/shard_map/ppermute | solution.py:173
  25.6 8.3 %collective-permute-start.7 = (bf16[96,4224]{1,0:T(8,128)(2,1)S(1)}, bf16[96,4224]{1,0:T(8,128)(2,1)S(1)}, u32[]{:S(2)}, u32[]{:S(2)}) collective-permute-start(bf16[96,4224]{1,0:T(8,128)(2,1)S(1)} %constant_dynamic-update-slice_fusion.2.refs_0_), channel_id=1, source_target_pairs={{0,1},{1,0},{2,3},{3,2},{4,5},{5,4},{6,7},{7,6},{8,9},{9,8},{10,11... | collective-permute-start | bytes 2433032 | tf_op jit(solution)/shard_map/ppermute | solution.py:167
  30.7 8.8 %collective-permute-start.11 = (bf16[48,4224]{1,0:T(8,128)(2,1)S(1)}, bf16[48,4224]{1,0:T(8,128)(2,1)S(1)}, u32[]{:S(2)}, u32[]{:S(2)}) collective-permute-start(bf16[48,4224]{1,0:T(8,128)(2,1)S(1)} %pad_maximum_fusion.1), channel_id=1, source_target_pairs={{0,2},{1,3},{2,0},{3,1},{4,6},{5,7},{6,4},{7,5},{8,10},{9,11},{10,... | collective-permute-start | bytes 1216520 | tf_op jit(solution)/shard_map/ppermute | solution.py:170
  32.3 1.5 %collective-permute-start.9 = (bf16[32,4224]{1,0:T(8,128)(2,1)S(1)}, bf16[32,4224]{1,0:T(8,128)(2,1)S(1)}, u32[]{:S(2)}, u32[]{:S(2)}) collective-permute-start(bf16[32,4224]{1,0:T(8,128)(2,1)S(1)} %collective-permute-done.8.refs_2_), channel_id=1, source_target_pairs={{0,1},{1,0},{2,3},{3,2},{4,5},{5,4},{6,7},{7,6},{8,9},{9,8},{10,11... | collective-permute-start | bytes 811016 | tf_op jit(solution)/shard_map/ppermute | solution.py:167
  39.5 2.0 %collective-permute-start.13 = (bf16[64,4096]{1,0:T(8,128)(2,1)S(1)}, bf16[64,4096]{1,0:T(8,128)(2,1)S(1)}, u32[]{:S(2)}, u32[]{:S(2)}) collective-permute-start(bf16[64,4096]{1,0:T(8,128)(2,1)S(1)} %get-tuple-element.79), channel_id=1, source_target_pairs={{0,1},{1,0},{2,3},{3,2},{4,5},{5,4},{6,7},{7,6},{8,9},{9,8},{10,11... | collective-permute-start | bytes 1572872 | tf_op jit(solution)/shard_map/ppermute | solution.py:167
  39.7 2.5 %collective-permute-start.12 = (bf16[64,4096]{1,0:T(8,128)(2,1)S(1)}, bf16[64,4096]{1,0:T(8,128)(2,1)S(1)}, u32[]{:S(2)}, u32[]{:S(2)}) collective-permute-start(bf16[64,4096]{1,0:T(8,128)(2,1)S(1)} %get-tuple-element.76), channel_id=1, source_target_pairs={{0,1},{1,0},{2,3},{3,2},{4,5},{5,4},{6,7},{7,6},{8,9},{9,8},{10,11... | collective-permute-start | bytes 1572872 | tf_op jit(solution)/shard_map/ppermute | solution.py:167
  42.4 2.8 %collective-permute-start.15 = (bf16[80,4224]{1,0:T(8,128)(2,1)S(1)}, bf16[80,4224]{1,0:T(8,128)(2,1)S(1)}, u32[]{:S(2)}, u32[]{:S(2)}) collective-permute-start(bf16[80,4224]{1,0:T(8,128)(2,1)S(1)} %constant_dynamic-update-slice_fusion.8.refs_0_), channel_id=1, source_target_pairs={{0,1},{1,0},{2,3},{3,2},{4,5},{5,4},{6,7},{7,6},{8,9},{9,8},{10,11... | collective-permute-start | bytes 2027528 | tf_op jit(solution)/shard_map/ppermute | solution.py:167
  42.6 2.6 %collective-permute-start.16 = (bf16[48,4224]{1,0:T(8,128)(2,1)S(1)}, bf16[48,4224]{1,0:T(8,128)(2,1)S(1)}, u32[]{:S(2)}, u32[]{:S(2)}) collective-permute-start(bf16[48,4224]{1,0:T(8,128)(2,1)S(1)} %collective-permute-done.11.refs_2_), channel_id=1, source_target_pairs={{0,1},{1,0},{2,3},{3,2},{4,5},{5,4},{6,7},{7,6},{8,9},{9,8},{10,11... | collective-permute-start | bytes 1216520 | tf_op jit(solution)/shard_map/ppermute | solution.py:167
  43.0 14.0 %collective-permute-start.14 = (bf16[64,4096]{1,0:T(8,128)(2,1)S(1)}, bf16[64,4096]{1,0:T(8,128)(2,1)S(1)}, u32[]{:S(2)}, u32[]{:S(2)}) collective-permute-start(bf16[64,4096]{1,0:T(8,128)(2,1)S(1)} %pad_maximum_fusion), channel_id=1, source_target_pairs={{0,2},{1,3},{2,0},{3,1},{4,6},{5,7},{6,4},{7,5},{8,10},{9,11},{10,... | collective-permute-start | bytes 1572872 | tf_op jit(solution)/shard_map/ppermute | solution.py:170
  50.8 6.2 %collective-permute-start.17 = (bf16[64,4096]{1,0:T(8,128)(2,1)S(1)}, bf16[64,4096]{1,0:T(8,128)(2,1)S(1)}, u32[]{:S(2)}, u32[]{:S(2)}) collective-permute-start(bf16[64,4096]{1,0:T(8,128)(2,1)S(1)} %get-tuple-element.88), channel_id=1, source_target_pairs={{0,1},{1,0},{2,3},{3,2},{4,5},{5,4},{6,7},{7,6},{8,9},{9,8},{10,11... | collective-permute-start | bytes 1572872 | tf_op jit(solution)/shard_map/ppermute | solution.py:167
  57.0 1.9 %collective-permute-start.21 = (bf16[64,4096]{1,0:T(8,128)(2,1)S(1)}, bf16[64,4096]{1,0:T(8,128)(2,1)S(1)}, u32[]{:S(2)}, u32[]{:S(2)}) collective-permute-start(bf16[64,4096]{1,0:T(8,128)(2,1)S(1)} %get-tuple-element.93), channel_id=1, source_target_pairs={{0,1},{1,0},{2,3},{3,2},{4,5},{5,4},{6,7},{7,6},{8,9},{9,8},{10,11... | collective-permute-start | bytes 1572872 | tf_op jit(solution)/shard_map/ppermute | solution.py:167
  57.2 8.8 %collective-permute-start.22 = (bf16[32,4096]{1,0:T(8,128)(2,1)S(1)}, bf16[32,4096]{1,0:T(8,128)(2,1)S(1)}, u32[]{:S(2)}, u32[]{:S(2)}) collective-permute-start(bf16[32,4096]{1,0:T(8,128)(2,1)S(1)} %fusion.3), channel_id=1, source_target_pairs={{0,2},{1,3},{2,0},{3,1},{4,6},{5,7},{6,4},{7,5},{8,10},{9,11},{10,... | collective-permute-start | bytes 786440 | tf_op jit(solution)/shard_map/ppermute | solution.py:170
  59.3 7.3 %collective-permute-start.19 = (bf16[16,4096]{1,0:T(8,128)(2,1)S(1)}, bf16[16,4096]{1,0:T(8,128)(2,1)S(1)}, u32[]{:S(2)}, u32[]{:S(2)}) collective-permute-start(bf16[16,4096]{1,0:T(8,128)(2,1)S(1)} %slice.178), channel_id=1, source_target_pairs={{0,4},{1,5},{2,6},{3,7},{4,0},{5,1},{6,2},{7,3},{8,12},{9,13},{10,... | collective-permute-start | bytes 393224 | tf_op jit(solution)/shard_map/ppermute | solution.py:173
  59.8 21.3 %collective-permute-start.18 = (bf16[16,4096]{1,0:T(8,128)(2,1)S(1)}, bf16[16,4096]{1,0:T(8,128)(2,1)S(1)}, u32[]{:S(2)}, u32[]{:S(2)}) collective-permute-start(bf16[16,4096]{1,0:T(8,128)(2,1)S(1)} %slice.179), channel_id=1, source_target_pairs={{0,4},{1,5},{2,6},{3,7},{4,0},{5,1},{6,2},{7,3},{8,12},{9,13},{10,... | collective-permute-start | bytes 393224 | tf_op jit(solution)/shard_map/ppermute | solution.py:173
  66.1 7.6 %collective-permute-start.24 = (bf16[16,4096]{1,0:T(8,128)(2,1)S(1)}, bf16[16,4096]{1,0:T(8,128)(2,1)S(1)}, u32[]{:S(2)}, u32[]{:S(2)}) collective-permute-start(bf16[16,4096]{1,0:T(8,128)(2,1)S(1)} %slice.177), channel_id=1, source_target_pairs={{0,4},{1,5},{2,6},{3,7},{4,0},{5,1},{6,2},{7,3},{8,12},{9,13},{10,... | collective-permute-start | bytes 393224 | tf_op jit(solution)/shard_map/ppermute | solution.py:173
  66.6 14.5 %collective-permute-start.20 = (bf16[16,4096]{1,0:T(8,128)(2,1)S(1)}, bf16[16,4096]{1,0:T(8,128)(2,1)S(1)}, u32[]{:S(2)}, u32[]{:S(2)}) collective-permute-start(bf16[16,4096]{1,0:T(8,128)(2,1)S(1)} %fusion.7), channel_id=1, source_target_pairs={{0,8},{1,9},{2,10},{3,11},{4,12},{5,13},{6,14},{7,15},{8,0},{9,1},... | collective-permute-start | bytes 393224 | tf_op jit(solution)/shard_map/ppermute | solution.py:173
  69.3 7.4 %collective-permute-start.23 = (bf16[32,4096]{1,0:T(8,128)(2,1)S(1)}, bf16[32,4096]{1,0:T(8,128)(2,1)S(1)}, u32[]{:S(2)}, u32[]{:S(2)}) collective-permute-start(bf16[32,4096]{1,0:T(8,128)(2,1)S(1)} %fusion.2), channel_id=1, source_target_pairs={{0,2},{1,3},{2,0},{3,1},{4,6},{5,7},{6,4},{7,5},{8,10},{9,11},{10,... | collective-permute-start | bytes 786440 | tf_op jit(solution)/shard_map/ppermute | solution.py:170
  73.7 7.3 %collective-permute-start.25 = (bf16[16,4096]{1,0:T(8,128)(2,1)S(1)}, bf16[16,4096]{1,0:T(8,128)(2,1)S(1)}, u32[]{:S(2)}, u32[]{:S(2)}) collective-permute-start(bf16[16,4096]{1,0:T(8,128)(2,1)S(1)} %slice_add_fusion.9), channel_id=1, source_target_pairs={{0,8},{1,9},{2,10},{3,11},{4,12},{5,13},{6,14},{7,15},{8,0},{9,1},... | collective-permute-start | bytes 393224 | tf_op jit(solution)/shard_map/ppermute | solution.py:173
  76.8 5.9 %collective-permute-start.26 = (bf16[16,4096]{1,0:T(8,128)(2,1)S(1)}, bf16[16,4096]{1,0:T(8,128)(2,1)S(1)}, u32[]{:S(2)}, u32[]{:S(2)}) collective-permute-start(bf16[16,4096]{1,0:T(8,128)(2,1)S(1)} %slice.176), channel_id=1, source_target_pairs={{0,4},{1,5},{2,6},{3,7},{4,0},{5,1},{6,2},{7,3},{8,12},{9,13},{10,... | collective-permute-start | bytes 393224 | tf_op jit(solution)/shard_map/ppermute | solution.py:173

commit v15 on v14

--- a/solution.py
+++ b/solution.py
@@ -205,7 +205,7 @@
     close = [messages[0], *[swap_far(messages[0], by) for by in places(strides)[1:]]]
     near_close = [swap_near(messages[0])]
     loaded = load_weights(w_gate, w_up)
-    far, close, near_close, loaded = lax.optimization_barrier((far, close, near_close, loaded))
+    loaded, near_close, close, far = lax.optimization_barrier((loaded, near_close, close, far))
     others = close[1:]
     near_close += [swap_near(block) for block in others]
     crossed = [swap_far(after(message, far), middle) for message in messages[1:]]

time: 83.6 us -> 84.3 us (level)
  starting transfers between devices: 25.1 us -> 28.7 us
  waiting for transfers between devices: 35.9 us -> 32.9 us
    ppermute x8, starting transfers between devices: 9.2 us -> 11.9 us  [swap_near(): lax.ppermute(x, 'expert', [(index(z, y, c), index(z, 1 - y, c)) for z, y,...]
    ppermute x8, waiting for transfers between devices: 5.9 us -> 3.87 us  [swap_core(): lax.ppermute(x, 'expert', [(index(z, y, c), index(z, y, 1 - c)) for z, y,...]
    ppermute x11, starting transfers between devices: 14.4 us -> 15.4 us  [swap_far(): lax.ppermute(x, 'expert', [(index(z, y, c), index(z ^ by, y, c)) for z, y...]
    ppermute x11, waiting for transfers between devices: 16.6 us -> 15.7 us  [swap_far(): lax.ppermute(x, 'expert', [(index(z, y, c), index(z ^ by, y, c)) for z, y...]
where the time goes in v15:
time: 84.3 us; the launch traced here: 84.1 us
  waiting for transfers between devices  32.9 us (39%)
  starting transfers between devices  28.7 us (34%)
  Pallas kernels  19.9 us (24%)
  other arithmetic  1.92 us (2%)
    ppermute x11, waiting for transfers between devices, swap_far(): lax.ppermute(x, 'expert', [(index(z, y, c), index(z ^ by, y, c)) for z, y...  15.7 us
    ppermute x11, starting transfers between devices, swap_far(): lax.ppermute(x, 'expert', [(index(z, y, c), index(z ^ by, y, c)) for z, y...  15.4 us
    ppermute x8, waiting for transfers between devices, swap_near(): lax.ppermute(x, 'expert', [(index(z, y, c), index(z, 1 - y, c)) for z, y,...  13.4 us
    ppermute x8, starting transfers between devices, swap_near(): lax.ppermute(x, 'expert', [(index(z, y, c), index(z, 1 - y, c)) for z, y,...  11.9 us
    pallas_call x2, Pallas kernels, run_expert(): pl.pallas_call(functools.partial(expert_kernel, swapped, count, plan), ou...  11.3 us
    pallas_call x2, Pallas kernels, load_weights(): pl.pallas_call(load_kernel, out_shape=[pltpu.VMEM(x.shape, x.dtype) for x...  7.43 us
    ppermute x8, waiting for transfers between devices, swap_core(): lax.ppermute(x, 'expert', [(index(z, y, c), index(z, y, 1 - c)) for z, y,...  3.87 us
  transfers between devices with their start and end apart: 27, of which 14 were waited for; matrix products, arithmetic and copies ran while one was open for 2% of the time, Pallas kernels for 22%

profile of v15, /device:TPU:0, one launch (start us, length us, event | category | flops | bytes accessed | tf_op | source)
XLA Modules:
  0.0 84.1 jit_solution(968194107791583060)
XLA Ops:
  0.0 1.2 %messages.1 = (bf16[16,4224]{1,0:T(8,128)(2,1)S(1)}, bf16[16,4224]{1,0:T(8,128)(2,1)S(1)}) custom-call(bf16[2,16,4096]{2,1,0:T(8,128)(2,1)} %states_ref.1, s32[2,8,16]{2,1,0:T(8,128)} %bitcast.12, f32[2,8,16]{2,1,0:T(8,128)} %bitcast.13), custom_call_target="tpu_custom_call" | custom-call | tf_op jit(solution)/shard_map/messages/pallas_call | solution.py:49
  1.2 4.0 %collective-permute-start.2 = (bf16[16,4224]{1,0:T(8,128)(2,1)S(1)}, bf16[16,4224]{1,0:T(8,128)(2,1)S(1)}, u32[]{:S(2)}, u32[]{:S(2)}) collective-permute-start(bf16[16,4224]{1,0:T(8,128)(2,1)S(1)} %get-tuple-element.65), channel_id=1, source_target_pairs={{0,8},{1,9},{2,10},{3,11},{4,12},{5,13},{6,14},{7,15},{8,0},{9,1},... | collective-permute-start | bytes 405512 | tf_op jit(solution)/shard_map/ppermute | solution.py:173
  5.3 1.6 %collective-permute-start.1 = (bf16[16,4224]{1,0:T(8,128)(2,1)S(1)}, bf16[16,4224]{1,0:T(8,128)(2,1)S(1)}, u32[]{:S(2)}, u32[]{:S(2)}) collective-permute-start(bf16[16,4224]{1,0:T(8,128)(2,1)S(1)} %get-tuple-element.65), channel_id=1, source_target_pairs={{0,4},{1,5},{2,6},{3,7},{4,0},{5,1},{6,2},{7,3},{8,12},{9,13},{10,... | collective-permute-start | bytes 405512 | tf_op jit(solution)/shard_map/ppermute | solution.py:173
  6.8 1.5 %collective-permute-start = (bf16[16,4224]{1,0:T(8,128)(2,1)S(1)}, bf16[16,4224]{1,0:T(8,128)(2,1)S(1)}, u32[]{:S(2)}, u32[]{:S(2)}) collective-permute-start(bf16[16,4224]{1,0:T(8,128)(2,1)S(1)} %get-tuple-element.65), channel_id=1, source_target_pairs={{0,2},{1,3},{2,0},{3,1},{4,6},{5,7},{6,4},{7,5},{8,10},{9,11},{10,... | collective-permute-start | bytes 405512 | tf_op jit(solution)/shard_map/ppermute | solution.py:170
  8.4 4.6 %load_weights.2 = (bf16[4096,768]{1,0:T(8,128)(2,1)S(1)}, bf16[4096,768]{1,0:T(8,128)(2,1)S(1)}) custom-call(bf16[4096,768]{1,0:T(8,128)(2,1)} %bitcast.9, bf16[4096,768]{1,0:T(8,128)(2,1)} %bitcast.10), custom_call_target="tpu_custom_call" | custom-call | tf_op jit(solution)/shard_map/load_weights/pallas_call | solution.py:73
  13.0 0.0 collective-permute-done.2
  13.0 0.0 collective-permute-done.1
  13.0 0.5 collective-permute-start.6
  13.6 1.5 %collective-permute-start.4 = (bf16[16,4224]{1,0:T(8,128)(2,1)S(1)}, bf16[16,4224]{1,0:T(8,128)(2,1)S(1)}, u32[]{:S(2)}, u32[]{:S(2)}) collective-permute-start(bf16[16,4224]{1,0:T(8,128)(2,1)S(1)} %collective-permute-done.1), channel_id=1, source_target_pairs={{0,2},{1,3},{2,0},{3,1},{4,6},{5,7},{6,4},{7,5},{8,10},{9,11},{10,... | collective-permute-start | bytes 405512 | tf_op jit(solution)/shard_map/ppermute | solution.py:170
  15.0 0.6 collective-permute-start.5
  15.6 2.3 %collective-permute-start.3 = (bf16[16,4224]{1,0:T(8,128)(2,1)S(1)}, bf16[16,4224]{1,0:T(8,128)(2,1)S(1)}, u32[]{:S(2)}, u32[]{:S(2)}) collective-permute-start(bf16[16,4224]{1,0:T(8,128)(2,1)S(1)} %get-tuple-element.62), channel_id=1, source_target_pairs={{0,8},{1,9},{2,10},{3,11},{4,12},{5,13},{6,14},{7,15},{8,0},{9,1},... | collective-permute-start | bytes 405512 | tf_op jit(solution)/shard_map/ppermute | solution.py:173
  18.0 0.9 %collective-permute-done.6 = bf16[16,4224]{1,0:T(8,128)(2,1)S(1)} collective-permute-done((bf16[16,4224]{1,0:T(8,128)(2,1)S(1)}, bf16[16,4224]{1,0:T(8,128)(2,1)S(1)}, u32[]{:S(2)}, u32[]{:S(2)}) %collective-permute-start.6) | collective-permute-done | bytes 135200 | tf_op jit(solution)/shard_map/ppermute | solution.py:173
  18.9 0.7 collective-permute-start.8
  19.6 2.8 %load_weights.3.down_ref = bf16[768,4096]{1,0:T(8,128)(2,1)S(1)} custom-call(bf16[768,4096]{1,0:T(8,128)(2,1)} %bitcast.11), custom_call_target="tpu_custom_call" | custom-call | tf_op jit(solution)/shard_map/load_weights/pallas_call | solution.py:73
  22.4 0.0 collective-permute-done.5
  22.4 1.3 %collective-permute-done.3 = bf16[16,4224]{1,0:T(8,128)(2,1)S(1)} collective-permute-done((bf16[16,4224]{1,0:T(8,128)(2,1)S(1)}, bf16[16,4224]{1,0:T(8,128)(2,1)S(1)}, u32[]{:S(2)}, u32[]{:S(2)}) %collective-permute-start.3) | collective-permute-done | bytes 135200 | tf_op jit(solution)/shard_map/ppermute | solution.py:173
  23.7 0.0 collective-permute-done.4
  23.8 0.9 %collective-permute-start.10 = (bf16[32,4224]{1,0:T(8,128)(2,1)S(1)}, bf16[32,4224]{1,0:T(8,128)(2,1)S(1)}, u32[]{:S(2)}, u32[]{:S(2)}) collective-permute-start(bf16[32,4224]{1,0:T(8,128)(2,1)S(1)} %pad_maximum_fusion.2), channel_id=1, source_target_pairs={{0,4},{1,5},{2,6},{3,7},{4,0},{5,1},{6,2},{7,3},{8,12},{9,13},{10,... | collective-permute-start | bytes 811016 | tf_op jit(solution)/shard_map/ppermute | solution.py:173
  24.7 0.1 collective-permute-start.7
  24.8 5.5 %collective-permute-done.10 = bf16[32,4224]{1,0:T(8,128)(2,1)S(1)} collective-permute-done((bf16[32,4224]{1,0:T(8,128)(2,1)S(1)}, bf16[32,4224]{1,0:T(8,128)(2,1)S(1)}, u32[]{:S(2)}, u32[]{:S(2)}) %collective-permute-start.10) | collective-permute-done | bytes 270368 | tf_op jit(solution)/shard_map/ppermute | solution.py:173
  30.3 2.3 %collective-permute-start.11 = (bf16[48,4224]{1,0:T(8,128)(2,1)S(1)}, bf16[48,4224]{1,0:T(8,128)(2,1)S(1)}, u32[]{:S(2)}, u32[]{:S(2)}) collective-permute-start(bf16[48,4224]{1,0:T(8,128)(2,1)S(1)} %pad_maximum_fusion.1), channel_id=1, source_target_pairs={{0,2},{1,3},{2,0},{3,1},{4,6},{5,7},{6,4},{7,5},{8,10},{9,11},{10,... | collective-permute-start | bytes 1216520 | tf_op jit(solution)/shard_map/ppermute | solution.py:170
  32.6 0.0 collective-permute-done.8.refs_2_
  32.6 0.0 collective-permute-start.9
  32.7 1.5 %collective-permute-done.9.refs_3_ = bf16[32,4224]{1,0:T(8,128)(2,1)S(1)} collective-permute-done((bf16[32,4224]{1,0:T(8,128)(2,1)S(1)}, bf16[32,4224]{1,0:T(8,128)(2,1)S(1)}, u32[]{:S(2)}, u32[]{:S(2)}) %collective-permute-start.9) | collective-permute-done | bytes 270368 | tf_op jit(solution)/shard_map/ppermute | solution.py:167
  34.2 0.0 collective-permute-done.7.refs_1_
  34.2 5.6 %expert.2 = (bf16[64,4096]{1,0:T(8,128)(2,1)S(1)}, bf16[64,4096]{1,0:T(8,128)(2,1)S(1)}, bf16[64,4096]{1,0:T(8,128)(2,1)S(1)}, bf16[64,4096]{1,0:T(8,128)(2,1)S(1)}) custom-call(s32[16]{0:T(128)S(1)} %copy-done, bf16[4096,768]{1,0:T(8,128)(2,1)S(1)} %get-tuple-element.55.gate_ref, bf16[4096,768]{1,0:T(8,128)(2,1)S(1)} %get-tuple-element.56.up_ref, ...), custom_call_target="tpu_custom_call" | custom-call | flops 4831838208 | bytes 4194304 | tf_op jit(solution)/shard_map/expert/pallas_call | solution.py:123
  39.8 0.2 collective-permute-done.11.refs_2_
  40.1 0.5 collective-permute-start.12
  40.6 1.4 %collective-permute-done.13 = bf16[64,4096]{1,0:T(8,128)(2,1)S(1)} collective-permute-done((bf16[64,4096]{1,0:T(8,128)(2,1)S(1)}, bf16[64,4096]{1,0:T(8,128)(2,1)S(1)}, u32[]{:S(2)}, u32[]{:S(2)}) %collective-permute-start.13) | collective-permute-done | bytes 524320 | tf_op jit(solution)/shard_map/ppermute | solution.py:167
  42.0 0.1 convert_element_type.85
  42.0 0.1 fusion.6
  42.1 0.6 collective-permute-done.12
  42.7 0.1 convert_element_type.87
  42.8 0.1 fusion.4
  42.9 0.2 collective-permute-start.15
  43.1 0.4 collective-permute-start.16
  43.5 1.8 %collective-permute-start.14 = (bf16[64,4096]{1,0:T(8,128)(2,1)S(1)}, bf16[64,4096]{1,0:T(8,128)(2,1)S(1)}, u32[]{:S(2)}, u32[]{:S(2)}) collective-permute-start(bf16[64,4096]{1,0:T(8,128)(2,1)S(1)} %pad_maximum_fusion), channel_id=1, source_target_pairs={{0,2},{1,3},{2,0},{3,1},{4,6},{5,7},{6,4},{7,5},{8,10},{9,11},{10,... | collective-permute-start | bytes 1572872 | tf_op jit(solution)/shard_map/ppermute | solution.py:170
  45.3 0.4 collective-permute-done.16.refs_3_
  45.6 5.6 %expert.3 = (bf16[64,4096]{1,0:T(8,128)(2,1)S(1)}, bf16[64,4096]{1,0:T(8,128)(2,1)S(1)}, bf16[64,4096]{1,0:T(8,128)(2,1)S(1)}, bf16[64,4096]{1,0:T(8,128)(2,1)S(1)}) custom-call(s32[16]{0:T(128)S(1)} %copy-done, bf16[4096,768]{1,0:T(8,128)(2,1)S(1)} %get-tuple-element.55.gate_ref, bf16[4096,768]{1,0:T(8,128)(2,1)S(1)} %get-tuple-element.56.up_ref, ...), custom_call_target="tpu_custom_call" | custom-call | flops 4831838208 | bytes 4194304 | tf_op jit(solution)/shard_map/expert/pallas_call | solution.py:123
  51.3 0.2 collective-permute-start.17
  51.5 6.0 %collective-permute-done.14 = bf16[64,4096]{1,0:T(8,128)(2,1)S(1)} collective-permute-done((bf16[64,4096]{1,0:T(8,128)(2,1)S(1)}, bf16[64,4096]{1,0:T(8,128)(2,1)S(1)}, u32[]{:S(2)}, u32[]{:S(2)}) %collective-permute-start.14) | collective-permute-done | bytes 524320 | tf_op jit(solution)/shard_map/ppermute | solution.py:170
  57.5 0.1 convert_element_type.91
  57.6 0.1 fusion.3
  57.7 1.8 %collective-permute-start.22 = (bf16[32,4096]{1,0:T(8,128)(2,1)S(1)}, bf16[32,4096]{1,0:T(8,128)(2,1)S(1)}, u32[]{:S(2)}, u32[]{:S(2)}) collective-permute-start(bf16[32,4096]{1,0:T(8,128)(2,1)S(1)} %fusion.3), channel_id=1, source_target_pairs={{0,2},{1,3},{2,0},{3,1},{4,6},{5,7},{6,4},{7,5},{8,10},{9,11},{10,... | collective-permute-start | bytes 786440 | tf_op jit(solution)/shard_map/ppermute | solution.py:170
  59.5 0.1 convert_element_type.93
  59.6 0.1 convert_element_type.99
  59.7 0.1 slice_add_fusion.3
  59.8 0.1 fusion.5
  59.9 0.1 fusion.2
  60.0 0.6 collective-permute-start.19
  60.6 1.5 %collective-permute-start.18 = (bf16[16,4096]{1,0:T(8,128)(2,1)S(1)}, bf16[16,4096]{1,0:T(8,128)(2,1)S(1)}, u32[]{:S(2)}, u32[]{:S(2)}) collective-permute-start(bf16[16,4096]{1,0:T(8,128)(2,1)S(1)} %slice.179), channel_id=1, source_target_pairs={{0,4},{1,5},{2,6},{3,7},{4,0},{5,1},{6,2},{7,3},{8,12},{9,13},{10,... | collective-permute-start | bytes 393224 | tf_op jit(solution)/shard_map/ppermute | solution.py:173
  62.1 4.4 %collective-permute-done.22 = bf16[32,4096]{1,0:T(8,128)(2,1)S(1)} collective-permute-done((bf16[32,4096]{1,0:T(8,128)(2,1)S(1)}, bf16[32,4096]{1,0:T(8,128)(2,1)S(1)}, u32[]{:S(2)}, u32[]{:S(2)}) %collective-permute-start.22) | collective-permute-done | bytes 262176 | tf_op jit(solution)/shard_map/ppermute | solution.py:170
  66.4 0.1 fusion
  66.6 0.6 collective-permute-start.24
  67.2 2.7 %collective-permute-start.20 = (bf16[16,4096]{1,0:T(8,128)(2,1)S(1)}, bf16[16,4096]{1,0:T(8,128)(2,1)S(1)}, u32[]{:S(2)}, u32[]{:S(2)}) collective-permute-start(bf16[16,4096]{1,0:T(8,128)(2,1)S(1)} %fusion.7), channel_id=1, source_target_pairs={{0,8},{1,9},{2,10},{3,11},{4,12},{5,13},{6,14},{7,15},{8,0},{9,1},... | collective-permute-start | bytes 393224 | tf_op jit(solution)/shard_map/ppermute | solution.py:173
  69.9 1.7 %collective-permute-start.23 = (bf16[32,4096]{1,0:T(8,128)(2,1)S(1)}, bf16[32,4096]{1,0:T(8,128)(2,1)S(1)}, u32[]{:S(2)}, u32[]{:S(2)}) collective-permute-start(bf16[32,4096]{1,0:T(8,128)(2,1)S(1)} %fusion.2), channel_id=1, source_target_pairs={{0,2},{1,3},{2,0},{3,1},{4,6},{5,7},{6,4},{7,5},{8,10},{9,11},{10,... | collective-permute-start | bytes 786440 | tf_op jit(solution)/shard_map/ppermute | solution.py:170
  71.7 2.6 %collective-permute-done.24 = bf16[16,4096]{1,0:T(8,128)(2,1)S(1)} collective-permute-done((bf16[16,4096]{1,0:T(8,128)(2,1)S(1)}, bf16[16,4096]{1,0:T(8,128)(2,1)S(1)}, u32[]{:S(2)}, u32[]{:S(2)}) %collective-permute-start.24) | collective-permute-done | bytes 131104 | tf_op jit(solution)/shard_map/ppermute | solution.py:173
  74.3 0.3 collective-permute-start.25
  74.6 2.7 %collective-permute-done.23 = bf16[32,4096]{1,0:T(8,128)(2,1)S(1)} collective-permute-done((bf16[32,4096]{1,0:T(8,128)(2,1)S(1)}, bf16[32,4096]{1,0:T(8,128)(2,1)S(1)}, u32[]{:S(2)}, u32[]{:S(2)}) %collective-permute-start.23) | collective-permute-done | bytes 262176 | tf_op jit(solution)/shard_map/ppermute | solution.py:170
  77.3 0.1 fusion.1
  77.4 0.4 collective-permute-start.26
  77.8 3.8 %collective-permute-done.25.second_ref = bf16[16,4096]{1,0:T(8,128)(2,1)S(1)} collective-permute-done((bf16[16,4096]{1,0:T(8,128)(2,1)S(1)}, bf16[16,4096]{1,0:T(8,128)(2,1)S(1)}, u32[]{:S(2)}, u32[]{:S(2)}) %collective-permute-start.25) | collective-permute-done | bytes 131104 | tf_op jit(solution)/shard_map/ppermute | solution.py:173
  81.7 1.6 %collective-permute-done.26 = bf16[16,4096]{1,0:T(8,128)(2,1)S(1)} collective-permute-done((bf16[16,4096]{1,0:T(8,128)(2,1)S(1)}, bf16[16,4096]{1,0:T(8,128)(2,1)S(1)}, u32[]{:S(2)}, u32[]{:S(2)}) %collective-permute-start.26) | collective-permute-done | bytes 131104 | tf_op jit(solution)/shard_map/ppermute | solution.py:173
  83.4 0.7 pad_maximum_fusion.3
  (35 shorter events, 0.6 us)
Async XLA Ops:
  1.2 11.8 %collective-permute-start.2 = (bf16[16,4224]{1,0:T(8,128)(2,1)S(1)}, bf16[16,4224]{1,0:T(8,128)(2,1)S(1)}, u32[]{:S(2)}, u32[]{:S(2)}) collective-permute-start(bf16[16,4224]{1,0:T(8,128)(2,1)S(1)} %get-tuple-element.65), channel_id=1, source_target_pairs={{0,8},{1,9},{2,10},{3,11},{4,12},{5,13},{6,14},{7,15},{8,0},{9,1},... | collective-permute-start | bytes 405512 | tf_op jit(solution)/shard_map/ppermute | solution.py:173
  5.3 7.8 %collective-permute-start.1 = (bf16[16,4224]{1,0:T(8,128)(2,1)S(1)}, bf16[16,4224]{1,0:T(8,128)(2,1)S(1)}, u32[]{:S(2)}, u32[]{:S(2)}) collective-permute-start(bf16[16,4224]{1,0:T(8,128)(2,1)S(1)} %get-tuple-element.65), channel_id=1, source_target_pairs={{0,4},{1,5},{2,6},{3,7},{4,0},{5,1},{6,2},{7,3},{8,12},{9,13},{10,... | collective-permute-start | bytes 405512 | tf_op jit(solution)/shard_map/ppermute | solution.py:173
  6.8 6.2 %collective-permute-start = (bf16[16,4224]{1,0:T(8,128)(2,1)S(1)}, bf16[16,4224]{1,0:T(8,128)(2,1)S(1)}, u32[]{:S(2)}, u32[]{:S(2)}) collective-permute-start(bf16[16,4224]{1,0:T(8,128)(2,1)S(1)} %get-tuple-element.65), channel_id=1, source_target_pairs={{0,2},{1,3},{2,0},{3,1},{4,6},{5,7},{6,4},{7,5},{8,10},{9,11},{10,... | collective-permute-start | bytes 405512 | tf_op jit(solution)/shard_map/ppermute | solution.py:170
  13.0 5.8 %collective-permute-start.6 = (bf16[16,4224]{1,0:T(8,128)(2,1)S(1)}, bf16[16,4224]{1,0:T(8,128)(2,1)S(1)}, u32[]{:S(2)}, u32[]{:S(2)}) collective-permute-start(bf16[16,4224]{1,0:T(8,128)(2,1)S(1)} %collective-permute-done.2), channel_id=1, source_target_pairs={{0,4},{1,5},{2,6},{3,7},{4,0},{5,1},{6,2},{7,3},{8,12},{9,13},{10,... | collective-permute-start | bytes 405512 | tf_op jit(solution)/shard_map/ppermute | solution.py:173
  13.6 10.2 %collective-permute-start.4 = (bf16[16,4224]{1,0:T(8,128)(2,1)S(1)}, bf16[16,4224]{1,0:T(8,128)(2,1)S(1)}, u32[]{:S(2)}, u32[]{:S(2)}) collective-permute-start(bf16[16,4224]{1,0:T(8,128)(2,1)S(1)} %collective-permute-done.1), channel_id=1, source_target_pairs={{0,2},{1,3},{2,0},{3,1},{4,6},{5,7},{6,4},{7,5},{8,10},{9,11},{10,... | collective-permute-start | bytes 405512 | tf_op jit(solution)/shard_map/ppermute | solution.py:170
  15.0 7.4 %collective-permute-start.5 = (bf16[16,4224]{1,0:T(8,128)(2,1)S(1)}, bf16[16,4224]{1,0:T(8,128)(2,1)S(1)}, u32[]{:S(2)}, u32[]{:S(2)}) collective-permute-start(bf16[16,4224]{1,0:T(8,128)(2,1)S(1)} %get-tuple-element.62), channel_id=1, source_target_pairs={{0,2},{1,3},{2,0},{3,1},{4,6},{5,7},{6,4},{7,5},{8,10},{9,11},{10,... | collective-permute-start | bytes 405512 | tf_op jit(solution)/shard_map/ppermute | solution.py:170
  15.6 8.1 %collective-permute-start.3 = (bf16[16,4224]{1,0:T(8,128)(2,1)S(1)}, bf16[16,4224]{1,0:T(8,128)(2,1)S(1)}, u32[]{:S(2)}, u32[]{:S(2)}) collective-permute-start(bf16[16,4224]{1,0:T(8,128)(2,1)S(1)} %get-tuple-element.62), channel_id=1, source_target_pairs={{0,8},{1,9},{2,10},{3,11},{4,12},{5,13},{6,14},{7,15},{8,0},{9,1},... | collective-permute-start | bytes 405512 | tf_op jit(solution)/shard_map/ppermute | solution.py:173
  18.9 13.8 %collective-permute-start.8 = (bf16[32,4224]{1,0:T(8,128)(2,1)S(1)}, bf16[32,4224]{1,0:T(8,128)(2,1)S(1)}, u32[]{:S(2)}, u32[]{:S(2)}) collective-permute-start(bf16[32,4224]{1,0:T(8,128)(2,1)S(1)} %get-tuple-element.100), channel_id=1, source_target_pairs={{0,2},{1,3},{2,0},{3,1},{4,6},{5,7},{6,4},{7,5},{8,10},{9,11},{10,... | collective-permute-start | bytes 811016 | tf_op jit(solution)/shard_map/ppermute | solution.py:170
  19.6 14.6 %copy-start = (s32[16]{0:T(128)S(1)}, s32[16]{0:T(128)}, u32[]{:S(2)}) copy-start(s32[16]{0:T(128)} %flags_ref.3) | copy-start | bytes 196
  23.8 6.5 %collective-permute-start.10 = (bf16[32,4224]{1,0:T(8,128)(2,1)S(1)}, bf16[32,4224]{1,0:T(8,128)(2,1)S(1)}, u32[]{:S(2)}, u32[]{:S(2)}) collective-permute-start(bf16[32,4224]{1,0:T(8,128)(2,1)S(1)} %pad_maximum_fusion.2), channel_id=1, source_target_pairs={{0,4},{1,5},{2,6},{3,7},{4,0},{5,1},{6,2},{7,3},{8,12},{9,13},{10,... | collective-permute-start | bytes 811016 | tf_op jit(solution)/shard_map/ppermute | solution.py:173
  24.7 9.5 %collective-permute-start.7 = (bf16[96,4224]{1,0:T(8,128)(2,1)S(1)}, bf16[96,4224]{1,0:T(8,128)(2,1)S(1)}, u32[]{:S(2)}, u32[]{:S(2)}) collective-permute-start(bf16[96,4224]{1,0:T(8,128)(2,1)S(1)} %constant_dynamic-update-slice_fusion.2.refs_0_), channel_id=1, source_target_pairs={{0,1},{1,0},{2,3},{3,2},{4,5},{5,4},{6,7},{7,6},{8,9},{9,8},{10,11... | collective-permute-start | bytes 2433032 | tf_op jit(solution)/shard_map/ppermute | solution.py:167
  30.3 9.7 %collective-permute-start.11 = (bf16[48,4224]{1,0:T(8,128)(2,1)S(1)}, bf16[48,4224]{1,0:T(8,128)(2,1)S(1)}, u32[]{:S(2)}, u32[]{:S(2)}) collective-permute-start(bf16[48,4224]{1,0:T(8,128)(2,1)S(1)} %pad_maximum_fusion.1), channel_id=1, source_target_pairs={{0,2},{1,3},{2,0},{3,1},{4,6},{5,7},{6,4},{7,5},{8,10},{9,11},{10,... | collective-permute-start | bytes 1216520 | tf_op jit(solution)/shard_map/ppermute | solution.py:170
  32.6 1.5 %collective-permute-start.9 = (bf16[32,4224]{1,0:T(8,128)(2,1)S(1)}, bf16[32,4224]{1,0:T(8,128)(2,1)S(1)}, u32[]{:S(2)}, u32[]{:S(2)}) collective-permute-start(bf16[32,4224]{1,0:T(8,128)(2,1)S(1)} %collective-permute-done.8.refs_2_), channel_id=1, source_target_pairs={{0,1},{1,0},{2,3},{3,2},{4,5},{5,4},{6,7},{7,6},{8,9},{9,8},{10,11... | collective-permute-start | bytes 811016 | tf_op jit(solution)/shard_map/ppermute | solution.py:167
  40.1 1.9 %collective-permute-start.13 = (bf16[64,4096]{1,0:T(8,128)(2,1)S(1)}, bf16[64,4096]{1,0:T(8,128)(2,1)S(1)}, u32[]{:S(2)}, u32[]{:S(2)}) collective-permute-start(bf16[64,4096]{1,0:T(8,128)(2,1)S(1)} %get-tuple-element.79), channel_id=1, source_target_pairs={{0,1},{1,0},{2,3},{3,2},{4,5},{5,4},{6,7},{7,6},{8,9},{9,8},{10,11... | collective-permute-start | bytes 1572872 | tf_op jit(solution)/shard_map/ppermute | solution.py:167
  40.1 2.7 %collective-permute-start.12 = (bf16[64,4096]{1,0:T(8,128)(2,1)S(1)}, bf16[64,4096]{1,0:T(8,128)(2,1)S(1)}, u32[]{:S(2)}, u32[]{:S(2)}) collective-permute-start(bf16[64,4096]{1,0:T(8,128)(2,1)S(1)} %get-tuple-element.76), channel_id=1, source_target_pairs={{0,1},{1,0},{2,3},{3,2},{4,5},{5,4},{6,7},{7,6},{8,9},{9,8},{10,11... | collective-permute-start | bytes 1572872 | tf_op jit(solution)/shard_map/ppermute | solution.py:167
  42.9 2.8 %collective-permute-start.15 = (bf16[80,4224]{1,0:T(8,128)(2,1)S(1)}, bf16[80,4224]{1,0:T(8,128)(2,1)S(1)}, u32[]{:S(2)}, u32[]{:S(2)}) collective-permute-start(bf16[80,4224]{1,0:T(8,128)(2,1)S(1)} %constant_dynamic-update-slice_fusion.8.refs_0_), channel_id=1, source_target_pairs={{0,1},{1,0},{2,3},{3,2},{4,5},{5,4},{6,7},{7,6},{8,9},{9,8},{10,11... | collective-permute-start | bytes 2027528 | tf_op jit(solution)/shard_map/ppermute | solution.py:167
  43.1 2.6 %collective-permute-start.16 = (bf16[48,4224]{1,0:T(8,128)(2,1)S(1)}, bf16[48,4224]{1,0:T(8,128)(2,1)S(1)}, u32[]{:S(2)}, u32[]{:S(2)}) collective-permute-start(bf16[48,4224]{1,0:T(8,128)(2,1)S(1)} %collective-permute-done.11.refs_2_), channel_id=1, source_target_pairs={{0,1},{1,0},{2,3},{3,2},{4,5},{5,4},{6,7},{7,6},{8,9},{9,8},{10,11... | collective-permute-start | bytes 1216520 | tf_op jit(solution)/shard_map/ppermute | solution.py:167
  43.5 14.0 %collective-permute-start.14 = (bf16[64,4096]{1,0:T(8,128)(2,1)S(1)}, bf16[64,4096]{1,0:T(8,128)(2,1)S(1)}, u32[]{:S(2)}, u32[]{:S(2)}) collective-permute-start(bf16[64,4096]{1,0:T(8,128)(2,1)S(1)} %pad_maximum_fusion), channel_id=1, source_target_pairs={{0,2},{1,3},{2,0},{3,1},{4,6},{5,7},{6,4},{7,5},{8,10},{9,11},{10,... | collective-permute-start | bytes 1572872 | tf_op jit(solution)/shard_map/ppermute | solution.py:170
  51.3 6.2 %collective-permute-start.17 = (bf16[64,4096]{1,0:T(8,128)(2,1)S(1)}, bf16[64,4096]{1,0:T(8,128)(2,1)S(1)}, u32[]{:S(2)}, u32[]{:S(2)}) collective-permute-start(bf16[64,4096]{1,0:T(8,128)(2,1)S(1)} %get-tuple-element.88), channel_id=1, source_target_pairs={{0,1},{1,0},{2,3},{3,2},{4,5},{5,4},{6,7},{7,6},{8,9},{9,8},{10,11... | collective-permute-start | bytes 1572872 | tf_op jit(solution)/shard_map/ppermute | solution.py:167
  57.5 2.1 %collective-permute-start.21 = (bf16[64,4096]{1,0:T(8,128)(2,1)S(1)}, bf16[64,4096]{1,0:T(8,128)(2,1)S(1)}, u32[]{:S(2)}, u32[]{:S(2)}) collective-permute-start(bf16[64,4096]{1,0:T(8,128)(2,1)S(1)} %get-tuple-element.93), channel_id=1, source_target_pairs={{0,1},{1,0},{2,3},{3,2},{4,5},{5,4},{6,7},{7,6},{8,9},{9,8},{10,11... | collective-permute-start | bytes 1572872 | tf_op jit(solution)/shard_map/ppermute | solution.py:167
  57.7 8.8 %collective-permute-start.22 = (bf16[32,4096]{1,0:T(8,128)(2,1)S(1)}, bf16[32,4096]{1,0:T(8,128)(2,1)S(1)}, u32[]{:S(2)}, u32[]{:S(2)}) collective-permute-start(bf16[32,4096]{1,0:T(8,128)(2,1)S(1)} %fusion.3), channel_id=1, source_target_pairs={{0,2},{1,3},{2,0},{3,1},{4,6},{5,7},{6,4},{7,5},{8,10},{9,11},{10,... | collective-permute-start | bytes 786440 | tf_op jit(solution)/shard_map/ppermute | solution.py:170
  60.0 7.2 %collective-permute-start.19 = (bf16[16,4096]{1,0:T(8,128)(2,1)S(1)}, bf16[16,4096]{1,0:T(8,128)(2,1)S(1)}, u32[]{:S(2)}, u32[]{:S(2)}) collective-permute-start(bf16[16,4096]{1,0:T(8,128)(2,1)S(1)} %slice.178), channel_id=1, source_target_pairs={{0,4},{1,5},{2,6},{3,7},{4,0},{5,1},{6,2},{7,3},{8,12},{9,13},{10,... | collective-permute-start | bytes 393224 | tf_op jit(solution)/shard_map/ppermute | solution.py:173
  60.6 21.0 %collective-permute-start.18 = (bf16[16,4096]{1,0:T(8,128)(2,1)S(1)}, bf16[16,4096]{1,0:T(8,128)(2,1)S(1)}, u32[]{:S(2)}, u32[]{:S(2)}) collective-permute-start(bf16[16,4096]{1,0:T(8,128)(2,1)S(1)} %slice.179), channel_id=1, source_target_pairs={{0,4},{1,5},{2,6},{3,7},{4,0},{5,1},{6,2},{7,3},{8,12},{9,13},{10,... | collective-permute-start | bytes 393224 | tf_op jit(solution)/shard_map/ppermute | solution.py:173
  66.6 7.7 %collective-permute-start.24 = (bf16[16,4096]{1,0:T(8,128)(2,1)S(1)}, bf16[16,4096]{1,0:T(8,128)(2,1)S(1)}, u32[]{:S(2)}, u32[]{:S(2)}) collective-permute-start(bf16[16,4096]{1,0:T(8,128)(2,1)S(1)} %slice.177), channel_id=1, source_target_pairs={{0,4},{1,5},{2,6},{3,7},{4,0},{5,1},{6,2},{7,3},{8,12},{9,13},{10,... | collective-permute-start | bytes 393224 | tf_op jit(solution)/shard_map/ppermute | solution.py:173
  67.2 14.4 %collective-permute-start.20 = (bf16[16,4096]{1,0:T(8,128)(2,1)S(1)}, bf16[16,4096]{1,0:T(8,128)(2,1)S(1)}, u32[]{:S(2)}, u32[]{:S(2)}) collective-permute-start(bf16[16,4096]{1,0:T(8,128)(2,1)S(1)} %fusion.7), channel_id=1, source_target_pairs={{0,8},{1,9},{2,10},{3,11},{4,12},{5,13},{6,14},{7,15},{8,0},{9,1},... | collective-permute-start | bytes 393224 | tf_op jit(solution)/shard_map/ppermute | solution.py:173
  69.9 7.4 %collective-permute-start.23 = (bf16[32,4096]{1,0:T(8,128)(2,1)S(1)}, bf16[32,4096]{1,0:T(8,128)(2,1)S(1)}, u32[]{:S(2)}, u32[]{:S(2)}) collective-permute-start(bf16[32,4096]{1,0:T(8,128)(2,1)S(1)} %fusion.2), channel_id=1, source_target_pairs={{0,2},{1,3},{2,0},{3,1},{4,6},{5,7},{6,4},{7,5},{8,10},{9,11},{10,... | collective-permute-start | bytes 786440 | tf_op jit(solution)/shard_map/ppermute | solution.py:170
  74.3 7.4 %collective-permute-start.25 = (bf16[16,4096]{1,0:T(8,128)(2,1)S(1)}, bf16[16,4096]{1,0:T(8,128)(2,1)S(1)}, u32[]{:S(2)}, u32[]{:S(2)}) collective-permute-start(bf16[16,4096]{1,0:T(8,128)(2,1)S(1)} %slice_add_fusion.9), channel_id=1, source_target_pairs={{0,8},{1,9},{2,10},{3,11},{4,12},{5,13},{6,14},{7,15},{8,0},{9,1},... | collective-permute-start | bytes 393224 | tf_op jit(solution)/shard_map/ppermute | solution.py:173
  77.4 5.9 %collective-permute-start.26 = (bf16[16,4096]{1,0:T(8,128)(2,1)S(1)}, bf16[16,4096]{1,0:T(8,128)(2,1)S(1)}, u32[]{:S(2)}, u32[]{:S(2)}) collective-permute-start(bf16[16,4096]{1,0:T(8,128)(2,1)S(1)} %slice.176), channel_id=1, source_target_pairs={{0,4},{1,5},{2,6},{3,7},{4,0},{5,1},{6,2},{7,3},{8,12},{9,13},{10,... | collective-permute-start | bytes 393224 | tf_op jit(solution)/shard_map/ppermute | solution.py:173
